TPU v7x, 32 devices: a whole 2x2x4 slice. The times are simulated.
32 devices in a mesh: dp: 16 (over z, y, x), tensor: 2 (over core).
Axes of the slice: x: 2, y: 2, z: 4, core: 2. Of those that a mesh axis runs over, the one named last changes fastest.
Arguments:
- layer_input: bfloat16 [8192, 2048], P(('dp', 'tensor')), may hold values from -6 to 6
- attn_norm: float32 [2048], replicated, may hold values from 0.5 to 1.5
- head_norms: float32 [2, 128], replicated, may hold values from 0.1 to 1.9
- query_weight: bfloat16 [2048, 2048], P('dp', 'tensor'), may hold values from -0.125 to 0.125
- key_matrix: bfloat16 [2048, 1024], P('dp', 'tensor'), may hold values from -0.125 to 0.125
- value_matrix: bfloat16 [2048, 1024], P('dp', 'tensor'), may hold values from -0.125 to 0.125
- output_weight: bfloat16 [2048, 2048], P(('tensor', 'dp')), may hold values from -1 to 1
- mlp_norm: float32 [2048], replicated, may hold values from 0.5 to 1.5
- gate_weight: bfloat16 [2048, 6144], P('dp', 'tensor'), may hold values from -0.125 to 0.125
- up_weight: bfloat16 [2048, 6144], P('dp', 'tensor'), may hold values from -0.125 to 0.125
- down_weight: bfloat16 [6144, 2048], P(('tensor', 'dp')), may hold values from -0.078125 to 0.078125
- grad_out: bfloat16 [8192, 2048], P(('dp', 'tensor')), may hold values from -6 to 6
- doc_lengths: int32 [16, 6], P('dp'), may hold values from 1 to 384, 512 in all within a row
Outputs:
- layer_out: bfloat16 [8192, 2048], P(('dp', 'tensor'))
- grad_input: float32 [8192, 2048], P(('dp', 'tensor'))
- grad_attn_norm: float32 [2048], replicated
- grad_head_norms: float32 [2, 128], replicated
- grad_query: float32 [2048, 2048], P('dp', 'tensor')
- grad_key: float32 [2048, 1024], P('dp', 'tensor')
- grad_value: float32 [2048, 1024], P('dp', 'tensor')
- grad_out_proj: float32 [2048, 2048], P(('tensor', 'dp'))
- grad_mlp_norm: float32 [2048], replicated
- grad_gate: float32 [2048, 6144], P('dp', 'tensor')
- grad_up: float32 [2048, 6144], P('dp', 'tensor')
- grad_down: float32 [6144, 2048], P(('tensor', 'dp'))
Inputs may be any that keep to these rules, and one draw needn't show every extreme that they name: `doc_lengths`: in every bucket the 6 lengths sum to 512 and the longest is exactly 384.
All inputs are finite; a program needn't handle non-finite values.
Results may differ from a plain program's by a relative error of at most 0.018.
Values may be sent and summed in bfloat16 or wider, within the bound.
A program may use at most 256 MiB of HBM per device.

v0:
```python
import jax
import jax.numpy as jnp
from jax import lax
from jax.sharding import PartitionSpec as P

QUERY_HEADS = 16
KEY_VALUE_HEADS = 8
HEAD_SIZE = 128


EPS = 1e-06
ROPE_BASE = 1000000.0
MASKED = -1e30


def matmul(left_mat, right_mat):
    return jnp.dot(left_mat, right_mat, preferred_element_type=jnp.float32)


def matmul_tn(left_mat, right_mat):
    return lax.dot_general(
        left_mat, right_mat, (((0,), (0,)), ((), ())), preferred_element_type=jnp.float32
    )


def matmul_nt(left_mat, right_mat):
    return lax.dot_general(
        left_mat, right_mat, (((1,), (1,)), ((), ())), preferred_element_type=jnp.float32
    )


def inv_rms(values):
    return lax.rsqrt(jnp.mean(values * values, axis=-1, keepdims=True) + EPS)


def norm_back(values, scales, gain_row, upstream):
    weighted = upstream * gain_row
    inner_mean = jnp.mean(weighted * values, axis=-1, keepdims=True)
    value_grad = scales * weighted - values * (scales * scales * scales) * inner_mean
    lead_axes = tuple(range(upstream.ndim - 1))
    return (value_grad, jnp.sum(upstream * values * scales, axis=lead_axes))


def rope_tables(position, head_width):
    half_dim = head_width // 2
    inverse = ROPE_BASE ** (-(jnp.arange(half_dim, dtype=jnp.float32) * (2.0 / head_width)))
    angles = position.astype(jnp.float32)[:, None] * inverse[None, :]
    return (jnp.cos(angles), jnp.sin(angles))


def rotate(values, cos_tab, sin_tab, direction):
    half_dim = values.shape[-1] // 2
    first_half = values[..., :half_dim]
    second_half = values[..., half_dim:]
    cosine = cos_tab[:, None, :]
    sine_tab = direction * sin_tab[:, None, :]
    return jnp.concatenate(
        [
            first_half * cosine - second_half * sine_tab,
            second_half * cosine + first_half * sine_tab,
        ],
        axis=-1,
    )


def doc_layout(lengths_row, group_rows):
    doc_ends = jnp.cumsum(lengths_row, dtype=jnp.int32)
    row_ids = jnp.arange(group_rows, dtype=jnp.int32)
    document_segment = jnp.sum(
        (row_ids[:, None] >= doc_ends[None, :]).astype(jnp.int32), axis=1, dtype=jnp.int32
    )
    doc_starts = doc_ends - lengths_row
    member = document_segment[:, None] == jnp.arange(lengths_row.shape[0], dtype=jnp.int32)[None, :]
    start_of = jnp.sum(jnp.where(member, doc_starts[None, :], 0), axis=1, dtype=jnp.int32)
    return (document_segment, row_ids - start_of)


def gather_rows(block_low):
    return lax.all_gather(block_low, "tensor", axis=0, tiled=True)


def sum_rows(partial_sum):
    return lax.psum_scatter(
        partial_sum.astype(jnp.bfloat16), "tensor", scatter_dimension=0, tiled=True
    ).astype(jnp.float32)


def shards(
    layer_input,
    attn_norm,
    head_norms,
    query_weight,
    key_matrix,
    value_matrix,
    output_weight,
    mlp_norm,
    gate_weight,
    up_weight,
    down_weight,
    grad_out,
    doc_lengths,
):
    tensor_extent = lax.axis_size("tensor")
    q_heads = QUERY_HEADS // tensor_extent
    key_value_heads = KEY_VALUE_HEADS // tensor_extent
    group_list = QUERY_HEADS // KEY_VALUE_HEADS
    local_rows = layer_input.shape[0]
    group_rows = local_rows * tensor_extent
    document_segment, position = doc_layout(doc_lengths[0], group_rows)
    cos_tab, sin_tab = rope_tables(position, HEAD_SIZE)
    row_ids = jnp.arange(group_rows, dtype=jnp.int32)
    allowed = (
        (document_segment[:, None] == document_segment[None, :])
        & (row_ids[None, :] <= row_ids[:, None])
    )[None, None]
    score_scale = HEAD_SIZE ** (-0.5)
    input_float = layer_input.astype(jnp.float32)
    scale_attn = inv_rms(input_float)
    normed_attn = gather_rows((input_float * scale_attn * attn_norm).astype(jnp.bfloat16))
    pieces = (
        lax.all_gather(query_weight, "dp", axis=0, tiled=True),
        lax.all_gather(key_matrix, "dp", axis=0, tiled=True),
        lax.all_gather(value_matrix, "dp", axis=0, tiled=True),
    )
    columns = normed_attn
    query_raw = matmul(columns, pieces[0])
    key_unnormed = matmul(columns, pieces[1])
    value_raw = matmul(columns, pieces[2])
    values_reduced = value_raw.astype(jnp.bfloat16).reshape(group_rows, key_value_heads, HEAD_SIZE)
    query_h = query_raw.reshape(group_rows, q_heads, HEAD_SIZE)
    key_per_head = key_unnormed.reshape(group_rows, key_value_heads, HEAD_SIZE)
    scale_query = inv_rms(query_h)
    scale_key = inv_rms(key_per_head)
    query_rows = (
        rotate(query_h * scale_query * head_norms[0], cos_tab, sin_tab, 1.0)
        .astype(jnp.bfloat16)
        .reshape(group_rows, key_value_heads, group_list, HEAD_SIZE)
    )
    keys_reduced = rotate(key_per_head * scale_key * head_norms[1], cos_tab, sin_tab, 1.0).astype(
        jnp.bfloat16
    )
    scores = (
        jnp.einsum("qkgd,tkd->kgqt", query_rows, keys_reduced, preferred_element_type=jnp.float32)
        * score_scale
    )
    masked = jnp.where(allowed, scores, MASKED)
    row_peak = jnp.max(masked, axis=-1, keepdims=True)
    exponent = jnp.exp(masked - row_peak)
    row_total = jnp.sum(exponent, axis=-1, keepdims=True)
    log_total = row_peak + jnp.log(row_total)
    probs_low = (exponent / row_total).astype(jnp.bfloat16)
    attended = jnp.einsum(
        "kgqt,tkd->qkgd", probs_low, values_reduced, preferred_element_type=jnp.float32
    )
    attended_low = attended.reshape(group_rows, q_heads * HEAD_SIZE).astype(jnp.bfloat16)
    projected = matmul(attended_low, lax.all_gather(output_weight, "dp", axis=0, tiled=True))
    hidden_state = input_float + sum_rows(projected)
    scale_mlp = inv_rms(hidden_state)
    normed_mlp = gather_rows((hidden_state * scale_mlp * mlp_norm).astype(jnp.bfloat16))
    pieces = (
        lax.all_gather(gate_weight, "dp", axis=0, tiled=True),
        lax.all_gather(up_weight, "dp", axis=0, tiled=True),
    )
    columns = normed_mlp
    gate_raw = matmul(columns, pieces[0])
    up_raw = matmul(columns, pieces[1])
    activated = jax.nn.silu(gate_raw)
    inner_low = (activated * up_raw).astype(jnp.bfloat16)
    mlp_part = matmul(inner_low, lax.all_gather(down_weight, "dp", axis=0, tiled=True))
    layer_out = (hidden_state + sum_rows(mlp_part)).astype(jnp.bfloat16)
    grad_all = gather_rows(grad_out)
    inner_grad = matmul_nt(grad_all, lax.all_gather(down_weight, "dp", axis=0, tiled=True))
    sigmoid_gate = jax.nn.sigmoid(gate_raw)
    gate_grad = (
        inner_grad * up_raw * sigmoid_gate * (1.0 + gate_raw * (1.0 - sigmoid_gate))
    ).astype(jnp.bfloat16)
    up_grad = (inner_grad * activated).astype(jnp.bfloat16)
    pieces = lax.all_gather((gate_weight, up_weight), "dp", axis=0, tiled=True)
    mlp_grad = matmul_nt(gate_grad, pieces[0]) + matmul_nt(up_grad, pieces[1])
    hidden_norm_grad, mlp_gain_part = norm_back(
        hidden_state, scale_mlp, mlp_norm, sum_rows(mlp_grad)
    )
    hidden_grad = grad_out.astype(jnp.float32) + hidden_norm_grad
    branch_grad = gather_rows(hidden_grad.astype(jnp.bfloat16))
    attended_grad = matmul_nt(branch_grad, lax.all_gather(output_weight, "dp", axis=0, tiled=True))
    attended_grad = attended_grad.astype(jnp.bfloat16).reshape(
        group_rows, key_value_heads, group_list, HEAD_SIZE
    )
    scores_again = (
        jnp.einsum("qkgd,tkd->kgqt", query_rows, keys_reduced, preferred_element_type=jnp.float32)
        * score_scale
    )
    probs = jnp.exp(jnp.where(allowed, scores_again, MASKED) - log_total)
    probs_grad = jnp.einsum(
        "qkgd,tkd->kgqt", attended_grad, values_reduced, preferred_element_type=jnp.float32
    )
    scores_grad = (
        probs * (probs_grad - jnp.sum(probs * probs_grad, axis=-1, keepdims=True))
    ).astype(jnp.bfloat16)
    query_grad = (
        jnp.einsum(
            "kgqt,tkd->qkgd", scores_grad, keys_reduced, preferred_element_type=jnp.float32
        ).reshape(group_rows, q_heads, HEAD_SIZE)
        * score_scale
    )
    key_grad = (
        jnp.einsum("kgqt,qkgd->tkd", scores_grad, query_rows, preferred_element_type=jnp.float32)
        * score_scale
    )
    value_grad = jnp.einsum(
        "kgqt,qkgd->tkd",
        probs.astype(jnp.bfloat16),
        attended_grad,
        preferred_element_type=jnp.float32,
    )
    query_raw_grad, query_gain_part = norm_back(
        query_h, scale_query, head_norms[0], rotate(query_grad, cos_tab, sin_tab, -1.0)
    )
    key_raw_grad, key_gain_part = norm_back(
        key_per_head, scale_key, head_norms[1], rotate(key_grad, cos_tab, sin_tab, -1.0)
    )
    query_low_grad = query_raw_grad.reshape(group_rows, q_heads * HEAD_SIZE).astype(jnp.bfloat16)
    key_low_grad = key_raw_grad.reshape(group_rows, key_value_heads * HEAD_SIZE).astype(
        jnp.bfloat16
    )
    value_low_grad = value_grad.reshape(group_rows, key_value_heads * HEAD_SIZE).astype(
        jnp.bfloat16
    )
    pieces = lax.all_gather((query_weight, key_matrix, value_matrix), "dp", axis=0, tiled=True)
    attn_grad = (
        matmul_nt(query_low_grad, pieces[0])
        + matmul_nt(key_low_grad, pieces[1])
        + matmul_nt(value_low_grad, pieces[2])
    )
    input_norm_grad, attn_gain_part = norm_back(
        input_float, scale_attn, attn_norm, sum_rows(attn_grad)
    )
    grad_input = hidden_grad + input_norm_grad
    weight_sums = (
        lax.psum_scatter(
            matmul_tn(normed_attn, query_low_grad), "dp", scatter_dimension=0, tiled=True
        ),
        lax.psum_scatter(
            matmul_tn(normed_attn, key_low_grad), "dp", scatter_dimension=0, tiled=True
        ),
        lax.psum_scatter(
            matmul_tn(normed_attn, value_low_grad), "dp", scatter_dimension=0, tiled=True
        ),
        lax.psum_scatter(
            matmul_tn(attended_low, branch_grad), "dp", scatter_dimension=0, tiled=True
        ),
        lax.psum_scatter(matmul_tn(normed_mlp, gate_grad), "dp", scatter_dimension=0, tiled=True),
        lax.psum_scatter(matmul_tn(normed_mlp, up_grad), "dp", scatter_dimension=0, tiled=True),
        lax.psum_scatter(matmul_tn(inner_low, grad_all), "dp", scatter_dimension=0, tiled=True),
    )
    gain_sums = lax.psum(
        (attn_gain_part, jnp.stack([query_gain_part, key_gain_part]), mlp_gain_part),
        ("dp", "tensor"),
    )
    return (
        layer_out,
        grad_input,
        gain_sums[0],
        gain_sums[1],
        weight_sums[0],
        weight_sums[1],
        weight_sums[2],
        weight_sums[3],
        gain_sums[2],
        weight_sums[4],
        weight_sums[5],
        weight_sums[6],
    )


def solution(mesh):
    return jax.shard_map(
        shards,
        mesh=mesh,
        in_specs=(
            P(("dp", "tensor"), None),
            P(),
            P(),
            P("dp", "tensor"),
            P("dp", "tensor"),
            P("dp", "tensor"),
            P(("tensor", "dp"), None),
            P(),
            P("dp", "tensor"),
            P("dp", "tensor"),
            P(("tensor", "dp"), None),
            P(("dp", "tensor"), None),
            P("dp", None),
        ),
        out_specs=(
            P(("dp", "tensor"), None),
            P(("dp", "tensor"), None),
            P(),
            P(),
            P("dp", "tensor"),
            P("dp", "tensor"),
            P("dp", "tensor"),
            P(("tensor", "dp"), None),
            P(),
            P("dp", "tensor"),
            P("dp", "tensor"),
            P(("tensor", "dp"), None),
        ),
        check_vma=False,
    )
```

profile of v0, /device:TPU:0, one launch (start us, length us, event | category | flops | bytes accessed | tf_op | source)
XLA Modules:
  0.0 2630.5 jit_solution(6193960844782840600)
XLA Ops:
  25.3 64.7 %all-gather.16.cloned.1.call-done = bf16[2048,512]{1,0:T(8,128)(2,1)} async-done(((bf16[128,512]{1,0:T(8,128)(2,1)}), bf16[2048,512]{1,0:T(8,128)(2,1)}) %all-gather.16.cloned.1.call-update) | async-done | bytes 2097168 | tf_op jit(solution)/shard_map/all_gather | solution.py:122
  95.7 56.5 %all-gather.14.cloned.1.call-done = bf16[2048,512]{1,0:T(8,128)(2,1)} async-done(((bf16[128,512]{1,0:T(8,128)(2,1)}), bf16[2048,512]{1,0:T(8,128)(2,1)}) %all-gather.14.cloned.1.call-update) | async-done | bytes 2097168 | tf_op jit(solution)/shard_map/all_gather | solution.py:123
  155.8 73.7 %all-gather.18.cloned.1.call-done = bf16[2048,1024]{1,0:T(8,128)(2,1)} async-done(((bf16[128,1024]{1,0:T(8,128)(2,1)}), bf16[2048,1024]{1,0:T(8,128)(2,1)}) %all-gather.18.cloned.1.call-update) | async-done | bytes 4194320 | tf_op jit(solution)/shard_map/all_gather | solution.py:121
  249.8 57.1 %all-gather.20.cloned.1.call-done = bf16[1024,2048]{1,0:T(8,128)(2,1)} async-done(((bf16[64,2048]{1,0:T(8,128)(2,1)}), bf16[1024,2048]{1,0:T(8,128)(2,1)}) %all-gather.20.cloned.1.call-update) | async-done | bytes 4194320 | tf_op jit(solution)/shard_map/all_gather | solution.py:156
  336.4 156.4 %all-gather.24.cloned.1.call-done = bf16[2048,3072]{1,0:T(8,128)(2,1)} async-done(((bf16[128,3072]{1,0:T(8,128)(2,1)}), bf16[2048,3072]{1,0:T(8,128)(2,1)}) %all-gather.24.cloned.1.call-update) | async-done | bytes 12582928 | tf_op jit(solution)/shard_map/all_gather | solution.py:161
  492.8 12.2 fusion.53
  505.0 141.2 %all-gather.26.cloned.1.call-done = bf16[2048,3072]{1,0:T(8,128)(2,1)} async-done(((bf16[128,3072]{1,0:T(8,128)(2,1)}), bf16[2048,3072]{1,0:T(8,128)(2,1)}) %all-gather.26.cloned.1.call-update) | async-done | bytes 12582928 | tf_op jit(solution)/shard_map/all_gather | solution.py:162
  646.2 12.0 fusion.54
  658.2 154.7 %all-gather.28.cloned.1.call-done = bf16[3072,2048]{1,0:T(8,128)(2,1)} async-done(((bf16[192,2048]{1,0:T(8,128)(2,1)}), bf16[3072,2048]{1,0:T(8,128)(2,1)}) %all-gather.28.cloned.1.call-update) | async-done | bytes 12582928 | tf_op jit(solution)/shard_map/all_gather | solution.py:169
  812.8 17.4 multiply_convert_fusion
  830.2 12.1 fusion.55
  842.3 13.5 add_convert_fusion.1
  868.6 11.0 all-gather.32.cloned.1.call-done
  934.6 11.6 convolution_convert_fusion
  973.4 14.0 fusion.62
  987.5 14.0 fusion.63
  1001.7 14.0 fusion.64
  1018.2 43.6 %all-reduce = (f32[2048]{0:T(1024)}, f32[2,128]{1,0:T(2,128)}, f32[2048]{0:T(1024)}) all-reduce(f32[2048]{0:T(1024)S(1)} %get-tuple-element.14, f32[2,128]{1,0:T(2,128)S(1)} %pad_maximum_fusion.5, f32[2048]{0:T(1024)S(1)} %get-tuple-element.12), channel_id=1, replica_groups=mesh['dp'=16,'tensor'=2] {'dp','tensor'}, use_global_device_ids=true, to_apply=%region_19.20 | all-reduce | flops 4352 | bytes 34816 | tf_op jit(solution)/shard_map/psum | solution.py:256
  1067.0 88.9 %reduce-scatter.24.cloned.1.call-done = f32[128,512]{1,0:T(8,128)} async-done(((f32[2048,512]{1,0:T(8,128)}), f32[128,512]{1,0:T(8,128)}) %reduce-scatter.24.cloned.1.call-update) | async-done | bytes 262160 | tf_op jit(solution)/shard_map/reduce_scatter | solution.py:246
  1156.0 180.2 %reduce-scatter.20.cloned.1.call-done = f32[128,1024]{1,0:T(8,128)} async-done(((f32[2048,1024]{1,0:T(8,128)}), f32[128,1024]{1,0:T(8,128)}) %reduce-scatter.20.cloned.1.call-update) | async-done | bytes 524304 | tf_op jit(solution)/shard_map/reduce_scatter | solution.py:240
  1336.2 183.1 %reduce-scatter.26.cloned.1.call-done = f32[64,2048]{1,0:T(8,128)} async-done(((f32[1024,2048]{1,0:T(8,128)}), f32[64,2048]{1,0:T(8,128)}) %reduce-scatter.26.cloned.1.call-update) | async-done | bytes 524304 | tf_op jit(solution)/shard_map/reduce_scatter | solution.py:249
  1519.3 370.2 %reduce-scatter.28.cloned.1.call-done = f32[128,3072]{1,0:T(8,128)} async-done(((f32[2048,3072]{1,0:T(8,128)}), f32[128,3072]{1,0:T(8,128)}) %reduce-scatter.28.cloned.1.call-update) | async-done | bytes 1572880 | tf_op jit(solution)/shard_map/reduce_scatter | solution.py:252
  1889.5 367.0 %reduce-scatter.30.cloned.1.call-done = f32[128,3072]{1,0:T(8,128)} async-done(((f32[2048,3072]{1,0:T(8,128)}), f32[128,3072]{1,0:T(8,128)}) %reduce-scatter.30.cloned.1.call-update) | async-done | bytes 1572880 | tf_op jit(solution)/shard_map/reduce_scatter | solution.py:253
  2256.5 367.0 %reduce-scatter.32.cloned.1.call-done = f32[192,2048]{1,0:T(8,128)} async-done(((f32[3072,2048]{1,0:T(8,128)}), f32[192,2048]{1,0:T(8,128)}) %reduce-scatter.32.cloned.1.call-update) | async-done | bytes 1572880 | tf_op jit(solution)/shard_map/reduce_scatter | solution.py:254
  (240 shorter events, 179.3 us)
Async XLA Ops:
  7.2 18.1 all-gather.12.cloned.1.call-start
  11.9 78.1 %all-gather.16.cloned.1.call-start = ((), (), s32[]{:S(2)}) async-start(), calls=%async_computation.13 | async-start | bytes 2228224 | tf_op jit(solution)/shard_map/all_gather | solution.py:122
  12.6 139.5 %all-gather.14.cloned.1.call-start = ((), (), s32[]{:S(2)}) async-start(), calls=%async_computation.12 | async-start | bytes 2228224 | tf_op jit(solution)/shard_map/all_gather | solution.py:123
  13.4 216.2 %all-gather.18.cloned.1.call-start = ((), (), s32[]{:S(2)}) async-start(), calls=%async_computation.14 | async-start | bytes 4456448 | tf_op jit(solution)/shard_map/all_gather | solution.py:121
  13.9 293.0 %all-gather.20.cloned.1.call-start = ((), (), s32[]{:S(2)}) async-start(), calls=%async_computation.15 | async-start | bytes 4456448 | tf_op jit(solution)/shard_map/all_gather | solution.py:156
  14.5 306.7 %reduce-scatter.12.cloned.1.call-start = ((), (), s32[]{:S(2)}) async-start(), calls=%async_computation.16 | async-start | bytes 3145728 | tf_op jit(solution)/shard_map/reduce_scatter | solution.py:83
  17.7 222.8 %copy-start.19 = (f32[512,64]{1,0:T(8,128)}, f32[512,64]{1,0:T(8,128)S(1)}, u32[]{:S(2)}) copy-start(f32[512,64]{1,0:T(8,128)S(1)} %get-tuple-element.48) | copy-start | bytes 393220
  95.7 146.1 %copy-start.22 = (bf16[512,4,64]{2,0,1:T(8,128)(2,1)}, bf16[512,4,64]{2,0,1:T(8,128)(2,1)S(1)}, u32[]{:S(2)}) copy-start(bf16[512,4,64]{2,0,1:T(8,128)(2,1)S(1)} %get-tuple-element.40) | copy-start | bytes 786436
  312.8 23.6 all-gather.22.cloned.1.call-start
  324.5 168.3 %all-gather.24.cloned.1.call-start = ((), (), s32[]{:S(2)}) async-start(), calls=%async_computation.18 | async-start | bytes 13369344 | tf_op jit(solution)/shard_map/all_gather | solution.py:161
  325.3 320.9 %all-gather.26.cloned.1.call-start = ((), (), s32[]{:S(2)}) async-start(), calls=%async_computation.19 | async-start | bytes 13369344 | tf_op jit(solution)/shard_map/all_gather | solution.py:162
  326.0 332.1 %all-gather.30.cloned.1.call-start = ((), (), s32[]{:S(2)}) async-start(), calls=%async_computation.22 | async-start | bytes 3145728 | tf_op jit(solution)/shard_map/all_gather | solution.py:79
  326.6 486.2 %all-gather.28.cloned.1.call-start = ((), (), s32[]{:S(2)}) async-start(), calls=%async_computation.20 | async-start | bytes 13369344 | tf_op jit(solution)/shard_map/all_gather | solution.py:169
  327.3 536.4 %reduce-scatter.16.cloned.1.call-start = ((), (), s32[]{:S(2)}) async-start(), calls=%async_computation.23 | async-start | bytes 3145728 | tf_op jit(solution)/shard_map/reduce_scatter | solution.py:83
  855.8 23.8 all-gather.32.cloned.1.call-start
  867.7 148.1 %reduce-scatter.18.cloned.1.call-start = ((), (), s32[]{:S(2)}) async-start(), calls=%async_computation.25 | async-start | bytes 3145728 | tf_op jit(solution)/shard_map/reduce_scatter | solution.py:83
  934.5 127.4 %reduce-scatter.14.cloned.1.call-start = ((), (), s32[]{:S(2)}) async-start(), calls=%async_computation.21 | async-start | bytes 3145728 | tf_op jit(solution)/shard_map/reduce_scatter | solution.py:83
  946.2 120.9 %reduce-scatter.22.cloned.1.call-start = ((), (), s32[]{:S(2)}) async-start(), calls=%async_computation.27 | async-start | bytes 4456448 | tf_op jit(solution)/shard_map/reduce_scatter | solution.py:243
  951.2 204.8 %reduce-scatter.24.cloned.1.call-start = ((), (), s32[]{:S(2)}) async-start(), calls=%async_computation.28 | async-start | bytes 4456448 | tf_op jit(solution)/shard_map/reduce_scatter | solution.py:246
  956.2 380.0 %reduce-scatter.20.cloned.1.call-start = ((), (), s32[]{:S(2)}) async-start(), calls=%async_computation.26 | async-start | bytes 8912896 | tf_op jit(solution)/shard_map/reduce_scatter | solution.py:240
  964.9 554.4 %reduce-scatter.26.cloned.1.call-start = ((), (), s32[]{:S(2)}) async-start(), calls=%async_computation.29 | async-start | bytes 8912896 | tf_op jit(solution)/shard_map/reduce_scatter | solution.py:249
  973.3 916.2 %reduce-scatter.28.cloned.1.call-start = ((), (), s32[]{:S(2)}) async-start(), calls=%async_computation.30 | async-start | bytes 26738688 | tf_op jit(solution)/shard_map/reduce_scatter | solution.py:252
  987.4 1269.0 %reduce-scatter.30.cloned.1.call-start = ((), (), s32[]{:S(2)}) async-start(), calls=%async_computation.31 | async-start | bytes 26738688 | tf_op jit(solution)/shard_map/reduce_scatter | solution.py:253
  1001.5 1622.0 %reduce-scatter.32.cloned.1.call-start = ((), (), s32[]{:S(2)}) async-start(), calls=%async_computation.32 | async-start | bytes 26738688 | tf_op jit(solution)/shard_map/reduce_scatter | solution.py:254
  (52 other events, 506.0 us)
Sparse Core Ops, SparseCore 0:
  12.0 13.2 all-gather.11
  28.1 61.8 all-gather.15
  92.8 59.3 all-gather.13
  154.8 74.7 all-gather.17
  232.2 74.6 all-gather.19
  313.0 8.2 reduce-scatter.11
  324.6 11.7 all-gather.21
  339.6 153.1 all-gather.23
  495.9 150.1 all-gather.25
  647.6 8.7 all-gather.29
  659.6 153.1 all-gather.27
  855.9 7.7 reduce-scatter.15
  867.8 11.7 all-gather.31
  934.6 10.7 reduce-scatter.17
  947.6 10.7 reduce-scatter.13
  961.2 97.0 reduce-scatter.21
  1061.0 94.9 reduce-scatter.23
  1158.7 177.4 reduce-scatter.19
  1339.0 180.2 reduce-scatter.25
  1525.5 363.9 reduce-scatter.27
  1895.8 360.6 reduce-scatter.29
  2262.8 360.6 reduce-scatter.31
where the time goes:
time: 2640 us; the launch traced here: 2630 us
  waiting for transfers between devices  2310 us (88%)
  matrix products  191 us (7%)
  other arithmetic  43.7 us (2%)
  blocking collectives  43.6 us (2%)
    reduce_scatter x1, waiting for transfers between devices, shards(): lax.psum_scatter(matmul_tn(normed_mlp, gate_grad), 'dp', scatter_dimensio...  370 us
    reduce_scatter x1, waiting for transfers between devices, shards(): lax.psum_scatter(matmul_tn(inner_low, grad_all), 'dp', scatter_dimension=...  367 us
    reduce_scatter x1, waiting for transfers between devices, shards(): lax.psum_scatter(matmul_tn(normed_mlp, up_grad), 'dp', scatter_dimension=...  367 us
    reduce_scatter x1, waiting for transfers between devices, shards(): lax.psum_scatter(matmul_tn(attended_low, branch_grad), 'dp', scatter_dime...  183 us
    reduce_scatter x1, waiting for transfers between devices, shards(): lax.psum_scatter(matmul_tn(normed_attn, query_low_grad), 'dp', scatter_di...  180 us
    all_gather x1, waiting for transfers between devices, shards(): lax.all_gather(gate_weight, 'dp', axis=0, tiled=True)  156 us
    all_gather x1, waiting for transfers between devices, shards(): lax.all_gather(down_weight, 'dp', axis=0, tiled=True)  155 us
    all_gather x1, waiting for transfers between devices, shards(): lax.all_gather(up_weight, 'dp', axis=0, tiled=True)  141 us
  transfers between devices with their start and end apart: 22, of which 18 were waited for; matrix products, arithmetic and copies ran while one was open for 5% of the time, Pallas kernels for 0%

commit v1 on v0

v1 whole, which is shorter than its diff:
```python
import jax
import jax.numpy as jnp
from jax import lax
from jax.sharding import Mesh, PartitionSpec as P

QUERY_HEADS = 16
KEY_VALUE_HEADS = 8
HEAD_SIZE = 128


EPS = 1e-06
ROPE_BASE = 1000000.0
MASKED = -1e30
LOW = jnp.bfloat16


def matmul(left_mat, right_mat):
    return jnp.dot(left_mat, right_mat, preferred_element_type=jnp.float32)


def matmul_tn(left_mat, right_mat):
    return lax.dot_general(
        left_mat, right_mat, (((0,), (0,)), ((), ())), preferred_element_type=jnp.float32
    )


def matmul_nt(left_mat, right_mat):
    return lax.dot_general(
        left_mat, right_mat, (((1,), (1,)), ((), ())), preferred_element_type=jnp.float32
    )


def inv_rms(values):
    return lax.rsqrt(jnp.mean(values * values, axis=-1, keepdims=True) + EPS)


def norm_back(values, scales, gain_row, upstream):
    weighted = upstream * gain_row
    inner_mean = jnp.mean(weighted * values, axis=-1, keepdims=True)
    value_grad = scales * weighted - values * (scales * scales * scales) * inner_mean
    lead_axes = tuple(range(upstream.ndim - 1))
    return (value_grad, jnp.sum(upstream * values * scales, axis=lead_axes))


def rope_tables(position, head_width):
    half_dim = head_width // 2
    inverse = ROPE_BASE ** (-(jnp.arange(half_dim, dtype=jnp.float32) * (2.0 / head_width)))
    angles = position.astype(jnp.float32)[:, None] * inverse[None, :]
    return (jnp.cos(angles), jnp.sin(angles))


def rotate(values, cos_tab, sin_tab, direction):
    half_dim = values.shape[-1] // 2
    first_half = values[..., :half_dim]
    second_half = values[..., half_dim:]
    cosine = cos_tab[:, None, :]
    sine_tab = direction * sin_tab[:, None, :]
    return jnp.concatenate(
        [
            first_half * cosine - second_half * sine_tab,
            second_half * cosine + first_half * sine_tab,
        ],
        axis=-1,
    )


def doc_layout(lengths_row, row_ids):
    doc_ends = jnp.cumsum(lengths_row, dtype=jnp.int32)
    document_segment = jnp.sum(
        (row_ids[:, None] >= doc_ends[None, :]).astype(jnp.int32), axis=1, dtype=jnp.int32
    )
    doc_starts = doc_ends - lengths_row
    member = document_segment[:, None] == jnp.arange(lengths_row.shape[0], dtype=jnp.int32)[None, :]
    start_of = jnp.sum(jnp.where(member, doc_starts[None, :], 0), axis=1, dtype=jnp.int32)
    return (document_segment, row_ids - start_of)


def f32(values):
    return values.astype(jnp.float32)


def low(values):
    return values.astype(LOW)


def swap(block, axis):
    return lax.ppermute(block, axis, [(0, 1), (1, 0)])


def plane_index():
    return 2 * lax.axis_index("ty") + lax.axis_index("tx")


def plane_gather(block):
    half = block.shape[0] // 2
    across_x = swap(block, "tx")
    across_y = swap(block, "ty")
    far = jnp.concatenate([swap(across_y[:half], "tx"), swap(across_x[half:], "ty")])
    return [block, across_x, across_y, far]


def plane_scatter(parts):
    own, for_x, for_y, for_far = parts
    half = own.shape[0] // 2
    pass_y = swap(for_far[:half], "tx")
    pass_x = swap(for_far[half:], "ty")
    x_top = swap(for_x[:half], "tx")
    y_end = swap(for_y[half:], "ty")
    y_top = swap(low(f32(for_y[:half]) + f32(pass_y)), "ty")
    x_end = swap(low(f32(for_x[half:]) + f32(pass_x)), "tx")
    return jnp.concatenate(
        [
            f32(own[:half]) + f32(x_top) + f32(y_top),
            f32(own[half:]) + f32(x_end) + f32(y_end),
        ]
    )


def plane_exchange(parts):
    own, for_x, for_y, for_far = parts
    half = own.shape[0] // 2
    far = jnp.concatenate(
        [
            swap(swap(for_far[:half], "tx"), "ty"),
            swap(swap(for_far[half:], "ty"), "tx"),
        ]
    )
    return [own, swap(for_x, "tx"), swap(for_y, "ty"), far]


def line_gather(block):
    extent = lax.axis_size("f")
    if extent != 4:
        return lax.all_gather(block, "f", axis=0)
    place = lax.axis_index("f")
    two_away = lax.ppermute(block, "f", [(0, 2), (2, 0), (1, 3), (3, 1)])
    above = lax.ppermute(block, "f", [(1, 0), (2, 1), (3, 2)])
    below = lax.ppermute(block, "f", [(0, 1), (1, 2), (2, 3)])
    passed = lax.ppermute(two_away, "f", [(1, 0), (2, 3)])
    blocks = [
        block,
        jnp.where(place == 3, passed, above),
        two_away,
        jnp.where(place == 0, passed, below),
    ]
    whole = jnp.zeros((4,) + block.shape, block.dtype)
    for step in range(4):
        whole = lax.dynamic_update_index_in_dim(whole, blocks[step], (place + step) % 4, 0)
    return whole


def line_scatter(parts):
    extent = lax.axis_size("f")
    if extent != 4:
        return f32(lax.psum_scatter(parts, "f", scatter_dimension=0))
    place = lax.axis_index("f")
    part = [
        lax.dynamic_index_in_dim(parts, (place + step) % 4, 0, keepdims=False) for step in range(4)
    ]
    passed = lax.ppermute(jnp.where(place == 0, part[3], part[1]), "f", [(0, 1), (3, 2)])
    above = lax.ppermute(part[3], "f", [(1, 0), (2, 1), (3, 2)])
    below = lax.ppermute(part[1], "f", [(0, 1), (1, 2), (2, 3)])
    two_away = lax.ppermute(
        low(f32(part[2]) + f32(passed)), "f", [(0, 2), (2, 0), (1, 3), (3, 1)]
    )
    return f32(part[0]) + f32(above) + f32(below) + f32(two_away)


def natural_plane(blocks, axis):
    own = plane_index()
    shape = list(blocks[0].shape)
    shape.insert(axis, 4)
    whole = jnp.zeros(shape, blocks[0].dtype)
    for step in range(4):
        whole = lax.dynamic_update_index_in_dim(whole, blocks[step], own ^ step, axis)
    return whole


def own_plane(whole, axis):
    own = plane_index()
    return [
        lax.dynamic_index_in_dim(whole, own ^ step, axis, keepdims=False) for step in range(4)
    ]


def full_gather(rows_block):
    rows, width = rows_block.shape
    line = line_gather(rows_block)
    extent = line.shape[0]
    blocks = plane_gather(line.reshape(extent * rows, width))
    whole = natural_plane([block.reshape(extent, rows, width) for block in blocks], 1)
    return whole.reshape(extent * 4 * rows, width)


def full_scatter(partial):
    extent = lax.axis_size("f")
    rows, width = partial.shape[0] // (4 * extent), partial.shape[1]
    parts = own_plane(partial.reshape(extent, 4, rows, width), 1)
    plane_sum = plane_scatter([part.reshape(extent * rows, width) for part in parts])
    return line_scatter(low(plane_sum).reshape(extent, rows, width))


def tokens_gather(block):
    near = plane_gather(block)
    return jnp.concatenate(near + [swap(piece, "tensor") for piece in near])


def tokens_scatter(partial):
    rows = partial.shape[0] // 8
    near = []
    for step in range(4):
        mine = partial[step * rows : (step + 1) * rows]
        other = partial[(4 + step) * rows : (5 + step) * rows]
        near.append(low(f32(mine) + f32(swap(other, "tensor"))))
    return plane_scatter(near)


def pair_gather(block):
    return jnp.concatenate([block, swap(block, "tensor")])


def pair_scatter(partial):
    rows = partial.shape[0] // 2
    return f32(partial[:rows]) + f32(swap(partial[rows:], "tensor"))


def total_sum(values):
    for axis in ("tensor", "tx", "ty"):
        values = values + swap(values, axis)
    if lax.axis_size("f") != 4:
        return lax.psum(values, "f")
    values = values + lax.ppermute(values, "f", [(0, 1), (1, 0), (2, 3), (3, 2)])
    return values + lax.ppermute(values, "f", [(0, 2), (2, 0), (1, 3), (3, 1)])


def shards(
    layer_input,
    attn_norm,
    head_norms,
    query_weight,
    key_matrix,
    value_matrix,
    output_weight,
    mlp_norm,
    gate_weight,
    up_weight,
    down_weight,
    grad_out,
    doc_lengths,
):
    tensor_extent = lax.axis_size("tensor")
    line_extent = lax.axis_size("f")
    core = lax.axis_index("tensor")
    q_heads = QUERY_HEADS // tensor_extent
    key_value_heads = KEY_VALUE_HEADS // tensor_extent
    group_list = QUERY_HEADS // KEY_VALUE_HEADS
    local_rows, model_width = layer_input.shape
    group_rows = local_rows * tensor_extent
    query_width = q_heads * HEAD_SIZE
    key_width = key_value_heads * HEAD_SIZE
    weight_rows = gate_weight.shape[0]
    down_rows = down_weight.shape[0]
    hidden_part = line_extent * down_rows
    score_scale = HEAD_SIZE ** (-0.5)

    qkv_all = full_gather(jnp.concatenate([query_weight, key_matrix, value_matrix], axis=1))
    out_all = full_gather(output_weight)

    def columns_of(weight):
        split = weight.reshape(weight_rows, line_extent, 4, down_rows)
        return [
            piece.reshape(weight_rows, hidden_part) for piece in own_plane(split, 2)
        ]

    gate_up_parts = [
        jnp.concatenate([gate_piece, up_piece], axis=1)
        for gate_piece, up_piece in zip(columns_of(gate_weight), columns_of(up_weight))
    ]
    gate_up_rows = natural_plane(plane_exchange(gate_up_parts), 0).reshape(
        4 * weight_rows, 2 * hidden_part
    )
    gate_up_all = line_gather(gate_up_rows).reshape(model_width, 2 * hidden_part)
    down_all = line_gather(down_weight).reshape(hidden_part, model_width)

    grad_all = tokens_gather(grad_out)

    local_ids = jnp.arange(local_rows, dtype=jnp.int32)
    row_ids = jnp.concatenate(
        [core * local_rows + local_ids, (1 - core) * local_rows + local_ids]
    )
    document_segment, position = doc_layout(doc_lengths[0], row_ids)
    cos_tab, sin_tab = rope_tables(position, HEAD_SIZE)
    allowed = (
        (document_segment[:, None] == document_segment[None, :])
        & (row_ids[None, :] <= row_ids[:, None])
    )[None, None]
    input_float = f32(layer_input)
    scale_attn = inv_rms(input_float)
    normed_attn = pair_gather(low(input_float * scale_attn * attn_norm))
    qkv_raw = matmul(normed_attn, qkv_all)
    query_raw = qkv_raw[:, :query_width]
    key_unnormed = qkv_raw[:, query_width : query_width + key_width]
    value_raw = qkv_raw[:, query_width + key_width :]
    values_reduced = low(value_raw).reshape(group_rows, key_value_heads, HEAD_SIZE)
    query_h = query_raw.reshape(group_rows, q_heads, HEAD_SIZE)
    key_per_head = key_unnormed.reshape(group_rows, key_value_heads, HEAD_SIZE)
    scale_query = inv_rms(query_h)
    scale_key = inv_rms(key_per_head)
    query_rows = low(rotate(query_h * scale_query * head_norms[0], cos_tab, sin_tab, 1.0)).reshape(
        group_rows, key_value_heads, group_list, HEAD_SIZE
    )
    keys_reduced = low(rotate(key_per_head * scale_key * head_norms[1], cos_tab, sin_tab, 1.0))
    scores = (
        jnp.einsum("qkgd,tkd->kgqt", query_rows, keys_reduced, preferred_element_type=jnp.float32)
        * score_scale
    )
    masked = jnp.where(allowed, scores, MASKED)
    row_peak = jnp.max(masked, axis=-1, keepdims=True)
    exponent = jnp.exp(masked - row_peak)
    row_total = jnp.sum(exponent, axis=-1, keepdims=True)
    probs = exponent / row_total
    probs_low = low(probs)
    attended = jnp.einsum(
        "kgqt,tkd->qkgd", probs_low, values_reduced, preferred_element_type=jnp.float32
    )
    attended_low = low(attended.reshape(group_rows, query_width))
    hidden_state = input_float + pair_scatter(low(matmul(attended_low, out_all)))

    scale_mlp = inv_rms(hidden_state)
    normed_mlp = tokens_gather(low(hidden_state * scale_mlp * mlp_norm))
    gate_raw = matmul(normed_mlp, gate_up_all[:, :hidden_part])
    up_raw = matmul(normed_mlp, gate_up_all[:, hidden_part:])
    activated = jax.nn.silu(gate_raw)
    inner_low = low(activated * up_raw)
    mlp_part = low(matmul(inner_low, down_all))
    layer_out = low(hidden_state + tokens_scatter(mlp_part))

    grad_down_part = low(matmul_tn(inner_low, grad_all))
    grad_down = line_scatter(grad_down_part.reshape(line_extent, down_rows, model_width))
    inner_grad = matmul_nt(grad_all, down_all)
    sigmoid_gate = jax.nn.sigmoid(gate_raw)
    gate_grad = low(inner_grad * up_raw * sigmoid_gate * (1.0 + gate_raw * (1.0 - sigmoid_gate)))
    up_grad = low(inner_grad * activated)
    gate_up_grad = jnp.concatenate([gate_grad, up_grad], axis=1)
    mlp_grad = low(matmul_nt(gate_up_grad, gate_up_all))
    hidden_norm_grad, mlp_gain_part = norm_back(
        hidden_state, scale_mlp, mlp_norm, tokens_scatter(mlp_grad)
    )
    grad_gate_up_part = low(matmul_tn(normed_mlp, gate_up_grad))
    grad_gate_up_rows = low(
        line_scatter(grad_gate_up_part.reshape(line_extent, 4 * weight_rows, 2 * hidden_part))
    )
    grad_pieces = natural_plane(
        plane_exchange(own_plane(grad_gate_up_rows.reshape(4, weight_rows, 2 * hidden_part), 0)),
        0,
    )
    grad_pieces = f32(grad_pieces).reshape(4, weight_rows, 2, line_extent, down_rows)
    grad_gate = grad_pieces[:, :, 0].transpose(1, 2, 0, 3).reshape(gate_weight.shape)
    grad_up = grad_pieces[:, :, 1].transpose(1, 2, 0, 3).reshape(up_weight.shape)

    hidden_grad = f32(grad_out) + hidden_norm_grad
    branch_grad = pair_gather(low(hidden_grad))
    attended_grad = low(matmul_nt(branch_grad, out_all)).reshape(
        group_rows, key_value_heads, group_list, HEAD_SIZE
    )
    grad_out_proj = full_scatter(low(matmul_tn(attended_low, branch_grad)))
    probs_grad = jnp.einsum(
        "qkgd,tkd->kgqt", attended_grad, values_reduced, preferred_element_type=jnp.float32
    )
    scores_grad = low(probs * (probs_grad - jnp.sum(probs * probs_grad, axis=-1, keepdims=True)))
    query_grad = (
        jnp.einsum(
            "kgqt,tkd->qkgd", scores_grad, keys_reduced, preferred_element_type=jnp.float32
        ).reshape(group_rows, q_heads, HEAD_SIZE)
        * score_scale
    )
    key_grad = (
        jnp.einsum("kgqt,qkgd->tkd", scores_grad, query_rows, preferred_element_type=jnp.float32)
        * score_scale
    )
    value_grad = jnp.einsum(
        "kgqt,qkgd->tkd", probs_low, attended_grad, preferred_element_type=jnp.float32
    )
    query_raw_grad, query_gain_part = norm_back(
        query_h, scale_query, head_norms[0], rotate(query_grad, cos_tab, sin_tab, -1.0)
    )
    key_raw_grad, key_gain_part = norm_back(
        key_per_head, scale_key, head_norms[1], rotate(key_grad, cos_tab, sin_tab, -1.0)
    )
    qkv_grad = jnp.concatenate(
        [
            low(query_raw_grad.reshape(group_rows, query_width)),
            low(key_raw_grad.reshape(group_rows, key_width)),
            low(value_grad.reshape(group_rows, key_width)),
        ],
        axis=1,
    )
    grad_qkv = full_scatter(low(matmul_tn(normed_attn, qkv_grad)))
    attn_grad = pair_scatter(low(matmul_nt(qkv_grad, qkv_all)))
    input_norm_grad, attn_gain_part = norm_back(input_float, scale_attn, attn_norm, attn_grad)
    grad_input = hidden_grad + input_norm_grad
    gains = total_sum(
        jnp.concatenate([attn_gain_part, mlp_gain_part, query_gain_part, key_gain_part]).reshape(
            -1, HEAD_SIZE
        )
    ).reshape(-1)
    return (
        layer_out,
        grad_input,
        gains[:model_width],
        gains[2 * model_width :].reshape(2, HEAD_SIZE),
        grad_qkv[:, :query_width],
        grad_qkv[:, query_width : query_width + key_width],
        grad_qkv[:, query_width + key_width :],
        grad_out_proj,
        gains[model_width : 2 * model_width],
        grad_gate,
        grad_up,
        grad_down,
    )


def solution(mesh):
    dp, tensor = mesh.shape["dp"], mesh.shape["tensor"]
    fine = Mesh(mesh.devices.reshape(dp // 4, 2, 2, tensor), ("f", "ty", "tx", "tensor"))
    rows = ("f", "ty", "tx")
    tokens = P(rows + ("tensor",), None)
    grid = P(rows, "tensor")
    units = P(("tensor",) + rows, None)
    return jax.shard_map(
        shards,
        mesh=fine,
        in_specs=(
            tokens, P(), P(), grid, grid, grid, units, P(), grid, grid, units, tokens, P(rows, None),
        ),
        out_specs=(tokens, tokens, P(), P(), grid, grid, grid, units, P(), grid, grid, units),
        check_vma=False,
    )
```

time: 2640 us -> 1000 us (0.38)
  waiting for transfers between devices: 2310 us -> 444 us
  starting transfers between devices: 1.46 us -> 166 us
  local copies, waits for them, and re-layouts: 25.6 us -> 138 us
  other arithmetic: 43.7 us -> 89.7 us
  blocking collectives: 43.6 us -> 0 us
  matrix products: 191 us -> 150 us
    reduce_scatter x11 -> x0, waiting for transfers between devices: 1570 us -> none  [the longest x1 370 us: shards(): lax.psum_scatter(matmul_tn(normed_mlp, gate_grad), 'dp', scatter_dimensio...]
    all_gather x11 -> x0, waiting for transfers between devices: 732 us -> none  [the longest x1 156 us: shards(): lax.all_gather(gate_weight, 'dp', axis=0, tiled=True)]
    ppermute x0 -> x109, waiting for transfers between devices: none -> 444 us  [the longest x75 201 us: swap(): return lax.ppermute(block, axis, [(0, 1), (1, 0)])]
    ppermute x0 -> x109, starting transfers between devices: none -> 166 us  [the longest x75 58.1 us: swap(): return lax.ppermute(block, axis, [(0, 1), (1, 0)])]
    psum x1 -> x0, blocking collectives: 43.6 us -> none  [shards(): lax.psum((attn_gain_part, jnp.stack([query_gain_part, key_gain_part]), ml...]
    dot_general x7 -> x4, matrix products: 66.5 us -> 34.6 us  [matmul_tn(): lax.dot_general(left_mat, right_mat, (((0,), (0,)), ((), ())), preferred_...]
    dot_general x7 -> x4, matrix products: 55.7 us -> 45.3 us  [matmul_nt(): lax.dot_general(left_mat, right_mat, (((1,), (1,)), ((), ())), preferred_...]
    dot_general x7 -> x5, matrix products: 53.4 us -> 47.4 us  [matmul(): return jnp.dot(left_mat, right_mat, preferred_element_type=jnp.float32)]
  transfers between devices with their start and end apart: 22 -> 109, of which waited for: 18 -> 35; matrix products, arithmetic and copies ran while one was open for 5% -> 27% of each run, Pallas kernels for 0% -> 0%
where the time goes in v1:
time: 1000 us; the launch traced here: 991 us
  waiting for transfers between devices  444 us (44%)
  starting transfers between devices  166 us (17%)
  matrix products  150 us (15%)
  local copies, waits for them, and re-layouts  138 us (14%)
  other arithmetic  89.7 us (9%)
    ppermute x75, waiting for transfers between devices, swap(): return lax.ppermute(block, axis, [(0, 1), (1, 0)])  201 us
    ppermute x4, waiting for transfers between devices, line_scatter(): lax.ppermute(low(f32(part[2]) + f32(passed)), 'f', [(0, 2), (2, 0), (1, 3...  115 us
    ppermute x4, waiting for transfers between devices, line_gather(): two_away = lax.ppermute(block, 'f', [(0, 2), (2, 0), (1, 3), (3, 1)])  64.7 us
    ppermute x75, starting transfers between devices, swap(): return lax.ppermute(block, axis, [(0, 1), (1, 0)])  58.1 us
    dot_general x5, matrix products, matmul(): return jnp.dot(left_mat, right_mat, preferred_element_type=jnp.float32)  47.4 us
    dot_general x4, matrix products, matmul_nt(): lax.dot_general(left_mat, right_mat, (((1,), (1,)), ((), ())), preferred_...  45.3 us
    unnamed x240, local copies, waits for them, and re-layouts  40.8 us
    dot_general x4, matrix products, matmul_tn(): lax.dot_general(left_mat, right_mat, (((0,), (0,)), ((), ())), preferred_...  34.6 us
  transfers between devices with their start and end apart: 109, of which 35 were waited for; matrix products, arithmetic and copies ran while one was open for 27% of the time, Pallas kernels for 0%

profile of v1, /device:TPU:0, one launch (start us, length us, event | category | flops | bytes accessed | tf_op | source)
XLA Modules:
  0.0 991.1 jit_solution(6817513395349743254)
XLA Ops:
  71.4 9.0 collective-permute-start.12
  117.8 20.1 %collective-permute-done.52 = bf16[128,2048]{1,0:T(8,128)(2,1)S(1)} collective-permute-done((bf16[128,2048]{1,0:T(8,128)(2,1)}, bf16[128,2048]{1,0:T(8,128)(2,1)S(1)}, u32[]{:S(2)}, u32[]{:S(2)}) %collective-permute-start.52) | collective-permute-done | bytes 524320 | tf_op jit(solution)/shard_map/ppermute | solution.py:87
  150.3 11.0 %collective-permute-done.38 = bf16[192,2048]{1,0:T(8,128)(2,1)S(1)} collective-permute-done((bf16[192,2048]{1,0:T(8,128)(2,1)}, bf16[192,2048]{1,0:T(8,128)(2,1)S(1)}, u32[]{:S(2)}, u32[]{:S(2)}) %collective-permute-start.38) | collective-permute-done | bytes 786464 | tf_op jit(solution)/shard_map/ppermute | solution.py:137
  162.8 14.9 %collective-permute-done.37 = bf16[192,2048]{1,0:T(8,128)(2,1)S(1)} collective-permute-done((bf16[192,2048]{1,0:T(8,128)(2,1)}, bf16[192,2048]{1,0:T(8,128)(2,1)S(1)}, u32[]{:S(2)}, u32[]{:S(2)}) %collective-permute-start.37) | collective-permute-done | bytes 786464 | tf_op jit(solution)/shard_map/ppermute | solution.py:139
  181.5 25.8 %collective-permute-done.15 = bf16[128,2048]{1,0:T(8,128)(2,1)S(1)} collective-permute-done((bf16[128,2048]{1,0:T(8,128)(2,1)S(1)}, bf16[128,2048]{1,0:T(8,128)(2,1)S(1)}, u32[]{:S(2)}, u32[]{:S(2)}) %collective-permute-start.15) | collective-permute-done | bytes 524320 | tf_op jit(solution)/shard_map/ppermute | solution.py:87
  216.5 64.7 %collective-permute-done.32 = bf16[512,1536]{1,0:T(8,128)(2,1)} collective-permute-done((bf16[512,1536]{1,0:T(8,128)(2,1)}, bf16[512,1536]{1,0:T(8,128)(2,1)}, u32[]{:S(2)}, u32[]{:S(2)}) %collective-permute-start.32) | collective-permute-done | bytes 1572896 | tf_op jit(solution)/shard_map/ppermute | solution.py:136
  328.7 12.2 %fusion.102 = f32[2048,768]{0,1:T(8,128)} fusion(bf16[2048,2048]{1,0:T(8,128)(2,1)} %constant_dynamic-update-slice_fusion.12, bf16[768,2048]{1,0:T(8,128)(2,1)} %bitcast.58), kind=kOutput, calls=%fused_computation.337 | convolution fusion | flops 6442450944 | bytes 17825792 | tf_op jit(solution)/shard_map/dot_general | solution.py:28
  350.5 18.5 %collective-permute-done.19 = bf16[256,2048]{1,0:T(8,128)(2,1)S(1)} collective-permute-done((bf16[256,2048]{1,0:T(8,128)(2,1)S(1)}, bf16[256,2048]{1,0:T(8,128)(2,1)S(1)}, u32[]{:S(2)}, u32[]{:S(2)}) %collective-permute-start.19) | collective-permute-done | bytes 1048608 | tf_op jit(solution)/shard_map/ppermute | solution.py:87
  390.9 11.9 %fusion.9 = f32[2048,768]{0,1:T(8,128)} fusion(bf16[2048,2048]{1,0:T(8,128)(2,1)} %constant_dynamic-update-slice_fusion.3, bf16[2048,1536]{1,0:T(8,128)(2,1)} %bitcast.53), kind=kOutput, calls=%fused_computation.31 | convolution fusion | flops 6442450944 | bytes 17825792 | tf_op jit(solution)/shard_map/dot_general | solution.py:18
  402.7 17.5 %multiply_convert_fusion.1 = (bf16[2048,768]{0,1:T(8,128)(2,1)}, bf16[2048,768]{0,1:T(8,128)(2,1)}, bf16[2048,768]{0,1:T(8,128)(2,1)S(1)}) fusion(f32[2048,768]{0,1:T(8,128)} %fusion.102, f32[2048,768]{0,1:T(8,128)} %fusion.9, bf16[2048,2048]{1,0:T(8,128)(2,1)} %constant_dynamic-update-slice_fusion.3, bf16[2048,1536]{1,0:T(8,128)(2,1)} %bitcast.53), kind=kOutput, calls=%fused_computation.15 | convolution fusion | flops 6466043904 | bytes 33554432 | tf_op jit(solution)/shard_map/dot_general | solution.py:18
  420.3 10.3 %convolution_convert_fusion.5 = bf16[768,2048]{1,0:T(8,128)(2,1)} fusion(bf16[2048,768]{0,1:T(8,128)(2,1)S(1)} %get-tuple-element.122, bf16[2048,2048]{1,0:T(8,128)(2,1)} %constant_dynamic-update-slice_fusion.12), kind=kOutput, calls=%fused_computation.30 | convolution fusion | flops 6444023808 | bytes 14680064 | tf_op jit(solution)/shard_map/dot_general | solution.py:22
  430.6 11.0 %convolution_convert_fusion.2 = bf16[2048,2048]{1,0:T(8,128)(2,1)} fusion(bf16[2048,768]{0,1:T(8,128)(2,1)S(1)} %get-tuple-element.122, bf16[768,2048]{1,0:T(8,128)(2,1)} %bitcast.58), kind=kOutput, calls=%fused_computation.10 | convolution fusion | flops 6446645248 | bytes 14680064 | tf_op jit(solution)/shard_map/dot_general | solution.py:18
  441.7 16.9 %convolution_convert_fusion.3 = bf16[2048,1536]{1,0:T(8,128)(2,1)S(1)} fusion(bf16[2048,2048]{1,0:T(8,128)(2,1)} %constant_dynamic-update-slice_fusion.3, bf16[2048,768]{0,1:T(8,128)(2,1)} %get-tuple-element.121, bf16[2048,768]{0,1:T(8,128)(2,1)S(1)} %copy-done.100), kind=kOutput, calls=%fused_computation.11 | convolution fusion | flops 12900630528 | bytes 20971520 | tf_op jit(solution)/shard_map/dot_general | solution.py:22
  458.5 21.5 %convolution_convert_fusion.1 = bf16[2048,2048]{1,0:T(8,128)(2,1)} fusion(bf16[2048,1536]{1,0:T(8,128)(2,1)} %bitcast.53, bf16[2048,768]{0,1:T(8,128)(2,1)} %get-tuple-element.121, bf16[2048,768]{0,1:T(8,128)(2,1)} %get-tuple-element.120), kind=kOutput, calls=%fused_computation.9 | convolution fusion | flops 12901679104 | bytes 20971520 | tf_op jit(solution)/shard_map/dot_general | solution.py:28
  497.8 8.6 collective-permute-done.107
  532.1 8.5 collective-permute-done.47
  555.5 8.6 collective-permute-done.66
  603.7 16.9 %collective-permute-start.98 = (bf16[512,1536]{1,0:T(8,128)(2,1)S(1)}, bf16[512,1536]{1,0:T(8,128)(2,1)}, u32[]{:S(2)}, u32[]{:S(2)}) collective-permute-start(bf16[512,1536]{1,0:T(8,128)(2,1)S(1)} %fusion.13), channel_id=1, source_target_pairs={{0,16},{16,0},{8,24},{24,8},{1,17},{17,1},{9,25},{25,9},{2,18},{18... | collective-permute-start | bytes 4718600 | tf_op jit(solution)/shard_map/ppermute | solution.py:163
  620.6 80.3 %collective-permute-done.108 = bf16[192,2048]{1,0:T(8,128)(2,1)S(1)} collective-permute-done((bf16[192,2048]{1,0:T(8,128)(2,1)}, bf16[192,2048]{1,0:T(8,128)(2,1)S(1)}, u32[]{:S(2)}, u32[]{:S(2)}) %collective-permute-start.108) | collective-permute-done | bytes 786464 | tf_op jit(solution)/shard_map/ppermute | solution.py:163
  802.8 10.9 %collective-permute-done.102 = bf16[64,1536]{1,0:T(8,128)(2,1)S(1)} collective-permute-done((bf16[64,1536]{1,0:T(8,128)(2,1)}, bf16[64,1536]{1,0:T(8,128)(2,1)S(1)}, u32[]{:S(2)}, u32[]{:S(2)}) %collective-permute-start.102) | collective-permute-done | bytes 196640 | tf_op jit(solution)/shard_map/ppermute | solution.py:87
  830.5 18.2 %collective-permute-done.76 = bf16[256,2048]{1,0:T(8,128)(2,1)S(1)} collective-permute-done((bf16[256,2048]{1,0:T(8,128)(2,1)}, bf16[256,2048]{1,0:T(8,128)(2,1)S(1)}, u32[]{:S(2)}, u32[]{:S(2)}) %collective-permute-start.76) | collective-permute-done | bytes 1048608 | tf_op jit(solution)/shard_map/ppermute | solution.py:87
  856.4 29.9 %collective-permute-done.87 = bf16[128,2048]{1,0:T(8,128)(2,1)S(1)} collective-permute-done((bf16[128,2048]{1,0:T(8,128)(2,1)S(1)}, bf16[128,2048]{1,0:T(8,128)(2,1)S(1)}, u32[]{:S(2)}, u32[]{:S(2)}) %collective-permute-start.87) | collective-permute-done | bytes 524320 | tf_op jit(solution)/shard_map/ppermute | solution.py:87
  892.0 22.4 %collective-permute-done.71 = f32[34,128]{1,0:T(8,128)S(1)} collective-permute-done((f32[34,128]{1,0:T(8,128)S(1)}, f32[34,128]{1,0:T(8,128)S(1)}, u32[]{:S(2)}, u32[]{:S(2)}) %collective-permute-start.71) | collective-permute-done | bytes 17440 | tf_op jit(solution)/shard_map/ppermute | solution.py:87
  966.6 22.2 %collective-permute-done.84 = bf16[128,2048]{1,0:T(8,128)(2,1)S(1)} collective-permute-done((bf16[128,2048]{1,0:T(8,128)(2,1)S(1)}, bf16[128,2048]{1,0:T(8,128)(2,1)S(1)}, u32[]{:S(2)}, u32[]{:S(2)}) %collective-permute-start.84) | collective-permute-done | bytes 524320 | tf_op jit(solution)/shard_map/ppermute | solution.py:163
  (645 shorter events, 496.3 us)
Async XLA Ops:
  42.4 70.3 %collective-permute-start.4 = (bf16[128,2048]{1,0:T(8,128)(2,1)}, bf16[128,2048]{1,0:T(8,128)(2,1)}, u32[]{:S(2)}, u32[]{:S(2)}) collective-permute-start(bf16[128,2048]{1,0:T(8,128)(2,1)} %copy-done.51), channel_id=1, source_target_pairs={{0,8},{8,16},{16,24},{1,9},{9,17},{17,25},{2,10},{10,18},{18,26},{... | collective-permute-start | bytes 1572872 | tf_op jit(solution)/shard_map/ppermute | solution.py:138
  147.3 63.1 %collective-permute-start.6 = (bf16[512,2048]{1,0:T(8,128)(2,1)S(1)}, bf16[512,2048]{1,0:T(8,128)(2,1)S(1)}, u32[]{:S(2)}, u32[]{:S(2)}) collective-permute-start(bf16[512,2048]{1,0:T(8,128)(2,1)S(1)} %bitcast.383), channel_id=1, source_target_pairs={{0,4},{4,0},{1,5},{5,1},{2,6},{6,2},{3,7},{7,3},{8,12},{12,8},{9,1... | collective-permute-start | bytes 6291464 | tf_op jit(solution)/shard_map/ppermute | solution.py:87
  148.5 62.2 %collective-permute-start.5 = (bf16[512,2048]{1,0:T(8,128)(2,1)S(1)}, bf16[512,2048]{1,0:T(8,128)(2,1)S(1)}, u32[]{:S(2)}, u32[]{:S(2)}) collective-permute-start(bf16[512,2048]{1,0:T(8,128)(2,1)S(1)} %bitcast.384), channel_id=1, source_target_pairs={{0,2},{2,0},{1,3},{3,1},{4,6},{6,4},{5,7},{7,5},{8,10},{10,8},{9,1... | collective-permute-start | bytes 6291464 | tf_op jit(solution)/shard_map/ppermute | solution.py:87
  209.0 72.2 %collective-permute-start.32 = (bf16[512,1536]{1,0:T(8,128)(2,1)}, bf16[512,1536]{1,0:T(8,128)(2,1)}, u32[]{:S(2)}, u32[]{:S(2)}) collective-permute-start(bf16[512,1536]{1,0:T(8,128)(2,1)} %bitcast.49), channel_id=1, source_target_pairs={{0,16},{16,0},{8,24},{24,8},{1,17},{17,1},{9,25},{25,9},{2,18},{18... | collective-permute-start | bytes 4718600 | tf_op jit(solution)/shard_map/ppermute | solution.py:136
  210.6 74.9 %collective-permute-start = (bf16[256,2048]{1,0:T(8,128)(2,1)S(1)}, bf16[256,2048]{1,0:T(8,128)(2,1)S(1)}, u32[]{:S(2)}, u32[]{:S(2)}) collective-permute-start(bf16[256,2048]{1,0:T(8,128)(2,1)S(1)} %copy-done.65), channel_id=1, source_target_pairs={{0,1},{1,0},{2,3},{3,2},{4,5},{5,4},{6,7},{7,6},{8,9},{9,8},{10,11... | collective-permute-start | bytes 3145736 | tf_op jit(solution)/shard_map/ppermute | solution.py:87
  210.8 72.9 %collective-permute-start.7 = (bf16[256,2048]{1,0:T(8,128)(2,1)S(1)}, bf16[256,2048]{1,0:T(8,128)(2,1)S(1)}, u32[]{:S(2)}, u32[]{:S(2)}) collective-permute-start(bf16[256,2048]{1,0:T(8,128)(2,1)S(1)} %slice.408), channel_id=1, source_target_pairs={{0,2},{2,0},{1,3},{3,1},{4,6},{6,4},{5,7},{7,5},{8,10},{10,8},{9,1... | collective-permute-start | bytes 3145736 | tf_op jit(solution)/shard_map/ppermute | solution.py:87
  211.5 73.4 %collective-permute-start.8 = (bf16[256,2048]{1,0:T(8,128)(2,1)S(1)}, bf16[256,2048]{1,0:T(8,128)(2,1)S(1)}, u32[]{:S(2)}, u32[]{:S(2)}) collective-permute-start(bf16[256,2048]{1,0:T(8,128)(2,1)S(1)} %slice.409), channel_id=1, source_target_pairs={{0,4},{4,0},{1,5},{5,1},{2,6},{6,2},{3,7},{7,3},{8,12},{12,8},{9,1... | collective-permute-start | bytes 3145736 | tf_op jit(solution)/shard_map/ppermute | solution.py:87
  213.5 131.4 %collective-permute-start.34 = (bf16[512,1536]{1,0:T(8,128)(2,1)}, bf16[512,1536]{1,0:T(8,128)(2,1)}, u32[]{:S(2)}, u32[]{:S(2)}) collective-permute-start(bf16[512,1536]{1,0:T(8,128)(2,1)} %bitcast.49), channel_id=1, source_target_pairs={{8,0},{16,8},{24,16},{9,1},{17,9},{25,17},{10,2},{18,10},{26,18},{... | collective-permute-start | bytes 4718600 | tf_op jit(solution)/shard_map/ppermute | solution.py:137
  281.2 90.9 %collective-permute-start.35 = (bf16[512,1536]{1,0:T(8,128)(2,1)}, bf16[512,1536]{1,0:T(8,128)(2,1)}, u32[]{:S(2)}, u32[]{:S(2)}) collective-permute-start(bf16[512,1536]{1,0:T(8,128)(2,1)} %bitcast.49), channel_id=1, source_target_pairs={{0,8},{8,16},{16,24},{1,9},{9,17},{17,25},{2,10},{10,18},{18,26},{... | collective-permute-start | bytes 4718600 | tf_op jit(solution)/shard_map/ppermute | solution.py:138
  283.7 61.2 %collective-permute-start.33 = (bf16[512,1536]{1,0:T(8,128)(2,1)}, bf16[512,1536]{1,0:T(8,128)(2,1)}, u32[]{:S(2)}, u32[]{:S(2)}) collective-permute-start(bf16[512,1536]{1,0:T(8,128)(2,1)} %collective-permute-done.32), channel_id=1, source_target_pairs={{8,0},{16,24},{9,1},{17,25},{10,2},{18,26},{11,3},{19,27},{12,4},{... | collective-permute-start | bytes 4718600 | tf_op jit(solution)/shard_map/ppermute | solution.py:139
  585.6 138.3 %collective-permute-start.95 = (bf16[512,1536]{1,0:T(8,128)(2,1)}, bf16[512,1536]{1,0:T(8,128)(2,1)}, u32[]{:S(2)}, u32[]{:S(2)}) collective-permute-start(bf16[512,1536]{1,0:T(8,128)(2,1)} %get-tuple-element.105), channel_id=1, source_target_pairs={{8,0},{16,8},{24,16},{9,1},{17,9},{25,17},{10,2},{18,10},{26,18},{... | collective-permute-start | bytes 4718600 | tf_op jit(solution)/shard_map/ppermute | solution.py:161
  586.9 114.0 %collective-permute-start.108 = (bf16[192,2048]{1,0:T(8,128)(2,1)}, bf16[192,2048]{1,0:T(8,128)(2,1)S(1)}, u32[]{:S(2)}, u32[]{:S(2)}) collective-permute-start(bf16[192,2048]{1,0:T(8,128)(2,1)} %fusion.43), channel_id=1, source_target_pairs={{0,16},{16,0},{8,24},{24,8},{1,17},{17,1},{9,25},{25,9},{2,18},{18... | collective-permute-start | bytes 2359304 | tf_op jit(solution)/shard_map/ppermute | solution.py:163
  595.2 108.4 %collective-permute-start.68 = (bf16[256,2048]{1,0:T(8,128)(2,1)S(1)}, bf16[256,2048]{1,0:T(8,128)(2,1)S(1)}, u32[]{:S(2)}, u32[]{:S(2)}) collective-permute-start(bf16[256,2048]{1,0:T(8,128)(2,1)S(1)} %get-tuple-element.114), channel_id=1, source_target_pairs={{0,1},{1,0},{2,3},{3,2},{4,5},{5,4},{6,7},{7,6},{8,9},{9,8},{10,11... | collective-permute-start | bytes 3145736 | tf_op jit(solution)/shard_map/ppermute | solution.py:87
  598.3 125.6 %collective-permute-start.96 = (bf16[512,1536]{1,0:T(8,128)(2,1)}, bf16[512,1536]{1,0:T(8,128)(2,1)}, u32[]{:S(2)}, u32[]{:S(2)}) collective-permute-start(bf16[512,1536]{1,0:T(8,128)(2,1)} %get-tuple-element.104), channel_id=1, source_target_pairs={{0,8},{8,16},{16,24},{1,9},{9,17},{17,25},{2,10},{10,18},{18,26},{... | collective-permute-start | bytes 4718600 | tf_op jit(solution)/shard_map/ppermute | solution.py:162
  603.7 128.3 %collective-permute-start.98 = (bf16[512,1536]{1,0:T(8,128)(2,1)S(1)}, bf16[512,1536]{1,0:T(8,128)(2,1)}, u32[]{:S(2)}, u32[]{:S(2)}) collective-permute-start(bf16[512,1536]{1,0:T(8,128)(2,1)S(1)} %fusion.13), channel_id=1, source_target_pairs={{0,16},{16,0},{8,24},{24,8},{1,17},{17,1},{9,25},{25,9},{2,18},{18... | collective-permute-start | bytes 4718600 | tf_op jit(solution)/shard_map/ppermute | solution.py:163
  737.9 57.2 %collective-permute-start.99 = (bf16[128,1536]{1,0:T(8,128)(2,1)}, bf16[128,1536]{1,0:T(8,128)(2,1)}, u32[]{:S(2)}, u32[]{:S(2)}) collective-permute-start(bf16[128,1536]{1,0:T(8,128)(2,1)} %get-tuple-element.175), channel_id=1, source_target_pairs={{0,2},{2,0},{1,3},{3,1},{4,6},{6,4},{5,7},{7,5},{8,10},{10,8},{9,1... | collective-permute-start | bytes 1179656 | tf_op jit(solution)/shard_map/ppermute | solution.py:87
  739.4 60.1 %collective-permute-start.100 = (bf16[128,1536]{1,0:T(8,128)(2,1)}, bf16[128,1536]{1,0:T(8,128)(2,1)}, u32[]{:S(2)}, u32[]{:S(2)}) collective-permute-start(bf16[128,1536]{1,0:T(8,128)(2,1)} %get-tuple-element.174), channel_id=1, source_target_pairs={{0,4},{4,0},{1,5},{5,1},{2,6},{6,2},{3,7},{7,3},{8,12},{12,8},{9,1... | collective-permute-start | bytes 1179656 | tf_op jit(solution)/shard_map/ppermute | solution.py:87
  741.4 56.0 %collective-permute-start.101 = (bf16[64,1536]{1,0:T(8,128)(2,1)}, bf16[64,1536]{1,0:T(8,128)(2,1)}, u32[]{:S(2)}, u32[]{:S(2)}) collective-permute-start(bf16[64,1536]{1,0:T(8,128)(2,1)} %get-tuple-element.172), channel_id=1, source_target_pairs={{0,2},{2,0},{1,3},{3,1},{4,6},{6,4},{5,7},{7,5},{8,10},{10,8},{9,1... | collective-permute-start | bytes 589832 | tf_op jit(solution)/shard_map/ppermute | solution.py:87
  742.0 56.7 %collective-permute-start.103 = (bf16[64,1536]{1,0:T(8,128)(2,1)}, bf16[64,1536]{1,0:T(8,128)(2,1)}, u32[]{:S(2)}, u32[]{:S(2)}) collective-permute-start(bf16[64,1536]{1,0:T(8,128)(2,1)} %get-tuple-element.173), channel_id=1, source_target_pairs={{0,4},{4,0},{1,5},{5,1},{2,6},{6,2},{3,7},{7,3},{8,12},{12,8},{9,1... | collective-permute-start | bytes 589832 | tf_op jit(solution)/shard_map/ppermute | solution.py:87
  747.3 75.1 %collective-permute-start.86 = (bf16[128,2048]{1,0:T(8,128)(2,1)}, bf16[128,2048]{1,0:T(8,128)(2,1)}, u32[]{:S(2)}, u32[]{:S(2)}) collective-permute-start(bf16[128,2048]{1,0:T(8,128)(2,1)} %bitcast.96), channel_id=1, source_target_pairs={{0,2},{2,0},{1,3},{3,1},{4,6},{6,4},{5,7},{7,5},{8,10},{10,8},{9,1... | collective-permute-start | bytes 1572872 | tf_op jit(solution)/shard_map/ppermute | solution.py:87
  795.2 59.9 %collective-permute-start.85 = (bf16[128,2048]{1,0:T(8,128)(2,1)}, bf16[128,2048]{1,0:T(8,128)(2,1)}, u32[]{:S(2)}, u32[]{:S(2)}) collective-permute-start(bf16[128,2048]{1,0:T(8,128)(2,1)} %bitcast.94), channel_id=1, source_target_pairs={{0,2},{2,0},{1,3},{3,1},{4,6},{6,4},{5,7},{7,5},{8,10},{10,8},{9,1... | collective-permute-start | bytes 1572872 | tf_op jit(solution)/shard_map/ppermute | solution.py:87
  813.7 74.9 %collective-permute-start.90 = (bf16[128,2048]{1,0:T(8,128)(2,1)}, bf16[128,2048]{1,0:T(8,128)(2,1)}, u32[]{:S(2)}, u32[]{:S(2)}) collective-permute-start(bf16[128,2048]{1,0:T(8,128)(2,1)} %bitcast.100), channel_id=1, source_target_pairs={{0,4},{4,0},{1,5},{5,1},{2,6},{6,2},{3,7},{7,3},{8,12},{12,8},{9,1... | collective-permute-start | bytes 1572872 | tf_op jit(solution)/shard_map/ppermute | solution.py:87
  825.2 100.4 %collective-permute-start.75 = (bf16[256,2048]{1,0:T(8,128)(2,1)}, bf16[256,2048]{1,0:T(8,128)(2,1)S(1)}, u32[]{:S(2)}, u32[]{:S(2)}) collective-permute-start(bf16[256,2048]{1,0:T(8,128)(2,1)} %bitcast.419), channel_id=1, source_target_pairs={{0,2},{2,0},{1,3},{3,1},{4,6},{6,4},{5,7},{7,5},{8,10},{10,8},{9,1... | collective-permute-start | bytes 3145736 | tf_op jit(solution)/shard_map/ppermute | solution.py:87
  848.7 78.5 %collective-permute-start.80 = (bf16[256,2048]{1,0:T(8,128)(2,1)S(1)}, bf16[256,2048]{1,0:T(8,128)(2,1)S(1)}, u32[]{:S(2)}, u32[]{:S(2)}) collective-permute-start(bf16[256,2048]{1,0:T(8,128)(2,1)S(1)} %bitcast.418), channel_id=1, source_target_pairs={{0,4},{4,0},{1,5},{5,1},{2,6},{6,2},{3,7},{7,3},{8,12},{12,8},{9,1... | collective-permute-start | bytes 3145736 | tf_op jit(solution)/shard_map/ppermute | solution.py:87
  (192 other events, 3795.7 us)

commit v2 on v1

v2 whole, which is shorter than its diff:
```python
import jax
import jax.numpy as jnp
from jax import lax
from jax.experimental import pallas as pl
from jax.experimental.pallas import tpu as pltpu
from jax.sharding import Mesh, PartitionSpec as P

QUERY_HEADS = 16
KEY_VALUE_HEADS = 8
HEAD_SIZE = 128


EPS = 1e-06
ROPE_BASE = 1000000.0
MASKED = -1e30
LOW = jnp.bfloat16


def matmul(left_mat, right_mat):
    return jnp.dot(left_mat, right_mat, preferred_element_type=jnp.float32)


def matmul_tn(left_mat, right_mat):
    return lax.dot_general(
        left_mat, right_mat, (((0,), (0,)), ((), ())), preferred_element_type=jnp.float32
    )


def matmul_nt(left_mat, right_mat):
    return lax.dot_general(
        left_mat, right_mat, (((1,), (1,)), ((), ())), preferred_element_type=jnp.float32
    )


def inv_rms(values):
    return lax.rsqrt(jnp.mean(values * values, axis=-1, keepdims=True) + EPS)


def norm_back(values, scales, gain_row, upstream):
    weighted = upstream * gain_row
    inner_mean = jnp.mean(weighted * values, axis=-1, keepdims=True)
    value_grad = scales * weighted - values * (scales * scales * scales) * inner_mean
    lead_axes = tuple(range(upstream.ndim - 1))
    return (value_grad, jnp.sum(upstream * values * scales, axis=lead_axes))


def rope_tables(position, head_width):
    half_dim = head_width // 2
    inverse = ROPE_BASE ** (-(jnp.arange(half_dim, dtype=jnp.float32) * (2.0 / head_width)))
    angles = position.astype(jnp.float32)[:, None] * inverse[None, :]
    return (jnp.cos(angles), jnp.sin(angles))


def rotate(values, cos_tab, sin_tab, direction):
    half_dim = values.shape[-1] // 2
    first_half = values[..., :half_dim]
    second_half = values[..., half_dim:]
    cosine = cos_tab[:, None, :]
    sine_tab = direction * sin_tab[:, None, :]
    return jnp.concatenate(
        [
            first_half * cosine - second_half * sine_tab,
            second_half * cosine + first_half * sine_tab,
        ],
        axis=-1,
    )


def doc_layout(lengths_row, row_ids):
    doc_ends = jnp.cumsum(lengths_row, dtype=jnp.int32)
    document_segment = jnp.sum(
        (row_ids[:, None] >= doc_ends[None, :]).astype(jnp.int32), axis=1, dtype=jnp.int32
    )
    doc_starts = doc_ends - lengths_row
    member = document_segment[:, None] == jnp.arange(lengths_row.shape[0], dtype=jnp.int32)[None, :]
    start_of = jnp.sum(jnp.where(member, doc_starts[None, :], 0), axis=1, dtype=jnp.int32)
    return (document_segment, row_ids - start_of)


def f32(values):
    return values.astype(jnp.float32)


def low(values):
    return values.astype(LOW)


def after(block, *earlier):
    return lax.optimization_barrier((block,) + earlier)[0]


def swap(block, axis):
    return lax.ppermute(block, axis, [(0, 1), (1, 0)])


def plane_index():
    return 2 * lax.axis_index("ty") + lax.axis_index("tx")


def plane_gather(block, second=()):
    half = block.shape[0] // 2
    across_x = swap(block, "tx")
    across_y = swap(block, "ty")
    top, end = after(across_y[:half], *second), after(across_x[half:], *second)
    far = jnp.concatenate([swap(top, "tx"), swap(end, "ty")])
    return [block, across_x, across_y, far]


def plane_scatter(parts, second=(), third=()):
    own, for_x, for_y, for_far = parts
    half = own.shape[0] // 2
    pass_y = swap(for_far[:half], "tx")
    pass_x = swap(for_far[half:], "ty")
    x_top = swap(for_x[:half], "tx")
    y_end = swap(for_y[half:], "ty")
    pass_y, pass_x = after(pass_y, *second), after(pass_x, *second)
    y_top = swap(low(f32(for_y[:half]) + f32(pass_y)), "ty")
    x_end = swap(low(f32(for_x[half:]) + f32(pass_x)), "tx")
    x_top, y_top = after(x_top, *third), after(y_top, *third)
    x_end, y_end = after(x_end, *third), after(y_end, *third)
    return jnp.concatenate(
        [
            f32(own[:half]) + f32(x_top) + f32(y_top),
            f32(own[half:]) + f32(x_end) + f32(y_end),
        ]
    )


def plane_exchange(parts):
    own, for_x, for_y, for_far = parts
    half = own.shape[0] // 2
    far = jnp.concatenate(
        [
            swap(swap(for_far[:half], "tx"), "ty"),
            swap(swap(for_far[half:], "ty"), "tx"),
        ]
    )
    return [own, swap(for_x, "tx"), swap(for_y, "ty"), far]


def plane_lengths(lengths):
    across_x, across_y = swap(lengths, "tx"), swap(lengths, "ty")
    return jnp.concatenate([lengths, across_x, across_y, swap(across_y, "tx")])


def line_gather(block, second=(), near=None):
    extent = lax.axis_size("f")
    if extent != 4:
        return lax.all_gather(block, "f", axis=0)
    place = lax.axis_index("f")
    two_away = lax.ppermute(block, "f", [(0, 2), (2, 0), (1, 3), (3, 1)])
    if near is None:
        above = lax.ppermute(block, "f", [(1, 0), (2, 1), (3, 2)])
        below = lax.ppermute(block, "f", [(0, 1), (1, 2), (2, 3)])
    else:
        above, below = near
    two_away = after(two_away, *second)
    passed = lax.ppermute(two_away, "f", [(1, 0), (2, 3)])
    blocks = [
        block,
        jnp.where(place == 3, passed, above),
        two_away,
        jnp.where(place == 0, passed, below),
    ]
    whole = jnp.zeros((4,) + block.shape, block.dtype)
    for step in range(4):
        whole = lax.dynamic_update_index_in_dim(whole, blocks[step], (place + step) % 4, 0)
    return whole


def line_scatter(parts, second=(), third=()):
    extent = lax.axis_size("f")
    if extent != 4:
        return f32(lax.psum_scatter(parts, "f", scatter_dimension=0))
    place = lax.axis_index("f")
    part = [
        lax.dynamic_index_in_dim(parts, (place + step) % 4, 0, keepdims=False) for step in range(4)
    ]
    passed = lax.ppermute(jnp.where(place == 0, part[3], part[1]), "f", [(0, 1), (3, 2)])
    above = lax.ppermute(part[3], "f", [(1, 0), (2, 1), (3, 2)])
    below = lax.ppermute(part[1], "f", [(0, 1), (1, 2), (2, 3)])
    passed = after(passed, *second)
    two_away = lax.ppermute(
        low(f32(part[2]) + f32(passed)), "f", [(0, 2), (2, 0), (1, 3), (3, 1)]
    )
    above, below, two_away = (after(block, *third) for block in (above, below, two_away))
    return f32(part[0]) + f32(above) + f32(below) + f32(two_away)


def natural_plane(blocks, axis):
    own = plane_index()
    shape = list(blocks[0].shape)
    shape.insert(axis, 4)
    whole = jnp.zeros(shape, blocks[0].dtype)
    for step in range(4):
        whole = lax.dynamic_update_index_in_dim(whole, blocks[step], own ^ step, axis)
    return whole


def own_plane(whole, axis):
    own = plane_index()
    return [
        lax.dynamic_index_in_dim(whole, own ^ step, axis, keepdims=False) for step in range(4)
    ]


def full_gather(rows_block):
    rows, width = rows_block.shape
    line = line_gather(rows_block)
    extent = line.shape[0]
    blocks = plane_gather(line.reshape(extent * rows, width))
    whole = natural_plane([block.reshape(extent, rows, width) for block in blocks], 1)
    return whole.reshape(extent * 4 * rows, width)


def full_scatter_plane(partial, second=(), third=()):
    extent = lax.axis_size("f")
    rows, width = partial.shape[0] // (4 * extent), partial.shape[1]
    parts = own_plane(partial.reshape(extent, 4, rows, width), 1)
    plane_sum = plane_scatter(
        [part.reshape(extent * rows, width) for part in parts], second, third
    )
    return low(plane_sum).reshape(extent, rows, width)


def tokens_gather(block, second=(), third=()):
    near = plane_gather(block, second)
    return jnp.concatenate(near + [swap(after(piece, *third), "tensor") for piece in near])


def tokens_scatter(partial, second=(), third=(), fourth=()):
    rows = partial.shape[0] // 8
    near = []
    for step in (3, 1, 2, 0):
        mine = partial[step * rows : (step + 1) * rows]
        other = swap(partial[(4 + step) * rows : (5 + step) * rows], "tensor")
        near.append(low(f32(mine) + f32(after(other, *second))))
    return plane_scatter([near[3], near[1], near[2], near[0]], third, fourth)


def pair_gather(block):
    return jnp.concatenate([block, swap(block, "tensor")])


def pair_scatter(partial):
    rows = partial.shape[0] // 2
    return f32(partial[:rows]) + f32(swap(partial[rows:], "tensor"))


def total_sum(values):
    for axis in ("tensor", "tx", "ty"):
        values = values + swap(values, axis)
    if lax.axis_size("f") != 4:
        return lax.psum(values, "f")
    values = values + lax.ppermute(values, "f", [(0, 1), (1, 0), (2, 3), (3, 2)])
    return values + lax.ppermute(values, "f", [(0, 2), (2, 0), (1, 3), (3, 1)])


class Place:
    def __init__(self):
        self.z = lax.axis_index("f")
        self.ty = lax.axis_index("ty")
        self.tx = lax.axis_index("tx")
        self.core = lax.axis_index("tensor")
        self.p = 2 * self.ty + self.tx
        self.px = 2 * self.ty + 1 - self.tx
        self.py = 2 * (1 - self.ty) + self.tx
        self.pd = 2 * (1 - self.ty) + 1 - self.tx
        self.x = {"tx": 1 - self.tx}
        self.y = {"ty": 1 - self.ty}
        self.d = {"tx": 1 - self.tx, "ty": 1 - self.ty}
        self.pair = {"tensor": 1 - self.core}
        self.up = {"f": self.z + 1}
        self.down = {"f": self.z - 1}
        self.two = {"f": (self.z + 2) % 4}

    def at(self, step):
        return (self.z + step) % 4


def remote(src, dst, send, recv, to):
    return pltpu.make_async_remote_copy(
        src_ref=src,
        dst_ref=dst,
        send_sem=send,
        recv_sem=recv,
        device_id=to,
        device_id_type=pl.DeviceIdType.MESH,
    )


def arrived(dst, recv, to):
    remote(dst, dst, recv, recv, to).wait_recv()


def greet(place, partners, line):
    barrier = pltpu.get_barrier_semaphore()
    for to in partners:
        pl.semaphore_signal(barrier, inc=1, device_id=to, device_id_type=pl.DeviceIdType.MESH)
    if not line:
        pl.semaphore_wait(barrier, len(partners))
        return

    @pl.when(place.z > 0)
    def _():
        pl.semaphore_signal(
            barrier, inc=1, device_id=place.down, device_id_type=pl.DeviceIdType.MESH
        )

    @pl.when(place.z < 3)
    def _():
        pl.semaphore_signal(barrier, inc=1, device_id=place.up, device_id_type=pl.DeviceIdType.MESH)

    pl.semaphore_signal(barrier, inc=1, device_id=place.two, device_id_type=pl.DeviceIdType.MESH)
    pl.semaphore_wait(barrier, len(partners) + 2 + (place.z + 1) // 2 % 2)


class LineGather:
    def __init__(self, place, own, slot, send, recv):
        self.place, self.own, self.slot, self.send, self.recv = place, own, slot, send, recv
        here = slot(place.z)
        self.to_down = remote(own, here, send.at[0], recv.at[1], place.down)
        self.to_up = remote(own, here, send.at[1], recv.at[3], place.up)
        self.to_two = remote(own, here, send.at[2], recv.at[2], place.two)
        two = slot(place.at(2))
        self.pass_down = remote(two, two, send.at[3], recv.at[3], place.down)
        self.pass_up = remote(two, two, send.at[3], recv.at[1], place.up)

    def start(self):
        pl.when(self.place.z > 0)(self.to_down.start)
        pl.when(self.place.z < 3)(self.to_up.start)
        self.to_two.start()

    def step(self, turn):
        if turn == 2:
            return 2
        if turn == 1:
            return jnp.where(self.place.z == 3, 3, 1)
        return jnp.where(self.place.z == 3, 1, 3)

    def wait(self, turn):
        step = self.step(turn)
        slot = self.slot(self.place.at(step))
        arrived(slot, self.recv.at[step], self.place.two)
        if turn == 2:
            pl.when(self.place.z == 1)(self.pass_down.start)
            pl.when(self.place.z == 2)(self.pass_up.start)

    def finish(self):
        pl.when(self.place.z > 0)(self.to_down.wait_send)
        pl.when(self.place.z < 3)(self.to_up.wait_send)
        self.to_two.wait_send()
        pl.when(self.place.z == 1)(self.pass_down.wait_send)
        pl.when(self.place.z == 2)(self.pass_up.wait_send)


class PlaneGather:
    def __init__(self, place, own, slot, rows, send, recv):
        half = rows // 2
        whole, top, end = pl.ds(0, rows), pl.ds(0, half), pl.ds(half, half)
        self.place, self.recv = place, recv
        self.to_x = remote(own, slot(place.p, whole), send.at[0], recv.at[0], place.x)
        self.to_y = remote(own, slot(place.p, whole), send.at[1], recv.at[1], place.y)
        self.from_x, self.from_y = slot(place.px, whole), slot(place.py, whole)
        self.far_top, self.far_end = slot(place.pd, top), slot(place.pd, end)
        pass_x, pass_y = slot(place.py, top), slot(place.px, end)
        self.pass_x = remote(pass_x, pass_x, send.at[2], recv.at[2], place.x)
        self.pass_y = remote(pass_y, pass_y, send.at[3], recv.at[3], place.y)

    def start(self):
        self.to_x.start()
        self.to_y.start()

    def forward(self):
        arrived(self.from_y, self.recv.at[1], self.place.y)
        self.pass_x.start()
        arrived(self.from_x, self.recv.at[0], self.place.x)
        self.pass_y.start()

    def wait_far(self):
        arrived(self.far_top, self.recv.at[2], self.place.x)
        arrived(self.far_end, self.recv.at[3], self.place.y)

    def finish(self):
        self.to_x.wait_send()
        self.to_y.wait_send()
        self.pass_x.wait_send()
        self.pass_y.wait_send()


ANYWHERE = pl.BlockSpec(memory_space=pl.ANY)
WHOLE = pl.BlockSpec(memory_space=pltpu.VMEM)


class Marks:
    def __init__(self, ref):
        self.ref, self.used = ref, 0

    def take(self, count=1):
        first = self.used
        self.used += count
        return self.ref.at[first] if count == 1 else self.ref.at[pl.ds(first, count)]


def each_rows(rows, chunk, work):
    def body(index, carry):
        work(pl.ds(pl.multiple_of(index * chunk, chunk), chunk))
        return carry

    lax.fori_loop(0, rows // chunk, body, 0)


class TokensGather:
    def __init__(self, place, own, whole, marks):
        half = own.shape[0] // 2
        top, end = pl.ds(0, half), pl.ds(half, half)
        self.place, self.whole = place, whole
        self.copy = pltpu.make_async_copy(own, whole.at[0], marks.take())
        self.recv = [marks.take() for _ in range(8)]
        x, y, pair = place.x, place.y, place.pair
        self.to_x = remote(own, whole.at[1], marks.take(), self.recv[0], x)
        self.to_y = remote(own, whole.at[2], marks.take(), self.recv[1], y)
        self.pass_x = remote(
            whole.at[2, top], whole.at[3, top], marks.take(), self.recv[2], x
        )
        self.pass_y = remote(
            whole.at[1, end], whole.at[3, end], marks.take(), self.recv[3], y
        )
        self.to_pair = [
            remote(
                own if step == 0 else whole.at[step],
                whole.at[4 + step],
                marks.take(),
                self.recv[4 + step],
                pair,
            )
            for step in range(4)
        ]
        self.far = (whole.at[3, top], whole.at[3, end])

    def start(self):
        self.to_x.start()
        self.to_y.start()
        self.to_pair[0].start()
        self.copy.start()

    def forward(self):
        arrived(self.whole.at[2], self.recv[1], self.place.y)
        self.pass_x.start()
        arrived(self.whole.at[1], self.recv[0], self.place.x)
        self.pass_y.start()
        self.to_pair[2].start()
        self.to_pair[1].start()

    def last(self):
        arrived(self.far[0], self.recv[2], self.place.x)
        arrived(self.far[1], self.recv[3], self.place.y)
        self.to_pair[3].start()

    def finish(self):
        for step in range(4):
            arrived(self.whole.at[4 + step], self.recv[4 + step], self.place.pair)
        for copy in [self.to_x, self.to_y, self.pass_x, self.pass_y] + self.to_pair:
            copy.wait_send()
        self.copy.wait()


class Exchange:
    def __init__(self, place, piece, slot, marks):
        self.place = place
        there = ((place.px, place.x), (place.py, place.y), (place.pd, place.d))
        self.copy = pltpu.make_async_copy(piece(place.p, 0), slot(place.p, 0), marks.take())
        self.sends, self.slots = [], []
        for index, (p, to) in enumerate(there):
            recv = marks.take()
            self.sends.append(
                remote(piece(p, index + 1), slot(place.p, index + 1), marks.take(), recv, to)
            )
            self.slots.append((slot(p, index + 1), recv, to))

    def start(self):
        for copy in (self.sends[2], self.sends[0], self.sends[1], self.copy):
            copy.start()

    def wait(self):
        self.copy.wait()
        for slot, recv, to in self.slots:
            arrived(slot, recv, to)

    def finish(self):
        for copy in self.sends:
            copy.wait_send()


class TokensScatter:
    SHAPES = 3 * 4 + 3

    @staticmethod
    def scratch(rows, width):
        return [
            pltpu.VMEM((4, rows, width), LOW),
            pltpu.VMEM((4, rows, width), LOW),
            pltpu.VMEM((4, rows, width), LOW),
            pltpu.VMEM((6, rows // 2, width), LOW),
        ]

    def __init__(self, place, parts, out, buffers, marks):
        self.place, self.parts, self.out = place, parts, out
        self.own, self.got, self.summed, self.landed = buffers
        self.rows = parts.shape[1]
        half = self.rows // 2
        top, end = pl.ds(0, half), pl.ds(half, half)
        x, y = place.x, place.y
        self.loads = [
            pltpu.make_async_copy(parts.at[step], self.own.at[step], marks.take())
            for step in range(4)
        ]
        self.recv_pair = [marks.take() for _ in range(4)]
        self.to_pair = [
            remote(
                parts.at[4 + step], self.got.at[step], marks.take(), self.recv_pair[step], place.pair
            )
            for step in range(4)
        ]
        self.recv = [marks.take() for _ in range(6)]
        routes = (
            (self.summed.at[3, top], x),
            (self.summed.at[3, end], y),
            (self.summed.at[1, top], x),
            (self.summed.at[1, end], x),
            (self.summed.at[2, top], y),
            (self.summed.at[2, end], y),
        )
        self.sends = [
            remote(src, self.landed.at[index], marks.take(), self.recv[index], to)
            for index, (src, to) in enumerate(routes)
        ]

    def start(self):
        for step in (3, 1, 2, 0):
            self.to_pair[step].start()
            self.loads[step].start()

    def joined(self, step):
        self.loads[step].wait()
        arrived(self.got.at[step], self.recv_pair[step], self.place.pair)
        if step == 0:
            return

        def work(rows):
            self.summed[step, rows] = low(f32(self.own[step, rows]) + f32(self.got[step, rows]))

        each_rows(self.rows, 16, work)

    def landed_at(self, index, to):
        arrived(self.landed.at[index], self.recv[index], to)

    def run(self):
        half = self.rows // 2
        place = self.place
        self.joined(3)
        self.sends[0].start()
        self.sends[1].start()
        self.joined(1)
        self.sends[2].start()
        self.joined(2)
        self.sends[5].start()
        self.landed_at(0, place.x)

        def top_work(rows):
            self.summed[2, rows] = low(f32(self.summed[2, rows]) + f32(self.landed[0, rows]))

        each_rows(half, 16, top_work)
        self.sends[4].start()
        self.landed_at(1, place.y)

        def end_work(rows):
            low_rows = pl.ds(pl.multiple_of(rows.start + half, 16), rows.size)
            self.summed[1, low_rows] = low(
                f32(self.summed[1, low_rows]) + f32(self.landed[1, rows])
            )

        each_rows(half, 16, end_work)
        self.sends[3].start()
        self.joined(0)

    def finish(self):
        half = self.rows // 2
        for index, to in ((2, self.place.x), (5, self.place.y), (4, self.place.y), (3, self.place.x)):
            self.landed_at(index, to)

        for base, first, second in ((0, 2, 4), (half, 3, 5)):

            def work(rows):
                own_rows = pl.ds(pl.multiple_of(rows.start + base, 16), rows.size)
                self.out[own_rows] = (
                    f32(self.own[0, own_rows])
                    + f32(self.got[0, own_rows])
                    + f32(self.landed[first, rows])
                    + f32(self.landed[second, rows])
                )

            each_rows(half, 16, work)
        for copy in self.to_pair + self.sends:
            copy.wait_send()


class LineScatter:
    @staticmethod
    def scratch(rows, width):
        return [pltpu.VMEM((6, rows, width), LOW)]

    def __init__(self, place, parts, out, buffers, marks):
        self.place, self.parts, self.out = place, parts, out
        self.kept = buffers[0]
        self.rows = parts.shape[1]
        self.passed, self.above, self.below, self.two, self.mid, self.own = (
            self.kept.at[index] for index in range(6)
        )
        self.recv = [marks.take() for _ in range(4)]
        z = place.z
        self.pass_up = remote(parts.at[3], self.passed, marks.take(), self.recv[0], place.up)
        self.pass_down = remote(parts.at[0], self.passed, marks.take(), self.recv[0], place.down)
        self.to_down = remote(
            parts.at[place.at(3)], self.above, marks.take(), self.recv[1], place.down
        )
        self.to_up = remote(parts.at[place.at(1)], self.below, marks.take(), self.recv[2], place.up)
        self.to_two = remote(self.mid, self.two, marks.take(), self.recv[3], place.two)
        self.load_mid = pltpu.make_async_copy(parts.at[place.at(2)], self.mid, marks.take())
        self.load_own = pltpu.make_async_copy(parts.at[z], self.own, marks.take())

    def start(self):
        z = self.place.z
        pl.when(z == 0)(self.pass_up.start)
        pl.when(z == 3)(self.pass_down.start)
        self.load_mid.start()
        pl.when(z > 0)(self.to_down.start)
        pl.when(z < 3)(self.to_up.start)
        self.load_own.start()
        self.load_mid.wait()
        pl.when((z == 0) | (z == 3))(self.to_two.start)

    def middle(self):
        z = self.place.z

        @pl.when((z == 1) | (z == 2))
        def _():
            arrived(self.passed, self.recv[0], self.place.two)

            def work(rows):
                self.kept[4, rows] = low(f32(self.kept[4, rows]) + f32(self.kept[0, rows]))

            each_rows(self.rows, 16, work)
            self.to_two.start()

    def finish(self):
        z, rows_all = self.place.z, self.rows
        out, kept = self.out, self.kept
        self.load_own.wait()

        @pl.when(z < 3)
        def _():
            arrived(self.above, self.recv[1], self.place.two)

            def work(rows):
                kept[5, rows] = low(f32(kept[5, rows]) + f32(kept[1, rows]))

            each_rows(rows_all, 16, work)

        @pl.when(z > 0)
        def _():
            arrived(self.below, self.recv[2], self.place.two)

            def work(rows):
                kept[5, rows] = low(f32(kept[5, rows]) + f32(kept[2, rows]))

            each_rows(rows_all, 16, work)

        arrived(self.two, self.recv[3], self.place.two)

        def work(rows):
            out[rows] = low(f32(kept[5, rows]) + f32(kept[3, rows]))

        each_rows(rows_all, 16, work)

    def drain(self):
        z = self.place.z
        pl.when(z == 0)(self.pass_up.wait_send)
        pl.when(z == 3)(self.pass_down.wait_send)
        pl.when(z > 0)(self.to_down.wait_send)
        pl.when(z < 3)(self.to_up.wait_send)
        self.to_two.wait_send()


def comm_params(number):
    return pltpu.CompilerParams(
        collective_id=number, has_side_effects=True, vmem_limit_bytes=56 * 1024 * 1024
    )


def comm_cost(micros):
    return pl.CostEstimate(flops=0, bytes_accessed=micros * 3_000_000, transcendentals=0)


def first_kernel(
    rows_ref,
    qkv_ref,
    out_ref,
    gate_ref,
    up_ref,
    down_ref,
    rows_all,
    qkv_all,
    out_all,
    gate_rows,
    up_rows,
    above_ref,
    below_ref,
    marks_ref,
):
    place = Place()
    marks = Marks(marks_ref)
    greet(place, [place.x, place.y, place.d, place.pair], True)
    qkv_pieces = Exchange(
        place, lambda p, step: qkv_ref.at[p], lambda p, step: qkv_all.at[place.z, p], marks
    )
    gate_pieces = Exchange(
        place, lambda p, step: gate_ref.at[p], lambda p, step: gate_rows.at[p], marks
    )
    up_pieces = Exchange(place, lambda p, step: up_ref.at[p], lambda p, step: up_rows.at[p], marks)
    tokens = TokensGather(place, rows_ref, rows_all, marks)
    qkv_line = LineGather(
        place,
        qkv_all.at[place.z],
        lambda z: qkv_all.at[z],
        marks.take(4),
        marks.take(4),
    )
    out_line = LineGather(
        place, out_ref, lambda z: out_all.at[z, place.p], marks.take(4), marks.take(4)
    )
    out_copy = pltpu.make_async_copy(out_ref, out_all.at[place.z, place.p], marks.take())
    near_recv = [marks.take(), marks.take()]
    to_down = remote(down_ref, above_ref, marks.take(), near_recv[0], place.down)
    to_up = remote(down_ref, below_ref, marks.take(), near_recv[1], place.up)
    out_planes = []
    for turn in range(4):
        z = place.z if turn == 0 else place.at(out_line.step(turn))
        out_planes.append(
            PlaneGather(
                place,
                out_ref if turn == 0 else out_all.at[z, place.p],
                lambda p, rows, z=z: out_all.at[z, p, rows],
                out_ref.shape[0],
                marks.take(4),
                marks.take(4),
            )
        )

    qkv_pieces.start()
    tokens.start()
    out_copy.start()
    qkv_pieces.wait()
    qkv_line.start()
    tokens.forward()
    out_planes[0].start()
    qkv_line.wait(1)
    out_line.start()
    qkv_line.wait(2)
    tokens.last()
    out_planes[0].forward()
    gate_pieces.start()
    out_line.wait(1)
    out_planes[1].start()
    out_line.wait(2)
    out_planes[2].start()
    qkv_line.wait(3)
    out_line.wait(3)
    out_planes[3].start()
    pl.when(place.z > 0)(to_down.start)
    pl.when(place.z < 3)(to_up.start)
    up_pieces.start()
    out_planes[1].forward()
    out_planes[2].forward()
    out_planes[3].forward()
    gate_pieces.wait()
    up_pieces.wait()
    for plane in out_planes:
        plane.wait_far()
    tokens.finish()
    for part in [qkv_pieces, gate_pieces, up_pieces, qkv_line, out_line] + out_planes:
        part.finish()
    out_copy.wait()

    @pl.when(place.z < 3)
    def _():
        arrived(above_ref, near_recv[0], place.two)
        to_up.wait_send()

    @pl.when(place.z > 0)
    def _():
        arrived(below_ref, near_recv[1], place.two)
        to_down.wait_send()


def first_gather(rows, qkv_pieces, output_weight, gate_pieces, up_pieces, down_weight):
    return pl.pallas_call(
        first_kernel,
        out_shape=(
            jax.ShapeDtypeStruct((8,) + rows.shape, LOW),
            jax.ShapeDtypeStruct((4,) + qkv_pieces.shape, LOW),
            jax.ShapeDtypeStruct((4, 4) + output_weight.shape, LOW),
            jax.ShapeDtypeStruct(gate_pieces.shape, LOW),
            jax.ShapeDtypeStruct(up_pieces.shape, LOW),
            jax.ShapeDtypeStruct(down_weight.shape, LOW),
            jax.ShapeDtypeStruct(down_weight.shape, LOW),
        ),
        in_specs=[ANYWHERE] * 6,
        out_specs=(ANYWHERE,) * 7,
        scratch_shapes=[pltpu.SemaphoreType.DMA((100,))],
        compiler_params=comm_params(0),
        cost_estimate=comm_cost(80),
    )(rows, qkv_pieces, output_weight, gate_pieces, up_pieces, down_weight)


def rows_kernel(rows_ref, line_ref, rows_all, line_all, marks_ref):
    place = Place()
    marks = Marks(marks_ref)
    greet(place, [place.x, place.y, place.pair], True)
    tokens = TokensGather(place, rows_ref, rows_all, marks)
    line = LineGather(place, line_ref, lambda z: line_all.at[z], marks.take(4), marks.take(4))
    copy = pltpu.make_async_copy(line_ref, line_all.at[place.z], marks.take())
    tokens.start()
    line.start()
    copy.start()
    tokens.forward()
    line.wait(2)
    tokens.last()
    line.wait(1)
    line.wait(3)
    tokens.finish()
    line.finish()
    copy.wait()


def rows_gather(rows, line_block):
    return pl.pallas_call(
        rows_kernel,
        out_shape=(
            jax.ShapeDtypeStruct((8,) + rows.shape, LOW),
            jax.ShapeDtypeStruct((4,) + line_block.shape, LOW),
        ),
        in_specs=[ANYWHERE] * 2,
        out_specs=(ANYWHERE,) * 2,
        scratch_shapes=[pltpu.SemaphoreType.DMA((40,))],
        compiler_params=comm_params(1),
        cost_estimate=comm_cost(50),
    )(rows, line_block)


def heads_out_kernel(heads_ref, own_ref, marks_ref):
    place = Place()
    greet(place, [place.x, place.y, place.d], False)
    exchange = Exchange(
        place,
        lambda p, step: heads_ref.at[:, step],
        lambda p, step: own_ref.at[p],
        Marks(marks_ref),
    )
    exchange.start()
    exchange.wait()
    exchange.finish()


def heads_to_tokens(heads):
    cores, _, rows, width = heads.shape
    return pl.pallas_call(
        heads_out_kernel,
        out_shape=jax.ShapeDtypeStruct((4, cores, rows, width), LOW),
        in_specs=[ANYWHERE],
        out_specs=ANYWHERE,
        scratch_shapes=[pltpu.SemaphoreType.DMA((8,))],
        compiler_params=comm_params(2),
        cost_estimate=comm_cost(15),
    )(heads)


def heads_in_kernel(own_ref, heads_ref, marks_ref):
    place = Place()
    greet(place, [place.x, place.y, place.d], False)
    width = heads_ref.shape[2]
    exchange = Exchange(
        place,
        lambda p, step: own_ref.at[:, pl.ds(pl.multiple_of(p * width, width), width)],
        lambda p, step: heads_ref.at[step],
        Marks(marks_ref),
    )
    exchange.start()
    exchange.wait()
    exchange.finish()


def tokens_to_heads(own):
    rows, width = own.shape
    return pl.pallas_call(
        heads_in_kernel,
        out_shape=jax.ShapeDtypeStruct((4, rows, width // 4), LOW),
        in_specs=[ANYWHERE],
        out_specs=ANYWHERE,
        scratch_shapes=[pltpu.SemaphoreType.DMA((8,))],
        compiler_params=comm_params(3),
        cost_estimate=comm_cost(15),
    )(own)


def sums_kernel(parts_ref, line_ref, out_ref, columns_ref, marks_ref, line_sum, *buffers):
    place = Place()
    marks = Marks(marks_ref)
    greet(place, [place.x, place.y, place.d, place.pair], True)
    tokens = TokensScatter(place, parts_ref, out_ref, buffers[:4], marks)
    line = LineScatter(place, line_ref, line_sum, buffers[4:], marks)
    rows = line_sum.shape[0] // 4
    pieces = Exchange(
        place,
        lambda p, step: line_sum.at[pl.ds(pl.multiple_of(p * rows, rows), rows)],
        lambda p, step: columns_ref.at[p],
        marks,
    )
    tokens.start()
    line.start()
    line.middle()
    tokens.run()
    line.finish()
    pieces.start()
    tokens.finish()
    line.drain()
    pieces.wait()
    pieces.finish()


def sums_scatter(parts, line_parts):
    rows, width = parts.shape[1:]
    line_rows, line_width = line_parts.shape[1:]
    return pl.pallas_call(
        sums_kernel,
        out_shape=(
            jax.ShapeDtypeStruct((rows, width), jnp.float32),
            jax.ShapeDtypeStruct((4, line_rows // 4, line_width), LOW),
        ),
        in_specs=[ANYWHERE] * 2,
        out_specs=(WHOLE, ANYWHERE),
        scratch_shapes=[
            pltpu.SemaphoreType.DMA((64,)),
            pltpu.VMEM((line_rows, line_width), LOW),
        ]
        + TokensScatter.scratch(rows, width)
        + LineScatter.scratch(line_rows, line_width),
        compiler_params=comm_params(4),
        cost_estimate=comm_cost(55),
    )(parts, line_parts)


def last_kernel(
    parts_ref,
    qkv_ref,
    proj_ref,
    gate_ref,
    input_ref,
    hidden_ref,
    norm_ref,
    gains_ref,
    grad_ref,
    qkv_columns,
    proj_out,
    gate_columns,
    gains_out,
    marks_ref,
    qkv_sum,
    row_sum,
    gain_rows,
    gain_mine,
    gain_got,
    *buffers,
):
    place = Place()
    marks = Marks(marks_ref)
    greet(place, [place.x, place.y, place.d, place.pair], True)
    tokens = TokensScatter(place, parts_ref, row_sum, buffers[:4], marks)
    qkv_line = LineScatter(place, qkv_ref, qkv_sum, buffers[4:5], marks)
    proj_line = LineScatter(place, proj_ref, proj_out, buffers[5:], marks)
    rows = qkv_sum.shape[0] // 4
    qkv_pieces = Exchange(
        place,
        lambda p, step: qkv_sum.at[pl.ds(pl.multiple_of(p * rows, rows), rows)],
        lambda p, step: qkv_columns.at[p],
        marks,
    )
    gate_pieces = Exchange(
        place, lambda p, step: gate_ref.at[p], lambda p, step: gate_columns.at[p], marks
    )
    near_z = {"f": place.z + 1 - 2 * (place.z % 2)}
    rounds = [
        remote(gain_mine.at[index], gain_got.at[index], marks.take(), marks.take(), to)
        for index, to in enumerate((place.pair, place.x, place.y, near_z, place.two))
    ]

    tokens.start()
    qkv_line.start()
    qkv_line.middle()
    proj_line.start()
    tokens.run()
    proj_line.middle()
    gate_pieces.start()
    qkv_line.finish()
    qkv_pieces.start()
    tokens.finish()

    gain_rows[...] = jnp.zeros_like(gain_rows)
    norm_row = norm_ref[...]

    def work(rows):
        values = f32(input_ref[rows])
        scales = inv_rms(values)
        upstream = row_sum[rows]
        weighted = upstream * norm_row
        inner_mean = jnp.mean(weighted * values, axis=-1, keepdims=True)
        grad_ref[rows] = (
            hidden_ref[rows]
            + scales * weighted
            - values * (scales * scales * scales) * inner_mean
        )
        parts = upstream * values * scales
        gain_rows[...] += parts[:8] + parts[8:]

    each_rows(row_sum.shape[0], 16, work)
    width = norm_row.shape[1]
    gain_mine[0, :, pl.ds(0, width)] = jnp.sum(gain_rows[...], axis=0, keepdims=True)
    gain_mine[0, :, pl.ds(width, gains_ref.shape[1])] = gains_ref[...]
    for index, copy in enumerate(rounds):
        copy.start()
        copy.wait()
        summed = gain_mine[index] + gain_got[index]
        if index < 4:
            gain_mine[index + 1] = summed
        else:
            gains_out[...] = summed
    proj_line.finish()
    qkv_line.drain()
    proj_line.drain()
    qkv_pieces.wait()
    qkv_pieces.finish()
    gate_pieces.wait()
    gate_pieces.finish()


def last_sums(parts, qkv_parts, proj_parts, gate_rows, layer_input, hidden_grad, norm, gains):
    rows, width = parts.shape[1:]
    qkv_rows, qkv_width = qkv_parts.shape[1:]
    gain_width = width + gains.shape[1]
    return pl.pallas_call(
        last_kernel,
        out_shape=(
            jax.ShapeDtypeStruct((rows, width), jnp.float32),
            jax.ShapeDtypeStruct((4, qkv_rows // 4, qkv_width), LOW),
            jax.ShapeDtypeStruct(proj_parts.shape[1:], LOW),
            jax.ShapeDtypeStruct(gate_rows.shape, LOW),
            jax.ShapeDtypeStruct((1, gain_width), jnp.float32),
        ),
        in_specs=[ANYWHERE] * 4 + [WHOLE] * 4,
        out_specs=(WHOLE, ANYWHERE, WHOLE, ANYWHERE, WHOLE),
        scratch_shapes=[
            pltpu.SemaphoreType.DMA((90,)),
            pltpu.VMEM((qkv_rows, qkv_width), LOW),
            pltpu.VMEM((rows, width), jnp.float32),
            pltpu.VMEM((8, width), jnp.float32),
            pltpu.VMEM((5, 1, gain_width), jnp.float32),
            pltpu.VMEM((5, 1, gain_width), jnp.float32),
        ]
        + TokensScatter.scratch(rows, width)
        + LineScatter.scratch(qkv_rows, qkv_width)
        + LineScatter.scratch(*proj_parts.shape[1:]),
        compiler_params=comm_params(5),
        cost_estimate=comm_cost(60),
    )(parts, qkv_parts, proj_parts, gate_rows, layer_input, hidden_grad, norm, gains)


def turn_pairs(values, cosine, sine):
    return values * cosine + pltpu.roll(values, HEAD_SIZE // 2, 1) * sine


def softmax_of(query, key, allowed):
    scores = matmul_nt(query, key) * HEAD_SIZE ** (-0.5)
    masked = jnp.where(allowed, scores, MASKED)
    exponent = jnp.exp(masked - jnp.max(masked, axis=-1, keepdims=True))
    return exponent / jnp.sum(exponent, axis=-1, keepdims=True)


def allowed_of(segment_col, segment_row, id_col, id_row):
    return (segment_col[0] == segment_row[0]) & (id_row[...] <= id_col[...])


def attend_kernel(
    raw_ref, cos_ref, sin_ref, segment_col, segment_row, id_col, id_row, gains_ref, low_ref, out_ref
):
    group_rows = cos_ref.shape[1]
    raw = raw_ref[...].reshape(group_rows, raw_ref.shape[3])
    heads = raw.shape[1] // HEAD_SIZE - 2
    cosine, sine = cos_ref[0], sin_ref[0]
    allowed = allowed_of(segment_col, segment_row, id_col, id_row)
    columns = [raw[:, head * HEAD_SIZE : (head + 1) * HEAD_SIZE] for head in range(heads + 2)]
    turned = []
    for head in range(heads + 1):
        gain = gains_ref[min(head // heads, 1)][None, :]
        turned.append(
            low(turn_pairs(columns[head] * inv_rms(columns[head]) * gain, cosine, sine))
        )
    value = low(columns[heads + 1])
    attended = [
        low(matmul(low(softmax_of(turned[head], turned[heads], allowed)), value))
        for head in range(heads)
    ]
    low_ref[...] = jnp.concatenate(turned + [value], axis=1).reshape(low_ref.shape)
    out_ref[...] = jnp.concatenate(attended, axis=1).reshape(out_ref.shape)


def attend_back_kernel(
    raw_ref,
    low_ref,
    grad_ref,
    cos_ref,
    sin_ref,
    segment_col,
    segment_row,
    id_col,
    id_row,
    gains_ref,
    out_ref,
    gain_out,
):
    group_rows = cos_ref.shape[1]
    raw = raw_ref[...].reshape(group_rows, raw_ref.shape[3])
    kept = low_ref[...].reshape(raw.shape)
    heads = raw.shape[1] // HEAD_SIZE - 2
    cosine, sine = cos_ref[0], sin_ref[0]
    allowed = allowed_of(segment_col, segment_row, id_col, id_row)
    lane = lambda values, head: values[:, head * HEAD_SIZE : (head + 1) * HEAD_SIZE]
    key, value = lane(kept, heads), lane(kept, heads + 1)
    scale = HEAD_SIZE ** (-0.5)
    turned_grads = []
    key_grad = jnp.zeros((group_rows, HEAD_SIZE), jnp.float32)
    value_grad = jnp.zeros((group_rows, HEAD_SIZE), jnp.float32)
    for head in range(heads):
        query, upstream = lane(kept, head), lane(grad_ref[0], head)
        probs = softmax_of(query, key, allowed)
        probs_grad = matmul_nt(upstream, value)
        scores_grad = low(
            probs * (probs_grad - jnp.sum(probs * probs_grad, axis=-1, keepdims=True))
        )
        turned_grads.append(matmul(scores_grad, key) * scale)
        key_grad = key_grad + matmul_tn(scores_grad, query)
        value_grad = value_grad + matmul_tn(low(probs), upstream)
    turned_grads.append(key_grad * scale)
    outs, gains = [], []
    for head in range(heads + 1):
        gain = gains_ref[min(head // heads, 1)][None, :]
        unnormed = lane(raw, head)
        upstream = turn_pairs(turned_grads[head], cosine, -sine)
        grad, gain_part = norm_back(unnormed, inv_rms(unnormed), gain, upstream)
        outs.append(low(grad))
        gains.append(gain_part[None, :])
    outs.append(low(value_grad))
    out_ref[...] = jnp.concatenate(outs, axis=1).reshape(out_ref.shape)
    query_gain = sum(gains[1:heads], gains[0])
    gain_out[0] = jnp.concatenate(
        [query_gain, gains[heads], jnp.zeros((6, HEAD_SIZE), jnp.float32)], axis=0
    )


def attention_specs(group_rows, rows):
    bucket = lambda width: pl.BlockSpec((2, 1, rows, width), lambda step: (0, step, 0, 0))
    tables = [
        pl.BlockSpec((1, group_rows, HEAD_SIZE), lambda step: (step, 0, 0)),
        pl.BlockSpec((1, group_rows, HEAD_SIZE), lambda step: (step, 0, 0)),
        pl.BlockSpec((1, group_rows, 1), lambda step: (step, 0, 0)),
        pl.BlockSpec((1, 1, group_rows), lambda step: (step, 0, 0)),
        pl.BlockSpec((group_rows, 1), lambda step: (0, 0)),
        pl.BlockSpec((1, group_rows), lambda step: (0, 0)),
        pl.BlockSpec((2, HEAD_SIZE), lambda step: (0, 0)),
    ]
    return bucket, tables


def attend(raw, tables):
    _, buckets, rows, width = raw.shape
    bucket, table_specs = attention_specs(2 * rows, rows)
    query_width = width - 2 * HEAD_SIZE
    return pl.pallas_call(
        attend_kernel,
        grid=(buckets,),
        out_shape=(
            jax.ShapeDtypeStruct(raw.shape, LOW),
            jax.ShapeDtypeStruct((2, buckets, rows, query_width), LOW),
        ),
        in_specs=[bucket(width)] + table_specs,
        out_specs=(bucket(width), bucket(query_width)),
        compiler_params=pltpu.CompilerParams(vmem_limit_bytes=48 * 1024 * 1024),
        cost_estimate=pl.CostEstimate(
            flops=30_000_000_000, bytes_accessed=20_000_000, transcendentals=0
        ),
    )(raw, *tables)


def attend_back(raw, kept, upstream, tables):
    _, buckets, rows, width = raw.shape
    bucket, table_specs = attention_specs(2 * rows, rows)
    return pl.pallas_call(
        attend_back_kernel,
        grid=(buckets,),
        out_shape=(
            jax.ShapeDtypeStruct(raw.shape, LOW),
            jax.ShapeDtypeStruct((buckets, 8, HEAD_SIZE), jnp.float32),
        ),
        in_specs=[
            bucket(width),
            bucket(width),
            pl.BlockSpec((1,) + upstream.shape[1:], lambda step: (step, 0, 0)),
        ]
        + table_specs,
        out_specs=(
            bucket(width),
            pl.BlockSpec((1, 8, HEAD_SIZE), lambda step: (step, 0, 0)),
        ),
        compiler_params=pltpu.CompilerParams(vmem_limit_bytes=48 * 1024 * 1024),
        cost_estimate=pl.CostEstimate(
            flops=40_000_000_000, bytes_accessed=20_000_000, transcendentals=0
        ),
    )(raw, kept, upstream, *tables)


def shards(
    layer_input,
    attn_norm,
    head_norms,
    query_weight,
    key_matrix,
    value_matrix,
    output_weight,
    mlp_norm,
    gate_weight,
    up_weight,
    down_weight,
    grad_out,
    doc_lengths,
):
    line_extent = lax.axis_size("f")
    on_line = line_extent == 4
    core = lax.axis_index("tensor")
    local_rows, model_width = layer_input.shape
    group_rows = 2 * local_rows
    all_rows = 8 * local_rows
    weight_rows = gate_weight.shape[0]
    down_rows = down_weight.shape[0]
    hidden_part = line_extent * down_rows
    query_part = query_weight.shape[1] // 4
    head_part = query_part + 2 * HEAD_SIZE

    def heads_of(weight):
        return weight.reshape(weight_rows, 4, -1).transpose(1, 0, 2)

    def units_of(weight):
        split = weight.reshape(weight_rows, line_extent, 4, down_rows)
        return split.transpose(2, 0, 1, 3).reshape(4, weight_rows, hidden_part)

    qkv_pieces = jnp.concatenate(
        [heads_of(query_weight), heads_of(key_matrix), heads_of(value_matrix)], axis=2
    )
    gate_pieces, up_pieces = units_of(gate_weight), units_of(up_weight)

    input_float = f32(layer_input)
    scale_attn = inv_rms(input_float)
    normed_own = low(input_float * scale_attn * attn_norm)
    if on_line:
        normed_attn, qkv_all, out_all, gate_rows, up_rows, *near_down = first_gather(
            normed_own, qkv_pieces, output_weight, gate_pieces, up_pieces, down_weight
        )
    else:
        normed_attn = tokens_gather(normed_own)
        exchanged = lambda pieces: natural_plane(plane_exchange(own_plane(pieces, 0)), 0)
        qkv_all = line_gather(exchanged(qkv_pieces))
        out_all = full_gather(output_weight)
        gate_rows, up_rows = exchanged(gate_pieces), exchanged(up_pieces)
        near_down = None
    normed_attn = normed_attn.reshape(all_rows, model_width)
    qkv_all = qkv_all.reshape(model_width, head_part)
    out_all = out_all.reshape(-1, model_width)
    gate_rows = gate_rows.reshape(4 * weight_rows, hidden_part)
    up_rows = up_rows.reshape(4 * weight_rows, hidden_part)

    lengths_list = plane_lengths(doc_lengths)
    local_ids = jnp.arange(local_rows, dtype=jnp.int32)
    row_ids = jnp.concatenate([core * local_rows + local_ids, (1 - core) * local_rows + local_ids])
    segments, positions = jax.vmap(lambda lengths: doc_layout(lengths, row_ids))(lengths_list)
    cos_tab, sin_tab = rope_tables(positions.reshape(-1), HEAD_SIZE)
    tables = (
        jnp.concatenate([cos_tab, cos_tab], axis=1).reshape(4, group_rows, HEAD_SIZE),
        jnp.concatenate([-sin_tab, sin_tab], axis=1).reshape(4, group_rows, HEAD_SIZE),
        segments[:, :, None],
        segments[:, None, :],
        row_ids[:, None],
        row_ids[None, :],
        head_norms,
    )
    qkv_raw = matmul(normed_attn, qkv_all).reshape(2, 4, local_rows, head_part)
    qkv_low, attended_heads = attend(qkv_raw, tables)
    gate_all = line_gather(gate_rows, (attended_heads,)).reshape(model_width, hidden_part)
    if on_line:
        attended = heads_to_tokens(attended_heads)
    else:
        attended = natural_plane(
            plane_exchange([attended_heads[:, step].reshape(group_rows, -1) for step in range(4)]),
            0,
        )
    attended = (
        attended.reshape(4, group_rows, query_part)
        .transpose(1, 0, 2)
        .reshape(group_rows, 4 * query_part)
    )
    hidden_state = input_float + pair_scatter(low(matmul(attended, out_all)))

    scale_mlp = inv_rms(hidden_state)
    normed_own = low(hidden_state * scale_mlp * mlp_norm)
    if on_line:
        normed_mlp, up_all = rows_gather(normed_own, up_rows)
    else:
        normed_mlp, up_all = tokens_gather(normed_own), line_gather(up_rows)
    normed_mlp = normed_mlp.reshape(all_rows, model_width)
    up_all = up_all.reshape(model_width, hidden_part)
    grad_all = tokens_gather(after(grad_out, normed_attn), (attended_heads,), (normed_mlp,))
    gate_raw = matmul(normed_mlp, gate_all)
    down_all = line_gather(after(down_weight, normed_mlp), (gate_raw,), near_down).reshape(
        hidden_part, model_width
    )
    up_raw = matmul(normed_mlp, up_all)
    activated = jax.nn.silu(gate_raw)
    inner_low = low(activated * up_raw)
    grad_down_part = low(matmul_tn(inner_low, grad_all))
    mlp_part = low(matmul(inner_low, down_all))
    inner_grad = matmul_nt(grad_all, down_all)
    sigmoid_gate = jax.nn.sigmoid(gate_raw)
    gate_grad = low(inner_grad * up_raw * sigmoid_gate * (1.0 + gate_raw * (1.0 - sigmoid_gate)))
    up_grad = low(inner_grad * activated)
    line_shape = (line_extent, 4 * weight_rows, hidden_part)
    grad_gate_part = low(matmul_tn(normed_mlp, gate_grad)).reshape(line_shape)
    grad_up_part = low(matmul_tn(normed_mlp, up_grad)).reshape(line_shape)
    mlp_grad = low(matmul_nt(gate_grad, gate_all) + matmul_nt(up_grad, up_all))
    if on_line:
        mlp_row_grad, grad_up_columns = sums_scatter(
            mlp_grad.reshape(8, local_rows, model_width), grad_up_part
        )
    else:
        mlp_row_grad = tokens_scatter(mlp_grad)
        grad_up_columns = exchanged(
            low(line_scatter(grad_up_part)).reshape(4, weight_rows, hidden_part)
        )
    hidden_norm_grad, mlp_gain_part = norm_back(hidden_state, scale_mlp, mlp_norm, mlp_row_grad)

    grad_down = line_scatter(
        grad_down_part.reshape(line_extent, down_rows, model_width), (up_grad,), (mlp_row_grad,)
    )
    mlp_rows = tokens_scatter(mlp_part, (up_grad,), (grad_up_part,), (mlp_row_grad,))
    layer_out = low(hidden_state + mlp_rows)

    hidden_grad = f32(grad_out) + hidden_norm_grad
    branch_grad = pair_gather(low(hidden_grad))
    attended_grad = low(matmul_nt(branch_grad, out_all))
    if on_line:
        heads_grad = tokens_to_heads(attended_grad)
    else:
        split = attended_grad.reshape(group_rows, 4, query_part).transpose(1, 0, 2)
        heads_grad = jnp.stack(plane_exchange(own_plane(split, 0)))
    qkv_grad, gain_parts = attend_back(qkv_raw, qkv_low, heads_grad, tables)
    qkv_grad = qkv_grad.reshape(all_rows, head_part)
    grad_qkv_part = low(matmul_tn(normed_attn, qkv_grad)).reshape(
        line_extent, 4 * weight_rows, head_part
    )
    attn_grad = low(matmul_nt(qkv_grad, qkv_all))
    grad_gate_rows = low(
        line_scatter(after(grad_gate_part, mlp_row_grad), (heads_grad,), (qkv_grad,))
    ).reshape(4, weight_rows, hidden_part)
    grad_proj_part = full_scatter_plane(
        low(matmul_tn(attended, branch_grad)), (heads_grad,), (qkv_grad,)
    )
    head_gains = jnp.sum(gain_parts, axis=0)[:2].reshape(-1)
    other_gains = jnp.concatenate([mlp_gain_part, head_gains])
    if on_line:
        grad_input, grad_qkv_columns, grad_out_proj, grad_gate_columns, gains = last_sums(
            attn_grad.reshape(8, local_rows, model_width),
            grad_qkv_part,
            grad_proj_part,
            grad_gate_rows,
            layer_input,
            hidden_grad,
            attn_norm[None],
            other_gains[None],
        )
        gains = gains.reshape(-1)
        grad_out_proj = f32(grad_out_proj)
    else:
        attn_row_grad = tokens_scatter(attn_grad)
        grad_qkv_columns = exchanged(
            low(line_scatter(grad_qkv_part)).reshape(4, weight_rows, head_part)
        )
        grad_gate_columns = exchanged(grad_gate_rows)
        grad_out_proj = line_scatter(grad_proj_part)
        input_norm_grad, attn_gain_part = norm_back(
            input_float, scale_attn, attn_norm, attn_row_grad
        )
        grad_input = hidden_grad + input_norm_grad
        gains = total_sum(
            jnp.concatenate([attn_gain_part, other_gains]).reshape(-1, HEAD_SIZE)
        ).reshape(-1)

    def heads_back(pieces):
        return f32(pieces).transpose(1, 0, 2).reshape(weight_rows, -1)

    def units_back(pieces):
        split = f32(pieces).reshape(4, weight_rows, line_extent, down_rows)
        return split.transpose(1, 2, 0, 3).reshape(weight_rows, -1)

    return (
        layer_out,
        grad_input,
        gains[:model_width],
        gains[2 * model_width :].reshape(2, HEAD_SIZE),
        heads_back(grad_qkv_columns[:, :, :query_part]),
        heads_back(grad_qkv_columns[:, :, query_part : query_part + HEAD_SIZE]),
        heads_back(grad_qkv_columns[:, :, query_part + HEAD_SIZE :]),
        grad_out_proj,
        gains[model_width : 2 * model_width],
        units_back(grad_gate_columns),
        units_back(grad_up_columns),
        grad_down,
    )


def solution(mesh):
    dp, tensor = mesh.shape["dp"], mesh.shape["tensor"]
    fine = Mesh(mesh.devices.reshape(dp // 4, 2, 2, tensor), ("f", "ty", "tx", "tensor"))
    rows = ("f", "ty", "tx")
    tokens = P(rows + ("tensor",), None)
    grid = P(rows, "tensor")
    units = P(("tensor",) + rows, None)
    return jax.shard_map(
        shards,
        mesh=fine,
        in_specs=(
            tokens, P(), P(), grid, grid, grid, units, P(), grid, grid, units, tokens, P(rows, None),
        ),
        out_specs=(tokens, tokens, P(), P(), grid, grid, grid, units, P(), grid, grid, units),
        check_vma=False,
    )
```

time: 1000 us -> 780 us (0.78)
  Pallas kernels: 0 us -> 375 us
  waiting for transfers between devices: 444 us -> 87 us
  starting transfers between devices: 166 us -> 62.6 us
  local copies, waits for them, and re-layouts: 138 us -> 58.5 us
  other arithmetic: 89.7 us -> 52.2 us
  matrix products: 150 us -> 138 us
    pallas_call x0 -> x8, Pallas kernels: none -> 375 us  [the longest x1 97.9 us: first_gather(): pl.pallas_call(first_kernel, out_shape=(jax.ShapeDtypeStruct((8,) + rows....]
    ppermute x75 -> x29, waiting for transfers between devices: 201 us -> 25.6 us  [swap(): return lax.ppermute(block, axis, [(0, 1), (1, 0)])]
    ppermute x4 -> x2, waiting for transfers between devices: 115 us -> 25 us  [line_scatter(): lax.ppermute(low(f32(part[2]) + f32(passed)), 'f', [(0, 2), (2, 0), (1, 3...]
    ppermute x4 -> x2, waiting for transfers between devices: 64.7 us -> 20.7 us  [line_gather(): two_away = lax.ppermute(block, 'f', [(0, 2), (2, 0), (1, 3), (3, 1)])]
    ppermute x75 -> x29, starting transfers between devices: 58.1 us -> 26.8 us  [swap(): return lax.ppermute(block, axis, [(0, 1), (1, 0)])]
    ppermute x4 -> x2, starting transfers between devices: 24 us -> 6.15 us  [line_scatter(): lax.ppermute(low(f32(part[2]) + f32(passed)), 'f', [(0, 2), (2, 0), (1, 3...]
    ppermute x4 -> x1, waiting for transfers between devices: 16.8 us -> 0.01 us  [line_gather(): above = lax.ppermute(block, 'f', [(1, 0), (2, 1), (3, 2)])]
    ppermute x4 -> x2, starting transfers between devices: 19.5 us -> 4.78 us  [line_scatter(): below = lax.ppermute(part[1], 'f', [(0, 1), (1, 2), (2, 3)])]
  transfers between devices with their start and end apart: 109 -> 43, of which waited for: 35 -> 9; matrix products, arithmetic and copies ran while one was open for 27% -> 24% of each run, Pallas kernels for 0% -> 38%
where the time goes in v2:
time: 780 us; the launch traced here: 776 us
  Pallas kernels  375 us (48%)
  matrix products  138 us (18%)
  waiting for transfers between devices  87 us (11%)
  starting transfers between devices  62.6 us (8%)
  local copies, waits for them, and re-layouts  58.5 us (8%)
  other arithmetic  52.2 us (7%)
    pallas_call x1, Pallas kernels, first_gather(): pl.pallas_call(first_kernel, out_shape=(jax.ShapeDtypeStruct((8,) + rows....  97.9 us
    pallas_call x1, Pallas kernels, last_sums(): pl.pallas_call(last_kernel, out_shape=(jax.ShapeDtypeStruct((rows, width)...  76.7 us
    pallas_call x1, Pallas kernels, rows_gather(): pl.pallas_call(rows_kernel, out_shape=(jax.ShapeDtypeStruct((8,) + rows.s...  75.3 us
    pallas_call x1, Pallas kernels, sums_scatter(): pl.pallas_call(sums_kernel, out_shape=(jax.ShapeDtypeStruct((rows, width)...  65.7 us
    dot_general x5, matrix products, matmul_nt(): lax.dot_general(left_mat, right_mat, (((1,), (1,)), ((), ())), preferred_...  52.1 us
    dot_general x5, matrix products, matmul_tn(): lax.dot_general(left_mat, right_mat, (((0,), (0,)), ((), ())), preferred_...  43.2 us
    dot_general x5, matrix products, matmul(): return jnp.dot(left_mat, right_mat, preferred_element_type=jnp.float32)  42.9 us
    unnamed x111, local copies, waits for them, and re-layouts  32 us
  transfers between devices with their start and end apart: 43, of which 9 were waited for; matrix products, arithmetic and copies ran while one was open for 24% of the time, Pallas kernels for 38%

profile of v2, /device:TPU:0, one launch (start us, length us, event | category | flops | bytes accessed | tf_op | source)
XLA Modules:
  0.0 775.6 jit_solution(15542372210260534991)
XLA Ops:
  18.2 97.9 %shard_map.220 = (bf16[8,256,2048]{2,1,0:T(8,128)(2,1)}, bf16[4,4,128,512]{3,2,1,0:T(8,128)(2,1)}, bf16[4,4,64,2048]{3,2,1,0:T(8,128)(2,1)}, bf16[4,128,768]{2,1...) custom-call(bf16[256,2048]{1,0:T(8,128)(2,1)} %fusion.3.rows_ref, ...), custom_call_target="tpu_custom_call" | custom-call | bytes 240000000 | tf_op jit(solution)/shard_map/pallas_call | solution.py:807
  119.2 10.5 %fusion.26.raw_ref = f32[2,4,256,512]{3,2,1,0:T(8,128)} fusion(bf16[2,4,256,2048]{3,2,1,0:T(8,128)(2,1)} %bitcast.200, bf16[2048,512,1,1]{1,0,3,2:T(8,128)(2,1)} %bitcast.212), kind=kOutput, calls=%fused_computation.122 | convolution fusion | flops 4294967296 | bytes 14680064 | tf_op jit(solution)/shard_map/dot_general | solution.py:20
  131.6 9.3 %collective-permute-done.2 = s32[1,6]{1,0:T(1,128)S(1)} collective-permute-done((s32[1,6]{1,0:T(1,128)}, s32[1,6]{1,0:T(1,128)S(1)}, u32[]{:S(2)}, u32[]{:S(2)}) %collective-permute-start.2) | collective-permute-done | bytes 56 | tf_op jit(solution)/shard_map/ppermute | solution.py:93
  147.6 20.0 %shard_map.221 = (bf16[2,4,256,512]{3,2,1,0:T(8,128)(2,1)}, bf16[2,4,256,256]{3,2,1,0:T(8,128)(2,1)S(1)}) custom-call(f32[2,4,256,512]{3,2,1,0:T(8,128)} %fusion.26.raw_ref, f32[4,512,128]{2,1,0:T(8,128)S(1)} %pad_maximum_fusion.3.cos_ref, f32[4,512,128]{2,1,0:T(8,128)S(1)} %pad_maximum_fusion.4.sin_ref, s32[4,512,1]{2,1,0:T(8,128)S(1)} %copy.103.segment_col, ...), custom_call_target="tpu_custom_call" | custom-call | flops 30000001024 | bytes 20000000 | tf_op jit(solution)/shard_map/pallas_call | solution.py:1197
  168.5 11.3 %shard_map.222 = bf16[4,2,256,256]{3,2,1,0:T(8,128)(2,1)} custom-call(bf16[2,4,256,256]{3,2,1,0:T(8,128)(2,1)} %copy-done.5), custom_call_target="tpu_custom_call" | custom-call | bytes 45000000 | tf_op jit(solution)/shard_map/pallas_call | solution.py:877
  212.7 75.3 %shard_map.223 = (bf16[8,256,2048]{2,1,0:T(8,128)(2,1)}, bf16[4,512,768]{2,1,0:T(8,128)(2,1)}) custom-call(bf16[256,2048]{1,0:T(8,128)(2,1)} %multiply_convert_fusion.3.rows_ref, bf16[512,768]{1,0:T(8,128)(2,1)} %bitcast.189), custom_call_target="tpu_custom_call" | custom-call | bytes 150000000 | tf_op jit(solution)/shard_map/pallas_call | solution.py:847
  288.0 11.9 %fusion.28 = f32[2048,768]{1,0:T(8,128)} fusion(bf16[2048,2048]{1,0:T(8,128)(2,1)} %bitcast.202, bf16[2048,768]{1,0:T(8,128)(2,1)} %bitcast.210), kind=kOutput, calls=%fused_computation.124 | convolution fusion | flops 6442450944 | bytes 17825792 | tf_op jit(solution)/shard_map/dot_general | solution.py:20
  307.5 8.5 %fusion.27 = f32[2048,768]{1,0:T(8,128)} fusion(bf16[2048,2048]{1,0:T(8,128)(2,1)S(1)} %bitcast.204, bf16[2048,768]{1,0:T(8,128)(2,1)S(1)} %bitcast.178), kind=kOutput, calls=%fused_computation.123 | convolution fusion | flops 6442450944 | bytes 17825792 | tf_op jit(solution)/shard_map/dot_general | solution.py:20
  316.0 20.7 %collective-permute-done.8 = bf16[192,2048]{1,0:T(8,128)(2,1)S(1)} collective-permute-done((bf16[192,2048]{1,0:T(8,128)(2,1)S(1)}, bf16[192,2048]{1,0:T(8,128)(2,1)S(1)}, u32[]{:S(2)}, u32[]{:S(2)}) %collective-permute-start.8) | collective-permute-done | bytes 786464 | tf_op jit(solution)/shard_map/ppermute | solution.py:151
  342.4 15.6 %collective-permute-done.9 = bf16[192,2048]{1,0:T(8,128)(2,1)S(1)} collective-permute-done((bf16[192,2048]{1,0:T(8,128)(2,1)S(1)}, bf16[192,2048]{1,0:T(8,128)(2,1)S(1)}, u32[]{:S(2)}, u32[]{:S(2)}) %collective-permute-start.9) | collective-permute-done | bytes 786464 | tf_op jit(solution)/shard_map/ppermute | solution.py:158
  358.7 16.5 %multiply_convert_fusion = (bf16[2048,768]{1,0:T(8,128)(2,1)}, bf16[2048,768]{1,0:T(8,128)(2,1)}, bf16[2048,768]{1,0:T(8,128)(2,1)}) fusion(f32[2048,768]{1,0:T(8,128)} %fusion.27, f32[2048,768]{1,0:T(8,128)} %fusion.28, bf16[2048,2048]{1,0:T(8,128)(2,1)} %constant_dynamic-update-slice_fusion, bf16[768,2048]{1,0:T(8,128)(2,1)S(1)} %bitcast.176), kind=kOutput, calls=%fused_computation.3 | convolution fusion | flops 6466043904 | bytes 33554432 | tf_op jit(solution)/shard_map/dot_general | solution.py:30
  375.1 10.3 %convolution_convert_fusion.3 = bf16[768,2048]{1,0:T(8,128)(2,1)S(1)} fusion(bf16[2048,768]{1,0:T(8,128)(2,1)} %get-tuple-element.172, bf16[2048,2048]{1,0:T(8,128)(2,1)} %constant_dynamic-update-slice_fusion), kind=kOutput, calls=%fused_computation.9 | convolution fusion | flops 6444023808 | bytes 14680064 | tf_op jit(solution)/shard_map/dot_general | solution.py:24
  400.6 10.1 %fusion.29 = f32[2048,2048]{1,0:T(8,128)} fusion(bf16[2048,768]{1,0:T(8,128)(2,1)S(1)} %copy-done.41, bf16[2048,768]{1,0:T(8,128)(2,1)S(1)} %bitcast.211), kind=kOutput, calls=%fused_computation.125 | convolution fusion | flops 6442450944 | bytes 23068672 | tf_op jit(solution)/shard_map/dot_general | solution.py:30
  410.6 13.2 %add_convert_fusion = bf16[2048,2048]{1,0:T(8,128)(2,1)} fusion(f32[2048,2048]{1,0:T(8,128)} %fusion.29, bf16[2048,768]{1,0:T(8,128)(2,1)} %get-tuple-element.170, bf16[2048,768]{1,0:T(8,128)(2,1)S(1)} %bitcast.179), kind=kOutput, calls=%fused_computation | convolution fusion | flops 6450839552 | bytes 31457280 | tf_op jit(solution)/shard_map/dot_general | solution.py:30
  433.4 10.5 %convolution_convert_fusion.5 = bf16[2048,768]{1,0:T(8,128)(2,1)} fusion(bf16[2048,2048]{1,0:T(8,128)(2,1)} %bitcast.203, bf16[2048,768]{1,0:T(8,128)(2,1)S(1)} %copy-done.42), kind=kOutput, calls=%fused_computation.11 | convolution fusion | flops 6444023808 | bytes 14680064 | tf_op jit(solution)/shard_map/dot_general | solution.py:24
  443.9 65.7 %shard_map.224 = (f32[256,2048]{1,0:T(8,128)}, bf16[4,128,768]{2,1,0:T(8,128)(2,1)}) custom-call(bf16[8,256,2048]{2,1,0:T(8,128)(2,1)} %bitcast.157, bf16[4,512,768]{2,1,0:T(8,128)(2,1)} %bitcast.180), custom_call_target="tpu_custom_call" | custom-call | bytes 165000000 | tf_op jit(solution)/shard_map/pallas_call | solution.py:944
  517.5 7.3 collective-permute-done.25
  544.2 8.5 %convolution_convert_fusion.4 = bf16[2048,768]{1,0:T(8,128)(2,1)} fusion(bf16[2048,2048]{1,0:T(8,128)(2,1)S(1)} %bitcast.207, bf16[2048,768]{1,0:T(8,128)(2,1)S(1)} %copy-done.43), kind=kOutput, calls=%fused_computation.10 | convolution fusion | flops 6444023808 | bytes 14680064 | tf_op jit(solution)/shard_map/dot_general | solution.py:24
  561.1 7.3 collective-permute-start.37
  571.9 19.5 %collective-permute-done.42 = bf16[192,2048]{1,0:T(8,128)(2,1)} collective-permute-done((bf16[192,2048]{1,0:T(8,128)(2,1)}, bf16[192,2048]{1,0:T(8,128)(2,1)}, u32[]{:S(2)}, u32[]{:S(2)}) %collective-permute-start.42) | collective-permute-done | bytes 786464 | tf_op jit(solution)/shard_map/ppermute | solution.py:183
  600.1 10.6 %shard_map.225.grad_ref = bf16[4,512,256]{2,1,0:T(8,128)(2,1)} custom-call(bf16[512,1024]{1,0:T(8,128)(2,1)} %convolution_convert_fusion.8.own_ref), custom_call_target="tpu_custom_call" | custom-call | bytes 45000000 | tf_op jit(solution)/shard_map/pallas_call | solution.py:905
  612.0 17.7 %shard_map.226 = (bf16[2,4,256,512]{3,2,1,0:T(8,128)(2,1)}, f32[4,8,128]{2,1,0:T(8,128)S(1)}) custom-call(f32[2,4,256,512]{3,2,1,0:T(8,128)} %fusion.26.raw_ref, bf16[2,4,256,512]{3,2,1,0:T(8,128)(2,1)} %get-tuple-element.98.low_ref, bf16[4,512,256]{2,1,0:T(8,128)(2,1)S(1)} %copy-done.4, f32[4,512,128]{2,1,0:T(8,128)S(1)} %copy-done.3, ...), custom_call_target="tpu_custom_call" | custom-call | flops 40000000000 | bytes 20000000 | tf_op jit(solution)/shard_map/pallas_call | solution.py:1216
  629.7 9.9 %convolution_convert_fusion.7 = bf16[2048,512]{1,0:T(8,128)(2,1)} fusion(bf16[2048,2048]{1,0:T(8,128)(2,1)} %bitcast.201, bf16[2048,512]{1,0:T(8,128)(2,1)} %bitcast.214), kind=kOutput, calls=%fused_computation.16 | convolution fusion | flops 4296015872 | bytes 12582912 | tf_op jit(solution)/shard_map/dot_general | solution.py:24
  683.9 76.7 %shard_map.227 = (f32[256,2048]{1,0:T(8,128)}, bf16[4,128,512]{2,1,0:T(8,128)(2,1)}, bf16[64,2048]{1,0:T(8,128)(2,1)}, bf16[4,128,768]{2,1,0:T(8,128)(2,1)}, f32[1,4352]{1,0:T(1,128)}) custom-call(bf16[8,256,2048]{2,1,0:T(8,128)(2,1)} %bitcast.156, bf16[4,512,512]{2,1,0:T(8,128)(2,1)} %bitcast.181, bf16[4,64,2048]{2,1,0:T(8,128)(2,1)} %bitcast.163, ...), custom_call_target="tpu_custom_call" | custom-call | bytes 180000000 | tf_op jit(solution)/shard_map/pallas_call | solution.py:1060
  (283 shorter events, 208.9 us)
Async XLA Ops:
  0.7 131.0 %collective-permute-start = (s32[1,6]{1,0:T(1,128)}, s32[1,6]{1,0:T(1,128)S(1)}, u32[]{:S(2)}, u32[]{:S(2)}) collective-permute-start(s32[1,6]{1,0:T(1,128)} %param.25), channel_id=1, source_target_pairs={{0,2},{2,0},{1,3},{3,1},{4,6},{6,4},{5,7},{7,5},{8,10},{10,8},{9,1... | collective-permute-start | bytes 80 | tf_op jit(solution)/shard_map/ppermute | solution.py:93
  3.7 126.0 %collective-permute-start.1 = (s32[1,6]{1,0:T(1,128)}, s32[1,6]{1,0:T(1,128)}, u32[]{:S(2)}, u32[]{:S(2)}) collective-permute-start(s32[1,6]{1,0:T(1,128)} %param.25), channel_id=1, source_target_pairs={{0,4},{4,0},{1,5},{5,1},{2,6},{6,2},{3,7},{7,3},{8,12},{12,8},{9,1... | collective-permute-start | bytes 80 | tf_op jit(solution)/shard_map/ppermute | solution.py:93
  116.2 86.8 %collective-permute-start.12 = (bf16[256,2048]{1,0:T(8,128)(2,1)S(1)}, bf16[256,2048]{1,0:T(8,128)(2,1)}, u32[]{:S(2)}, u32[]{:S(2)}) collective-permute-start(bf16[256,2048]{1,0:T(8,128)(2,1)S(1)} %copy-done.13), channel_id=1, source_target_pairs={{0,4},{4,0},{1,5},{5,1},{2,6},{6,2},{3,7},{7,3},{8,12},{12,8},{9,1... | collective-permute-start | bytes 3145736 | tf_op jit(solution)/shard_map/ppermute | solution.py:93
  117.8 81.8 %collective-permute-start.11 = (bf16[256,2048]{1,0:T(8,128)(2,1)S(1)}, bf16[256,2048]{1,0:T(8,128)(2,1)}, u32[]{:S(2)}, u32[]{:S(2)}) collective-permute-start(bf16[256,2048]{1,0:T(8,128)(2,1)S(1)} %copy-done.13), channel_id=1, source_target_pairs={{0,2},{2,0},{1,3},{3,1},{4,6},{6,4},{5,7},{7,5},{8,10},{10,8},{9,1... | collective-permute-start | bytes 3145736 | tf_op jit(solution)/shard_map/ppermute | solution.py:93
  118.3 79.7 %collective-permute-start.4 = (bf16[512,768]{1,0:T(8,128)(2,1)}, bf16[512,768]{1,0:T(8,128)(2,1)}, u32[]{:S(2)}, u32[]{:S(2)}) collective-permute-start(bf16[512,768]{1,0:T(8,128)(2,1)} %bitcast.26), channel_id=1, source_target_pairs={{0,16},{16,0},{8,24},{24,8},{1,17},{17,1},{9,25},{25,9},{2,18},{18... | collective-permute-start | bytes 2359304 | tf_op jit(solution)/shard_map/ppermute | solution.py:151
  189.4 117.5 %collective-permute-start.7 = (bf16[512,768]{1,0:T(8,128)(2,1)}, bf16[512,768]{1,0:T(8,128)(2,1)}, u32[]{:S(2)}, u32[]{:S(2)}) collective-permute-start(bf16[512,768]{1,0:T(8,128)(2,1)} %bitcast.26), channel_id=1, source_target_pairs={{0,8},{8,16},{16,24},{1,9},{9,17},{17,25},{2,10},{10,18},{18,26},{... | collective-permute-start | bytes 2359304 | tf_op jit(solution)/shard_map/ppermute | solution.py:154
  198.0 105.0 %collective-permute-start.6 = (bf16[512,768]{1,0:T(8,128)(2,1)}, bf16[512,768]{1,0:T(8,128)(2,1)}, u32[]{:S(2)}, u32[]{:S(2)}) collective-permute-start(bf16[512,768]{1,0:T(8,128)(2,1)} %bitcast.26), channel_id=1, source_target_pairs={{8,0},{16,8},{24,16},{9,1},{17,9},{25,17},{10,2},{18,10},{26,18},{... | collective-permute-start | bytes 2359304 | tf_op jit(solution)/shard_map/ppermute | solution.py:153
  199.6 104.0 %collective-permute-start.5 = (bf16[512,768]{1,0:T(8,128)(2,1)}, bf16[512,768]{1,0:T(8,128)(2,1)S(1)}, u32[]{:S(2)}, u32[]{:S(2)}) collective-permute-start(bf16[512,768]{1,0:T(8,128)(2,1)} %collective-permute-done.4), channel_id=1, source_target_pairs={{8,0},{16,24},{9,1},{17,25},{10,2},{18,26},{11,3},{19,27},{12,4},{... | collective-permute-start | bytes 2359304 | tf_op jit(solution)/shard_map/ppermute | solution.py:158
  204.0 97.1 %collective-permute-start.13 = (bf16[128,2048]{1,0:T(8,128)(2,1)S(1)}, bf16[128,2048]{1,0:T(8,128)(2,1)S(1)}, u32[]{:S(2)}, u32[]{:S(2)}) collective-permute-start(bf16[128,2048]{1,0:T(8,128)(2,1)S(1)} %slice.173), channel_id=1, source_target_pairs={{0,2},{2,0},{1,3},{3,1},{4,6},{6,4},{5,7},{7,5},{8,10},{10,8},{9,1... | collective-permute-start | bytes 1572872 | tf_op jit(solution)/shard_map/ppermute | solution.py:93
  208.1 93.0 %collective-permute-start.14 = (bf16[128,2048]{1,0:T(8,128)(2,1)}, bf16[128,2048]{1,0:T(8,128)(2,1)S(1)}, u32[]{:S(2)}, u32[]{:S(2)}) collective-permute-start(bf16[128,2048]{1,0:T(8,128)(2,1)} %slice.174), channel_id=1, source_target_pairs={{0,4},{4,0},{1,5},{5,1},{2,6},{6,2},{3,7},{7,3},{8,12},{12,8},{9,1... | collective-permute-start | bytes 1572872 | tf_op jit(solution)/shard_map/ppermute | solution.py:93
  301.1 35.6 %collective-permute-start.8 = (bf16[192,2048]{1,0:T(8,128)(2,1)S(1)}, bf16[192,2048]{1,0:T(8,128)(2,1)S(1)}, u32[]{:S(2)}, u32[]{:S(2)}) collective-permute-start(bf16[192,2048]{1,0:T(8,128)(2,1)S(1)} %copy-done.15), channel_id=1, source_target_pairs={{0,16},{16,0},{8,24},{24,8},{1,17},{17,1},{9,25},{25,9},{2,18},{18... | collective-permute-start | bytes 2359304 | tf_op jit(solution)/shard_map/ppermute | solution.py:151
  301.2 36.8 %collective-permute-start.15 = (bf16[256,2048]{1,0:T(8,128)(2,1)S(1)}, bf16[256,2048]{1,0:T(8,128)(2,1)S(1)}, u32[]{:S(2)}, u32[]{:S(2)}) collective-permute-start(bf16[256,2048]{1,0:T(8,128)(2,1)S(1)} %copy-done.13), channel_id=1, source_target_pairs={{0,1},{1,0},{2,3},{3,2},{4,5},{5,4},{6,7},{7,6},{8,9},{9,8},{10,11... | collective-permute-start | bytes 3145736 | tf_op jit(solution)/shard_map/ppermute | solution.py:93
  303.1 36.0 %collective-permute-start.16 = (bf16[256,2048]{1,0:T(8,128)(2,1)}, bf16[256,2048]{1,0:T(8,128)(2,1)S(1)}, u32[]{:S(2)}, u32[]{:S(2)}) collective-permute-start(bf16[256,2048]{1,0:T(8,128)(2,1)} %collective-permute-done.11), channel_id=1, source_target_pairs={{0,1},{1,0},{2,3},{3,2},{4,5},{5,4},{6,7},{7,6},{8,9},{9,8},{10,11... | collective-permute-start | bytes 3145736 | tf_op jit(solution)/shard_map/ppermute | solution.py:93
  303.6 36.6 %collective-permute-start.17 = (bf16[256,2048]{1,0:T(8,128)(2,1)}, bf16[256,2048]{1,0:T(8,128)(2,1)S(1)}, u32[]{:S(2)}, u32[]{:S(2)}) collective-permute-start(bf16[256,2048]{1,0:T(8,128)(2,1)} %collective-permute-done.12), channel_id=1, source_target_pairs={{0,1},{1,0},{2,3},{3,2},{4,5},{5,4},{6,7},{7,6},{8,9},{9,8},{10,11... | collective-permute-start | bytes 3145736 | tf_op jit(solution)/shard_map/ppermute | solution.py:93
  306.9 34.4 %collective-permute-start.18 = (bf16[256,2048]{1,0:T(8,128)(2,1)S(1)}, bf16[256,2048]{1,0:T(8,128)(2,1)S(1)}, u32[]{:S(2)}, u32[]{:S(2)}) collective-permute-start(bf16[256,2048]{1,0:T(8,128)(2,1)S(1)} %pad_maximum_fusion.5), channel_id=1, source_target_pairs={{0,1},{1,0},{2,3},{3,2},{4,5},{5,4},{6,7},{7,6},{8,9},{9,8},{10,11... | collective-permute-start | bytes 3145736 | tf_op jit(solution)/shard_map/ppermute | solution.py:93
  394.3 132.0 %collective-permute-start.41 = (bf16[192,2048]{1,0:T(8,128)(2,1)}, bf16[192,2048]{1,0:T(8,128)(2,1)}, u32[]{:S(2)}, u32[]{:S(2)}) collective-permute-start(bf16[192,2048]{1,0:T(8,128)(2,1)} %get-tuple-element.160), channel_id=1, source_target_pairs={{0,8},{24,16},{1,9},{25,17},{2,10},{26,18},{3,11},{27,19},{4,12},{... | collective-permute-start | bytes 2359304 | tf_op jit(solution)/shard_map/ppermute | solution.py:179
  432.0 83.3 %collective-permute-start.23 = (bf16[128,2048]{1,0:T(8,128)(2,1)}, bf16[128,2048]{1,0:T(8,128)(2,1)}, u32[]{:S(2)}, u32[]{:S(2)}) collective-permute-start(bf16[128,2048]{1,0:T(8,128)(2,1)} %get-tuple-element.192), channel_id=1, source_target_pairs={{0,2},{2,0},{1,3},{3,1},{4,6},{6,4},{5,7},{7,5},{8,10},{10,8},{9,1... | collective-permute-start | bytes 1572872 | tf_op jit(solution)/shard_map/ppermute | solution.py:93
  526.3 42.2 %collective-permute-start.40 = (bf16[192,2048]{1,0:T(8,128)(2,1)}, bf16[192,2048]{1,0:T(8,128)(2,1)}, u32[]{:S(2)}, u32[]{:S(2)}) collective-permute-start(bf16[192,2048]{1,0:T(8,128)(2,1)} %get-tuple-element.161), channel_id=1, source_target_pairs={{0,8},{8,16},{16,24},{1,9},{9,17},{17,25},{2,10},{10,18},{18,26},{... | collective-permute-start | bytes 2359304 | tf_op jit(solution)/shard_map/ppermute | solution.py:181
  531.4 39.2 %collective-permute-start.39 = (bf16[192,2048]{1,0:T(8,128)(2,1)}, bf16[192,2048]{1,0:T(8,128)(2,1)}, u32[]{:S(2)}, u32[]{:S(2)}) collective-permute-start(bf16[192,2048]{1,0:T(8,128)(2,1)} %get-tuple-element.162), channel_id=1, source_target_pairs={{8,0},{16,8},{24,16},{9,1},{17,9},{25,17},{10,2},{18,10},{26,18},{... | collective-permute-start | bytes 2359304 | tf_op jit(solution)/shard_map/ppermute | solution.py:180
  532.8 58.6 %collective-permute-start.42 = (bf16[192,2048]{1,0:T(8,128)(2,1)}, bf16[192,2048]{1,0:T(8,128)(2,1)}, u32[]{:S(2)}, u32[]{:S(2)}) collective-permute-start(bf16[192,2048]{1,0:T(8,128)(2,1)} %fusion.5), channel_id=1, source_target_pairs={{0,16},{16,0},{8,24},{24,8},{1,17},{17,1},{9,25},{25,9},{2,18},{18... | collective-permute-start | bytes 2359304 | tf_op jit(solution)/shard_map/ppermute | solution.py:183
  542.6 52.3 %collective-permute-start.28 = (bf16[256,2048]{1,0:T(8,128)(2,1)}, bf16[256,2048]{1,0:T(8,128)(2,1)}, u32[]{:S(2)}, u32[]{:S(2)}) collective-permute-start(bf16[256,2048]{1,0:T(8,128)(2,1)} %get-tuple-element.166), channel_id=1, source_target_pairs={{0,1},{1,0},{2,3},{3,2},{4,5},{5,4},{6,7},{7,6},{8,9},{9,8},{10,11... | collective-permute-start | bytes 3145736 | tf_op jit(solution)/shard_map/ppermute | solution.py:93
  561.1 93.3 %collective-permute-start.37 = (bf16[512,768]{1,0:T(8,128)(2,1)S(1)}, bf16[512,768]{1,0:T(8,128)(2,1)S(1)}, u32[]{:S(2)}, u32[]{:S(2)}) collective-permute-start(bf16[512,768]{1,0:T(8,128)(2,1)S(1)} %get-tuple-element.163), channel_id=1, source_target_pairs={{0,8},{24,16},{1,9},{25,17},{2,10},{26,18},{3,11},{27,19},{4,12},{... | collective-permute-start | bytes 2359304 | tf_op jit(solution)/shard_map/ppermute | solution.py:179
  568.4 95.1 %collective-permute-start.36 = (bf16[512,768]{1,0:T(8,128)(2,1)}, bf16[512,768]{1,0:T(8,128)(2,1)}, u32[]{:S(2)}, u32[]{:S(2)}) collective-permute-start(bf16[512,768]{1,0:T(8,128)(2,1)} %get-tuple-element.164), channel_id=1, source_target_pairs={{0,8},{8,16},{16,24},{1,9},{9,17},{17,25},{2,10},{10,18},{18,26},{... | collective-permute-start | bytes 2359304 | tf_op jit(solution)/shard_map/ppermute | solution.py:181
  570.6 93.6 %collective-permute-start.35 = (bf16[512,768]{1,0:T(8,128)(2,1)}, bf16[512,768]{1,0:T(8,128)(2,1)}, u32[]{:S(2)}, u32[]{:S(2)}) collective-permute-start(bf16[512,768]{1,0:T(8,128)(2,1)} %get-tuple-element.165), channel_id=1, source_target_pairs={{8,0},{16,8},{24,16},{9,1},{17,9},{25,17},{10,2},{18,10},{26,18},{... | collective-permute-start | bytes 2359304 | tf_op jit(solution)/shard_map/ppermute | solution.py:180
  (65 other events, 850.7 us)

commit v3 on v2

--- a/solution.py
+++ b/solution.py
@@ -492,142 +492,29 @@
             copy.wait_send()
 
 
-class TokensScatter:
-    SHAPES = 3 * 4 + 3
-
-    @staticmethod
-    def scratch(rows, width):
-        return [
-            pltpu.VMEM((4, rows, width), LOW),
-            pltpu.VMEM((4, rows, width), LOW),
-            pltpu.VMEM((4, rows, width), LOW),
-            pltpu.VMEM((6, rows // 2, width), LOW),
-        ]
-
-    def __init__(self, place, parts, out, buffers, marks):
-        self.place, self.parts, self.out = place, parts, out
-        self.own, self.got, self.summed, self.landed = buffers
-        self.rows = parts.shape[1]
-        half = self.rows // 2
-        top, end = pl.ds(0, half), pl.ds(half, half)
-        x, y = place.x, place.y
-        self.loads = [
-            pltpu.make_async_copy(parts.at[step], self.own.at[step], marks.take())
-            for step in range(4)
-        ]
-        self.recv_pair = [marks.take() for _ in range(4)]
-        self.to_pair = [
-            remote(
-                parts.at[4 + step], self.got.at[step], marks.take(), self.recv_pair[step], place.pair
-            )
-            for step in range(4)
-        ]
-        self.recv = [marks.take() for _ in range(6)]
-        routes = (
-            (self.summed.at[3, top], x),
-            (self.summed.at[3, end], y),
-            (self.summed.at[1, top], x),
-            (self.summed.at[1, end], x),
-            (self.summed.at[2, top], y),
-            (self.summed.at[2, end], y),
-        )
-        self.sends = [
-            remote(src, self.landed.at[index], marks.take(), self.recv[index], to)
-            for index, (src, to) in enumerate(routes)
-        ]
-
-    def start(self):
-        for step in (3, 1, 2, 0):
-            self.to_pair[step].start()
-            self.loads[step].start()
-
-    def joined(self, step):
-        self.loads[step].wait()
-        arrived(self.got.at[step], self.recv_pair[step], self.place.pair)
-        if step == 0:
-            return
-
-        def work(rows):
-            self.summed[step, rows] = low(f32(self.own[step, rows]) + f32(self.got[step, rows]))
-
-        each_rows(self.rows, 16, work)
-
-    def landed_at(self, index, to):
-        arrived(self.landed.at[index], self.recv[index], to)
-
-    def run(self):
-        half = self.rows // 2
-        place = self.place
-        self.joined(3)
-        self.sends[0].start()
-        self.sends[1].start()
-        self.joined(1)
-        self.sends[2].start()
-        self.joined(2)
-        self.sends[5].start()
-        self.landed_at(0, place.x)
-
-        def top_work(rows):
-            self.summed[2, rows] = low(f32(self.summed[2, rows]) + f32(self.landed[0, rows]))
-
-        each_rows(half, 16, top_work)
-        self.sends[4].start()
-        self.landed_at(1, place.y)
-
-        def end_work(rows):
-            low_rows = pl.ds(pl.multiple_of(rows.start + half, 16), rows.size)
-            self.summed[1, low_rows] = low(
-                f32(self.summed[1, low_rows]) + f32(self.landed[1, rows])
-            )
-
-        each_rows(half, 16, end_work)
-        self.sends[3].start()
-        self.joined(0)
-
-    def finish(self):
-        half = self.rows // 2
-        for index, to in ((2, self.place.x), (5, self.place.y), (4, self.place.y), (3, self.place.x)):
-            self.landed_at(index, to)
-
-        for base, first, second in ((0, 2, 4), (half, 3, 5)):
-
-            def work(rows):
-                own_rows = pl.ds(pl.multiple_of(rows.start + base, 16), rows.size)
-                self.out[own_rows] = (
-                    f32(self.own[0, own_rows])
-                    + f32(self.got[0, own_rows])
-                    + f32(self.landed[first, rows])
-                    + f32(self.landed[second, rows])
-                )
-
-            each_rows(half, 16, work)
-        for copy in self.to_pair + self.sends:
-            copy.wait_send()
-
-
 class LineScatter:
     @staticmethod
     def scratch(rows, width):
         return [pltpu.VMEM((6, rows, width), LOW)]
 
-    def __init__(self, place, parts, out, buffers, marks):
-        self.place, self.parts, self.out = place, parts, out
+    def __init__(self, place, part, out, buffers, marks):
+        self.place, self.out = place, out
         self.kept = buffers[0]
-        self.rows = parts.shape[1]
+        self.rows = self.kept.shape[1]
         self.passed, self.above, self.below, self.two, self.mid, self.own = (
             self.kept.at[index] for index in range(6)
         )
         self.recv = [marks.take() for _ in range(4)]
         z = place.z
-        self.pass_up = remote(parts.at[3], self.passed, marks.take(), self.recv[0], place.up)
-        self.pass_down = remote(parts.at[0], self.passed, marks.take(), self.recv[0], place.down)
+        self.pass_up = remote(part(3), self.passed, marks.take(), self.recv[0], place.up)
+        self.pass_down = remote(part(0), self.passed, marks.take(), self.recv[0], place.down)
         self.to_down = remote(
-            parts.at[place.at(3)], self.above, marks.take(), self.recv[1], place.down
-        )
-        self.to_up = remote(parts.at[place.at(1)], self.below, marks.take(), self.recv[2], place.up)
+            part(place.at(3)), self.above, marks.take(), self.recv[1], place.down
+        )
+        self.to_up = remote(part(place.at(1)), self.below, marks.take(), self.recv[2], place.up)
         self.to_two = remote(self.mid, self.two, marks.take(), self.recv[3], place.two)
-        self.load_mid = pltpu.make_async_copy(parts.at[place.at(2)], self.mid, marks.take())
-        self.load_own = pltpu.make_async_copy(parts.at[z], self.own, marks.take())
+        self.load_mid = pltpu.make_async_copy(part(place.at(2)), self.mid, marks.take())
+        self.load_own = pltpu.make_async_copy(part(z), self.own, marks.take())
 
     def start(self):
         z = self.place.z
@@ -694,7 +581,7 @@
 
 def comm_params(number):
     return pltpu.CompilerParams(
-        collective_id=number, has_side_effects=True, vmem_limit_bytes=56 * 1024 * 1024
+        collective_id=number, has_side_effects=True, vmem_limit_bytes=62 * 1024 * 1024
     )
 
 
@@ -823,41 +710,6 @@
     )(rows, qkv_pieces, output_weight, gate_pieces, up_pieces, down_weight)
 
 
-def rows_kernel(rows_ref, line_ref, rows_all, line_all, marks_ref):
-    place = Place()
-    marks = Marks(marks_ref)
-    greet(place, [place.x, place.y, place.pair], True)
-    tokens = TokensGather(place, rows_ref, rows_all, marks)
-    line = LineGather(place, line_ref, lambda z: line_all.at[z], marks.take(4), marks.take(4))
-    copy = pltpu.make_async_copy(line_ref, line_all.at[place.z], marks.take())
-    tokens.start()
-    line.start()
-    copy.start()
-    tokens.forward()
-    line.wait(2)
-    tokens.last()
-    line.wait(1)
-    line.wait(3)
-    tokens.finish()
-    line.finish()
-    copy.wait()
-
-
-def rows_gather(rows, line_block):
-    return pl.pallas_call(
-        rows_kernel,
-        out_shape=(
-            jax.ShapeDtypeStruct((8,) + rows.shape, LOW),
-            jax.ShapeDtypeStruct((4,) + line_block.shape, LOW),
-        ),
-        in_specs=[ANYWHERE] * 2,
-        out_specs=(ANYWHERE,) * 2,
-        scratch_shapes=[pltpu.SemaphoreType.DMA((40,))],
-        compiler_params=comm_params(1),
-        cost_estimate=comm_cost(50),
-    )(rows, line_block)
-
-
 def heads_out_kernel(heads_ref, own_ref, marks_ref):
     place = Place()
     greet(place, [place.x, place.y, place.d], False)
@@ -885,86 +737,387 @@
     )(heads)
 
 
-def heads_in_kernel(own_ref, heads_ref, marks_ref):
-    place = Place()
-    greet(place, [place.x, place.y, place.d], False)
-    width = heads_ref.shape[2]
-    exchange = Exchange(
-        place,
-        lambda p, step: own_ref.at[:, pl.ds(pl.multiple_of(p * width, width), width)],
-        lambda p, step: heads_ref.at[step],
-        Marks(marks_ref),
-    )
-    exchange.start()
-    exchange.wait()
-    exchange.finish()
-
-
-def tokens_to_heads(own):
-    rows, width = own.shape
-    return pl.pallas_call(
-        heads_in_kernel,
-        out_shape=jax.ShapeDtypeStruct((4, rows, width // 4), LOW),
-        in_specs=[ANYWHERE],
-        out_specs=ANYWHERE,
-        scratch_shapes=[pltpu.SemaphoreType.DMA((8,))],
-        compiler_params=comm_params(3),
-        cost_estimate=comm_cost(15),
-    )(own)
-
-
-def sums_kernel(parts_ref, line_ref, out_ref, columns_ref, marks_ref, line_sum, *buffers):
+class PlaneScatter:
+    @staticmethod
+    def scratch(rows, width):
+        return [pltpu.VMEM((6, rows // 2, width), LOW)]
+
+    def __init__(self, place, summed, out, buffers, marks, at=(0, 1, 2, 3)):
+        self.place, self.summed, self.out, self.at = place, summed, out, at
+        self.landed = buffers[0]
+        self.rows = summed.shape[1]
+        half = self.rows // 2
+        top, end = pl.ds(0, half), pl.ds(half, half)
+        x, y = place.x, place.y
+        self.recv = [marks.take() for _ in range(6)]
+        routes = (
+            (summed.at[at[3], top], x),
+            (summed.at[at[3], end], y),
+            (summed.at[at[1], top], x),
+            (summed.at[at[1], end], x),
+            (summed.at[at[2], top], y),
+            (summed.at[at[2], end], y),
+        )
+        self.sends = [
+            remote(src, self.landed.at[index], marks.take(), self.recv[index], to)
+            for index, (src, to) in enumerate(routes)
+        ]
+
+    def start(self):
+        for index in (0, 1, 2, 5):
+            self.sends[index].start()
+
+    def landed_at(self, index, to):
+        arrived(self.landed.at[index], self.recv[index], to)
+
+    def middle(self):
+        half = self.rows // 2
+        summed, landed = self.summed, self.landed
+        _, for_x, for_y, _ = self.at
+        self.landed_at(0, self.place.x)
+
+        def top_work(rows):
+            summed[for_y, rows] = low(f32(summed[for_y, rows]) + f32(landed[0, rows]))
+
+        each_rows(half, 16, top_work)
+        self.sends[4].start()
+        self.landed_at(1, self.place.y)
+
+        def end_work(rows):
+            end_rows = pl.ds(pl.multiple_of(rows.start + half, 16), rows.size)
+            summed[for_x, end_rows] = low(f32(summed[for_x, end_rows]) + f32(landed[1, rows]))
+
+        each_rows(half, 16, end_work)
+        self.sends[3].start()
+
+    def finish(self):
+        half = self.rows // 2
+        for index, to in ((2, self.place.x), (5, self.place.y), (4, self.place.y), (3, self.place.x)):
+            self.landed_at(index, to)
+
+        for base, first, second in ((0, 2, 4), (half, 3, 5)):
+
+            def work(rows):
+                own_rows = pl.ds(pl.multiple_of(rows.start + base, 16), rows.size)
+                self.out[own_rows] = (
+                    f32(self.summed[self.at[0], own_rows])
+                    + f32(self.landed[first, rows])
+                    + f32(self.landed[second, rows])
+                ).astype(self.out.dtype)
+
+            each_rows(half, 16, work)
+
+    def drain(self):
+        for copy in self.sends:
+            copy.wait_send()
+
+
+def units_kernel(
+    rows_ref,
+    line_ref,
+    gate_ref,
+    down_ref,
+    upstream_ref,
+    rows_all,
+    inner_out,
+    gate_grad_out,
+    up_grad_out,
+    part_sums,
+    grad_sums,
+    marks_ref,
+    gate_mat,
+    up_mat,
+    down_mat,
+    row_block,
+    grad_block,
+    part_stage,
+    grad_stage,
+    part_got,
+    grad_got,
+):
     place = Place()
     marks = Marks(marks_ref)
-    greet(place, [place.x, place.y, place.d, place.pair], True)
-    tokens = TokensScatter(place, parts_ref, out_ref, buffers[:4], marks)
-    line = LineScatter(place, line_ref, line_sum, buffers[4:], marks)
-    rows = line_sum.shape[0] // 4
-    pieces = Exchange(
-        place,
-        lambda p, step: line_sum.at[pl.ds(pl.multiple_of(p * rows, rows), rows)],
-        lambda p, step: columns_ref.at[p],
-        marks,
-    )
+    greet(place, [place.x, place.y, place.pair], True)
+    tokens = TokensGather(place, rows_ref, rows_all, marks)
+    line = LineGather(place, line_ref, lambda z: up_mat.at[z], marks.take(4), marks.take(4))
+    copies = [
+        pltpu.make_async_copy(line_ref, up_mat.at[place.z], marks.take()),
+        pltpu.make_async_copy(gate_ref, gate_mat, marks.take()),
+        pltpu.make_async_copy(down_ref, down_mat, marks.take()),
+    ]
+    fetch_marks = marks.take(4)
+    send_marks, recv_marks = marks.take(8), marks.take(8)
+
     tokens.start()
     line.start()
-    line.middle()
-    tokens.run()
+    for copy in copies:
+        copy.start()
+    tokens.forward()
+    line.wait(2)
+    tokens.last()
+    line.wait(1)
+    line.wait(3)
+    for copy in copies:
+        copy.wait()
+    tokens.finish()
     line.finish()
-    pieces.start()
-    tokens.finish()
-    line.drain()
-    pieces.wait()
-    pieces.finish()
-
-
-def sums_scatter(parts, line_parts):
-    rows, width = parts.shape[1:]
-    line_rows, line_width = line_parts.shape[1:]
+
+    def fetches(index):
+        step, slot = 3 - index // 2, index % 2
+        block = step + 4 * (1 - slot)
+        return (
+            pltpu.make_async_copy(rows_all.at[block], row_block.at[slot], fetch_marks.at[slot]),
+            pltpu.make_async_copy(
+                upstream_ref.at[block], grad_block.at[slot], fetch_marks.at[2 + slot]
+            ),
+        )
+
+    def sends(step):
+        return (
+            remote(
+                part_stage.at[step],
+                part_got.at[step],
+                send_marks.at[step],
+                recv_marks.at[step],
+                place.pair,
+            ),
+            remote(
+                grad_stage.at[step],
+                grad_got.at[step],
+                send_marks.at[4 + step],
+                recv_marks.at[4 + step],
+                place.pair,
+            ),
+        )
+
+    units = gate_mat.shape[1]
+    for copy in fetches(0):
+        copy.start()
+
+    def blocks(turn, carry):
+        step = 3 - turn
+        for slot in range(2):
+            index = 2 * turn + slot
+            block = step + 4 * (1 - slot)
+            for copy in fetches(index):
+                copy.wait()
+
+            @pl.when(index < 7)
+            def _():
+                for copy in fetches(index + 1):
+                    copy.start()
+
+            rows = row_block[slot]
+            gate_raw = matmul(rows, gate_mat[...])
+            up_raw = matmul(rows, up_mat[...].reshape(-1, units))
+            inner_grad = matmul_nt(grad_block[slot], down_mat[...])
+            sigmoid_gate = jax.nn.sigmoid(gate_raw)
+            activated = gate_raw * sigmoid_gate
+            inner = low(activated * up_raw)
+            gate_grad = low(
+                inner_grad * up_raw * sigmoid_gate * (1.0 + gate_raw * (1.0 - sigmoid_gate))
+            )
+            up_grad = low(inner_grad * activated)
+            inner_out[block] = inner
+            gate_grad_out[block] = gate_grad
+            up_grad_out[block] = up_grad
+            part = matmul(inner, down_mat[...])
+            grad = matmul_nt(gate_grad, gate_mat[...]) + matmul_nt(
+                up_grad, up_mat[...].reshape(-1, units)
+            )
+            if slot == 0:
+                part_stage[step] = low(part)
+                grad_stage[step] = low(grad)
+                for copy in sends(step):
+                    copy.start()
+            else:
+                for copy in sends(step):
+                    copy.wait_recv()
+                part_sums[step] = low(part + f32(part_got[step]))
+                grad_sums[step] = low(grad + f32(grad_got[step]))
+        return carry
+
+    lax.fori_loop(0, 4, blocks, 0)
+    for step in range(4):
+        for copy in sends(step):
+            copy.wait_send()
+
+
+def units_products(rows, up_rows, gate_all, down_all, upstream):
+    block_rows, width = rows.shape
+    units = gate_all.shape[1]
+    block = lambda count: pltpu.VMEM((count, block_rows, width), LOW)
+    hidden = jax.ShapeDtypeStruct((8, block_rows, units), LOW)
+    sums = jax.ShapeDtypeStruct((4, block_rows, width), LOW)
     return pl.pallas_call(
-        sums_kernel,
+        units_kernel,
         out_shape=(
-            jax.ShapeDtypeStruct((rows, width), jnp.float32),
-            jax.ShapeDtypeStruct((4, line_rows // 4, line_width), LOW),
+            jax.ShapeDtypeStruct((8, block_rows, width), LOW),
+            hidden,
+            hidden,
+            hidden,
+            sums,
+            sums,
         ),
-        in_specs=[ANYWHERE] * 2,
-        out_specs=(WHOLE, ANYWHERE),
+        in_specs=[ANYWHERE] * 5,
+        out_specs=(ANYWHERE,) + (WHOLE,) * 5,
         scratch_shapes=[
             pltpu.SemaphoreType.DMA((64,)),
-            pltpu.VMEM((line_rows, line_width), LOW),
+            pltpu.VMEM(gate_all.shape, LOW),
+            pltpu.VMEM((4,) + up_rows.shape, LOW),
+            pltpu.VMEM(down_all.shape, LOW),
+            block(2),
+            block(2),
+            block(4),
+            block(4),
+            block(4),
+            block(4),
+        ],
+        compiler_params=comm_params(1),
+        cost_estimate=comm_cost(110),
+    )(rows, up_rows, gate_all, down_all, upstream)
+
+
+def unit_grads_kernel(
+    rows_all,
+    upstream_ref,
+    inner_ref,
+    gate_grad_ref,
+    up_grad_ref,
+    part_sums,
+    grad_sums,
+    row_grad,
+    row_part,
+    down_out,
+    gate_part,
+    up_part,
+    marks_ref,
+    upstream,
+    inner,
+    gate_grad,
+    up_grad,
+    row_slab,
+    down_part,
+    *buffers,
+):
+    place = Place()
+    marks = Marks(marks_ref)
+    greet(place, [place.x, place.y], True)
+    grad_plane = PlaneScatter(place, grad_sums, row_grad, buffers[:1], marks)
+    part_plane = PlaneScatter(place, part_sums, row_part, buffers[1:2], marks)
+    down_rows = down_out.shape[0]
+    down_line = LineScatter(
+        place,
+        lambda z: down_part.at[pl.ds(pl.multiple_of(z * down_rows, 16), down_rows)],
+        down_out,
+        buffers[2:],
+        marks,
+    )
+    loads = [
+        pltpu.make_async_copy(upstream_ref, upstream, marks.take()),
+        pltpu.make_async_copy(inner_ref, inner, marks.take()),
+        pltpu.make_async_copy(gate_grad_ref, gate_grad, marks.take()),
+        pltpu.make_async_copy(up_grad_ref, up_grad, marks.take()),
+    ]
+    slab_marks = marks.take(2)
+    tile = row_slab.shape[3]
+    tiles = rows_all.shape[2] // tile
+    units = inner.shape[2]
+    all_rows = inner.shape[0] * inner.shape[1]
+
+    def slab(index):
+        return pltpu.make_async_copy(
+            rows_all.at[:, :, pl.ds(pl.multiple_of(index * tile, tile), tile)],
+            row_slab.at[index % 2],
+            slab_marks.at[index % 2],
+        )
+
+    grad_plane.start()
+    for copy in loads:
+        copy.start()
+    slab(0).start()
+    loads[0].wait()
+    loads[1].wait()
+
+    def down_tile(index, carry):
+        columns = pl.ds(pl.multiple_of(index * tile, tile), tile)
+        down_part[columns] = low(
+            matmul_tn(
+                inner[:, :, columns].reshape(all_rows, tile),
+                upstream[...].reshape(all_rows, upstream.shape[2]),
+            )
+        )
+        return carry
+
+    lax.fori_loop(0, units // tile, down_tile, 0)
+    down_line.start()
+    loads[2].wait()
+    loads[3].wait()
+
+    def row_tile(index, carry):
+        slab(index).wait()
+
+        @pl.when(index < tiles - 1)
+        def _():
+            slab(index + 1).start()
+
+        columns = row_slab[index % 2].reshape(all_rows, tile)
+        out_rows = pl.ds(pl.multiple_of(index * tile, tile), tile)
+        gate_part[out_rows] = low(matmul_tn(columns, gate_grad[...].reshape(all_rows, units)))
+        up_part[out_rows] = low(matmul_tn(columns, up_grad[...].reshape(all_rows, units)))
+        return carry
+
+    lax.fori_loop(0, tiles // 4, row_tile, 0)
+    grad_plane.middle()
+    down_line.middle()
+    lax.fori_loop(tiles // 4, tiles, row_tile, 0)
+    grad_plane.finish()
+    part_plane.start()
+    part_plane.middle()
+    down_line.finish()
+    part_plane.finish()
+    down_line.drain()
+    grad_plane.drain()
+    part_plane.drain()
+
+
+def unit_grads(rows_all, upstream, inner, gate_grad, up_grad, part_sums, grad_sums):
+    _, block_rows, width = rows_all.shape
+    units = inner.shape[2]
+    down_rows = units // 4
+    tile = 256
+    return pl.pallas_call(
+        unit_grads_kernel,
+        out_shape=(
+            jax.ShapeDtypeStruct((block_rows, width), jnp.float32),
+            jax.ShapeDtypeStruct((block_rows, width), jnp.float32),
+            jax.ShapeDtypeStruct((down_rows, width), LOW),
+            jax.ShapeDtypeStruct((width, units), LOW),
+            jax.ShapeDtypeStruct((width, units), LOW),
+        ),
+        in_specs=[ANYWHERE] * 5 + [WHOLE] * 2,
+        out_specs=(WHOLE,) * 5,
+        scratch_shapes=[
+            pltpu.SemaphoreType.DMA((64,)),
+            pltpu.VMEM(upstream.shape, LOW),
+            pltpu.VMEM(inner.shape, LOW),
+            pltpu.VMEM(inner.shape, LOW),
+            pltpu.VMEM(inner.shape, LOW),
+            pltpu.VMEM((2, 8, block_rows, tile), LOW),
+            pltpu.VMEM((units, width), LOW),
         ]
-        + TokensScatter.scratch(rows, width)
-        + LineScatter.scratch(line_rows, line_width),
+        + PlaneScatter.scratch(block_rows, width) * 2
+        + LineScatter.scratch(down_rows, width),
+        input_output_aliases={},
         compiler_params=comm_params(4),
-        cost_estimate=comm_cost(55),
-    )(parts, line_parts)
+        cost_estimate=comm_cost(70),
+    )(rows_all, upstream, inner, gate_grad, up_grad, part_sums, grad_sums)
 
 
 def last_kernel(
     parts_ref,
     qkv_ref,
     proj_ref,
-    gate_ref,
     input_ref,
     hidden_ref,
     norm_ref,
@@ -972,7 +1125,6 @@
     grad_ref,
     qkv_columns,
     proj_out,
-    gate_columns,
     gains_out,
     marks_ref,
     qkv_sum,
@@ -985,9 +1137,9 @@
     place = Place()
     marks = Marks(marks_ref)
     greet(place, [place.x, place.y, place.d, place.pair], True)
-    tokens = TokensScatter(place, parts_ref, row_sum, buffers[:4], marks)
-    qkv_line = LineScatter(place, qkv_ref, qkv_sum, buffers[4:5], marks)
-    proj_line = LineScatter(place, proj_ref, proj_out, buffers[5:], marks)
+    tokens = PlaneScatter(place, parts_ref, row_sum, buffers[:1], marks)
+    qkv_line = LineScatter(place, lambda z: qkv_ref.at[z], qkv_sum, buffers[1:2], marks)
+    proj_line = LineScatter(place, lambda z: proj_ref.at[z], proj_out, buffers[2:], marks)
     rows = qkv_sum.shape[0] // 4
     qkv_pieces = Exchange(
         place,
@@ -995,9 +1147,6 @@
         lambda p, step: qkv_columns.at[p],
         marks,
     )
-    gate_pieces = Exchange(
-        place, lambda p, step: gate_ref.at[p], lambda p, step: gate_columns.at[p], marks
-    )
     near_z = {"f": place.z + 1 - 2 * (place.z % 2)}
     rounds = [
         remote(gain_mine.at[index], gain_got.at[index], marks.take(), marks.take(), to)
@@ -1008,13 +1157,12 @@
     qkv_line.start()
     qkv_line.middle()
     proj_line.start()
-    tokens.run()
+    tokens.middle()
     proj_line.middle()
-    gate_pieces.start()
+    tokens.finish()
+
     qkv_line.finish()
     qkv_pieces.start()
-    tokens.finish()
-
     gain_rows[...] = jnp.zeros_like(gain_rows)
     norm_row = norm_ref[...]
 
@@ -1047,13 +1195,12 @@
     proj_line.finish()
     qkv_line.drain()
     proj_line.drain()
+    tokens.drain()
     qkv_pieces.wait()
     qkv_pieces.finish()
-    gate_pieces.wait()
-    gate_pieces.finish()
-
-
-def last_sums(parts, qkv_parts, proj_parts, gate_rows, layer_input, hidden_grad, norm, gains):
+
+
+def last_sums(parts, qkv_parts, proj_parts, layer_input, hidden_grad, norm, gains):
     rows, width = parts.shape[1:]
     qkv_rows, qkv_width = qkv_parts.shape[1:]
     gain_width = width + gains.shape[1]
@@ -1063,25 +1210,24 @@
             jax.ShapeDtypeStruct((rows, width), jnp.float32),
             jax.ShapeDtypeStruct((4, qkv_rows // 4, qkv_width), LOW),
             jax.ShapeDtypeStruct(proj_parts.shape[1:], LOW),
-            jax.ShapeDtypeStruct(gate_rows.shape, LOW),
             jax.ShapeDtypeStruct((1, gain_width), jnp.float32),
         ),
-        in_specs=[ANYWHERE] * 4 + [WHOLE] * 4,
-        out_specs=(WHOLE, ANYWHERE, WHOLE, ANYWHERE, WHOLE),
+        in_specs=[WHOLE] + [ANYWHERE] * 2 + [WHOLE] * 4,
+        out_specs=(WHOLE, ANYWHERE, WHOLE, WHOLE),
         scratch_shapes=[
-            pltpu.SemaphoreType.DMA((90,)),
+            pltpu.SemaphoreType.DMA((100,)),
             pltpu.VMEM((qkv_rows, qkv_width), LOW),
             pltpu.VMEM((rows, width), jnp.float32),
             pltpu.VMEM((8, width), jnp.float32),
             pltpu.VMEM((5, 1, gain_width), jnp.float32),
             pltpu.VMEM((5, 1, gain_width), jnp.float32),
         ]
-        + TokensScatter.scratch(rows, width)
+        + PlaneScatter.scratch(rows, width)
         + LineScatter.scratch(qkv_rows, qkv_width)
         + LineScatter.scratch(*proj_parts.shape[1:]),
         compiler_params=comm_params(5),
         cost_estimate=comm_cost(60),
-    )(parts, qkv_parts, proj_parts, gate_rows, layer_input, hidden_grad, norm, gains)
+    )(parts, qkv_parts, proj_parts, layer_input, hidden_grad, norm, gains)
 
 
 def turn_pairs(values, cosine, sine):
@@ -1123,10 +1269,55 @@
     out_ref[...] = jnp.concatenate(attended, axis=1).reshape(out_ref.shape)
 
 
-def attend_back_kernel(
+def lanes(values, head):
+    return values[:, head * HEAD_SIZE : (head + 1) * HEAD_SIZE]
+
+
+def roll_half(values):
+    return pltpu.roll(values, HEAD_SIZE // 2, 1)
+
+
+def attend_back_values(raw, kept, grad, allowed, cosine, sine, gains_ref, roll=roll_half):
+    group_rows = raw.shape[0]
+    heads = raw.shape[1] // HEAD_SIZE - 2
+    key, value = lanes(kept, heads), lanes(kept, heads + 1)
+    scale = HEAD_SIZE ** (-0.5)
+    turned_grads = []
+    key_grad = jnp.zeros((group_rows, HEAD_SIZE), jnp.float32)
+    value_grad = jnp.zeros((group_rows, HEAD_SIZE), jnp.float32)
+    for head in range(heads):
+        query, upstream = lanes(kept, head), lanes(grad, head)
+        probs = softmax_of(query, key, allowed)
+        probs_grad = matmul_nt(upstream, value)
+        scores_grad = low(
+            probs * (probs_grad - jnp.sum(probs * probs_grad, axis=-1, keepdims=True))
+        )
+        turned_grads.append(matmul(scores_grad, key) * scale)
+        key_grad = key_grad + matmul_tn(scores_grad, query)
+        value_grad = value_grad + matmul_tn(low(probs), upstream)
+    turned_grads.append(key_grad * scale)
+    outs, gains = [], []
+    for head in range(heads + 1):
+        gain = gains_ref[min(head // heads, 1)][None, :]
+        unnormed = lanes(raw, head)
+        upstream = turned_grads[head] * cosine - roll(turned_grads[head]) * sine
+        grad_raw, gain_part = norm_back(unnormed, inv_rms(unnormed), gain, upstream)
+        outs.append(low(grad_raw))
+        gains.append(gain_part[None, :])
+    outs.append(low(value_grad))
+    query_gain = sum(gains[1:heads], gains[0])
+    return (jnp.concatenate(outs, axis=1), jnp.concatenate([query_gain, gains[heads]], axis=1))
+
+
+def heads_back_kernel(
+    hidden_ref,
+    row_grad_ref,
+    upstream_ref,
+    norm_ref,
+    out_ref,
+    attended_ref,
     raw_ref,
     low_ref,
-    grad_ref,
     cos_ref,
     sin_ref,
     segment_col,
@@ -1134,45 +1325,290 @@
     id_col,
     id_row,
     gains_ref,
-    out_ref,
-    gain_out,
+    rows_all,
+    qkv_ref,
+    gate_part,
+    up_part,
+    hidden_grad,
+    mlp_gain,
+    head_gain,
+    qkv_part,
+    proj_sum,
+    grad_sums,
+    gate_columns,
+    up_columns,
+    marks_ref,
+    out_mat,
+    qkv_mat,
+    attended,
+    branch,
+    own_grad,
+    heads_grad,
+    raw_block,
+    low_block,
+    qkv_grad,
+    row_slab,
+    proj_part,
+    gain_rows,
+    line_sum,
+    *buffers,
 ):
-    group_rows = cos_ref.shape[1]
-    raw = raw_ref[...].reshape(group_rows, raw_ref.shape[3])
-    kept = low_ref[...].reshape(raw.shape)
-    heads = raw.shape[1] // HEAD_SIZE - 2
-    cosine, sine = cos_ref[0], sin_ref[0]
-    allowed = allowed_of(segment_col, segment_row, id_col, id_row)
-    lane = lambda values, head: values[:, head * HEAD_SIZE : (head + 1) * HEAD_SIZE]
-    key, value = lane(kept, heads), lane(kept, heads + 1)
-    scale = HEAD_SIZE ** (-0.5)
-    turned_grads = []
-    key_grad = jnp.zeros((group_rows, HEAD_SIZE), jnp.float32)
-    value_grad = jnp.zeros((group_rows, HEAD_SIZE), jnp.float32)
-    for head in range(heads):
-        query, upstream = lane(kept, head), lane(grad_ref[0], head)
-        probs = softmax_of(query, key, allowed)
-        probs_grad = matmul_nt(upstream, value)
-        scores_grad = low(
-            probs * (probs_grad - jnp.sum(probs * probs_grad, axis=-1, keepdims=True))
-        )
-        turned_grads.append(matmul(scores_grad, key) * scale)
-        key_grad = key_grad + matmul_tn(scores_grad, query)
-        value_grad = value_grad + matmul_tn(low(probs), upstream)
-    turned_grads.append(key_grad * scale)
-    outs, gains = [], []
-    for head in range(heads + 1):
-        gain = gains_ref[min(head // heads, 1)][None, :]
-        unnormed = lane(raw, head)
-        upstream = turn_pairs(turned_grads[head], cosine, -sine)
-        grad, gain_part = norm_back(unnormed, inv_rms(unnormed), gain, upstream)
-        outs.append(low(grad))
-        gains.append(gain_part[None, :])
-    outs.append(low(value_grad))
-    out_ref[...] = jnp.concatenate(outs, axis=1).reshape(out_ref.shape)
-    query_gain = sum(gains[1:heads], gains[0])
-    gain_out[0] = jnp.concatenate(
-        [query_gain, gains[heads], jnp.zeros((6, HEAD_SIZE), jnp.float32)], axis=0
+    place = Place()
+    marks = Marks(marks_ref)
+    greet(place, [place.x, place.y, place.d, place.pair], True)
+    rows, width = hidden_ref.shape
+    half_heads = heads_grad.shape[2]
+    group_rows = 2 * rows
+    gate_line = LineScatter(
+        place, lambda z: gate_part.at[z], line_sum.at[0], buffers[0:1], marks
+    )
+    up_line = LineScatter(place, lambda z: up_part.at[z], line_sum.at[1], buffers[1:2], marks)
+    quarter = line_sum.shape[1] // 4
+    columns = [
+        Exchange(
+            place,
+            lambda p, step, index=index: line_sum.at[
+                index, pl.ds(pl.multiple_of(p * quarter, quarter), quarter)
+            ],
+            lambda p, step, out=out: out.at[p],
+            marks,
+        )
+        for index, out in enumerate((gate_columns, up_columns))
+    ]
+    proj_plane = PlaneScatter(
+        place,
+        proj_part,
+        proj_sum,
+        buffers[2:3],
+        marks,
+        (place.p, place.px, place.py, place.pd),
+    )
+    heads = Exchange(
+        place, lambda p, step: own_grad.at[p], lambda p, step: heads_grad.at[step], marks
+    )
+    to_pair = remote(branch.at[0], branch.at[1], marks.take(), marks.take(), place.pair)
+    loads = [
+        pltpu.make_async_copy(out_ref, out_mat, marks.take()),
+        pltpu.make_async_copy(attended_ref, attended, marks.take()),
+        pltpu.make_async_copy(qkv_ref, qkv_mat, marks.take()),
+    ]
+    fetch_marks, slab_marks = marks.take(4), marks.take(2)
+    send_marks, recv_marks = marks.take(4), marks.take(4)
+
+    gate_line.start()
+    for copy in loads:
+        copy.start()
+
+    gain_rows[...] = jnp.zeros_like(gain_rows)
+    norm_row = norm_ref[...]
+
+    def norm_work(part):
+        values = hidden_ref[part]
+        scales = inv_rms(values)
+        upstream = row_grad_ref[part]
+        weighted = upstream * norm_row
+        inner_mean = jnp.mean(weighted * values, axis=-1, keepdims=True)
+        grad = (
+            f32(upstream_ref[part])
+            + scales * weighted
+            - values * (scales * scales * scales) * inner_mean
+        )
+        hidden_grad[part] = grad
+        branch[0, part] = low(grad)
+        parts = upstream * values * scales
+        gain_rows[...] += parts[:8] + parts[8:]
+
+    each_rows(rows, 16, norm_work)
+    to_pair.start()
+    mlp_gain[...] = jnp.sum(gain_rows[...], axis=0, keepdims=True)
+    for copy in loads:
+        copy.wait()
+
+    def own_half(core_step):
+        grad = low(matmul_nt(branch[core_step], out_mat[...]))
+        for p in range(4):
+            own_grad[p, pl.ds(core_step * rows, rows)] = grad[
+                :, p * half_heads : (p + 1) * half_heads
+            ]
+
+    own_half(0)
+    to_pair.wait()
+    own_half(1)
+    heads.start()
+    gate_line.middle()
+    up_line.start()
+
+    def proj_work(z, carry):
+        block = attended[z].reshape(group_rows, half_heads)
+        grad = low(matmul_tn(block, branch[...].reshape(group_rows, width)))
+        part = half_heads // 4
+        for p in range(4):
+            proj_part[p, pl.ds(pl.multiple_of(z * part, part), part)] = grad[
+                p * part : (p + 1) * part
+            ]
+        return carry
+
+    def fetches(step):
+        return (
+            pltpu.make_async_copy(raw_ref.at[:, step], raw_block, fetch_marks.at[0]),
+            pltpu.make_async_copy(low_ref.at[:, step], low_block, fetch_marks.at[1]),
+        )
+
+    lax.fori_loop(0, 4, proj_work, 0)
+    heads.wait()
+    proj_plane.start()
+    head_gain[...] = jnp.zeros_like(head_gain)
+
+    def sends(step):
+        return remote(
+            out_mat.at[pl.ds(pl.multiple_of(step * rows, rows), rows)],
+            grad_sums.at[step],
+            send_marks.at[step],
+            recv_marks.at[step],
+            place.pair,
+        )
+
+    def bucket(step, carry):
+        for copy in fetches(step):
+            copy.start()
+        for copy in fetches(step):
+            copy.wait()
+        allowed = (segment_col[step] == segment_row[step]) & (id_row[...] <= id_col[...])
+        grads, gains = attend_back_values(
+            raw_block[...].reshape(group_rows, -1),
+            low_block[...].reshape(group_rows, -1),
+            heads_grad[step],
+            allowed,
+            cos_ref[step],
+            sin_ref[step],
+            gains_ref,
+        )
+        head_gain[...] += gains
+        qkv_grad[0, step] = grads[:rows]
+        qkv_grad[1, step] = grads[rows:]
+        out_mat[pl.ds(pl.multiple_of(step * rows, rows), rows)] = low(
+            matmul_nt(grads[rows:], qkv_mat[...])
+        )
+        sends(step).start()
+        return carry
+
+    lax.fori_loop(0, 2, bucket, 0)
+    proj_plane.middle()
+    up_line.middle()
+    lax.fori_loop(2, 4, bucket, 0)
+
+    tile = row_slab.shape[3]
+    tiles = width // tile
+
+    def slab(index):
+        return pltpu.make_async_copy(
+            rows_all.at[:, :, pl.ds(pl.multiple_of(index * tile, tile), tile)],
+            row_slab.at[index % 2],
+            slab_marks.at[index % 2],
+        )
+
+    slab(0).start()
+
+    def own_work(step, carry):
+        copy = sends(step)
+        copy.wait_recv()
+        grad = matmul_nt(qkv_grad[0, step], qkv_mat[...])
+        grad_sums[step] = low(grad + f32(grad_sums[step]))
+        return carry
+
+    lax.fori_loop(0, 4, own_work, 0)
+    gate_line.finish()
+    columns[0].start()
+
+    def row_tile(index, carry):
+        slab(index).wait()
+
+        @pl.when(index < tiles - 1)
+        def _():
+            slab(index + 1).start()
+
+        block = row_slab[index % 2].reshape(4 * group_rows, tile)
+        out_rows = pl.ds(pl.multiple_of(index * tile, tile), tile)
+        qkv_part[out_rows] = low(
+            matmul_tn(block, qkv_grad[...].reshape(4 * group_rows, qkv_grad.shape[3]))
+        )
+        return carry
+
+    lax.fori_loop(0, tiles, row_tile, 0)
+    proj_plane.finish()
+    up_line.finish()
+    columns[1].start()
+    for step in range(4):
+        sends(step).wait_send()
+    heads.finish()
+    proj_plane.drain()
+    gate_line.drain()
+    up_line.drain()
+    for part in columns:
+        part.wait()
+        part.finish()
+
+
+def heads_backward(
+    hidden, row_grad, upstream, norm, out_all, attended, raw, kept, tables, rows_all, qkv_all, gate_part, up_part
+):
+    rows, width = hidden.shape
+    head_part = raw.shape[3]
+    query_part = head_part - 2 * HEAD_SIZE
+    line_rows, units = gate_part.shape[1:]
+    tile = 256
+    pieces = jax.ShapeDtypeStruct((4, line_rows // 4, units), LOW)
+    return pl.pallas_call(
+        heads_back_kernel,
+        out_shape=(
+            jax.ShapeDtypeStruct((rows, width), jnp.float32),
+            jax.ShapeDtypeStruct((1, width), jnp.float32),
+            jax.ShapeDtypeStruct((1, 2 * HEAD_SIZE), jnp.float32),
+            jax.ShapeDtypeStruct((width, head_part), LOW),
+            jax.ShapeDtypeStruct((query_part, width), LOW),
+            jax.ShapeDtypeStruct((4, rows, width), LOW),
+            pieces,
+            pieces,
+        ),
+        in_specs=[WHOLE] * 4
+        + [ANYWHERE] * 4
+        + [WHOLE] * len(tables)
+        + [ANYWHERE] * 4,
+        out_specs=(WHOLE,) * 6 + (ANYWHERE,) * 2,
+        scratch_shapes=[
+            pltpu.SemaphoreType.DMA((100,)),
+            pltpu.VMEM(out_all.shape, LOW),
+            pltpu.VMEM(qkv_all.shape, LOW),
+            pltpu.VMEM(attended.shape, LOW),
+            pltpu.VMEM((2, rows, width), LOW),
+            pltpu.VMEM((4, 2 * rows, query_part), LOW),
+            pltpu.VMEM((4, 2 * rows, query_part), LOW),
+            pltpu.VMEM((2, rows, head_part), jnp.float32),
+            pltpu.VMEM((2, rows, head_part), LOW),
+            pltpu.VMEM((2, 4, rows, head_part), LOW),
+            pltpu.VMEM((2, 8, rows, tile), LOW),
+            pltpu.VMEM((4, query_part, width), LOW),
+            pltpu.VMEM((8, width), jnp.float32),
+            pltpu.VMEM((2, line_rows, units), LOW),
+        ]
+        + LineScatter.scratch(line_rows, units) * 2
+        + PlaneScatter.scratch(query_part, width),
+        compiler_params=comm_params(3),
+        cost_estimate=comm_cost(115),
+    )(
+        hidden,
+        row_grad,
+        upstream,
+        norm,
+        out_all,
+        attended,
+        raw,
+        kept,
+        *tables,
+        rows_all,
+        qkv_all,
+        gate_part,
+        up_part,
     )
 
 
@@ -1208,33 +1644,6 @@
             flops=30_000_000_000, bytes_accessed=20_000_000, transcendentals=0
         ),
     )(raw, *tables)
-
-
-def attend_back(raw, kept, upstream, tables):
-    _, buckets, rows, width = raw.shape
-    bucket, table_specs = attention_specs(2 * rows, rows)
-    return pl.pallas_call(
-        attend_back_kernel,
-        grid=(buckets,),
-        out_shape=(
-            jax.ShapeDtypeStruct(raw.shape, LOW),
-            jax.ShapeDtypeStruct((buckets, 8, HEAD_SIZE), jnp.float32),
-        ),
-        in_specs=[
-            bucket(width),
-            bucket(width),
-            pl.BlockSpec((1,) + upstream.shape[1:], lambda step: (step, 0, 0)),
-        ]
-        + table_specs,
-        out_specs=(
-            bucket(width),
-            pl.BlockSpec((1, 8, HEAD_SIZE), lambda step: (step, 0, 0)),
-        ),
-        compiler_params=pltpu.CompilerParams(vmem_limit_bytes=48 * 1024 * 1024),
-        cost_estimate=pl.CostEstimate(
-            flops=40_000_000_000, bytes_accessed=20_000_000, transcendentals=0
-        ),
-    )(raw, kept, upstream, *tables)
 
 
 def shards(
@@ -1320,6 +1729,7 @@
             plane_exchange([attended_heads[:, step].reshape(group_rows, -1) for step in range(4)]),
             0,
         )
+    attended_own = attended
     attended = (
         attended.reshape(4, group_rows, query_part)
         .transpose(1, 0, 2)
@@ -1329,95 +1739,128 @@
 
     scale_mlp = inv_rms(hidden_state)
     normed_own = low(hidden_state * scale_mlp * mlp_norm)
+    line_shape = (line_extent, 4 * weight_rows, hidden_part)
+    grad_all = tokens_gather(after(grad_out, normed_attn), (attended_heads,))
+    down_all = line_gather(
+        after(down_weight, normed_attn), (attended_heads,), near_down
+    ).reshape(hidden_part, model_width)
     if on_line:
-        normed_mlp, up_all = rows_gather(normed_own, up_rows)
+        grad_blocks = grad_all.reshape(8, local_rows, model_width)
+        rows_all, inner_low, gate_grad, up_grad, part_sums, grad_sums = units_products(
+            normed_own, up_rows, gate_all, down_all, grad_blocks
+        )
+        mlp_row_grad, mlp_rows, grad_down, grad_gate_part, grad_up_part = unit_grads(
+            rows_all, grad_blocks, inner_low, gate_grad, up_grad, part_sums, grad_sums
+        )
+        grad_down = f32(grad_down)
+        grad_gate_part = grad_gate_part.reshape(line_shape)
+        grad_up_part = grad_up_part.reshape(line_shape)
     else:
         normed_mlp, up_all = tokens_gather(normed_own), line_gather(up_rows)
-    normed_mlp = normed_mlp.reshape(all_rows, model_width)
-    up_all = up_all.reshape(model_width, hidden_part)
-    grad_all = tokens_gather(after(grad_out, normed_attn), (attended_heads,), (normed_mlp,))
-    gate_raw = matmul(normed_mlp, gate_all)
-    down_all = line_gather(after(down_weight, normed_mlp), (gate_raw,), near_down).reshape(
-        hidden_part, model_width
-    )
-    up_raw = matmul(normed_mlp, up_all)
-    activated = jax.nn.silu(gate_raw)
-    inner_low = low(activated * up_raw)
-    grad_down_part = low(matmul_tn(inner_low, grad_all))
-    mlp_part = low(matmul(inner_low, down_all))
-    inner_grad = matmul_nt(grad_all, down_all)
-    sigmoid_gate = jax.nn.sigmoid(gate_raw)
-    gate_grad = low(inner_grad * up_raw * sigmoid_gate * (1.0 + gate_raw * (1.0 - sigmoid_gate)))
-    up_grad = low(inner_grad * activated)
-    line_shape = (line_extent, 4 * weight_rows, hidden_part)
-    grad_gate_part = low(matmul_tn(normed_mlp, gate_grad)).reshape(line_shape)
-    grad_up_part = low(matmul_tn(normed_mlp, up_grad)).reshape(line_shape)
-    mlp_grad = low(matmul_nt(gate_grad, gate_all) + matmul_nt(up_grad, up_all))
+        normed_mlp = normed_mlp.reshape(all_rows, model_width)
+        up_all = up_all.reshape(model_width, hidden_part)
+        gate_raw = matmul(normed_mlp, gate_all)
+        up_raw = matmul(normed_mlp, up_all)
+        activated = jax.nn.silu(gate_raw)
+        inner_low = low(activated * up_raw)
+        grad_down_part = low(matmul_tn(inner_low, grad_all))
+        mlp_rows = tokens_scatter(low(matmul(inner_low, down_all)))
+        inner_grad = matmul_nt(grad_all, down_all)
+        sigmoid_gate = jax.nn.sigmoid(gate_raw)
+        gate_grad = low(
+            inner_grad * up_raw * sigmoid_gate * (1.0 + gate_raw * (1.0 - sigmoid_gate))
+        )
+        up_grad = low(inner_grad * activated)
+        grad_gate_part = low(matmul_tn(normed_mlp, gate_grad)).reshape(line_shape)
+        grad_up_part = low(matmul_tn(normed_mlp, up_grad)).reshape(line_shape)
+        mlp_row_grad = tokens_scatter(
+            low(matmul_nt(gate_grad, gate_all) + matmul_nt(up_grad, up_all))
+        )
+        grad_down = line_scatter(grad_down_part.reshape(line_extent, down_rows, model_width))
+    layer_out = low(hidden_state + mlp_rows)
+
     if on_line:
-        mlp_row_grad, grad_up_columns = sums_scatter(
-            mlp_grad.reshape(8, local_rows, model_width), grad_up_part
-        )
-    else:
-        mlp_row_grad = tokens_scatter(mlp_grad)
-        grad_up_columns = exchanged(
-            low(line_scatter(grad_up_part)).reshape(4, weight_rows, hidden_part)
-        )
-    hidden_norm_grad, mlp_gain_part = norm_back(hidden_state, scale_mlp, mlp_norm, mlp_row_grad)
-
-    grad_down = line_scatter(
-        grad_down_part.reshape(line_extent, down_rows, model_width), (up_grad,), (mlp_row_grad,)
-    )
-    mlp_rows = tokens_scatter(mlp_part, (up_grad,), (grad_up_part,), (mlp_row_grad,))
-    layer_out = low(hidden_state + mlp_rows)
-
-    hidden_grad = f32(grad_out) + hidden_norm_grad
-    branch_grad = pair_gather(low(hidden_grad))
-    attended_grad = low(matmul_nt(branch_grad, out_all))
-    if on_line:
-        heads_grad = tokens_to_heads(attended_grad)
-    else:
-        split = attended_grad.reshape(group_rows, 4, query_part).transpose(1, 0, 2)
-        heads_grad = jnp.stack(plane_exchange(own_plane(split, 0)))
-    qkv_grad, gain_parts = attend_back(qkv_raw, qkv_low, heads_grad, tables)
-    qkv_grad = qkv_grad.reshape(all_rows, head_part)
-    grad_qkv_part = low(matmul_tn(normed_attn, qkv_grad)).reshape(
-        line_extent, 4 * weight_rows, head_part
-    )
-    attn_grad = low(matmul_nt(qkv_grad, qkv_all))
-    grad_gate_rows = low(
-        line_scatter(after(grad_gate_part, mlp_row_grad), (heads_grad,), (qkv_grad,))
-    ).reshape(4, weight_rows, hidden_part)
-    grad_proj_part = full_scatter_plane(
-        low(matmul_tn(attended, branch_grad)), (heads_grad,), (qkv_grad,)
-    )
-    head_gains = jnp.sum(gain_parts, axis=0)[:2].reshape(-1)
-    other_gains = jnp.concatenate([mlp_gain_part, head_gains])
-    if on_line:
-        grad_input, grad_qkv_columns, grad_out_proj, grad_gate_columns, gains = last_sums(
-            attn_grad.reshape(8, local_rows, model_width),
+        (
+            hidden_grad,
+            mlp_gain_part,
+            head_gains,
             grad_qkv_part,
             grad_proj_part,
-            grad_gate_rows,
+            grad_sums,
+            grad_gate_columns,
+            grad_up_columns,
+        ) = heads_backward(
+            hidden_state,
+            mlp_row_grad,
+            grad_out,
+            mlp_norm[None],
+            out_all,
+            attended_own,
+            qkv_raw,
+            qkv_low,
+            tables,
+            normed_attn.reshape(8, local_rows, model_width),
+            qkv_all,
+            grad_gate_part,
+            grad_up_part,
+        )
+        grad_input, grad_qkv_columns, grad_out_proj, gains = last_sums(
+            grad_sums,
+            grad_qkv_part.reshape(4, 4 * weight_rows, head_part),
+            grad_proj_part.reshape(4, output_weight.shape[0], model_width),
             layer_input,
             hidden_grad,
             attn_norm[None],
-            other_gains[None],
+            jnp.concatenate([mlp_gain_part, head_gains], axis=1),
         )
         gains = gains.reshape(-1)
         grad_out_proj = f32(grad_out_proj)
     else:
-        attn_row_grad = tokens_scatter(attn_grad)
+        hidden_norm_grad, mlp_gain_part = norm_back(
+            hidden_state, scale_mlp, mlp_norm, mlp_row_grad
+        )
+        hidden_grad = f32(grad_out) + hidden_norm_grad
+        branch_grad = pair_gather(low(hidden_grad))
+        attended_grad = low(matmul_nt(branch_grad, out_all))
+        split = attended_grad.reshape(group_rows, 4, query_part).transpose(1, 0, 2)
+        heads_grad = plane_exchange(own_plane(split, 0))
+        grad_proj_part = full_scatter_plane(low(matmul_tn(attended, branch_grad)))
+        back = [
+            attend_back_values(
+                qkv_raw[:, step].reshape(group_rows, head_part),
+                qkv_low[:, step].reshape(group_rows, head_part),
+                heads_grad[step],
+                (segments[step][:, None] == segments[step][None, :])
+                & (row_ids[None, :] <= row_ids[:, None]),
+                tables[0][step],
+                tables[1][step],
+                head_norms,
+                lambda values: jnp.roll(values, HEAD_SIZE // 2, 1),
+            )
+            for step in range(4)
+        ]
+        qkv_grad = jnp.stack([grads for grads, _ in back]).reshape(4, 2, local_rows, head_part)
+        qkv_grad = qkv_grad.transpose(1, 0, 2, 3).reshape(all_rows, head_part)
+        grad_qkv_part = low(matmul_tn(normed_attn, qkv_grad)).reshape(
+            line_extent, 4 * weight_rows, head_part
+        )
+        attn_row_grad = tokens_scatter(low(matmul_nt(qkv_grad, qkv_all)))
+        grad_rows = lambda part: low(line_scatter(part))
         grad_qkv_columns = exchanged(
-            low(line_scatter(grad_qkv_part)).reshape(4, weight_rows, head_part)
-        )
-        grad_gate_columns = exchanged(grad_gate_rows)
+            grad_rows(grad_qkv_part).reshape(4, weight_rows, head_part)
+        )
+        grad_gate_columns = exchanged(
+            grad_rows(grad_gate_part).reshape(4, weight_rows, hidden_part)
+        )
+        grad_up_columns = exchanged(grad_rows(grad_up_part).reshape(4, weight_rows, hidden_part))
         grad_out_proj = line_scatter(grad_proj_part)
         input_norm_grad, attn_gain_part = norm_back(
             input_float, scale_attn, attn_norm, attn_row_grad
         )
         grad_input = hidden_grad + input_norm_grad
+        head_gains = sum(gains for _, gains in back)[0]
         gains = total_sum(
-            jnp.concatenate([attn_gain_part, other_gains]).reshape(-1, HEAD_SIZE)
+            jnp.concatenate([attn_gain_part, mlp_gain_part, head_gains]).reshape(-1, HEAD_SIZE)
         ).reshape(-1)
 
     def heads_back(pieces):

time: 780 us -> 690 us (0.88)
  Pallas kernels: 375 us -> 525 us
  matrix products: 138 us -> 15.1 us
  waiting for transfers between devices: 87 us -> 41.5 us
  starting transfers between devices: 62.6 us -> 24.6 us
  other arithmetic: 52.2 us -> 25.7 us
    pallas_call x4 -> x3, Pallas kernels: 169 us -> 332 us  [the longest x1 127 us: units_products(): pl.pallas_call(units_kernel, out_shape=(jax.ShapeDtypeStruct((8, block_ro...]
    dot_general x10 -> x0, matrix products: 95.3 us -> none  [the longest x5 52.1 us: matmul_nt(): lax.dot_general(left_mat, right_mat, (((1,), (1,)), ((), ())), preferred_...]
    dot_general x5 -> x2, matrix products: 42.9 us -> 15.1 us  [matmul(): return jnp.dot(left_mat, right_mat, preferred_element_type=jnp.float32)]
    ppermute x8 -> x0, waiting for transfers between devices: 25 us -> none  [the longest x2 25 us: line_scatter(): lax.ppermute(low(f32(part[2]) + f32(passed)), 'f', [(0, 2), (2, 0), (1, 3...]
    ppermute x8 -> x0, starting transfers between devices: 23.7 us -> none  [the longest x2 10.1 us: line_scatter(): lax.ppermute(jnp.where(place == 0, part[3], part[1]), 'f', [(0, 1), (3, 2)])]
    ppermute x2, waiting for transfers between devices: 20.7 us -> 0.01 us  [line_gather(): two_away = lax.ppermute(block, 'f', [(0, 2), (2, 0), (1, 3), (3, 1)])]
    ppermute x29 -> x12, starting transfers between devices: 26.8 us -> 10.9 us  [swap(): return lax.ppermute(block, axis, [(0, 1), (1, 0)])]
    convert_element_type x11 -> x3, other arithmetic: 21.3 us -> 6.15 us  [low(): return values.astype(LOW)]
  transfers between devices with their start and end apart: 43 -> 18, of which waited for: 9 -> 5; matrix products, arithmetic and copies ran while one was open for 24% -> 10% of each run, Pallas kernels for 38% -> 19%
where the time goes in v3:
time: 690 us; the launch traced here: 686 us
  Pallas kernels  525 us (76%)
  local copies, waits for them, and re-layouts  52.6 us (8%)
  waiting for transfers between devices  41.5 us (6%)
  other arithmetic  25.7 us (4%)
  starting transfers between devices  24.6 us (4%)
  matrix products  15.1 us (2%)
    pallas_call x1, Pallas kernels, units_products(): pl.pallas_call(units_kernel, out_shape=(jax.ShapeDtypeStruct((8, block_ro...  127 us
    pallas_call x1, Pallas kernels, heads_backward(): pl.pallas_call(heads_back_kernel, out_shape=(jax.ShapeDtypeStruct((rows,...  126 us
    pallas_call x1, Pallas kernels, first_gather(): pl.pallas_call(first_kernel, out_shape=(jax.ShapeDtypeStruct((8,) + rows....  97.7 us
    pallas_call x1, Pallas kernels, unit_grads(): pl.pallas_call(unit_grads_kernel, out_shape=(jax.ShapeDtypeStruct((block_...  79.2 us
    pallas_call x1, Pallas kernels, last_sums(): pl.pallas_call(last_kernel, out_shape=(jax.ShapeDtypeStruct((rows, width)...  63.8 us
    ppermute x2, waiting for transfers between devices, line_gather(): passed = lax.ppermute(two_away, 'f', [(1, 0), (2, 3)])  28.4 us
    unnamed x73, local copies, waits for them, and re-layouts  27.8 us
    pallas_call x1, Pallas kernels, attend(): pl.pallas_call(attend_kernel, grid=(buckets,), out_shape=(jax.ShapeDtypeS...  20.2 us
  transfers between devices with their start and end apart: 18, of which 5 were waited for; matrix products, arithmetic and copies ran while one was open for 10% of the time, Pallas kernels for 19%

profile of v3, /device:TPU:0, one launch (start us, length us, event | category | flops | bytes accessed | tf_op | source)
XLA Modules:
  0.0 686.2 jit_solution(7550962100054109227)
XLA Ops:
  0.7 3.0 collective-permute-start
  18.2 97.7 %shard_map.220 = (bf16[8,256,2048]{2,1,0:T(8,128)(2,1)}, bf16[4,4,128,512]{3,2,1,0:T(8,128)(2,1)}, bf16[4,4,64,2048]{3,2,1,0:T(8,128)(2,1)}, bf16[4,128,768]{2,1...) custom-call(bf16[256,2048]{1,0:T(8,128)(2,1)} %fusion.2.rows_ref, ...), custom_call_target="tpu_custom_call" | custom-call | bytes 240000000 | tf_op jit(solution)/shard_map/pallas_call | solution.py:694
  118.9 2.3 constant_dynamic-update-slice_fusion.8
  121.4 10.6 %fusion.6.raw_ref = f32[2,4,256,512]{3,2,1,0:T(8,128)} fusion(bf16[2,4,256,2048]{3,2,1,0:T(8,128)(2,1)} %bitcast.86, bf16[2048,512,1,1]{1,0,3,2:T(8,128)(2,1)} %bitcast.99), kind=kOutput, calls=%fused_computation.51 | convolution fusion | flops 4294967296 | bytes 14680064 | tf_op jit(solution)/shard_map/dot_general | solution.py:20
  135.6 5.0 collective-permute-done.2
  142.7 3.7 fusion.3
  147.2 20.2 %shard_map.221 = (bf16[2,4,256,512]{3,2,1,0:T(8,128)(2,1)}, bf16[2,4,256,256]{3,2,1,0:T(8,128)(2,1)S(1)}) custom-call(f32[2,4,256,512]{3,2,1,0:T(8,128)} %fusion.6.raw_ref, f32[4,512,128]{2,1,0:T(8,128)S(1)} %pad_maximum_fusion.cos_ref, f32[4,512,128]{2,1,0:T(8,128)S(1)} %pad_maximum_fusion.1.sin_ref, s32[4,512,1]{2,1,0:T(8,128)S(1)} %copy.103.segment_col, ...), custom_call_target="tpu_custom_call" | custom-call | flops 30000001024 | bytes 20000000 | tf_op jit(solution)/shard_map/pallas_call | solution.py:1633
  168.4 11.1 %shard_map.222.attended_ref = bf16[4,2,256,256]{3,2,1,0:T(8,128)(2,1)} custom-call(bf16[2,4,256,256]{3,2,1,0:T(8,128)(2,1)} %copy-done.4), custom_call_target="tpu_custom_call" | custom-call | bytes 45000000 | tf_op jit(solution)/shard_map/pallas_call | solution.py:729
  181.0 4.6 convolution_convert_fusion
  189.1 2.2 bitcast_dynamic-update-slice_fusion.7
  191.8 6.9 %collective-permute-start.7 = (bf16[512,768]{1,0:T(8,128)(2,1)}, bf16[512,768]{1,0:T(8,128)(2,1)S(1)}, u32[]{:S(2)}, u32[]{:S(2)}) collective-permute-start(bf16[512,768]{1,0:T(8,128)(2,1)} %bitcast.25), channel_id=1, source_target_pairs={{0,8},{8,16},{16,24},{1,9},{9,17},{17,25},{2,10},{10,18},{18,26},{... | collective-permute-start | bytes 2359304 | tf_op jit(solution)/shard_map/ppermute | solution.py:154
  203.8 2.3 constant_dynamic-update-slice_fusion.7
  206.1 2.3 constant_dynamic-update-slice_fusion.6
  212.2 4.4 collective-permute-done.12
  218.8 3.6 collective-permute-done.13
  225.8 13.4 %collective-permute-done.9 = bf16[192,2048]{1,0:T(8,128)(2,1)S(1)} collective-permute-done((bf16[192,2048]{1,0:T(8,128)(2,1)}, bf16[192,2048]{1,0:T(8,128)(2,1)S(1)}, u32[]{:S(2)}, u32[]{:S(2)}) %collective-permute-start.9) | collective-permute-done | bytes 786464 | tf_op jit(solution)/shard_map/ppermute | solution.py:158
  240.0 15.0 %collective-permute-done.5 = bf16[512,768]{1,0:T(8,128)(2,1)S(1)} collective-permute-done((bf16[512,768]{1,0:T(8,128)(2,1)}, bf16[512,768]{1,0:T(8,128)(2,1)S(1)}, u32[]{:S(2)}, u32[]{:S(2)}) %collective-permute-start.5) | collective-permute-done | bytes 786464 | tf_op jit(solution)/shard_map/ppermute | solution.py:158
  264.5 126.8 %shard_map.223 = (bf16[8,256,2048]{2,1,0:T(8,128)(2,1)}, bf16[8,256,768]{2,1,0:T(8,128)(2,1)}, bf16[8,256,768]{2,1,0:T(8,128)(2,1)}, bf16[8,256,768]{2,1,0:T(8,1...) custom-call(bf16[256,2048]{1,0:T(8,128)(2,1)} %multiply_convert_fusion.rows_ref, ...), custom_call_target="tpu_custom_call" | custom-call | bytes 330000000 | tf_op jit(solution)/shard_map/pallas_call | solution.py:952
  391.3 79.2 %shard_map.224 = (f32[256,2048]{1,0:T(8,128)}, f32[256,2048]{1,0:T(8,128)}, bf16[192,2048]{1,0:T(8,128)(2,1)}, bf16[2048,768]{1,0:T(8,128)(2,1)}, bf16[2048,768]{1,0:T(8,128)(2,1)}) custom-call(bf16[8,256,2048]{2,1,0:T(8,128)(2,1)} %get-tuple-element.64.rows_all, bf16[8,256,2048]{2,1,0:T(8,128)(2,1)} %bitcast.36.upstream_ref, ...), custom_call_target="tpu_custom_call" | custom-call | bytes 210000000 | tf_op jit(solution)/shard_map/pallas_call | solution.py:1089
  470.4 126.5 %shard_map.225 = (f32[256,2048]{1,0:T(8,128)}, f32[1,2048]{1,0:T(1,128)}, f32[1,256]{1,0:T(1,128)}, bf16[2048,512]{1,0:T(8,128)(2,1)}, bf16[256,2048]{1,0:T(8,12...) custom-call(f32[256,2048]{1,0:T(8,128)} %copy-done.8, ...), custom_call_target="tpu_custom_call" | custom-call | bytes 345000000 | tf_op jit(solution)/shard_map/pallas_call | solution.py:1561
  598.3 63.8 %shard_map.226 = (f32[256,2048]{1,0:T(8,128)}, bf16[4,128,512]{2,1,0:T(8,128)(2,1)}, bf16[64,2048]{1,0:T(8,128)(2,1)}, f32[1,4352]{1,0:T(1,128)}) custom-call(bf16[4,256,2048]{2,1,0:T(8,128)(2,1)} %get-tuple-element.75.parts_ref, bf16[4,512,512]{2,1,0:T(8,128)(2,1)} %bitcast.102, bf16[4,64,2048]{2,1,0:T(8,128)(2,1)} %bitcast.108, ...), custom_call_target="tpu_custom_call" | custom-call | bytes 180000000 | tf_op jit(solution)/shard_map/pallas_call | solution.py:1207
  666.6 3.5 add_convert_fusion
  675.6 3.0 copy.118
  680.2 3.2 copy.119
  (156 shorter events, 70.6 us)
Async XLA Ops:
  0.7 131.4 %collective-permute-start = (s32[1,6]{1,0:T(1,128)}, s32[1,6]{1,0:T(1,128)S(1)}, u32[]{:S(2)}, u32[]{:S(2)}) collective-permute-start(s32[1,6]{1,0:T(1,128)} %param.25), channel_id=1, source_target_pairs={{0,2},{2,0},{1,3},{3,1},{4,6},{6,4},{5,7},{7,5},{8,10},{10,8},{9,1... | collective-permute-start | bytes 80 | tf_op jit(solution)/shard_map/ppermute | solution.py:93
  3.7 130.4 %collective-permute-start.1 = (s32[1,6]{1,0:T(1,128)}, s32[1,6]{1,0:T(1,128)}, u32[]{:S(2)}, u32[]{:S(2)}) collective-permute-start(s32[1,6]{1,0:T(1,128)} %param.25), channel_id=1, source_target_pairs={{0,4},{4,0},{1,5},{5,1},{2,6},{6,2},{3,7},{7,3},{8,12},{12,8},{9,1... | collective-permute-start | bytes 80 | tf_op jit(solution)/shard_map/ppermute | solution.py:93
  16.2 101.8 %copy-start.12 = (bf16[192,2048]{1,0:T(8,128)(2,1)S(1)}, bf16[192,2048]{1,0:T(8,128)(2,1)}, u32[]{:S(2)}) copy-start(bf16[192,2048]{1,0:T(8,128)(2,1)} %down_ref.1) | copy-start | bytes 2359300
  115.9 85.3 %collective-permute-start.11 = (bf16[256,2048]{1,0:T(8,128)(2,1)}, bf16[256,2048]{1,0:T(8,128)(2,1)}, u32[]{:S(2)}, u32[]{:S(2)}) collective-permute-start(bf16[256,2048]{1,0:T(8,128)(2,1)} %upstream_ref.1), channel_id=1, source_target_pairs={{0,4},{4,0},{1,5},{5,1},{2,6},{6,2},{3,7},{7,3},{8,12},{12,8},{9,1... | collective-permute-start | bytes 3145736 | tf_op jit(solution)/shard_map/ppermute | solution.py:93
  117.5 82.5 %collective-permute-start.10 = (bf16[256,2048]{1,0:T(8,128)(2,1)}, bf16[256,2048]{1,0:T(8,128)(2,1)}, u32[]{:S(2)}, u32[]{:S(2)}) collective-permute-start(bf16[256,2048]{1,0:T(8,128)(2,1)} %upstream_ref.1), channel_id=1, source_target_pairs={{0,2},{2,0},{1,3},{3,1},{4,6},{6,4},{5,7},{7,5},{8,10},{10,8},{9,1... | collective-permute-start | bytes 3145736 | tf_op jit(solution)/shard_map/ppermute | solution.py:93
  118.0 73.8 %collective-permute-start.8 = (bf16[192,2048]{1,0:T(8,128)(2,1)S(1)}, bf16[192,2048]{1,0:T(8,128)(2,1)}, u32[]{:S(2)}, u32[]{:S(2)}) collective-permute-start(bf16[192,2048]{1,0:T(8,128)(2,1)S(1)} %copy-done.12), channel_id=1, source_target_pairs={{0,16},{16,0},{8,24},{24,8},{1,17},{17,1},{9,25},{25,9},{2,18},{18... | collective-permute-start | bytes 2359304 | tf_op jit(solution)/shard_map/ppermute | solution.py:151
  121.2 25.9 %copy-start.5 = (s32[512]{0:T(512)}, s32[512]{0:T(512)S(1)}, u32[]{:S(2)}) copy-start(s32[512]{0:T(512)S(1)} %pad_add_fusion) | copy-start | bytes 6148
  121.4 25.8 %copy-start.3 = (s32[512,1]{1,0:T(8,128)}, s32[512,1]{1,0:T(8,128)S(1)}, u32[]{:S(2)}) copy-start(s32[512,1]{1,0:T(8,128)S(1)} %copy.104.id_col) | copy-start | bytes 6148
  132.0 66.7 %collective-permute-start.4 = (bf16[512,768]{1,0:T(8,128)(2,1)}, bf16[512,768]{1,0:T(8,128)(2,1)}, u32[]{:S(2)}, u32[]{:S(2)}) collective-permute-start(bf16[512,768]{1,0:T(8,128)(2,1)} %bitcast.25), channel_id=1, source_target_pairs={{0,16},{16,0},{8,24},{24,8},{1,17},{17,1},{9,25},{25,9},{2,18},{18... | collective-permute-start | bytes 2359304 | tf_op jit(solution)/shard_map/ppermute | solution.py:151
  134.1 6.5 collective-permute-start.2
  146.8 20.6 %copy-start.2 = (f32[4,512,128]{2,1,0:T(8,128)}, f32[4,512,128]{2,1,0:T(8,128)S(1)}, u32[]{:S(2)}) copy-start(f32[4,512,128]{2,1,0:T(8,128)S(1)} %pad_maximum_fusion.cos_ref) | copy-start | bytes 3145732
  147.2 20.3 %copy-start = (f32[4,512,128]{2,1,0:T(8,128)}, f32[4,512,128]{2,1,0:T(8,128)S(1)}, u32[]{:S(2)}) copy-start(f32[4,512,128]{2,1,0:T(8,128)S(1)} %pad_maximum_fusion.1.sin_ref) | copy-start | bytes 3145732
  186.7 21.7 %collective-permute-start.3 = (bf16[256,2048]{1,0:T(8,128)(2,1)}, bf16[256,2048]{1,0:T(8,128)(2,1)}, u32[]{:S(2)}, u32[]{:S(2)}) collective-permute-start(bf16[256,2048]{1,0:T(8,128)(2,1)} %slice.50), channel_id=1, source_target_pairs={{0,1},{1,0},{2,3},{3,2},{4,5},{5,4},{6,7},{7,6},{8,9},{9,8},{10,11... | collective-permute-start | bytes 3145736 | tf_op jit(solution)/shard_map/ppermute | solution.py:93
  191.8 67.8 %collective-permute-start.7 = (bf16[512,768]{1,0:T(8,128)(2,1)}, bf16[512,768]{1,0:T(8,128)(2,1)S(1)}, u32[]{:S(2)}, u32[]{:S(2)}) collective-permute-start(bf16[512,768]{1,0:T(8,128)(2,1)} %bitcast.25), channel_id=1, source_target_pairs={{0,8},{8,16},{16,24},{1,9},{9,17},{17,25},{2,10},{10,18},{18,26},{... | collective-permute-start | bytes 2359304 | tf_op jit(solution)/shard_map/ppermute | solution.py:154
  198.7 40.8 %collective-permute-start.6 = (bf16[512,768]{1,0:T(8,128)(2,1)}, bf16[512,768]{1,0:T(8,128)(2,1)S(1)}, u32[]{:S(2)}, u32[]{:S(2)}) collective-permute-start(bf16[512,768]{1,0:T(8,128)(2,1)} %bitcast.25), channel_id=1, source_target_pairs={{8,0},{16,8},{24,16},{9,1},{17,9},{25,17},{10,2},{18,10},{26,18},{... | collective-permute-start | bytes 2359304 | tf_op jit(solution)/shard_map/ppermute | solution.py:153
  200.0 24.7 %collective-permute-start.14 = (bf16[256,2048]{1,0:T(8,128)(2,1)S(1)}, bf16[256,2048]{1,0:T(8,128)(2,1)S(1)}, u32[]{:S(2)}, u32[]{:S(2)}) collective-permute-start(bf16[256,2048]{1,0:T(8,128)(2,1)S(1)} %copy-done.11), channel_id=1, source_target_pairs={{0,1},{1,0},{2,3},{3,2},{4,5},{5,4},{6,7},{7,6},{8,9},{9,8},{10,11... | collective-permute-start | bytes 3145736 | tf_op jit(solution)/shard_map/ppermute | solution.py:93
  202.3 14.4 %collective-permute-start.12 = (bf16[128,2048]{1,0:T(8,128)(2,1)S(1)}, bf16[128,2048]{1,0:T(8,128)(2,1)S(1)}, u32[]{:S(2)}, u32[]{:S(2)}) collective-permute-start(bf16[128,2048]{1,0:T(8,128)(2,1)S(1)} %slice.51), channel_id=1, source_target_pairs={{0,2},{2,0},{1,3},{3,1},{4,6},{6,4},{5,7},{7,5},{8,10},{10,8},{9,1... | collective-permute-start | bytes 1572872 | tf_op jit(solution)/shard_map/ppermute | solution.py:93
  208.4 14.0 %collective-permute-start.13 = (bf16[128,2048]{1,0:T(8,128)(2,1)S(1)}, bf16[128,2048]{1,0:T(8,128)(2,1)S(1)}, u32[]{:S(2)}, u32[]{:S(2)}) collective-permute-start(bf16[128,2048]{1,0:T(8,128)(2,1)S(1)} %slice.52), channel_id=1, source_target_pairs={{0,4},{4,0},{1,5},{5,1},{2,6},{6,2},{3,7},{7,3},{8,12},{12,8},{9,1... | collective-permute-start | bytes 1572872 | tf_op jit(solution)/shard_map/ppermute | solution.py:93
  212.2 27.0 %copy-start.19 = (bf16[192,2048]{1,0:T(8,128)(2,1)S(1)}, bf16[192,2048]{1,0:T(8,128)(2,1)}, u32[]{:S(2)}) copy-start(bf16[192,2048]{1,0:T(8,128)(2,1)} %get-tuple-element.59) | copy-start | bytes 2359300
  216.7 22.5 %collective-permute-start.9 = (bf16[192,2048]{1,0:T(8,128)(2,1)}, bf16[192,2048]{1,0:T(8,128)(2,1)S(1)}, u32[]{:S(2)}, u32[]{:S(2)}) collective-permute-start(bf16[192,2048]{1,0:T(8,128)(2,1)} %collective-permute-done.8), channel_id=1, source_target_pairs={{8,0},{16,24},{9,1},{17,25},{10,2},{18,26},{11,3},{19,27},{12,4},{... | collective-permute-start | bytes 2359304 | tf_op jit(solution)/shard_map/ppermute | solution.py:158
  222.4 32.6 %collective-permute-start.5 = (bf16[512,768]{1,0:T(8,128)(2,1)}, bf16[512,768]{1,0:T(8,128)(2,1)S(1)}, u32[]{:S(2)}, u32[]{:S(2)}) collective-permute-start(bf16[512,768]{1,0:T(8,128)(2,1)} %collective-permute-done.4), channel_id=1, source_target_pairs={{8,0},{16,24},{9,1},{17,25},{10,2},{18,26},{11,3},{19,27},{12,4},{... | collective-permute-start | bytes 2359304 | tf_op jit(solution)/shard_map/ppermute | solution.py:158
  224.7 37.5 %collective-permute-start.16 = (bf16[256,2048]{1,0:T(8,128)(2,1)}, bf16[256,2048]{1,0:T(8,128)(2,1)S(1)}, u32[]{:S(2)}, u32[]{:S(2)}) collective-permute-start(bf16[256,2048]{1,0:T(8,128)(2,1)} %collective-permute-done.11), channel_id=1, source_target_pairs={{0,1},{1,0},{2,3},{3,2},{4,5},{5,4},{6,7},{7,6},{8,9},{9,8},{10,11... | collective-permute-start | bytes 3145736 | tf_op jit(solution)/shard_map/ppermute | solution.py:93
  239.2 21.8 %collective-permute-start.15 = (bf16[256,2048]{1,0:T(8,128)(2,1)}, bf16[256,2048]{1,0:T(8,128)(2,1)S(1)}, u32[]{:S(2)}, u32[]{:S(2)}) collective-permute-start(bf16[256,2048]{1,0:T(8,128)(2,1)} %collective-permute-done.10), channel_id=1, source_target_pairs={{0,1},{1,0},{2,3},{3,2},{4,5},{5,4},{6,7},{7,6},{8,9},{9,8},{10,11... | collective-permute-start | bytes 3145736 | tf_op jit(solution)/shard_map/ppermute | solution.py:93
  239.5 23.8 %collective-permute-start.17 = (bf16[256,2048]{1,0:T(8,128)(2,1)S(1)}, bf16[256,2048]{1,0:T(8,128)(2,1)S(1)}, u32[]{:S(2)}, u32[]{:S(2)}) collective-permute-start(bf16[256,2048]{1,0:T(8,128)(2,1)S(1)} %pad_maximum_fusion.2), channel_id=1, source_target_pairs={{0,1},{1,0},{2,3},{3,2},{4,5},{5,4},{6,7},{7,6},{8,9},{9,8},{10,11... | collective-permute-start | bytes 3145736 | tf_op jit(solution)/shard_map/ppermute | solution.py:93
  (21 other events, 127.6 us)

commit v4 on v3

--- a/solution.py
+++ b/solution.py
@@ -85,10 +85,6 @@
     return values.astype(LOW)
 
 
-def after(block, *earlier):
-    return lax.optimization_barrier((block,) + earlier)[0]
-
-
 def swap(block, axis):
     return lax.ppermute(block, axis, [(0, 1), (1, 0)])
 
@@ -97,94 +93,33 @@
     return 2 * lax.axis_index("ty") + lax.axis_index("tx")
 
 
-def plane_gather(block, second=()):
-    half = block.shape[0] // 2
+def plane_gather(block):
     across_x = swap(block, "tx")
     across_y = swap(block, "ty")
-    top, end = after(across_y[:half], *second), after(across_x[half:], *second)
-    far = jnp.concatenate([swap(top, "tx"), swap(end, "ty")])
-    return [block, across_x, across_y, far]
-
-
-def plane_scatter(parts, second=(), third=()):
+    return [block, across_x, across_y, swap(across_y, "tx")]
+
+
+def plane_scatter(parts):
     own, for_x, for_y, for_far = parts
-    half = own.shape[0] // 2
-    pass_y = swap(for_far[:half], "tx")
-    pass_x = swap(for_far[half:], "ty")
-    x_top = swap(for_x[:half], "tx")
-    y_end = swap(for_y[half:], "ty")
-    pass_y, pass_x = after(pass_y, *second), after(pass_x, *second)
-    y_top = swap(low(f32(for_y[:half]) + f32(pass_y)), "ty")
-    x_end = swap(low(f32(for_x[half:]) + f32(pass_x)), "tx")
-    x_top, y_top = after(x_top, *third), after(y_top, *third)
-    x_end, y_end = after(x_end, *third), after(y_end, *third)
-    return jnp.concatenate(
-        [
-            f32(own[:half]) + f32(x_top) + f32(y_top),
-            f32(own[half:]) + f32(x_end) + f32(y_end),
-        ]
-    )
+    for_y = low(f32(for_y) + f32(swap(for_far, "tx")))
+    return f32(own) + f32(swap(for_x, "tx")) + f32(swap(for_y, "ty"))
 
 
 def plane_exchange(parts):
     own, for_x, for_y, for_far = parts
-    half = own.shape[0] // 2
-    far = jnp.concatenate(
-        [
-            swap(swap(for_far[:half], "tx"), "ty"),
-            swap(swap(for_far[half:], "ty"), "tx"),
-        ]
-    )
-    return [own, swap(for_x, "tx"), swap(for_y, "ty"), far]
+    return [own, swap(for_x, "tx"), swap(for_y, "ty"), swap(swap(for_far, "tx"), "ty")]
 
 
 def plane_lengths(lengths):
-    across_x, across_y = swap(lengths, "tx"), swap(lengths, "ty")
-    return jnp.concatenate([lengths, across_x, across_y, swap(across_y, "tx")])
-
-
-def line_gather(block, second=(), near=None):
-    extent = lax.axis_size("f")
-    if extent != 4:
-        return lax.all_gather(block, "f", axis=0)
-    place = lax.axis_index("f")
-    two_away = lax.ppermute(block, "f", [(0, 2), (2, 0), (1, 3), (3, 1)])
-    if near is None:
-        above = lax.ppermute(block, "f", [(1, 0), (2, 1), (3, 2)])
-        below = lax.ppermute(block, "f", [(0, 1), (1, 2), (2, 3)])
-    else:
-        above, below = near
-    two_away = after(two_away, *second)
-    passed = lax.ppermute(two_away, "f", [(1, 0), (2, 3)])
-    blocks = [
-        block,
-        jnp.where(place == 3, passed, above),
-        two_away,
-        jnp.where(place == 0, passed, below),
-    ]
-    whole = jnp.zeros((4,) + block.shape, block.dtype)
-    for step in range(4):
-        whole = lax.dynamic_update_index_in_dim(whole, blocks[step], (place + step) % 4, 0)
-    return whole
-
-
-def line_scatter(parts, second=(), third=()):
-    extent = lax.axis_size("f")
-    if extent != 4:
-        return f32(lax.psum_scatter(parts, "f", scatter_dimension=0))
-    place = lax.axis_index("f")
-    part = [
-        lax.dynamic_index_in_dim(parts, (place + step) % 4, 0, keepdims=False) for step in range(4)
-    ]
-    passed = lax.ppermute(jnp.where(place == 0, part[3], part[1]), "f", [(0, 1), (3, 2)])
-    above = lax.ppermute(part[3], "f", [(1, 0), (2, 1), (3, 2)])
-    below = lax.ppermute(part[1], "f", [(0, 1), (1, 2), (2, 3)])
-    passed = after(passed, *second)
-    two_away = lax.ppermute(
-        low(f32(part[2]) + f32(passed)), "f", [(0, 2), (2, 0), (1, 3), (3, 1)]
-    )
-    above, below, two_away = (after(block, *third) for block in (above, below, two_away))
-    return f32(part[0]) + f32(above) + f32(below) + f32(two_away)
+    return jnp.concatenate(plane_gather(lengths))
+
+
+def line_gather(block):
+    return lax.all_gather(block, "f", axis=0)
+
+
+def line_scatter(parts):
+    return f32(lax.psum_scatter(parts, "f", scatter_dimension=0))
 
 
 def natural_plane(blocks, axis):
@@ -213,29 +148,27 @@
     return whole.reshape(extent * 4 * rows, width)
 
 
-def full_scatter_plane(partial, second=(), third=()):
+def full_scatter_plane(partial):
     extent = lax.axis_size("f")
     rows, width = partial.shape[0] // (4 * extent), partial.shape[1]
     parts = own_plane(partial.reshape(extent, 4, rows, width), 1)
-    plane_sum = plane_scatter(
-        [part.reshape(extent * rows, width) for part in parts], second, third
-    )
+    plane_sum = plane_scatter([part.reshape(extent * rows, width) for part in parts])
     return low(plane_sum).reshape(extent, rows, width)
 
 
-def tokens_gather(block, second=(), third=()):
-    near = plane_gather(block, second)
-    return jnp.concatenate(near + [swap(after(piece, *third), "tensor") for piece in near])
-
-
-def tokens_scatter(partial, second=(), third=(), fourth=()):
+def tokens_gather(block):
+    near = plane_gather(block)
+    return jnp.concatenate(near + [swap(piece, "tensor") for piece in near])
+
+
+def tokens_scatter(partial):
     rows = partial.shape[0] // 8
     near = []
-    for step in (3, 1, 2, 0):
+    for step in range(4):
         mine = partial[step * rows : (step + 1) * rows]
         other = swap(partial[(4 + step) * rows : (5 + step) * rows], "tensor")
-        near.append(low(f32(mine) + f32(after(other, *second))))
-    return plane_scatter([near[3], near[1], near[2], near[0]], third, fourth)
+        near.append(low(f32(mine) + f32(other)))
+    return plane_scatter(near)
 
 
 def pair_gather(block):
@@ -248,12 +181,7 @@
 
 
 def total_sum(values):
-    for axis in ("tensor", "tx", "ty"):
-        values = values + swap(values, axis)
-    if lax.axis_size("f") != 4:
-        return lax.psum(values, "f")
-    values = values + lax.ppermute(values, "f", [(0, 1), (1, 0), (2, 3), (3, 2)])
-    return values + lax.ppermute(values, "f", [(0, 2), (2, 0), (1, 3), (3, 1)])
+    return lax.psum(values, ("f", "ty", "tx", "tensor"))
 
 
 class Place:
@@ -589,25 +517,71 @@
     return pl.CostEstimate(flops=0, bytes_accessed=micros * 3_000_000, transcendentals=0)
 
 
+def tables_of(lengths_row, id_col, id_row, inverse, count):
+    zero = jnp.zeros((1, 1), jnp.int32)
+    segment_col, segment_row = jnp.zeros_like(id_col), jnp.zeros_like(id_row)
+    ends, starts, end = [], [], zero
+    for index in range(count):
+        starts.append(end)
+        end = end + lengths_row[:, index : index + 1]
+        ends.append(end)
+        segment_col = segment_col + jnp.where(id_col >= end, 1, 0)
+        segment_row = segment_row + jnp.where(id_row >= end, 1, 0)
+    start_of = jnp.zeros_like(id_col)
+    for index in range(count):
+        start_of = start_of + jnp.where(segment_col == index, starts[index], 0)
+    angles = f32(id_col - start_of) * inverse
+    return segment_col, segment_row, jnp.cos(angles), jnp.sin(angles)
+
+
 def first_kernel(
+    documents,
     rows_ref,
     qkv_ref,
     out_ref,
     gate_ref,
     up_ref,
     down_ref,
+    lengths_ref,
+    id_col,
+    id_row,
+    inverse_ref,
+    head_norms,
+    input_ref,
+    norm_ref,
     rows_all,
+    gate_rows,
+    up_rows,
+    gate_all,
+    above_ref,
+    below_ref,
     qkv_all,
     out_all,
-    gate_rows,
-    up_rows,
-    above_ref,
-    below_ref,
+    raw_out,
+    low_out,
+    cos_out,
+    sin_out,
+    segment_col,
+    segment_row,
+    attended,
+    hidden,
+    normed,
     marks_ref,
+    lengths_all,
+    row_block,
+    heads_stage,
+    pair_stage,
+    pair_got,
 ):
     place = Place()
     marks = Marks(marks_ref)
     greet(place, [place.x, place.y, place.d, place.pair], True)
+    rows, width = rows_ref.shape
+    head_part = raw_out.shape[3]
+    heads = head_part // HEAD_SIZE - 2
+    lengths = Exchange(
+        place, lambda p, step: lengths_ref, lambda p, step: lengths_all.at[step], marks
+    )
     qkv_pieces = Exchange(
         place, lambda p, step: qkv_ref.at[p], lambda p, step: qkv_all.at[place.z, p], marks
     )
@@ -617,16 +591,18 @@
     up_pieces = Exchange(place, lambda p, step: up_ref.at[p], lambda p, step: up_rows.at[p], marks)
     tokens = TokensGather(place, rows_ref, rows_all, marks)
     qkv_line = LineGather(
-        place,
-        qkv_all.at[place.z],
-        lambda z: qkv_all.at[z],
-        marks.take(4),
-        marks.take(4),
+        place, qkv_all.at[place.z], lambda z: qkv_all.at[z], marks.take(4), marks.take(4)
+    )
+    gate_line = LineGather(
+        place, gate_rows, lambda z: gate_all.at[z], marks.take(4), marks.take(4)
     )
     out_line = LineGather(
         place, out_ref, lambda z: out_all.at[z, place.p], marks.take(4), marks.take(4)
     )
-    out_copy = pltpu.make_async_copy(out_ref, out_all.at[place.z, place.p], marks.take())
+    own_copies = [
+        pltpu.make_async_copy(out_ref, out_all.at[place.z, place.p], marks.take()),
+    ]
+    gate_copy = pltpu.make_async_copy(gate_rows, gate_all.at[place.z], marks.take())
     near_recv = [marks.take(), marks.take()]
     to_down = remote(down_ref, above_ref, marks.take(), near_recv[0], place.down)
     to_up = remote(down_ref, below_ref, marks.take(), near_recv[1], place.up)
@@ -637,47 +613,145 @@
             PlaneGather(
                 place,
                 out_ref if turn == 0 else out_all.at[z, place.p],
-                lambda p, rows, z=z: out_all.at[z, p, rows],
+                lambda p, part, z=z: out_all.at[z, p, part],
                 out_ref.shape[0],
                 marks.take(4),
                 marks.take(4),
             )
         )
-
+    heads_out = Exchange(
+        place, lambda p, step: heads_stage.at[step], lambda p, step: attended.at[p], marks
+    )
+    to_pair = remote(pair_stage, pair_got, marks.take(), marks.take(), place.pair)
+    fetch_marks = marks.take(2)
+
+    lengths.start()
     qkv_pieces.start()
     tokens.start()
-    out_copy.start()
+    for copy in own_copies:
+        copy.start()
+    lengths.wait()
     qkv_pieces.wait()
     qkv_line.start()
+
+    def table_work(step, carry):
+        seg_col, seg_row, cosine, sine = tables_of(
+            lengths_all[step][:1], id_col[...], id_row[...], inverse_ref[...], documents
+        )
+        segment_col[step] = seg_col
+        segment_row[step] = seg_row
+        cos_out[step] = cosine
+        lane = lax.broadcasted_iota(jnp.int32, sine.shape, 1)
+        sin_out[step] = jnp.where(lane < HEAD_SIZE // 2, -sine, sine)
+        return carry
+
+    lax.fori_loop(0, 2, table_work, 0)
     tokens.forward()
     out_planes[0].start()
+    lax.fori_loop(2, 4, table_work, 0)
     qkv_line.wait(1)
+    qkv_line.wait(2)
     out_line.start()
-    qkv_line.wait(2)
     tokens.last()
     out_planes[0].forward()
     gate_pieces.start()
+    qkv_line.wait(3)
+    tokens.finish()
+
+    def fetches(step):
+        return (
+            pltpu.make_async_copy(rows_all.at[step], row_block.at[0], fetch_marks.at[0]),
+            pltpu.make_async_copy(rows_all.at[4 + step], row_block.at[1], fetch_marks.at[1]),
+        )
+
+    def bucket(turn, carry):
+        step = 3 - turn
+        for copy in fetches(step):
+            copy.start()
+        for copy in fetches(step):
+            copy.wait()
+        raw = matmul(
+            row_block[...].reshape(2 * rows, width), qkv_all[...].reshape(width, head_part)
+        )
+        raw_out[0, step] = raw[:rows]
+        raw_out[1, step] = raw[rows:]
+        allowed = (segment_col[step] == segment_row[step]) & (id_row[...] <= id_col[...])
+        turned = []
+        for head in range(heads + 1):
+            gain = head_norms[min(head // heads, 1)][None, :]
+            unnormed = lanes(raw, head)
+            turned.append(
+                low(
+                    turn_pairs(
+                        unnormed * inv_rms(unnormed) * gain, cos_out[step], sin_out[step]
+                    )
+                )
+            )
+        value = low(lanes(raw, heads + 1))
+        outs = [
+            low(matmul(low(softmax_of(turned[head], turned[heads], allowed)), value))
+            for head in range(heads)
+        ]
+        kept = jnp.concatenate(turned + [value], axis=1)
+        low_out[0, step] = kept[:rows]
+        low_out[1, step] = kept[rows:]
+        outs = jnp.concatenate(outs, axis=1)
+        heads_stage[step, 0] = outs[:rows]
+        heads_stage[step, 1] = outs[rows:]
+        for index, at in enumerate((1, 2, 3)):
+            pl.when(step == at)(heads_out.sends[index].start)
+        pl.when(step == 0)(heads_out.copy.start)
+        return carry
+
+    lax.fori_loop(0, 1, bucket, 0)
     out_line.wait(1)
     out_planes[1].start()
+    gate_pieces.wait()
     out_line.wait(2)
+    gate_line.start()
+    gate_copy.start()
     out_planes[2].start()
-    qkv_line.wait(3)
+    lax.fori_loop(1, 2, bucket, 0)
     out_line.wait(3)
     out_planes[3].start()
+    out_planes[1].forward()
+    lax.fori_loop(2, 3, bucket, 0)
+    out_planes[2].forward()
+    out_planes[3].forward()
+    lax.fori_loop(3, 4, bucket, 0)
+    for plane in out_planes:
+        plane.wait_far()
+    for copy in own_copies:
+        copy.wait()
+    heads_out.wait()
+    gate_line.wait(2)
     pl.when(place.z > 0)(to_down.start)
     pl.when(place.z < 3)(to_up.start)
+
+    def projected(core_step):
+        block = jnp.concatenate([attended[p, core_step] for p in range(4)], axis=1)
+        return matmul(block, out_all[...].reshape(block.shape[1], width))
+
+    pair_stage[...] = low(projected(1))
+    to_pair.start()
     up_pieces.start()
-    out_planes[1].forward()
-    out_planes[2].forward()
-    out_planes[3].forward()
-    gate_pieces.wait()
+    hidden[...] = f32(input_ref[...]) + projected(0)
+    to_pair.wait()
+    norm_row = norm_ref[...]
+
+    def norm_work(part):
+        values = hidden[part] + f32(pair_got[part])
+        hidden[part] = values
+        normed[part] = low(values * inv_rms(values) * norm_row)
+
+    each_rows(rows, 16, norm_work)
+    gate_line.wait(1)
+    gate_line.wait(3)
     up_pieces.wait()
-    for plane in out_planes:
-        plane.wait_far()
-    tokens.finish()
-    for part in [qkv_pieces, gate_pieces, up_pieces, qkv_line, out_line] + out_planes:
+    gate_copy.wait()
+    parts = [lengths, qkv_pieces, gate_pieces, up_pieces, heads_out, qkv_line, gate_line, out_line]
+    for part in parts + out_planes:
         part.finish()
-    out_copy.wait()
 
     @pl.when(place.z < 3)
     def _():
@@ -690,51 +764,77 @@
         to_down.wait_send()
 
 
-def first_gather(rows, qkv_pieces, output_weight, gate_pieces, up_pieces, down_weight):
+def first_part(
+    rows,
+    qkv_pieces,
+    output_weight,
+    gate_pieces,
+    up_pieces,
+    down_weight,
+    doc_lengths,
+    row_ids,
+    head_norms,
+    layer_input,
+    mlp_norm,
+):
+    block_rows, width = rows.shape
+    group_rows = 2 * block_rows
+    weight_rows, head_part = qkv_pieces.shape[1:]
+    query_part = head_part - 2 * HEAD_SIZE
+    documents = doc_lengths.shape[1]
+    lengths = jnp.pad(doc_lengths, ((0, 7), (0, HEAD_SIZE - documents)))
+    half = jnp.arange(HEAD_SIZE // 2, dtype=jnp.float32)
+    inverse = ROPE_BASE ** (-(half * (2.0 / HEAD_SIZE)))
+    low_like = lambda *shape: jax.ShapeDtypeStruct(shape, LOW)
+    table = jax.ShapeDtypeStruct((4, group_rows, HEAD_SIZE), jnp.float32)
     return pl.pallas_call(
-        first_kernel,
+        lambda *refs: first_kernel(documents, *refs),
         out_shape=(
-            jax.ShapeDtypeStruct((8,) + rows.shape, LOW),
-            jax.ShapeDtypeStruct((4,) + qkv_pieces.shape, LOW),
-            jax.ShapeDtypeStruct((4, 4) + output_weight.shape, LOW),
-            jax.ShapeDtypeStruct(gate_pieces.shape, LOW),
-            jax.ShapeDtypeStruct(up_pieces.shape, LOW),
-            jax.ShapeDtypeStruct(down_weight.shape, LOW),
-            jax.ShapeDtypeStruct(down_weight.shape, LOW),
+            low_like(8, block_rows, width),
+            low_like(*gate_pieces.shape),
+            low_like(*up_pieces.shape),
+            low_like(4, *gate_pieces.shape),
+            low_like(*down_weight.shape),
+            low_like(*down_weight.shape),
+            low_like(4, *qkv_pieces.shape),
+            low_like(4, 4, *output_weight.shape),
+            jax.ShapeDtypeStruct((2, 4, block_rows, head_part), jnp.float32),
+            low_like(2, 4, block_rows, head_part),
+            table,
+            table,
+            jax.ShapeDtypeStruct((4, group_rows, 1), jnp.int32),
+            jax.ShapeDtypeStruct((4, 1, group_rows), jnp.int32),
+            low_like(4, 2, block_rows, query_part),
+            jax.ShapeDtypeStruct((block_rows, width), jnp.float32),
+            low_like(block_rows, width),
         ),
-        in_specs=[ANYWHERE] * 6,
-        out_specs=(ANYWHERE,) * 7,
-        scratch_shapes=[pltpu.SemaphoreType.DMA((100,))],
+        in_specs=[ANYWHERE] * 6 + [WHOLE] * 7,
+        out_specs=(ANYWHERE,) * 6 + (WHOLE,) * 11,
+        scratch_shapes=[
+            pltpu.SemaphoreType.DMA((140,)),
+            pltpu.VMEM((4,) + lengths.shape, jnp.int32),
+            pltpu.VMEM((2, block_rows, width), LOW),
+            pltpu.VMEM((4, 2, block_rows, query_part), LOW),
+            pltpu.VMEM((block_rows, width), LOW),
+            pltpu.VMEM((block_rows, width), LOW),
+        ],
         compiler_params=comm_params(0),
-        cost_estimate=comm_cost(80),
-    )(rows, qkv_pieces, output_weight, gate_pieces, up_pieces, down_weight)
-
-
-def heads_out_kernel(heads_ref, own_ref, marks_ref):
-    place = Place()
-    greet(place, [place.x, place.y, place.d], False)
-    exchange = Exchange(
-        place,
-        lambda p, step: heads_ref.at[:, step],
-        lambda p, step: own_ref.at[p],
-        Marks(marks_ref),
-    )
-    exchange.start()
-    exchange.wait()
-    exchange.finish()
-
-
-def heads_to_tokens(heads):
-    cores, _, rows, width = heads.shape
-    return pl.pallas_call(
-        heads_out_kernel,
-        out_shape=jax.ShapeDtypeStruct((4, cores, rows, width), LOW),
-        in_specs=[ANYWHERE],
-        out_specs=ANYWHERE,
-        scratch_shapes=[pltpu.SemaphoreType.DMA((8,))],
-        compiler_params=comm_params(2),
-        cost_estimate=comm_cost(15),
-    )(heads)
+        cost_estimate=comm_cost(130),
+    )(
+        rows,
+        qkv_pieces,
+        output_weight,
+        gate_pieces,
+        up_pieces,
+        down_weight,
+        lengths,
+        row_ids[:, None],
+        row_ids[None, :],
+        jnp.concatenate([inverse, inverse])[None],
+        head_norms,
+        layer_input,
+        mlp_norm[None],
+    )
 
 
 class PlaneScatter:
@@ -814,11 +914,14 @@
 
 def units_kernel(
     rows_ref,
+    upstream_ref,
     line_ref,
     gate_ref,
     down_ref,
-    upstream_ref,
+    above_ref,
+    below_ref,
     rows_all,
+    upstream_all,
     inner_out,
     gate_grad_out,
     up_grad_out,
@@ -829,88 +932,132 @@
     up_mat,
     down_mat,
     row_block,
-    grad_block,
+    gate_raws,
+    inner_grads,
     part_stage,
     grad_stage,
-    part_got,
-    grad_got,
 ):
     place = Place()
     marks = Marks(marks_ref)
     greet(place, [place.x, place.y, place.pair], True)
     tokens = TokensGather(place, rows_ref, rows_all, marks)
+    upstream = TokensGather(place, upstream_ref, upstream_all, marks)
     line = LineGather(place, line_ref, lambda z: up_mat.at[z], marks.take(4), marks.take(4))
+    down_line = LineGather(
+        place, down_ref, lambda z: down_mat.at[z], marks.take(4), marks.take(4)
+    )
     copies = [
         pltpu.make_async_copy(line_ref, up_mat.at[place.z], marks.take()),
         pltpu.make_async_copy(gate_ref, gate_mat, marks.take()),
-        pltpu.make_async_copy(down_ref, down_mat, marks.take()),
+        pltpu.make_async_copy(down_ref, down_mat.at[place.z], marks.take()),
     ]
-    fetch_marks = marks.take(4)
+    above = pltpu.make_async_copy(above_ref, down_mat.at[place.at(1)], marks.take())
+    below = pltpu.make_async_copy(below_ref, down_mat.at[place.at(3)], marks.take())
+    fetch_marks = marks.take(2)
     send_marks, recv_marks = marks.take(8), marks.take(8)
-
+    units = gate_mat.shape[1]
+    width = rows_ref.shape[1]
+
+    down_line.to_two.start()
     tokens.start()
-    line.start()
     for copy in copies:
         copy.start()
+    pl.when(place.z < 3)(above.start)
+    pl.when(place.z > 0)(below.start)
     tokens.forward()
+    upstream.start()
+    down_line.wait(2)
+    line.start()
+    tokens.last()
+    for copy in copies:
+        copy.wait()
+    pl.when(place.z < 3)(above.wait)
+    pl.when(place.z > 0)(below.wait)
+    tokens.finish()
+
+    def blocks_of(source, first, last, work):
+        def fetch(block):
+            return pltpu.make_async_copy(
+                source.at[block], row_block.at[block % 2], fetch_marks.at[block % 2]
+            )
+
+        fetch(first).start()
+
+        def body(block, carry):
+            fetch(block).wait()
+
+            @pl.when(block < last - 1)
+            def _():
+                fetch(block + 1).start()
+
+            work(block, row_block[block % 2])
+            return carry
+
+        lax.fori_loop(first, last, body, 0)
+
+    def gate_work(block, values):
+        gate_raws[block] = matmul(values, gate_mat[...])
+
+    def inner_work(block, values):
+        inner_grads[block] = matmul_nt(values, down_mat[...].reshape(units, width))
+
+    upstream.forward()
+    blocks_of(rows_all, 0, 8, gate_work)
+    upstream.last()
     line.wait(2)
-    tokens.last()
+
+    @pl.when(place.z == 0)
+    def _():
+        arrived(down_mat.at[3], down_line.recv.at[3], place.two)
+
+    @pl.when(place.z == 3)
+    def _():
+        arrived(down_mat.at[0], down_line.recv.at[1], place.two)
+
+    upstream.finish()
+    blocks_of(upstream_all, 0, 8, inner_work)
     line.wait(1)
     line.wait(3)
-    for copy in copies:
-        copy.wait()
-    tokens.finish()
-    line.finish()
-
-    def fetches(index):
+
+    def fetch(index):
         step, slot = 3 - index // 2, index % 2
-        block = step + 4 * (1 - slot)
-        return (
-            pltpu.make_async_copy(rows_all.at[block], row_block.at[slot], fetch_marks.at[slot]),
-            pltpu.make_async_copy(
-                upstream_ref.at[block], grad_block.at[slot], fetch_marks.at[2 + slot]
-            ),
+        return pltpu.make_async_copy(
+            rows_all.at[step + 4 * (1 - slot)], row_block.at[slot], fetch_marks.at[slot]
         )
 
     def sends(step):
         return (
             remote(
                 part_stage.at[step],
-                part_got.at[step],
+                part_sums.at[step],
                 send_marks.at[step],
                 recv_marks.at[step],
                 place.pair,
             ),
             remote(
                 grad_stage.at[step],
-                grad_got.at[step],
+                grad_sums.at[step],
                 send_marks.at[4 + step],
                 recv_marks.at[4 + step],
                 place.pair,
             ),
         )
 
-    units = gate_mat.shape[1]
-    for copy in fetches(0):
-        copy.start()
+    fetch(0).start()
 
     def blocks(turn, carry):
         step = 3 - turn
         for slot in range(2):
             index = 2 * turn + slot
             block = step + 4 * (1 - slot)
-            for copy in fetches(index):
-                copy.wait()
+            fetch(index).wait()
 
             @pl.when(index < 7)
             def _():
-                for copy in fetches(index + 1):
-                    copy.start()
-
-            rows = row_block[slot]
-            gate_raw = matmul(rows, gate_mat[...])
-            up_raw = matmul(rows, up_mat[...].reshape(-1, units))
-            inner_grad = matmul_nt(grad_block[slot], down_mat[...])
+                fetch(index + 1).start()
+
+            up_raw = matmul(row_block[slot], up_mat[...].reshape(-1, units))
+            gate_raw, inner_grad = gate_raws[block], inner_grads[block]
             sigmoid_gate = jax.nn.sigmoid(gate_raw)
             activated = gate_raw * sigmoid_gate
             inner = low(activated * up_raw)
@@ -921,7 +1068,7 @@
             inner_out[block] = inner
             gate_grad_out[block] = gate_grad
             up_grad_out[block] = up_grad
-            part = matmul(inner, down_mat[...])
+            part = matmul(inner, down_mat[...].reshape(units, width))
             grad = matmul_nt(gate_grad, gate_mat[...]) + matmul_nt(
                 up_grad, up_mat[...].reshape(-1, units)
             )
@@ -933,49 +1080,46 @@
             else:
                 for copy in sends(step):
                     copy.wait_recv()
-                part_sums[step] = low(part + f32(part_got[step]))
-                grad_sums[step] = low(grad + f32(grad_got[step]))
+                part_sums[step] = low(part + f32(part_sums[step]))
+                grad_sums[step] = low(grad + f32(grad_sums[step]))
         return carry
 
     lax.fori_loop(0, 4, blocks, 0)
     for step in range(4):
         for copy in sends(step):
             copy.wait_send()
-
-
-def units_products(rows, up_rows, gate_all, down_all, upstream):
+    line.finish()
+    down_line.to_two.wait_send()
+    pl.when(place.z == 1)(down_line.pass_down.wait_send)
+    pl.when(place.z == 2)(down_line.pass_up.wait_send)
+
+
+def units_products(rows, upstream, up_rows, gate_all, down_weight, above, below):
     block_rows, width = rows.shape
     units = gate_all.shape[1]
     block = lambda count: pltpu.VMEM((count, block_rows, width), LOW)
     hidden = jax.ShapeDtypeStruct((8, block_rows, units), LOW)
     sums = jax.ShapeDtypeStruct((4, block_rows, width), LOW)
+    blocks = jax.ShapeDtypeStruct((8, block_rows, width), LOW)
     return pl.pallas_call(
         units_kernel,
-        out_shape=(
-            jax.ShapeDtypeStruct((8, block_rows, width), LOW),
-            hidden,
-            hidden,
-            hidden,
-            sums,
-            sums,
-        ),
-        in_specs=[ANYWHERE] * 5,
-        out_specs=(ANYWHERE,) + (WHOLE,) * 5,
+        out_shape=(blocks, blocks, hidden, hidden, hidden, sums, sums),
+        in_specs=[ANYWHERE] * 7,
+        out_specs=(ANYWHERE,) * 2 + (WHOLE,) * 5,
         scratch_shapes=[
-            pltpu.SemaphoreType.DMA((64,)),
+            pltpu.SemaphoreType.DMA((100,)),
             pltpu.VMEM(gate_all.shape, LOW),
             pltpu.VMEM((4,) + up_rows.shape, LOW),
-            pltpu.VMEM(down_all.shape, LOW),
+            pltpu.VMEM((4,) + down_weight.shape, LOW),
             block(2),
-            block(2),
-            block(4),
-            block(4),
+            pltpu.VMEM((8, block_rows, units), jnp.float32),
+            pltpu.VMEM((8, block_rows, units), jnp.float32),
             block(4),
             block(4),
         ],
         compiler_params=comm_params(1),
-        cost_estimate=comm_cost(110),
-    )(rows, up_rows, gate_all, down_all, upstream)
+        cost_estimate=comm_cost(130),
+    )(rows, upstream, up_rows, gate_all, down_weight, above, below)
 
 
 def unit_grads_kernel(
@@ -1239,34 +1383,6 @@
     masked = jnp.where(allowed, scores, MASKED)
     exponent = jnp.exp(masked - jnp.max(masked, axis=-1, keepdims=True))
     return exponent / jnp.sum(exponent, axis=-1, keepdims=True)
-
-
-def allowed_of(segment_col, segment_row, id_col, id_row):
-    return (segment_col[0] == segment_row[0]) & (id_row[...] <= id_col[...])
-
-
-def attend_kernel(
-    raw_ref, cos_ref, sin_ref, segment_col, segment_row, id_col, id_row, gains_ref, low_ref, out_ref
-):
-    group_rows = cos_ref.shape[1]
-    raw = raw_ref[...].reshape(group_rows, raw_ref.shape[3])
-    heads = raw.shape[1] // HEAD_SIZE - 2
-    cosine, sine = cos_ref[0], sin_ref[0]
-    allowed = allowed_of(segment_col, segment_row, id_col, id_row)
-    columns = [raw[:, head * HEAD_SIZE : (head + 1) * HEAD_SIZE] for head in range(heads + 2)]
-    turned = []
-    for head in range(heads + 1):
-        gain = gains_ref[min(head // heads, 1)][None, :]
-        turned.append(
-            low(turn_pairs(columns[head] * inv_rms(columns[head]) * gain, cosine, sine))
-        )
-    value = low(columns[heads + 1])
-    attended = [
-        low(matmul(low(softmax_of(turned[head], turned[heads], allowed)), value))
-        for head in range(heads)
-    ]
-    low_ref[...] = jnp.concatenate(turned + [value], axis=1).reshape(low_ref.shape)
-    out_ref[...] = jnp.concatenate(attended, axis=1).reshape(out_ref.shape)
 
 
 def lanes(values, head):
@@ -1612,41 +1728,166 @@
     )
 
 
-def attention_specs(group_rows, rows):
-    bucket = lambda width: pl.BlockSpec((2, 1, rows, width), lambda step: (0, step, 0, 0))
-    tables = [
-        pl.BlockSpec((1, group_rows, HEAD_SIZE), lambda step: (step, 0, 0)),
-        pl.BlockSpec((1, group_rows, HEAD_SIZE), lambda step: (step, 0, 0)),
-        pl.BlockSpec((1, group_rows, 1), lambda step: (step, 0, 0)),
-        pl.BlockSpec((1, 1, group_rows), lambda step: (step, 0, 0)),
-        pl.BlockSpec((group_rows, 1), lambda step: (0, 0)),
-        pl.BlockSpec((1, group_rows), lambda step: (0, 0)),
-        pl.BlockSpec((2, HEAD_SIZE), lambda step: (0, 0)),
-    ]
-    return bucket, tables
-
-
-def attend(raw, tables):
-    _, buckets, rows, width = raw.shape
-    bucket, table_specs = attention_specs(2 * rows, rows)
-    query_width = width - 2 * HEAD_SIZE
-    return pl.pallas_call(
-        attend_kernel,
-        grid=(buckets,),
-        out_shape=(
-            jax.ShapeDtypeStruct(raw.shape, LOW),
-            jax.ShapeDtypeStruct((2, buckets, rows, query_width), LOW),
-        ),
-        in_specs=[bucket(width)] + table_specs,
-        out_specs=(bucket(width), bucket(query_width)),
-        compiler_params=pltpu.CompilerParams(vmem_limit_bytes=48 * 1024 * 1024),
-        cost_estimate=pl.CostEstimate(
-            flops=30_000_000_000, bytes_accessed=20_000_000, transcendentals=0
-        ),
-    )(raw, *tables)
-
-
-def shards(
+def row_ids_of(local_rows):
+    core = lax.axis_index("tensor")
+    local_ids = jnp.arange(local_rows, dtype=jnp.int32)
+    return jnp.concatenate([core * local_rows + local_ids, (1 - core) * local_rows + local_ids])
+
+
+def heads_of(weight):
+    return weight.reshape(weight.shape[0], 4, -1).transpose(1, 0, 2)
+
+
+def heads_back(pieces):
+    return f32(pieces).transpose(1, 0, 2).reshape(pieces.shape[1], -1)
+
+
+def units_of(weight, down_rows):
+    split = weight.reshape(weight.shape[0], -1, 4, down_rows)
+    return split.transpose(2, 0, 1, 3).reshape(4, weight.shape[0], -1)
+
+
+def units_back(pieces, down_rows):
+    rows = pieces.shape[1]
+    return f32(pieces).reshape(4, rows, -1, down_rows).transpose(1, 2, 0, 3).reshape(rows, -1)
+
+
+def shards(*arguments):
+    if lax.axis_size("f") == 4:
+        return line_of_four(*arguments)
+    return any_line(*arguments)
+
+
+def line_of_four(
+    layer_input,
+    attn_norm,
+    head_norms,
+    query_weight,
+    key_matrix,
+    value_matrix,
+    output_weight,
+    mlp_norm,
+    gate_weight,
+    up_weight,
+    down_weight,
+    grad_out,
+    doc_lengths,
+):
+    local_rows, model_width = layer_input.shape
+    weight_rows = gate_weight.shape[0]
+    down_rows = down_weight.shape[0]
+    hidden_part = 4 * down_rows
+    qkv_pieces = jnp.concatenate(
+        [heads_of(query_weight), heads_of(key_matrix), heads_of(value_matrix)], axis=2
+    )
+    head_part = qkv_pieces.shape[2]
+    query_part = head_part - 2 * HEAD_SIZE
+    input_float = f32(layer_input)
+    row_ids = row_ids_of(local_rows)
+    (
+        normed_attn,
+        _,
+        up_rows,
+        gate_all,
+        above,
+        below,
+        qkv_all,
+        out_all,
+        qkv_raw,
+        qkv_low,
+        cos_tab,
+        sin_tab,
+        segment_col,
+        segment_row,
+        attended,
+        hidden_state,
+        normed_mlp,
+    ) = first_part(
+        low(input_float * inv_rms(input_float) * attn_norm),
+        qkv_pieces,
+        output_weight,
+        units_of(gate_weight, down_rows),
+        units_of(up_weight, down_rows),
+        down_weight,
+        doc_lengths,
+        row_ids,
+        head_norms,
+        layer_input,
+        mlp_norm,
+    )
+    tables = (
+        cos_tab,
+        sin_tab,
+        segment_col,
+        segment_row,
+        row_ids[:, None],
+        row_ids[None, :],
+        head_norms,
+    )
+    rows_all, grad_all, inner_low, gate_grad, up_grad, part_sums, grad_sums = units_products(
+        normed_mlp,
+        grad_out,
+        up_rows.reshape(-1, hidden_part),
+        gate_all.reshape(model_width, hidden_part),
+        down_weight,
+        above,
+        below,
+    )
+    mlp_row_grad, mlp_rows, grad_down, grad_gate_part, grad_up_part = unit_grads(
+        rows_all, grad_all, inner_low, gate_grad, up_grad, part_sums, grad_sums
+    )
+    line_shape = (4, 4 * weight_rows, hidden_part)
+    (
+        hidden_grad,
+        mlp_gain_part,
+        head_gains,
+        grad_qkv_part,
+        grad_proj_part,
+        grad_sums,
+        grad_gate_columns,
+        grad_up_columns,
+    ) = heads_backward(
+        hidden_state,
+        mlp_row_grad,
+        grad_out,
+        mlp_norm[None],
+        out_all.reshape(-1, model_width),
+        attended,
+        qkv_raw,
+        qkv_low,
+        tables,
+        normed_attn,
+        qkv_all.reshape(model_width, head_part),
+        grad_gate_part.reshape(line_shape),
+        grad_up_part.reshape(line_shape),
+    )
+    grad_input, grad_qkv_columns, grad_out_proj, gains = last_sums(
+        grad_sums,
+        grad_qkv_part.reshape(4, 4 * weight_rows, head_part),
+        grad_proj_part.reshape((4,) + output_weight.shape),
+        layer_input,
+        hidden_grad,
+        attn_norm[None],
+        jnp.concatenate([mlp_gain_part, head_gains], axis=1),
+    )
+    gains = gains.reshape(-1)
+    return (
+        low(hidden_state + mlp_rows),
+        grad_input,
+        gains[:model_width],
+        gains[2 * model_width :].reshape(2, HEAD_SIZE),
+        heads_back(grad_qkv_columns[:, :, :query_part]),
+        heads_back(grad_qkv_columns[:, :, query_part : query_part + HEAD_SIZE]),
+        heads_back(grad_qkv_columns[:, :, query_part + HEAD_SIZE :]),
+        f32(grad_out_proj),
+        gains[model_width : 2 * model_width],
+        units_back(grad_gate_columns, down_rows),
+        units_back(grad_up_columns, down_rows),
+        f32(grad_down),
+    )
+
+
+def any_line(
     layer_input,
     attn_norm,
     head_norms,
@@ -1662,217 +1903,114 @@
     doc_lengths,
 ):
     line_extent = lax.axis_size("f")
-    on_line = line_extent == 4
-    core = lax.axis_index("tensor")
     local_rows, model_width = layer_input.shape
     group_rows = 2 * local_rows
     all_rows = 8 * local_rows
     weight_rows = gate_weight.shape[0]
     down_rows = down_weight.shape[0]
     hidden_part = line_extent * down_rows
-    query_part = query_weight.shape[1] // 4
-    head_part = query_part + 2 * HEAD_SIZE
-
-    def heads_of(weight):
-        return weight.reshape(weight_rows, 4, -1).transpose(1, 0, 2)
-
-    def units_of(weight):
-        split = weight.reshape(weight_rows, line_extent, 4, down_rows)
-        return split.transpose(2, 0, 1, 3).reshape(4, weight_rows, hidden_part)
-
     qkv_pieces = jnp.concatenate(
         [heads_of(query_weight), heads_of(key_matrix), heads_of(value_matrix)], axis=2
     )
-    gate_pieces, up_pieces = units_of(gate_weight), units_of(up_weight)
+    head_part = qkv_pieces.shape[2]
+    query_part = head_part - 2 * HEAD_SIZE
+    heads = head_part // HEAD_SIZE - 2
+
+    def exchanged(pieces):
+        return natural_plane(plane_exchange(own_plane(pieces, 0)), 0)
+
+    def line_rows(pieces):
+        return line_gather(exchanged(pieces)).reshape(model_width, -1)
+
+    def line_sums(partial):
+        parts = low(partial).reshape(line_extent, 4 * weight_rows, -1)
+        return exchanged(low(line_scatter(parts)).reshape(4, weight_rows, -1))
+
+    qkv_all = line_rows(qkv_pieces)
+    out_all = full_gather(output_weight)
+    gate_all = line_rows(units_of(gate_weight, down_rows))
+    up_all = line_rows(units_of(up_weight, down_rows))
+    down_all = line_gather(down_weight).reshape(hidden_part, model_width)
 
     input_float = f32(layer_input)
     scale_attn = inv_rms(input_float)
-    normed_own = low(input_float * scale_attn * attn_norm)
-    if on_line:
-        normed_attn, qkv_all, out_all, gate_rows, up_rows, *near_down = first_gather(
-            normed_own, qkv_pieces, output_weight, gate_pieces, up_pieces, down_weight
-        )
-    else:
-        normed_attn = tokens_gather(normed_own)
-        exchanged = lambda pieces: natural_plane(plane_exchange(own_plane(pieces, 0)), 0)
-        qkv_all = line_gather(exchanged(qkv_pieces))
-        out_all = full_gather(output_weight)
-        gate_rows, up_rows = exchanged(gate_pieces), exchanged(up_pieces)
-        near_down = None
-    normed_attn = normed_attn.reshape(all_rows, model_width)
-    qkv_all = qkv_all.reshape(model_width, head_part)
-    out_all = out_all.reshape(-1, model_width)
-    gate_rows = gate_rows.reshape(4 * weight_rows, hidden_part)
-    up_rows = up_rows.reshape(4 * weight_rows, hidden_part)
-
-    lengths_list = plane_lengths(doc_lengths)
-    local_ids = jnp.arange(local_rows, dtype=jnp.int32)
-    row_ids = jnp.concatenate([core * local_rows + local_ids, (1 - core) * local_rows + local_ids])
-    segments, positions = jax.vmap(lambda lengths: doc_layout(lengths, row_ids))(lengths_list)
-    cos_tab, sin_tab = rope_tables(positions.reshape(-1), HEAD_SIZE)
-    tables = (
-        jnp.concatenate([cos_tab, cos_tab], axis=1).reshape(4, group_rows, HEAD_SIZE),
-        jnp.concatenate([-sin_tab, sin_tab], axis=1).reshape(4, group_rows, HEAD_SIZE),
-        segments[:, :, None],
-        segments[:, None, :],
-        row_ids[:, None],
-        row_ids[None, :],
-        head_norms,
+    normed_attn = tokens_gather(low(input_float * scale_attn * attn_norm))
+    row_ids = row_ids_of(local_rows)
+    segments, positions = jax.vmap(lambda lengths: doc_layout(lengths, row_ids))(
+        plane_lengths(doc_lengths)
     )
     qkv_raw = matmul(normed_attn, qkv_all).reshape(2, 4, local_rows, head_part)
-    qkv_low, attended_heads = attend(qkv_raw, tables)
-    gate_all = line_gather(gate_rows, (attended_heads,)).reshape(model_width, hidden_part)
-    if on_line:
-        attended = heads_to_tokens(attended_heads)
-    else:
-        attended = natural_plane(
-            plane_exchange([attended_heads[:, step].reshape(group_rows, -1) for step in range(4)]),
-            0,
-        )
-    attended_own = attended
-    attended = (
-        attended.reshape(4, group_rows, query_part)
-        .transpose(1, 0, 2)
-        .reshape(group_rows, 4 * query_part)
-    )
+    roll = lambda values: jnp.roll(values, HEAD_SIZE // 2, 1)
+    buckets, attended_parts = [], []
+    for step in range(4):
+        cos_tab, sin_tab = rope_tables(positions[step], HEAD_SIZE)
+        cosine = jnp.concatenate([cos_tab, cos_tab], axis=1)
+        sine = jnp.concatenate([-sin_tab, sin_tab], axis=1)
+        allowed = (segments[step][:, None] == segments[step][None, :]) & (
+            row_ids[None, :] <= row_ids[:, None]
+        )
+        raw = qkv_raw[:, step].reshape(group_rows, head_part)
+        turned = []
+        for head in range(heads + 1):
+            unnormed = lanes(raw, head)
+            normed = unnormed * inv_rms(unnormed) * head_norms[min(head // heads, 1)]
+            turned.append(low(normed * cosine + roll(normed) * sine))
+        value = low(lanes(raw, heads + 1))
+        attended_parts.append(
+            jnp.concatenate(
+                [
+                    low(matmul(low(softmax_of(turned[head], turned[heads], allowed)), value))
+                    for head in range(heads)
+                ],
+                axis=1,
+            )
+        )
+        buckets.append((raw, jnp.concatenate(turned + [value], axis=1), allowed, cosine, sine))
+    attended = natural_plane(plane_exchange(attended_parts), 0)
+    attended = attended.transpose(1, 0, 2).reshape(group_rows, 4 * query_part)
     hidden_state = input_float + pair_scatter(low(matmul(attended, out_all)))
 
     scale_mlp = inv_rms(hidden_state)
-    normed_own = low(hidden_state * scale_mlp * mlp_norm)
-    line_shape = (line_extent, 4 * weight_rows, hidden_part)
-    grad_all = tokens_gather(after(grad_out, normed_attn), (attended_heads,))
-    down_all = line_gather(
-        after(down_weight, normed_attn), (attended_heads,), near_down
-    ).reshape(hidden_part, model_width)
-    if on_line:
-        grad_blocks = grad_all.reshape(8, local_rows, model_width)
-        rows_all, inner_low, gate_grad, up_grad, part_sums, grad_sums = units_products(
-            normed_own, up_rows, gate_all, down_all, grad_blocks
-        )
-        mlp_row_grad, mlp_rows, grad_down, grad_gate_part, grad_up_part = unit_grads(
-            rows_all, grad_blocks, inner_low, gate_grad, up_grad, part_sums, grad_sums
-        )
-        grad_down = f32(grad_down)
-        grad_gate_part = grad_gate_part.reshape(line_shape)
-        grad_up_part = grad_up_part.reshape(line_shape)
-    else:
-        normed_mlp, up_all = tokens_gather(normed_own), line_gather(up_rows)
-        normed_mlp = normed_mlp.reshape(all_rows, model_width)
-        up_all = up_all.reshape(model_width, hidden_part)
-        gate_raw = matmul(normed_mlp, gate_all)
-        up_raw = matmul(normed_mlp, up_all)
-        activated = jax.nn.silu(gate_raw)
-        inner_low = low(activated * up_raw)
-        grad_down_part = low(matmul_tn(inner_low, grad_all))
-        mlp_rows = tokens_scatter(low(matmul(inner_low, down_all)))
-        inner_grad = matmul_nt(grad_all, down_all)
-        sigmoid_gate = jax.nn.sigmoid(gate_raw)
-        gate_grad = low(
-            inner_grad * up_raw * sigmoid_gate * (1.0 + gate_raw * (1.0 - sigmoid_gate))
-        )
-        up_grad = low(inner_grad * activated)
-        grad_gate_part = low(matmul_tn(normed_mlp, gate_grad)).reshape(line_shape)
-        grad_up_part = low(matmul_tn(normed_mlp, up_grad)).reshape(line_shape)
-        mlp_row_grad = tokens_scatter(
-            low(matmul_nt(gate_grad, gate_all) + matmul_nt(up_grad, up_all))
-        )
-        grad_down = line_scatter(grad_down_part.reshape(line_extent, down_rows, model_width))
-    layer_out = low(hidden_state + mlp_rows)
-
-    if on_line:
-        (
-            hidden_grad,
-            mlp_gain_part,
-            head_gains,
-            grad_qkv_part,
-            grad_proj_part,
-            grad_sums,
-            grad_gate_columns,
-            grad_up_columns,
-        ) = heads_backward(
-            hidden_state,
-            mlp_row_grad,
-            grad_out,
-            mlp_norm[None],
-            out_all,
-            attended_own,
-            qkv_raw,
-            qkv_low,
-            tables,
-            normed_attn.reshape(8, local_rows, model_width),
-            qkv_all,
-            grad_gate_part,
-            grad_up_part,
-        )
-        grad_input, grad_qkv_columns, grad_out_proj, gains = last_sums(
-            grad_sums,
-            grad_qkv_part.reshape(4, 4 * weight_rows, head_part),
-            grad_proj_part.reshape(4, output_weight.shape[0], model_width),
-            layer_input,
-            hidden_grad,
-            attn_norm[None],
-            jnp.concatenate([mlp_gain_part, head_gains], axis=1),
-        )
-        gains = gains.reshape(-1)
-        grad_out_proj = f32(grad_out_proj)
-    else:
-        hidden_norm_grad, mlp_gain_part = norm_back(
-            hidden_state, scale_mlp, mlp_norm, mlp_row_grad
-        )
-        hidden_grad = f32(grad_out) + hidden_norm_grad
-        branch_grad = pair_gather(low(hidden_grad))
-        attended_grad = low(matmul_nt(branch_grad, out_all))
-        split = attended_grad.reshape(group_rows, 4, query_part).transpose(1, 0, 2)
-        heads_grad = plane_exchange(own_plane(split, 0))
-        grad_proj_part = full_scatter_plane(low(matmul_tn(attended, branch_grad)))
-        back = [
-            attend_back_values(
-                qkv_raw[:, step].reshape(group_rows, head_part),
-                qkv_low[:, step].reshape(group_rows, head_part),
-                heads_grad[step],
-                (segments[step][:, None] == segments[step][None, :])
-                & (row_ids[None, :] <= row_ids[:, None]),
-                tables[0][step],
-                tables[1][step],
-                head_norms,
-                lambda values: jnp.roll(values, HEAD_SIZE // 2, 1),
-            )
-            for step in range(4)
-        ]
-        qkv_grad = jnp.stack([grads for grads, _ in back]).reshape(4, 2, local_rows, head_part)
-        qkv_grad = qkv_grad.transpose(1, 0, 2, 3).reshape(all_rows, head_part)
-        grad_qkv_part = low(matmul_tn(normed_attn, qkv_grad)).reshape(
-            line_extent, 4 * weight_rows, head_part
-        )
-        attn_row_grad = tokens_scatter(low(matmul_nt(qkv_grad, qkv_all)))
-        grad_rows = lambda part: low(line_scatter(part))
-        grad_qkv_columns = exchanged(
-            grad_rows(grad_qkv_part).reshape(4, weight_rows, head_part)
-        )
-        grad_gate_columns = exchanged(
-            grad_rows(grad_gate_part).reshape(4, weight_rows, hidden_part)
-        )
-        grad_up_columns = exchanged(grad_rows(grad_up_part).reshape(4, weight_rows, hidden_part))
-        grad_out_proj = line_scatter(grad_proj_part)
-        input_norm_grad, attn_gain_part = norm_back(
-            input_float, scale_attn, attn_norm, attn_row_grad
-        )
-        grad_input = hidden_grad + input_norm_grad
-        head_gains = sum(gains for _, gains in back)[0]
-        gains = total_sum(
-            jnp.concatenate([attn_gain_part, mlp_gain_part, head_gains]).reshape(-1, HEAD_SIZE)
-        ).reshape(-1)
-
-    def heads_back(pieces):
-        return f32(pieces).transpose(1, 0, 2).reshape(weight_rows, -1)
-
-    def units_back(pieces):
-        split = f32(pieces).reshape(4, weight_rows, line_extent, down_rows)
-        return split.transpose(1, 2, 0, 3).reshape(weight_rows, -1)
-
+    normed_mlp = tokens_gather(low(hidden_state * scale_mlp * mlp_norm))
+    grad_all = tokens_gather(grad_out)
+    gate_raw = matmul(normed_mlp, gate_all)
+    up_raw = matmul(normed_mlp, up_all)
+    activated = jax.nn.silu(gate_raw)
+    inner_low = low(activated * up_raw)
+    layer_out = low(hidden_state + tokens_scatter(low(matmul(inner_low, down_all))))
+    inner_grad = matmul_nt(grad_all, down_all)
+    sigmoid_gate = jax.nn.sigmoid(gate_raw)
+    gate_grad = low(inner_grad * up_raw * sigmoid_gate * (1.0 + gate_raw * (1.0 - sigmoid_gate)))
+    up_grad = low(inner_grad * activated)
+    mlp_row_grad = tokens_scatter(
+        low(matmul_nt(gate_grad, gate_all) + matmul_nt(up_grad, up_all))
+    )
+    grad_down = line_scatter(
+        low(matmul_tn(inner_low, grad_all)).reshape(line_extent, down_rows, model_width)
+    )
+
+    hidden_norm_grad, mlp_gain_part = norm_back(hidden_state, scale_mlp, mlp_norm, mlp_row_grad)
+    hidden_grad = f32(grad_out) + hidden_norm_grad
+    branch_grad = pair_gather(low(hidden_grad))
+    split = low(matmul_nt(branch_grad, out_all)).reshape(group_rows, 4, query_part)
+    heads_grad = plane_exchange(own_plane(split.transpose(1, 0, 2), 0))
+    grad_out_proj = line_scatter(full_scatter_plane(low(matmul_tn(attended, branch_grad))))
+    back = [
+        attend_back_values(raw, kept, heads_grad[step], allowed, cosine, sine, head_norms, roll)
+        for step, (raw, kept, allowed, cosine, sine) in enumerate(buckets)
+    ]
+    qkv_grad = jnp.stack([grads for grads, _ in back]).reshape(4, 2, local_rows, head_part)
+    qkv_grad = qkv_grad.transpose(1, 0, 2, 3).reshape(all_rows, head_part)
+    attn_row_grad = tokens_scatter(low(matmul_nt(qkv_grad, qkv_all)))
+    grad_qkv_columns = line_sums(matmul_tn(normed_attn, qkv_grad))
+    input_norm_grad, attn_gain_part = norm_back(input_float, scale_attn, attn_norm, attn_row_grad)
+    head_gains = sum(gains for _, gains in back)[0]
+    gains = total_sum(
+        jnp.concatenate([attn_gain_part, mlp_gain_part, head_gains]).reshape(-1, HEAD_SIZE)
+    ).reshape(-1)
     return (
         layer_out,
-        grad_input,
+        hidden_grad + input_norm_grad,
         gains[:model_width],
         gains[2 * model_width :].reshape(2, HEAD_SIZE),
         heads_back(grad_qkv_columns[:, :, :query_part]),
@@ -1880,8 +2018,8 @@
         heads_back(grad_qkv_columns[:, :, query_part + HEAD_SIZE :]),
         grad_out_proj,
         gains[model_width : 2 * model_width],
-        units_back(grad_gate_columns),
-        units_back(grad_up_columns),
+        units_back(line_sums(matmul_tn(normed_mlp, gate_grad)), down_rows),
+        units_back(line_sums(matmul_tn(normed_mlp, up_grad)), down_rows),
         grad_down,
     )
 

time: 690 us -> 627 us (0.909)
  Pallas kernels: 525 us -> 586 us
  waiting for transfers between devices: 41.5 us -> 0 us
  local copies, waits for them, and re-layouts: 52.6 us -> 21 us
  starting transfers between devices: 24.6 us -> 0 us
  matrix products: 15.1 us -> 0 us
  other arithmetic: 25.7 us -> 12.5 us
    pallas_call x4 -> x2, Pallas kernels: 256 us -> 315 us  [the longest x1 160 us: first_part(): pl.pallas_call(lambda *refs: first_kernel(documents, *refs), out_shape=(l...]
    ppermute x18 -> x0, waiting for transfers between devices: 41.5 us -> none  [the longest x2 28.4 us: line_gather(): passed = lax.ppermute(two_away, 'f', [(1, 0), (2, 3)])]
    ppermute x18 -> x0, starting transfers between devices: 24.6 us -> none  [the longest x12 10.9 us: swap(): return lax.ppermute(block, axis, [(0, 1), (1, 0)])]
    unnamed x73 -> x35, local copies, waits for them, and re-layouts: 27.8 us -> 11.1 us
    dot_general x2 -> x0, matrix products: 15.1 us -> none  [matmul(): return jnp.dot(left_mat, right_mat, preferred_element_type=jnp.float32)]
  transfers between devices with their start and end apart: 18 -> 0, of which waited for: 5 -> 0; matrix products, arithmetic and copies ran while one was open for 10% -> 0% of each run, Pallas kernels for 19% -> 0%
where the time goes in v4:
time: 627 us; the launch traced here: 621 us
  Pallas kernels  586 us (93%)
  local copies, waits for them, and re-layouts  21 us (3%)
  other arithmetic  12.5 us (2%)
    pallas_call x1, Pallas kernels, first_part(): pl.pallas_call(lambda *refs: first_kernel(documents, *refs), out_shape=(l...  160 us
    pallas_call x1, Pallas kernels, units_products(): pl.pallas_call(units_kernel, out_shape=(blocks, blocks, hidden, hidden, h...  155 us
    pallas_call x1, Pallas kernels, heads_backward(): pl.pallas_call(heads_back_kernel, out_shape=(jax.ShapeDtypeStruct((rows,...  125 us
    pallas_call x1, Pallas kernels, unit_grads(): pl.pallas_call(unit_grads_kernel, out_shape=(jax.ShapeDtypeStruct((block_...  81.6 us
    pallas_call x1, Pallas kernels, last_sums(): pl.pallas_call(last_kernel, out_shape=(jax.ShapeDtypeStruct((rows, width)...  65.1 us

profile of v4, /device:TPU:0, one launch (start us, length us, event | category | flops | bytes accessed | tf_op | source)
XLA Modules:
  0.0 620.8 jit_solution(12620842391930331910)
XLA Ops:
  1.3 1.6 fusion
  2.9 1.3 pad.4.refs_6_
  4.2 1.0 copy.31
  5.3 1.0 copy.33
  6.5 0.9 copy.41.refs_7_.id_col
  9.0 1.2 copy.39.refs_3_
  10.6 1.2 copy.40.refs_4_
  11.8 1.3 fusion.2.refs_0_
  13.0 160.3 %shard_map.220 = (bf16[8,256,2048]{2,1,0:T(8,128)(2,1)}, bf16[4,128,768]{2,1,0:T(8,128)(2,1)}, bf16[4,128,768]{2,1,0:T(8,128)(2,1)}, bf16[4,4,128,768]{3,2,1,0:T...) custom-call(bf16[256,2048]{1,0:T(8,128)(2,1)} %fusion.2.refs_0_, ...), custom_call_target="tpu_custom_call" | custom-call | bytes 390000000 | tf_op jit(solution)/shard_map/pallas_call | solution.py:790
  173.3 154.6 %shard_map.221 = (bf16[8,256,2048]{2,1,0:T(8,128)(2,1)}, bf16[8,256,2048]{2,1,0:T(8,128)(2,1)}, bf16[8,256,768]{2,1,0:T(8,128)(2,1)}, bf16[8,256,768]{2,1,0:T(8,...) custom-call(bf16[256,2048]{1,0:T(8,128)(2,1)} %get-tuple-element.53.rows_ref, ...), custom_call_target="tpu_custom_call" | custom-call | bytes 390000000 | tf_op jit(solution)/shard_map/pallas_call | solution.py:1104
  327.9 81.6 %shard_map.222 = (f32[256,2048]{1,0:T(8,128)}, f32[256,2048]{1,0:T(8,128)}, bf16[192,2048]{1,0:T(8,128)(2,1)}, bf16[2048,768]{1,0:T(8,128)(2,1)}, bf16[2048,768]{1,0:T(8,128)(2,1)}) custom-call(bf16[8,256,2048]{2,1,0:T(8,128)(2,1)} %get-tuple-element.58.rows_all, bf16[8,256,2048]{2,1,0:T(8,128)(2,1)} %get-tuple-element.59.upstream_ref, ...), custom_call_target="tpu_custom_call" | custom-call | bytes 210000000 | tf_op jit(solution)/shard_map/pallas_call | solution.py:1233
  409.5 124.5 %shard_map.223 = (f32[256,2048]{1,0:T(8,128)}, f32[1,2048]{1,0:T(1,128)}, f32[1,256]{1,0:T(1,128)}, bf16[2048,512]{1,0:T(8,128)(2,1)}, bf16[256,2048]{1,0:T(8,12...) custom-call(f32[256,2048]{1,0:T(8,128)} %get-tuple-element.52.hidden_ref, ...), custom_call_target="tpu_custom_call" | custom-call | bytes 345000000 | tf_op jit(solution)/shard_map/pallas_call | solution.py:1677
  534.1 3.5 add_convert_fusion
  538.1 65.1 %shard_map.224 = (f32[256,2048]{1,0:T(8,128)}, bf16[4,128,512]{2,1,0:T(8,128)(2,1)}, bf16[64,2048]{1,0:T(8,128)(2,1)}, f32[1,4352]{1,0:T(1,128)}) custom-call(bf16[4,256,2048]{2,1,0:T(8,128)(2,1)} %get-tuple-element.79.parts_ref, bf16[4,512,512]{2,1,0:T(8,128)(2,1)} %bitcast.62, bf16[4,64,2048]{2,1,0:T(8,128)(2,1)} %bitcast.67, bf16[256,2048]{1,0:T(8,128)(2,1)} %input_ref.1, ...), custom_call_target="tpu_custom_call" | custom-call | bytes 180000000 | tf_op jit(solution)/shard_map/pallas_call | solution.py:1351
  603.2 1.2 slice.27
  604.4 1.3 fusion.3
  605.8 1.8 convert_element_type.23
  607.5 1.0 convert_bitcast_fusion
  608.7 1.0 copy.50
  612.1 1.6 copy.53
  613.8 1.4 copy.48
  615.3 1.6 copy.54
  616.9 1.3 convert_element_type.24
  619.1 1.3 copy.56
  (48 shorter events, 7.1 us)
Async XLA Ops:
  0.6 6.7 %copy-start.7 = (bf16[128,1024]{1,0:T(8,128)(2,1)S(1)}, bf16[128,1024]{1,0:T(8,128)(2,1)}, u32[]{:S(2)}) copy-start(bf16[128,1024]{1,0:T(8,128)(2,1)} %param.16) | copy-start | bytes 786436
  1.3 7.3 %copy-start.2 = (bf16[128,3072]{1,0:T(8,128)(2,1)S(1)}, bf16[128,3072]{1,0:T(8,128)(2,1)}, u32[]{:S(2)}) copy-start(bf16[128,3072]{1,0:T(8,128)(2,1)} %param.21) | copy-start | bytes 2359300
  2.9 6.0 copy-start.8
  8.5 1.6 copy-start.3
  10.1 1.6 copy-start
  10.2 1.6 copy-start.9
  534.0 3.5 copy-start.10
  534.0 3.5 copy-start.11
  603.2 6.5 %copy-start.6 = (bf16[4,128,512]{2,1,0:T(8,128)(2,1)S(1)}, bf16[4,128,512]{2,1,0:T(8,128)(2,1)}, u32[]{:S(2)}) copy-start(bf16[4,128,512]{2,1,0:T(8,128)(2,1)} %get-tuple-element.87) | copy-start | bytes 1572868
  608.7 3.0 copy-start.5
  615.3 1.6 copy-start.4
  616.9 2.2 copy-start.1

commit v5 on v4

--- a/solution.py
+++ b/solution.py
@@ -255,9 +255,10 @@
         self.pass_up = remote(two, two, send.at[3], recv.at[1], place.up)
 
     def start(self):
-        pl.when(self.place.z > 0)(self.to_down.start)
-        pl.when(self.place.z < 3)(self.to_up.start)
+        z = self.place.z
         self.to_two.start()
+        pl.when((z == 1) | (z == 3))(self.to_down.start)
+        pl.when((z == 0) | (z == 2))(self.to_up.start)
 
     def step(self, turn):
         if turn == 2:
@@ -273,6 +274,8 @@
         if turn == 2:
             pl.when(self.place.z == 1)(self.pass_down.start)
             pl.when(self.place.z == 2)(self.pass_up.start)
+            pl.when(self.place.z == 1)(self.to_up.start)
+            pl.when(self.place.z == 2)(self.to_down.start)
 
     def finish(self):
         pl.when(self.place.z > 0)(self.to_down.wait_send)
@@ -422,18 +425,22 @@
 
 class LineScatter:
     @staticmethod
-    def scratch(rows, width):
-        return [pltpu.VMEM((6, rows, width), LOW)]
-
-    def __init__(self, place, part, out, buffers, marks):
-        self.place, self.out = place, out
-        self.kept = buffers[0]
-        self.rows = self.kept.shape[1]
-        self.passed, self.above, self.below, self.two, self.mid, self.own = (
-            self.kept.at[index] for index in range(6)
-        )
+    def scratch(rows, width, here=False):
+        return [pltpu.VMEM((4 if here else 6, rows, width), LOW)]
+
+    def __init__(self, place, part, out, buffers, marks, here=False):
+        self.place, self.out, self.here = place, out, here
+        kept = buffers[0]
+        self.rows = kept.shape[1]
+        self.passed, self.above, self.below, self.two = (kept.at[index] for index in range(4))
+        z = place.z
+        if here:
+            self.mid, self.own = part(place.at(2)), part(z)
+        else:
+            self.mid, self.own = kept.at[4], kept.at[5]
+            self.load_mid = pltpu.make_async_copy(part(place.at(2)), self.mid, marks.take())
+            self.load_own = pltpu.make_async_copy(part(z), self.own, marks.take())
         self.recv = [marks.take() for _ in range(4)]
-        z = place.z
         self.pass_up = remote(part(3), self.passed, marks.take(), self.recv[0], place.up)
         self.pass_down = remote(part(0), self.passed, marks.take(), self.recv[0], place.down)
         self.to_down = remote(
@@ -441,67 +448,65 @@
         )
         self.to_up = remote(part(place.at(1)), self.below, marks.take(), self.recv[2], place.up)
         self.to_two = remote(self.mid, self.two, marks.take(), self.recv[3], place.two)
-        self.load_mid = pltpu.make_async_copy(part(place.at(2)), self.mid, marks.take())
-        self.load_own = pltpu.make_async_copy(part(z), self.own, marks.take())
 
     def start(self):
         z = self.place.z
         pl.when(z == 0)(self.pass_up.start)
         pl.when(z == 3)(self.pass_down.start)
-        self.load_mid.start()
-        pl.when(z > 0)(self.to_down.start)
-        pl.when(z < 3)(self.to_up.start)
-        self.load_own.start()
-        self.load_mid.wait()
-        pl.when((z == 0) | (z == 3))(self.to_two.start)
+        if not self.here:
+            self.load_mid.start()
+        pl.when((z == 1) | (z == 2))(self.to_down.start)
+        pl.when((z == 1) | (z == 2))(self.to_up.start)
+        if not self.here:
+            self.load_own.start()
+
+    def add(self, target, other):
+        def work(rows):
+            target[rows] = low(f32(target[rows]) + f32(other[rows]))
+
+        each_rows(self.rows, 16, work)
 
     def middle(self):
         z = self.place.z
+        if not self.here:
+            self.load_mid.wait()
+        pl.when(z == 0)(self.pass_up.wait_send)
+        pl.when(z == 3)(self.pass_down.wait_send)
 
         @pl.when((z == 1) | (z == 2))
         def _():
             arrived(self.passed, self.recv[0], self.place.two)
-
-            def work(rows):
-                self.kept[4, rows] = low(f32(self.kept[4, rows]) + f32(self.kept[0, rows]))
-
-            each_rows(self.rows, 16, work)
-            self.to_two.start()
+            self.add(self.mid, self.passed)
+
+        self.to_two.start()
+        pl.when(z == 0)(self.to_up.start)
+        pl.when(z == 3)(self.to_down.start)
 
     def finish(self):
-        z, rows_all = self.place.z, self.rows
-        out, kept = self.out, self.kept
-        self.load_own.wait()
+        z = self.place.z
+        if not self.here:
+            self.load_own.wait()
 
         @pl.when(z < 3)
         def _():
             arrived(self.above, self.recv[1], self.place.two)
-
-            def work(rows):
-                kept[5, rows] = low(f32(kept[5, rows]) + f32(kept[1, rows]))
-
-            each_rows(rows_all, 16, work)
+            self.add(self.own, self.above)
 
         @pl.when(z > 0)
         def _():
             arrived(self.below, self.recv[2], self.place.two)
-
-            def work(rows):
-                kept[5, rows] = low(f32(kept[5, rows]) + f32(kept[2, rows]))
-
-            each_rows(rows_all, 16, work)
+            self.add(self.own, self.below)
 
         arrived(self.two, self.recv[3], self.place.two)
+        out, own, two = self.out, self.own, self.two
 
         def work(rows):
-            out[rows] = low(f32(kept[5, rows]) + f32(kept[3, rows]))
-
-        each_rows(rows_all, 16, work)
+            out[rows] = low(f32(own[rows]) + f32(two[rows]))
+
+        each_rows(self.rows, 16, work)
 
     def drain(self):
         z = self.place.z
-        pl.when(z == 0)(self.pass_up.wait_send)
-        pl.when(z == 3)(self.pass_down.wait_send)
         pl.when(z > 0)(self.to_down.wait_send)
         pl.when(z < 3)(self.to_up.wait_send)
         self.to_two.wait_send()
@@ -549,24 +554,32 @@
     head_norms,
     input_ref,
     norm_ref,
+    upstream_ref,
     rows_all,
     gate_rows,
     up_rows,
     gate_all,
     above_ref,
     below_ref,
+    upstream_all,
+    qkv_hbm,
+    out_hbm,
+    raw_hbm,
+    low_hbm,
+    cos_hbm,
+    sin_hbm,
+    segment_col,
+    segment_row,
+    attended,
+    hidden,
+    normed,
+    marks_ref,
     qkv_all,
     out_all,
     raw_out,
     low_out,
     cos_out,
     sin_out,
-    segment_col,
-    segment_row,
-    attended,
-    hidden,
-    normed,
-    marks_ref,
     lengths_all,
     row_block,
     heads_stage,
@@ -590,6 +603,7 @@
     )
     up_pieces = Exchange(place, lambda p, step: up_ref.at[p], lambda p, step: up_rows.at[p], marks)
     tokens = TokensGather(place, rows_ref, rows_all, marks)
+    upstream = TokensGather(place, upstream_ref, upstream_all, marks)
     qkv_line = LineGather(
         place, qkv_all.at[place.z], lambda z: qkv_all.at[z], marks.take(4), marks.take(4)
     )
@@ -624,9 +638,20 @@
     )
     to_pair = remote(pair_stage, pair_got, marks.take(), marks.take(), place.pair)
     fetch_marks = marks.take(2)
+    qkv_copy = pltpu.make_async_copy(qkv_all, qkv_hbm, marks.take())
+    out_copy = pltpu.make_async_copy(out_all, out_hbm, marks.take())
+    bucket_copies = [
+        pltpu.make_async_copy(raw_out, raw_hbm, marks.take()),
+        pltpu.make_async_copy(low_out, low_hbm, marks.take()),
+    ]
+    table_copies = [
+        pltpu.make_async_copy(cos_out, cos_hbm, marks.take()),
+        pltpu.make_async_copy(sin_out, sin_hbm, marks.take()),
+    ]
 
     lengths.start()
     qkv_pieces.start()
+    gate_pieces.start()
     tokens.start()
     for copy in own_copies:
         copy.start()
@@ -649,13 +674,20 @@
     tokens.forward()
     out_planes[0].start()
     lax.fori_loop(2, 4, table_work, 0)
-    qkv_line.wait(1)
     qkv_line.wait(2)
     out_line.start()
     tokens.last()
     out_planes[0].forward()
-    gate_pieces.start()
+    qkv_line.wait(1)
     qkv_line.wait(3)
+    out_line.wait(2)
+    out_planes[2].start()
+    gate_pieces.wait()
+    gate_line.start()
+    gate_copy.start()
+    for copy in table_copies:
+        copy.start()
+    qkv_copy.start()
     tokens.finish()
 
     def fetches(step):
@@ -705,28 +737,29 @@
 
     lax.fori_loop(0, 1, bucket, 0)
     out_line.wait(1)
+    out_line.wait(3)
     out_planes[1].start()
-    gate_pieces.wait()
-    out_line.wait(2)
-    gate_line.start()
-    gate_copy.start()
-    out_planes[2].start()
+    out_planes[3].start()
+    up_pieces.start()
     lax.fori_loop(1, 2, bucket, 0)
-    out_line.wait(3)
-    out_planes[3].start()
+    out_planes[2].forward()
+    upstream.start()
+    lax.fori_loop(2, 3, bucket, 0)
     out_planes[1].forward()
-    lax.fori_loop(2, 3, bucket, 0)
-    out_planes[2].forward()
     out_planes[3].forward()
     lax.fori_loop(3, 4, bucket, 0)
+    for copy in bucket_copies:
+        copy.start()
+    gate_line.wait(2)
+    pl.when(place.z > 0)(to_down.start)
+    pl.when(place.z < 3)(to_up.start)
     for plane in out_planes:
         plane.wait_far()
     for copy in own_copies:
         copy.wait()
+    out_copy.start()
     heads_out.wait()
-    gate_line.wait(2)
-    pl.when(place.z > 0)(to_down.start)
-    pl.when(place.z < 3)(to_up.start)
+    upstream.forward()
 
     def projected(core_step):
         block = jnp.concatenate([attended[p, core_step] for p in range(4)], axis=1)
@@ -734,7 +767,6 @@
 
     pair_stage[...] = low(projected(1))
     to_pair.start()
-    up_pieces.start()
     hidden[...] = f32(input_ref[...]) + projected(0)
     to_pair.wait()
     norm_row = norm_ref[...]
@@ -747,8 +779,12 @@
     each_rows(rows, 16, norm_work)
     gate_line.wait(1)
     gate_line.wait(3)
+    upstream.last()
     up_pieces.wait()
     gate_copy.wait()
+    for copy in [qkv_copy, out_copy] + bucket_copies + table_copies:
+        copy.wait()
+    upstream.finish()
     parts = [lengths, qkv_pieces, gate_pieces, up_pieces, heads_out, qkv_line, gate_line, out_line]
     for part in parts + out_planes:
         part.finish()
@@ -776,6 +812,7 @@
     head_norms,
     layer_input,
     mlp_norm,
+    grad_out,
 ):
     block_rows, width = rows.shape
     group_rows = 2 * block_rows
@@ -796,6 +833,7 @@
             low_like(4, *gate_pieces.shape),
             low_like(*down_weight.shape),
             low_like(*down_weight.shape),
+            low_like(8, block_rows, width),
             low_like(4, *qkv_pieces.shape),
             low_like(4, 4, *output_weight.shape),
             jax.ShapeDtypeStruct((2, 4, block_rows, head_part), jnp.float32),
@@ -808,10 +846,16 @@
             jax.ShapeDtypeStruct((block_rows, width), jnp.float32),
             low_like(block_rows, width),
         ),
-        in_specs=[ANYWHERE] * 6 + [WHOLE] * 7,
-        out_specs=(ANYWHERE,) * 6 + (WHOLE,) * 11,
+        in_specs=[ANYWHERE] * 6 + [WHOLE] * 7 + [ANYWHERE],
+        out_specs=(ANYWHERE,) * 13 + (WHOLE,) * 5,
         scratch_shapes=[
-            pltpu.SemaphoreType.DMA((140,)),
+            pltpu.SemaphoreType.DMA((160,)),
+            pltpu.VMEM((4,) + qkv_pieces.shape, LOW),
+            pltpu.VMEM((4, 4) + output_weight.shape, LOW),
+            pltpu.VMEM((2, 4, block_rows, head_part), jnp.float32),
+            pltpu.VMEM((2, 4, block_rows, head_part), LOW),
+            pltpu.VMEM(table.shape, jnp.float32),
+            pltpu.VMEM(table.shape, jnp.float32),
             pltpu.VMEM((4,) + lengths.shape, jnp.int32),
             pltpu.VMEM((2, block_rows, width), LOW),
             pltpu.VMEM((4, 2, block_rows, query_part), LOW),
@@ -834,7 +878,91 @@
         head_norms,
         layer_input,
         mlp_norm[None],
-    )
+        grad_out,
+    )
+
+
+class FarScatter:
+    @staticmethod
+    def scratch(rows, width):
+        return [pltpu.VMEM((2, rows // 2, width), LOW)]
+
+    def __init__(self, place, summed, buffers, marks):
+        self.place, self.summed, self.landed = place, summed, buffers[0]
+        self.half = summed.shape[1] // 2
+        self.recv = [marks.take(), marks.take()]
+        self.sends = [
+            remote(
+                summed.at[3, pl.ds(index * self.half, self.half)],
+                self.landed.at[index],
+                marks.take(),
+                self.recv[index],
+                to,
+            )
+            for index, to in enumerate((place.x, place.y))
+        ]
+
+    def start(self):
+        for copy in self.sends:
+            copy.start()
+
+    def add(self):
+        summed, landed = self.summed, self.landed
+        for index, block, base, to in (
+            (0, 2, 0, self.place.x),
+            (1, 1, self.half, self.place.y),
+        ):
+            arrived(landed.at[index], self.recv[index], to)
+
+            def work(rows):
+                own_rows = pl.ds(pl.multiple_of(rows.start + base, 16), rows.size)
+                summed[block, own_rows] = low(
+                    f32(summed[block, own_rows]) + f32(landed[index, rows])
+                )
+
+            each_rows(self.half, 16, work)
+
+    def drain(self):
+        for copy in self.sends:
+            copy.wait_send()
+
+
+class NearScatter:
+    @staticmethod
+    def scratch(rows, width):
+        return [pltpu.VMEM((3, rows, width), LOW)]
+
+    def __init__(self, place, summed, buffers, marks):
+        self.place, self.landed = place, buffers[0]
+        self.load = pltpu.make_async_copy(summed.at[0], self.landed.at[2], marks.take())
+        self.recv = [marks.take(), marks.take()]
+        self.sends = [
+            remote(summed.at[1 + index], self.landed.at[index], marks.take(), self.recv[index], to)
+            for index, to in enumerate((place.x, place.y))
+        ]
+
+    def start(self):
+        self.load.start()
+        for copy in self.sends:
+            copy.start()
+
+    def finish(self, work):
+        landed = self.landed
+        self.load.wait()
+        for index, to in enumerate((self.place.x, self.place.y)):
+            arrived(self.landed.at[index], self.recv[index], to)
+
+        def total(rows):
+            work(
+                rows,
+                f32(landed[0, rows]) + f32(landed[1, rows]) + f32(landed[2, rows]),
+            )
+
+        each_rows(landed.shape[1], 16, total)
+
+    def drain(self):
+        for copy in self.sends:
+            copy.wait_send()
 
 
 class PlaneScatter:
@@ -912,112 +1040,160 @@
             copy.wait_send()
 
 
+def blocks_of(source, block_ref, marks, first, last, work):
+    def fetch(block):
+        return pltpu.make_async_copy(
+            source(block), block_ref.at[block % 2], marks.at[block % 2]
+        )
+
+    fetch(first).start()
+
+    def body(block, carry):
+        fetch(block).wait()
+
+        @pl.when(block < last - 1)
+        def _():
+            fetch(block + 1).start()
+
+        work(block, block_ref[block % 2])
+        return carry
+
+    lax.fori_loop(first, last, body, 0)
+
+
+def unit_values(raws, inner_grad):
+    units = inner_grad.shape[1]
+    gate_raw, up_raw = raws[:, :units], raws[:, units:]
+    sigmoid_gate = jax.nn.sigmoid(gate_raw)
+    activated = gate_raw * sigmoid_gate
+    gate_grad = inner_grad * up_raw * sigmoid_gate * (1.0 + gate_raw * (1.0 - sigmoid_gate))
+    return low(activated * up_raw), jnp.concatenate(
+        [low(gate_grad), low(inner_grad * activated)], axis=1
+    )
+
+
 def units_kernel(
     rows_ref,
     upstream_ref,
     line_ref,
-    gate_ref,
+    first_ref,
     down_ref,
     above_ref,
     below_ref,
     rows_all,
-    upstream_all,
     inner_out,
-    gate_grad_out,
-    up_grad_out,
+    second_grad,
+    first_sum,
+    down_part,
     part_sums,
     grad_sums,
     marks_ref,
-    gate_mat,
-    up_mat,
+    first_mat,
+    second_mat,
     down_mat,
+    upstream,
     row_block,
-    gate_raws,
+    row_slab,
+    inner_first,
+    first_grad,
     inner_grads,
-    part_stage,
-    grad_stage,
+    first_part,
+    inner_stage,
+    second_stage,
+    *buffers,
 ):
     place = Place()
     marks = Marks(marks_ref)
     greet(place, [place.x, place.y, place.pair], True)
     tokens = TokensGather(place, rows_ref, rows_all, marks)
-    upstream = TokensGather(place, upstream_ref, upstream_all, marks)
-    line = LineGather(place, line_ref, lambda z: up_mat.at[z], marks.take(4), marks.take(4))
-    down_line = LineGather(
-        place, down_ref, lambda z: down_mat.at[z], marks.take(4), marks.take(4)
-    )
+    line = LineGather(place, line_ref, lambda z: second_mat.at[z], marks.take(4), marks.take(4))
+    far_recv = marks.take(2)
+    two = down_mat.at[:, place.at(2)]
+    to_two = remote(down_ref, down_mat.at[:, place.z], marks.take(), far_recv.at[0], place.two)
+    pass_mark = marks.take()
+    pass_down = remote(two, two, pass_mark, far_recv.at[1], place.down)
+    pass_up = remote(two, two, pass_mark, far_recv.at[1], place.up)
     copies = [
-        pltpu.make_async_copy(line_ref, up_mat.at[place.z], marks.take()),
-        pltpu.make_async_copy(gate_ref, gate_mat, marks.take()),
-        pltpu.make_async_copy(down_ref, down_mat.at[place.z], marks.take()),
+        pltpu.make_async_copy(line_ref, second_mat.at[place.z], marks.take()),
+        pltpu.make_async_copy(first_ref, first_mat, marks.take()),
+        pltpu.make_async_copy(down_ref, down_mat.at[:, place.z], marks.take()),
+        pltpu.make_async_copy(upstream_ref, upstream, marks.take()),
     ]
-    above = pltpu.make_async_copy(above_ref, down_mat.at[place.at(1)], marks.take())
-    below = pltpu.make_async_copy(below_ref, down_mat.at[place.at(3)], marks.take())
-    fetch_marks = marks.take(2)
+    above = pltpu.make_async_copy(above_ref, down_mat.at[:, place.at(1)], marks.take())
+    below = pltpu.make_async_copy(below_ref, down_mat.at[:, place.at(3)], marks.take())
+    line_rows = first_sum.shape[0]
+    first_line = LineScatter(
+        place,
+        lambda z: first_part.at[pl.ds(pl.multiple_of(z * line_rows, 16), line_rows)],
+        first_sum,
+        buffers[:1],
+        marks,
+        True,
+    )
+    part_far = FarScatter(place, part_sums, buffers[1:2], marks)
+    grad_far = FarScatter(place, grad_sums, buffers[2:], marks)
+    fetch_marks, slab_marks = marks.take(2), marks.take(2)
     send_marks, recv_marks = marks.take(8), marks.take(8)
-    units = gate_mat.shape[1]
     width = rows_ref.shape[1]
-
-    down_line.to_two.start()
+    half = inner_first.shape[2]
+    all_rows = 8 * rows_ref.shape[0]
+
+    to_two.start()
     tokens.start()
     for copy in copies:
         copy.start()
     pl.when(place.z < 3)(above.start)
     pl.when(place.z > 0)(below.start)
     tokens.forward()
-    upstream.start()
-    down_line.wait(2)
+    arrived(two, far_recv.at[0], place.two)
+    pl.when(place.z == 1)(pass_down.start)
+    pl.when(place.z == 2)(pass_up.start)
     line.start()
     tokens.last()
     for copy in copies:
         copy.wait()
     pl.when(place.z < 3)(above.wait)
     pl.when(place.z > 0)(below.wait)
-    tokens.finish()
-
-    def blocks_of(source, first, last, work):
-        def fetch(block):
-            return pltpu.make_async_copy(
-                source.at[block], row_block.at[block % 2], fetch_marks.at[block % 2]
-            )
-
-        fetch(first).start()
-
-        def body(block, carry):
-            fetch(block).wait()
-
-            @pl.when(block < last - 1)
-            def _():
-                fetch(block + 1).start()
-
-            work(block, row_block[block % 2])
-            return carry
-
-        lax.fori_loop(first, last, body, 0)
-
-    def gate_work(block, values):
-        gate_raws[block] = matmul(values, gate_mat[...])
-
-    def inner_work(block, values):
-        inner_grads[block] = matmul_nt(values, down_mat[...].reshape(units, width))
-
-    upstream.forward()
-    blocks_of(rows_all, 0, 8, gate_work)
-    upstream.last()
-    line.wait(2)
 
     @pl.when(place.z == 0)
     def _():
-        arrived(down_mat.at[3], down_line.recv.at[3], place.two)
+        arrived(down_mat.at[:, 3], far_recv.at[1], place.two)
 
     @pl.when(place.z == 3)
     def _():
-        arrived(down_mat.at[0], down_line.recv.at[1], place.two)
-
-    upstream.finish()
-    blocks_of(upstream_all, 0, 8, inner_work)
+        arrived(down_mat.at[:, 0], far_recv.at[1], place.two)
+
+    tokens.finish()
+
+    def first_work(block, values):
+        grads = matmul_nt(upstream[block], down_mat[...].reshape(2 * half, width))
+        inner_grads[block] = low(grads[:, half:])
+        inner, grad = unit_values(matmul(values, first_mat[...]), grads[:, :half])
+        inner_first[block] = inner
+        first_grad[block] = grad
+
+    blocks_of(lambda block: rows_all.at[block], row_block, fetch_marks, 0, 8, first_work)
+    line.wait(2)
+    tile = row_slab.shape[3]
+    tiles = width // tile
+
+    def slab(index):
+        return rows_all.at[:, :, pl.ds(pl.multiple_of(index * tile, tile), tile)]
+
+    def slab_work(index, values):
+        first_part[pl.ds(pl.multiple_of(index * tile, tile), tile)] = low(
+            matmul_tn(values.reshape(all_rows, tile), first_grad[...].reshape(all_rows, 2 * half))
+        )
+
+    down_part[...] = low(
+        matmul_tn(
+            inner_first[...].reshape(all_rows, half), upstream[...].reshape(all_rows, width)
+        )
+    )
+    blocks_of(slab, row_slab, slab_marks, 0, tiles, slab_work)
     line.wait(1)
     line.wait(3)
+    first_line.start()
 
     def fetch(index):
         step, slot = 3 - index // 2, index % 2
@@ -1028,18 +1204,30 @@
     def sends(step):
         return (
             remote(
-                part_stage.at[step],
+                upstream.at[step],
                 part_sums.at[step],
                 send_marks.at[step],
                 recv_marks.at[step],
                 place.pair,
             ),
             remote(
-                grad_stage.at[step],
+                upstream.at[4 + step],
                 grad_sums.at[step],
                 send_marks.at[4 + step],
                 recv_marks.at[4 + step],
                 place.pair,
+            ),
+        )
+
+    store_marks = marks.take(4)
+
+    def stores(slot, block):
+        return (
+            pltpu.make_async_copy(
+                inner_stage.at[slot], inner_out.at[block], store_marks.at[slot]
+            ),
+            pltpu.make_async_copy(
+                second_stage.at[slot], second_grad.at[block], store_marks.at[2 + slot]
             ),
         )
 
@@ -1056,25 +1244,26 @@
             def _():
                 fetch(index + 1).start()
 
-            up_raw = matmul(row_block[slot], up_mat[...].reshape(-1, units))
-            gate_raw, inner_grad = gate_raws[block], inner_grads[block]
-            sigmoid_gate = jax.nn.sigmoid(gate_raw)
-            activated = gate_raw * sigmoid_gate
-            inner = low(activated * up_raw)
-            gate_grad = low(
-                inner_grad * up_raw * sigmoid_gate * (1.0 + gate_raw * (1.0 - sigmoid_gate))
+            second = second_mat[...].reshape(width, 2 * half)
+            inner, grad = unit_values(matmul(row_block[slot], second), f32(inner_grads[block]))
+
+            @pl.when(turn > 0)
+            def _():
+                for copy in stores(slot, block + 1):
+                    copy.wait()
+
+            inner_stage[slot] = inner
+            second_stage[slot] = grad
+            for copy in stores(slot, block):
+                copy.start()
+            part = matmul(
+                jnp.concatenate([inner_first[block], inner], axis=1),
+                down_mat[...].reshape(2 * half, width),
             )
-            up_grad = low(inner_grad * activated)
-            inner_out[block] = inner
-            gate_grad_out[block] = gate_grad
-            up_grad_out[block] = up_grad
-            part = matmul(inner, down_mat[...].reshape(units, width))
-            grad = matmul_nt(gate_grad, gate_mat[...]) + matmul_nt(
-                up_grad, up_mat[...].reshape(-1, units)
-            )
+            grad = matmul_nt(first_grad[block], first_mat[...]) + matmul_nt(grad, second)
             if slot == 0:
-                part_stage[step] = low(part)
-                grad_stage[step] = low(grad)
+                upstream[step] = low(part)
+                upstream[4 + step] = low(grad)
                 for copy in sends(step):
                     copy.start()
             else:
@@ -1084,184 +1273,241 @@
                 grad_sums[step] = low(grad + f32(grad_sums[step]))
         return carry
 
-    lax.fori_loop(0, 4, blocks, 0)
+    lax.fori_loop(0, 1, blocks, 0)
+    grad_far.start()
+    part_far.start()
+    lax.fori_loop(1, 2, blocks, 0)
+    first_line.middle()
+    lax.fori_loop(2, 4, blocks, 0)
+    for slot in range(2):
+        for copy in stores(slot, 4 * (1 - slot)):
+            copy.wait()
+    grad_far.add()
+    part_far.add()
+    first_line.finish()
+    first_line.drain()
+    grad_far.drain()
+    part_far.drain()
     for step in range(4):
         for copy in sends(step):
             copy.wait_send()
     line.finish()
-    down_line.to_two.wait_send()
-    pl.when(place.z == 1)(down_line.pass_down.wait_send)
-    pl.when(place.z == 2)(down_line.pass_up.wait_send)
-
-
-def units_products(rows, upstream, up_rows, gate_all, down_weight, above, below):
+    to_two.wait_send()
+    pl.when(place.z == 1)(pass_down.wait_send)
+    pl.when(place.z == 2)(pass_up.wait_send)
+
+
+def units_products(rows, upstream, second_rows, first_all, down_weight, above, below):
     block_rows, width = rows.shape
-    units = gate_all.shape[1]
-    block = lambda count: pltpu.VMEM((count, block_rows, width), LOW)
-    hidden = jax.ShapeDtypeStruct((8, block_rows, units), LOW)
+    half = first_all.shape[1] // 2
+    half_rows = down_weight.shape[1]
+    hidden = lambda count: jax.ShapeDtypeStruct((8, block_rows, count * half), LOW)
     sums = jax.ShapeDtypeStruct((4, block_rows, width), LOW)
     blocks = jax.ShapeDtypeStruct((8, block_rows, width), LOW)
     return pl.pallas_call(
         units_kernel,
-        out_shape=(blocks, blocks, hidden, hidden, hidden, sums, sums),
+        out_shape=(
+            blocks,
+            hidden(1),
+            hidden(2),
+            jax.ShapeDtypeStruct(second_rows.shape, LOW),
+            jax.ShapeDtypeStruct((half, width), LOW),
+            sums,
+            sums,
+        ),
         in_specs=[ANYWHERE] * 7,
-        out_specs=(ANYWHERE,) * 2 + (WHOLE,) * 5,
+        out_specs=(ANYWHERE,) * 3 + (WHOLE,) * 4,
         scratch_shapes=[
             pltpu.SemaphoreType.DMA((100,)),
-            pltpu.VMEM(gate_all.shape, LOW),
-            pltpu.VMEM((4,) + up_rows.shape, LOW),
-            pltpu.VMEM((4,) + down_weight.shape, LOW),
-            block(2),
-            pltpu.VMEM((8, block_rows, units), jnp.float32),
-            pltpu.VMEM((8, block_rows, units), jnp.float32),
-            block(4),
-            block(4),
-        ],
+            pltpu.VMEM(first_all.shape, LOW),
+            pltpu.VMEM((4,) + second_rows.shape, LOW),
+            pltpu.VMEM((2, 4, half_rows, width), LOW),
+            pltpu.VMEM((8, block_rows, width), LOW),
+            pltpu.VMEM((2, block_rows, width), LOW),
+            pltpu.VMEM((2, 8, block_rows, 256), LOW),
+            pltpu.VMEM((8, block_rows, half), LOW),
+            pltpu.VMEM((8, block_rows, 2 * half), LOW),
+            pltpu.VMEM((8, block_rows, half), LOW),
+            pltpu.VMEM((width, 2 * half), LOW),
+            pltpu.VMEM((2, block_rows, half), LOW),
+            pltpu.VMEM((2, block_rows, 2 * half), LOW),
+        ]
+        + LineScatter.scratch(*second_rows.shape, True)
+        + FarScatter.scratch(block_rows, width) * 2,
         compiler_params=comm_params(1),
-        cost_estimate=comm_cost(130),
-    )(rows, upstream, up_rows, gate_all, down_weight, above, below)
+        cost_estimate=comm_cost(150),
+    )(rows, upstream, second_rows, first_all, down_weight, above, below)
 
 
 def unit_grads_kernel(
     rows_all,
     upstream_ref,
     inner_ref,
-    gate_grad_ref,
-    up_grad_ref,
+    second_ref,
+    down_first,
     part_sums,
     grad_sums,
-    row_grad,
-    row_part,
+    hidden_ref,
+    upstream_own,
+    norm_ref,
+    layer_out,
+    hidden_grad,
+    branch,
+    mlp_gain,
     down_out,
-    gate_part,
-    up_part,
+    second_part,
     marks_ref,
     upstream,
     inner,
-    gate_grad,
-    up_grad,
+    second_grad,
     row_slab,
+    gain_rows,
     down_part,
     *buffers,
 ):
     place = Place()
     marks = Marks(marks_ref)
     greet(place, [place.x, place.y], True)
-    grad_plane = PlaneScatter(place, grad_sums, row_grad, buffers[:1], marks)
-    part_plane = PlaneScatter(place, part_sums, row_part, buffers[1:2], marks)
-    down_rows = down_out.shape[0]
-    down_line = LineScatter(
+    grad_near = NearScatter(place, grad_sums, buffers[:1], marks)
+    part_near = NearScatter(place, part_sums, buffers[1:2], marks)
+    half_rows = down_out.shape[1]
+    first_line = LineScatter(
+        place, lambda z: down_first.at[z], down_out.at[0], buffers[2:3], marks
+    )
+    second_line = LineScatter(
         place,
-        lambda z: down_part.at[pl.ds(pl.multiple_of(z * down_rows, 16), down_rows)],
-        down_out,
-        buffers[2:],
+        lambda z: down_part.at[pl.ds(pl.multiple_of(z * half_rows, 16), half_rows)],
+        down_out.at[1],
+        buffers[3:],
         marks,
+        True,
     )
     loads = [
         pltpu.make_async_copy(upstream_ref, upstream, marks.take()),
         pltpu.make_async_copy(inner_ref, inner, marks.take()),
-        pltpu.make_async_copy(gate_grad_ref, gate_grad, marks.take()),
-        pltpu.make_async_copy(up_grad_ref, up_grad, marks.take()),
+        pltpu.make_async_copy(second_ref, second_grad, marks.take()),
     ]
     slab_marks = marks.take(2)
+    rows, width = hidden_ref.shape
+    half = inner.shape[2]
+    all_rows = 8 * rows
     tile = row_slab.shape[3]
-    tiles = rows_all.shape[2] // tile
-    units = inner.shape[2]
-    all_rows = inner.shape[0] * inner.shape[1]
+    tiles = width // tile
 
     def slab(index):
-        return pltpu.make_async_copy(
-            rows_all.at[:, :, pl.ds(pl.multiple_of(index * tile, tile), tile)],
-            row_slab.at[index % 2],
-            slab_marks.at[index % 2],
-        )
-
-    grad_plane.start()
+        return rows_all.at[:, :, pl.ds(pl.multiple_of(index * tile, tile), tile)]
+
+    def slab_work(index, values):
+        second_part[pl.ds(pl.multiple_of(index * tile, tile), tile)] = low(
+            matmul_tn(values.reshape(all_rows, tile), second_grad[...].reshape(all_rows, 2 * half))
+        )
+
+    first_line.start()
+    grad_near.start()
     for copy in loads:
         copy.start()
-    slab(0).start()
     loads[0].wait()
     loads[1].wait()
-
-    def down_tile(index, carry):
-        columns = pl.ds(pl.multiple_of(index * tile, tile), tile)
-        down_part[columns] = low(
-            matmul_tn(
-                inner[:, :, columns].reshape(all_rows, tile),
-                upstream[...].reshape(all_rows, upstream.shape[2]),
-            )
-        )
-        return carry
-
-    lax.fori_loop(0, units // tile, down_tile, 0)
-    down_line.start()
+    down_part[...] = low(
+        matmul_tn(inner[...].reshape(all_rows, half), upstream[...].reshape(all_rows, width))
+    )
     loads[2].wait()
-    loads[3].wait()
-
-    def row_tile(index, carry):
-        slab(index).wait()
-
-        @pl.when(index < tiles - 1)
-        def _():
-            slab(index + 1).start()
-
-        columns = row_slab[index % 2].reshape(all_rows, tile)
-        out_rows = pl.ds(pl.multiple_of(index * tile, tile), tile)
-        gate_part[out_rows] = low(matmul_tn(columns, gate_grad[...].reshape(all_rows, units)))
-        up_part[out_rows] = low(matmul_tn(columns, up_grad[...].reshape(all_rows, units)))
-        return carry
-
-    lax.fori_loop(0, tiles // 4, row_tile, 0)
-    grad_plane.middle()
-    down_line.middle()
-    lax.fori_loop(tiles // 4, tiles, row_tile, 0)
-    grad_plane.finish()
-    part_plane.start()
-    part_plane.middle()
-    down_line.finish()
-    part_plane.finish()
-    down_line.drain()
-    grad_plane.drain()
-    part_plane.drain()
-
-
-def unit_grads(rows_all, upstream, inner, gate_grad, up_grad, part_sums, grad_sums):
-    _, block_rows, width = rows_all.shape
-    units = inner.shape[2]
-    down_rows = units // 4
-    tile = 256
+    blocks_of(slab, row_slab, slab_marks, 0, tiles // 2, slab_work)
+    first_line.middle()
+    second_line.start()
+    blocks_of(slab, row_slab, slab_marks, tiles // 2, tiles, slab_work)
+    second_line.middle()
+    part_near.start()
+    gain_rows[...] = jnp.zeros_like(gain_rows)
+    norm_row = norm_ref[...]
+
+    def norm_work(rows, row_grad):
+        values = hidden_ref[rows]
+        scales = inv_rms(values)
+        weighted = row_grad * norm_row
+        inner_mean = jnp.mean(weighted * values, axis=-1, keepdims=True)
+        grad = (
+            f32(upstream_own[rows])
+            + scales * weighted
+            - values * (scales * scales * scales) * inner_mean
+        )
+        hidden_grad[rows] = grad
+        branch[rows] = low(grad)
+        parts = row_grad * values * scales
+        gain_rows[...] += parts[:8] + parts[8:]
+
+    def out_work(rows, row_part):
+        layer_out[rows] = low(hidden_ref[rows] + row_part)
+
+    grad_near.finish(norm_work)
+    mlp_gain[...] = jnp.sum(gain_rows[...], axis=0, keepdims=True)
+    part_near.finish(out_work)
+    first_line.finish()
+    second_line.finish()
+    for part in (first_line, second_line, grad_near, part_near):
+        part.drain()
+
+
+def unit_grads(
+    rows_all,
+    upstream,
+    inner,
+    second_grad,
+    down_first,
+    part_sums,
+    grad_sums,
+    hidden,
+    upstream_own,
+    norm,
+):
+    _, rows, width = rows_all.shape
+    half = inner.shape[2]
+    half_rows = down_first.shape[1]
     return pl.pallas_call(
         unit_grads_kernel,
         out_shape=(
-            jax.ShapeDtypeStruct((block_rows, width), jnp.float32),
-            jax.ShapeDtypeStruct((block_rows, width), jnp.float32),
-            jax.ShapeDtypeStruct((down_rows, width), LOW),
-            jax.ShapeDtypeStruct((width, units), LOW),
-            jax.ShapeDtypeStruct((width, units), LOW),
+            jax.ShapeDtypeStruct((rows, width), LOW),
+            jax.ShapeDtypeStruct((rows, width), jnp.float32),
+            jax.ShapeDtypeStruct((rows, width), LOW),
+            jax.ShapeDtypeStruct((1, width), jnp.float32),
+            jax.ShapeDtypeStruct((2, half_rows, width), LOW),
+            jax.ShapeDtypeStruct((width, 2 * half), LOW),
         ),
-        in_specs=[ANYWHERE] * 5 + [WHOLE] * 2,
-        out_specs=(WHOLE,) * 5,
+        in_specs=[ANYWHERE] * 7 + [WHOLE] * 3,
+        out_specs=(WHOLE,) * 6,
         scratch_shapes=[
             pltpu.SemaphoreType.DMA((64,)),
             pltpu.VMEM(upstream.shape, LOW),
             pltpu.VMEM(inner.shape, LOW),
-            pltpu.VMEM(inner.shape, LOW),
-            pltpu.VMEM(inner.shape, LOW),
-            pltpu.VMEM((2, 8, block_rows, tile), LOW),
-            pltpu.VMEM((units, width), LOW),
+            pltpu.VMEM(second_grad.shape, LOW),
+            pltpu.VMEM((2, 8, rows, 256), LOW),
+            pltpu.VMEM((8, width), jnp.float32),
+            pltpu.VMEM((half, width), LOW),
         ]
-        + PlaneScatter.scratch(block_rows, width) * 2
-        + LineScatter.scratch(down_rows, width),
-        input_output_aliases={},
+        + NearScatter.scratch(rows, width) * 2
+        + LineScatter.scratch(half_rows, width)
+        + LineScatter.scratch(half_rows, width, True),
         compiler_params=comm_params(4),
-        cost_estimate=comm_cost(70),
-    )(rows_all, upstream, inner, gate_grad, up_grad, part_sums, grad_sums)
+        cost_estimate=comm_cost(65),
+    )(
+        rows_all,
+        upstream,
+        inner,
+        second_grad,
+        down_first,
+        part_sums,
+        grad_sums,
+        hidden,
+        upstream_own,
+        norm,
+    )
 
 
 def last_kernel(
     parts_ref,
     qkv_ref,
     proj_ref,
+    second_ref,
     input_ref,
     hidden_ref,
     norm_ref,
@@ -1269,6 +1515,7 @@
     grad_ref,
     qkv_columns,
     proj_out,
+    second_columns,
     gains_out,
     marks_ref,
     qkv_sum,
@@ -1291,6 +1538,9 @@
         lambda p, step: qkv_columns.at[p],
         marks,
     )
+    second_pieces = Exchange(
+        place, lambda p, step: second_ref.at[p], lambda p, step: second_columns.at[p], marks
+    )
     near_z = {"f": place.z + 1 - 2 * (place.z % 2)}
     rounds = [
         remote(gain_mine.at[index], gain_got.at[index], marks.take(), marks.take(), to)
@@ -1300,10 +1550,11 @@
     tokens.start()
     qkv_line.start()
     qkv_line.middle()
+    tokens.middle()
+    second_pieces.start()
     proj_line.start()
-    tokens.middle()
+    tokens.finish()
     proj_line.middle()
-    tokens.finish()
 
     qkv_line.finish()
     qkv_pieces.start()
@@ -1342,9 +1593,11 @@
     tokens.drain()
     qkv_pieces.wait()
     qkv_pieces.finish()
-
-
-def last_sums(parts, qkv_parts, proj_parts, layer_input, hidden_grad, norm, gains):
+    second_pieces.wait()
+    second_pieces.finish()
+
+
+def last_sums(parts, qkv_parts, proj_parts, second_rows, layer_input, hidden_grad, norm, gains):
     rows, width = parts.shape[1:]
     qkv_rows, qkv_width = qkv_parts.shape[1:]
     gain_width = width + gains.shape[1]
@@ -1354,10 +1607,11 @@
             jax.ShapeDtypeStruct((rows, width), jnp.float32),
             jax.ShapeDtypeStruct((4, qkv_rows // 4, qkv_width), LOW),
             jax.ShapeDtypeStruct(proj_parts.shape[1:], LOW),
+            jax.ShapeDtypeStruct(second_rows.shape, LOW),
             jax.ShapeDtypeStruct((1, gain_width), jnp.float32),
         ),
-        in_specs=[WHOLE] + [ANYWHERE] * 2 + [WHOLE] * 4,
-        out_specs=(WHOLE, ANYWHERE, WHOLE, WHOLE),
+        in_specs=[WHOLE] + [ANYWHERE] * 3 + [WHOLE] * 4,
+        out_specs=(WHOLE, ANYWHERE, WHOLE, ANYWHERE, WHOLE),
         scratch_shapes=[
             pltpu.SemaphoreType.DMA((100,)),
             pltpu.VMEM((qkv_rows, qkv_width), LOW),
@@ -1371,7 +1625,7 @@
         + LineScatter.scratch(*proj_parts.shape[1:]),
         compiler_params=comm_params(5),
         cost_estimate=comm_cost(60),
-    )(parts, qkv_parts, proj_parts, layer_input, hidden_grad, norm, gains)
+    )(parts, qkv_parts, proj_parts, second_rows, layer_input, hidden_grad, norm, gains)
 
 
 def turn_pairs(values, cosine, sine):
@@ -1426,10 +1680,7 @@
 
 
 def heads_back_kernel(
-    hidden_ref,
-    row_grad_ref,
-    upstream_ref,
-    norm_ref,
+    branch_ref,
     out_ref,
     attended_ref,
     raw_ref,
@@ -1443,16 +1694,14 @@
     gains_ref,
     rows_all,
     qkv_ref,
-    gate_part,
-    up_part,
-    hidden_grad,
-    mlp_gain,
+    second_part,
+    first_rows,
     head_gain,
     qkv_part,
     proj_sum,
     grad_sums,
-    gate_columns,
-    up_columns,
+    line_sum,
+    first_columns,
     marks_ref,
     out_mat,
     qkv_mat,
@@ -1465,44 +1714,30 @@
     qkv_grad,
     row_slab,
     proj_part,
-    gain_rows,
-    line_sum,
     *buffers,
 ):
     place = Place()
     marks = Marks(marks_ref)
     greet(place, [place.x, place.y, place.d, place.pair], True)
-    rows, width = hidden_ref.shape
+    rows, width = branch_ref.shape
     half_heads = heads_grad.shape[2]
     group_rows = 2 * rows
-    gate_line = LineScatter(
-        place, lambda z: gate_part.at[z], line_sum.at[0], buffers[0:1], marks
-    )
-    up_line = LineScatter(place, lambda z: up_part.at[z], line_sum.at[1], buffers[1:2], marks)
-    quarter = line_sum.shape[1] // 4
-    columns = [
-        Exchange(
-            place,
-            lambda p, step, index=index: line_sum.at[
-                index, pl.ds(pl.multiple_of(p * quarter, quarter), quarter)
-            ],
-            lambda p, step, out=out: out.at[p],
-            marks,
-        )
-        for index, out in enumerate((gate_columns, up_columns))
-    ]
+    second_line = LineScatter(place, lambda z: second_part.at[z], line_sum, buffers[0:1], marks)
+    first_pieces = Exchange(
+        place, lambda p, step: first_rows.at[p], lambda p, step: first_columns.at[p], marks
+    )
     proj_plane = PlaneScatter(
         place,
         proj_part,
         proj_sum,
-        buffers[2:3],
+        buffers[1:],
         marks,
         (place.p, place.px, place.py, place.pd),
     )
     heads = Exchange(
         place, lambda p, step: own_grad.at[p], lambda p, step: heads_grad.at[step], marks
     )
-    to_pair = remote(branch.at[0], branch.at[1], marks.take(), marks.take(), place.pair)
+    to_pair = remote(branch_ref, branch.at[1], marks.take(), marks.take(), place.pair)
     loads = [
         pltpu.make_async_copy(out_ref, out_mat, marks.take()),
         pltpu.make_async_copy(attended_ref, attended, marks.take()),
@@ -1511,32 +1746,11 @@
     fetch_marks, slab_marks = marks.take(4), marks.take(2)
     send_marks, recv_marks = marks.take(4), marks.take(4)
 
-    gate_line.start()
+    to_pair.start()
+    second_line.start()
     for copy in loads:
         copy.start()
-
-    gain_rows[...] = jnp.zeros_like(gain_rows)
-    norm_row = norm_ref[...]
-
-    def norm_work(part):
-        values = hidden_ref[part]
-        scales = inv_rms(values)
-        upstream = row_grad_ref[part]
-        weighted = upstream * norm_row
-        inner_mean = jnp.mean(weighted * values, axis=-1, keepdims=True)
-        grad = (
-            f32(upstream_ref[part])
-            + scales * weighted
-            - values * (scales * scales * scales) * inner_mean
-        )
-        hidden_grad[part] = grad
-        branch[0, part] = low(grad)
-        parts = upstream * values * scales
-        gain_rows[...] += parts[:8] + parts[8:]
-
-    each_rows(rows, 16, norm_work)
-    to_pair.start()
-    mlp_gain[...] = jnp.sum(gain_rows[...], axis=0, keepdims=True)
+    branch[0] = branch_ref[...]
     for copy in loads:
         copy.wait()
 
@@ -1551,8 +1765,7 @@
     to_pair.wait()
     own_half(1)
     heads.start()
-    gate_line.middle()
-    up_line.start()
+    second_line.middle()
 
     def proj_work(z, carry):
         block = attended[z].reshape(group_rows, half_heads)
@@ -1573,6 +1786,7 @@
     lax.fori_loop(0, 4, proj_work, 0)
     heads.wait()
     proj_plane.start()
+    first_pieces.start()
     head_gain[...] = jnp.zeros_like(head_gain)
 
     def sends(step):
@@ -1610,7 +1824,6 @@
 
     lax.fori_loop(0, 2, bucket, 0)
     proj_plane.middle()
-    up_line.middle()
     lax.fori_loop(2, 4, bucket, 0)
 
     tile = row_slab.shape[3]
@@ -1633,8 +1846,6 @@
         return carry
 
     lax.fori_loop(0, 4, own_work, 0)
-    gate_line.finish()
-    columns[0].start()
 
     def row_tile(index, carry):
         slab(index).wait()
@@ -1651,48 +1862,48 @@
         return carry
 
     lax.fori_loop(0, tiles, row_tile, 0)
+    second_line.finish()
     proj_plane.finish()
-    up_line.finish()
-    columns[1].start()
     for step in range(4):
         sends(step).wait_send()
     heads.finish()
-    proj_plane.drain()
-    gate_line.drain()
-    up_line.drain()
-    for part in columns:
-        part.wait()
-        part.finish()
+    for part in (proj_plane, second_line):
+        part.drain()
+    first_pieces.wait()
+    first_pieces.finish()
 
 
 def heads_backward(
-    hidden, row_grad, upstream, norm, out_all, attended, raw, kept, tables, rows_all, qkv_all, gate_part, up_part
+    branch,
+    out_all,
+    attended,
+    raw,
+    kept,
+    tables,
+    rows_all,
+    qkv_all,
+    second_part,
+    first_rows,
 ):
-    rows, width = hidden.shape
+    rows, width = branch.shape
     head_part = raw.shape[3]
     query_part = head_part - 2 * HEAD_SIZE
-    line_rows, units = gate_part.shape[1:]
+    line_rows, units = second_part.shape[1:]
     tile = 256
-    pieces = jax.ShapeDtypeStruct((4, line_rows // 4, units), LOW)
     return pl.pallas_call(
         heads_back_kernel,
         out_shape=(
-            jax.ShapeDtypeStruct((rows, width), jnp.float32),
-            jax.ShapeDtypeStruct((1, width), jnp.float32),
             jax.ShapeDtypeStruct((1, 2 * HEAD_SIZE), jnp.float32),
             jax.ShapeDtypeStruct((width, head_part), LOW),
             jax.ShapeDtypeStruct((query_part, width), LOW),
             jax.ShapeDtypeStruct((4, rows, width), LOW),
-            pieces,
-            pieces,
+            jax.ShapeDtypeStruct((line_rows, units), LOW),
+            jax.ShapeDtypeStruct((4, line_rows // 4, units), LOW),
         ),
-        in_specs=[WHOLE] * 4
-        + [ANYWHERE] * 4
-        + [WHOLE] * len(tables)
-        + [ANYWHERE] * 4,
-        out_specs=(WHOLE,) * 6 + (ANYWHERE,) * 2,
+        in_specs=[WHOLE] + [ANYWHERE] * 4 + [WHOLE] * len(tables) + [ANYWHERE] * 4,
+        out_specs=(WHOLE,) * 5 + (ANYWHERE,),
         scratch_shapes=[
-            pltpu.SemaphoreType.DMA((100,)),
+            pltpu.SemaphoreType.DMA((120,)),
             pltpu.VMEM(out_all.shape, LOW),
             pltpu.VMEM(qkv_all.shape, LOW),
             pltpu.VMEM(attended.shape, LOW),
@@ -1704,18 +1915,13 @@
             pltpu.VMEM((2, 4, rows, head_part), LOW),
             pltpu.VMEM((2, 8, rows, tile), LOW),
             pltpu.VMEM((4, query_part, width), LOW),
-            pltpu.VMEM((8, width), jnp.float32),
-            pltpu.VMEM((2, line_rows, units), LOW),
         ]
-        + LineScatter.scratch(line_rows, units) * 2
+        + LineScatter.scratch(line_rows, units)
         + PlaneScatter.scratch(query_part, width),
         compiler_params=comm_params(3),
-        cost_estimate=comm_cost(115),
+        cost_estimate=comm_cost(90),
     )(
-        hidden,
-        row_grad,
-        upstream,
-        norm,
+        branch,
         out_all,
         attended,
         raw,
@@ -1723,8 +1929,8 @@
         *tables,
         rows_all,
         qkv_all,
-        gate_part,
-        up_part,
+        second_part,
+        first_rows,
     )
 
 
@@ -1776,21 +1982,36 @@
     local_rows, model_width = layer_input.shape
     weight_rows = gate_weight.shape[0]
     down_rows = down_weight.shape[0]
-    hidden_part = 4 * down_rows
+    half_rows = down_rows // 2
+    half = 4 * half_rows
     qkv_pieces = jnp.concatenate(
         [heads_of(query_weight), heads_of(key_matrix), heads_of(value_matrix)], axis=2
     )
     head_part = qkv_pieces.shape[2]
     query_part = head_part - 2 * HEAD_SIZE
     input_float = f32(layer_input)
+
+    def half_pieces(index):
+        return jnp.concatenate(
+            [
+                weight.reshape(weight_rows, 4, 4, 2, half_rows)[:, :, :, index]
+                .transpose(2, 0, 1, 3)
+                .reshape(4, weight_rows, half)
+                for weight in (gate_weight, up_weight)
+            ],
+            axis=2,
+        )
+
+    down_halves = down_weight.reshape(2, half_rows, model_width)
     row_ids = row_ids_of(local_rows)
     (
         normed_attn,
         _,
-        up_rows,
-        gate_all,
+        second_rows,
+        first_all,
         above,
         below,
+        grad_all,
         qkv_all,
         out_all,
         qkv_raw,
@@ -1806,14 +2027,15 @@
         low(input_float * inv_rms(input_float) * attn_norm),
         qkv_pieces,
         output_weight,
-        units_of(gate_weight, down_rows),
-        units_of(up_weight, down_rows),
-        down_weight,
+        half_pieces(0),
+        half_pieces(1),
+        down_halves,
         doc_lengths,
         row_ids,
         head_norms,
         layer_input,
         mlp_norm,
+        grad_out,
     )
     tables = (
         cos_tab,
@@ -1824,33 +2046,46 @@
         row_ids[None, :],
         head_norms,
     )
-    rows_all, grad_all, inner_low, gate_grad, up_grad, part_sums, grad_sums = units_products(
-        normed_mlp,
+    rows_all, inner_low, second_grad, first_rows, grad_down_first, part_sums, grad_sums = (
+        units_products(
+            normed_mlp,
+            grad_all,
+            second_rows.reshape(-1, 2 * half),
+            first_all.reshape(model_width, 2 * half),
+            down_halves,
+            above,
+            below,
+        )
+    )
+    line_shape = (4, 4 * weight_rows, 2 * half)
+    (
+        layer_out,
+        hidden_grad,
+        branch_grad,
+        mlp_gain_part,
+        grad_down,
+        grad_second,
+    ) = unit_grads(
+        rows_all,
+        grad_all,
+        inner_low,
+        second_grad,
+        grad_down_first.reshape(4, half_rows, model_width),
+        part_sums,
+        grad_sums,
+        hidden_state,
         grad_out,
-        up_rows.reshape(-1, hidden_part),
-        gate_all.reshape(model_width, hidden_part),
-        down_weight,
-        above,
-        below,
-    )
-    mlp_row_grad, mlp_rows, grad_down, grad_gate_part, grad_up_part = unit_grads(
-        rows_all, grad_all, inner_low, gate_grad, up_grad, part_sums, grad_sums
-    )
-    line_shape = (4, 4 * weight_rows, hidden_part)
+        mlp_norm[None],
+    )
     (
-        hidden_grad,
-        mlp_gain_part,
         head_gains,
         grad_qkv_part,
         grad_proj_part,
         grad_sums,
-        grad_gate_columns,
-        grad_up_columns,
+        second_rows,
+        first_columns,
     ) = heads_backward(
-        hidden_state,
-        mlp_row_grad,
-        grad_out,
-        mlp_norm[None],
+        branch_grad,
         out_all.reshape(-1, model_width),
         attended,
         qkv_raw,
@@ -1858,21 +2093,31 @@
         tables,
         normed_attn,
         qkv_all.reshape(model_width, head_part),
-        grad_gate_part.reshape(line_shape),
-        grad_up_part.reshape(line_shape),
-    )
-    grad_input, grad_qkv_columns, grad_out_proj, gains = last_sums(
+        grad_second.reshape(line_shape),
+        first_rows.reshape(4, weight_rows, 2 * half),
+    )
+    grad_input, grad_qkv_columns, grad_out_proj, second_columns, gains = last_sums(
         grad_sums,
         grad_qkv_part.reshape(4, 4 * weight_rows, head_part),
         grad_proj_part.reshape((4,) + output_weight.shape),
+        second_rows.reshape(4, weight_rows, 2 * half),
         layer_input,
         hidden_grad,
         attn_norm[None],
         jnp.concatenate([mlp_gain_part, head_gains], axis=1),
     )
     gains = gains.reshape(-1)
+
+    def units_joined(offset):
+        halves = [
+            f32(columns[:, :, offset : offset + half]).reshape(4, weight_rows, 4, 1, half_rows)
+            for columns in (first_columns, second_columns)
+        ]
+        joined = jnp.concatenate(halves, axis=3)
+        return joined.transpose(1, 2, 0, 3, 4).reshape(weight_rows, -1)
+
     return (
-        low(hidden_state + mlp_rows),
+        layer_out,
         grad_input,
         gains[:model_width],
         gains[2 * model_width :].reshape(2, HEAD_SIZE),
@@ -1881,9 +2126,9 @@
         heads_back(grad_qkv_columns[:, :, query_part + HEAD_SIZE :]),
         f32(grad_out_proj),
         gains[model_width : 2 * model_width],
-        units_back(grad_gate_columns, down_rows),
-        units_back(grad_up_columns, down_rows),
-        f32(grad_down),
+        units_joined(0),
+        units_joined(half),
+        f32(grad_down).reshape(down_weight.shape),
     )
 
 

time: 627 us -> 587 us (0.936)
  Pallas kernels: 586 us -> 548 us
    pallas_call x3, Pallas kernels: 361 us -> 319 us  [the longest x1 175 us: units_products(): pl.pallas_call(units_kernel, out_shape=(blocks, hidden(1), hidden(2), jax...]
where the time goes in v5:
time: 587 us; the launch traced here: 581 us
  Pallas kernels  548 us (93%)
  local copies, waits for them, and re-layouts  19.7 us (3%)
  other arithmetic  11.3 us (2%)
    pallas_call x1, Pallas kernels, units_products(): pl.pallas_call(units_kernel, out_shape=(blocks, hidden(1), hidden(2), jax...  175 us
    pallas_call x1, Pallas kernels, first_part(): pl.pallas_call(lambda *refs: first_kernel(documents, *refs), out_shape=(l...  162 us
    pallas_call x1, Pallas kernels, unit_grads(): pl.pallas_call(unit_grads_kernel, out_shape=(jax.ShapeDtypeStruct((rows,...  73.6 us
    pallas_call x1, Pallas kernels, heads_backward(): pl.pallas_call(heads_back_kernel, out_shape=(jax.ShapeDtypeStruct((1, 2 *...  70.5 us
    pallas_call x1, Pallas kernels, last_sums(): pl.pallas_call(last_kernel, out_shape=(jax.ShapeDtypeStruct((rows, width)...  68 us

profile of v5, /device:TPU:0, one launch (start us, length us, event | category | flops | bytes accessed | tf_op | source)
XLA Modules:
  0.0 580.8 jit_solution(256873431659566251)
XLA Ops:
  1.3 1.6 fusion
  2.9 1.3 pad.4.refs_6_
  4.2 1.0 copy.33
  5.3 1.0 copy.35
  6.5 0.9 copy.47.refs_7_.id_col
  7.7 0.8 pad_maximum_fusion.2.refs_1_
  11.0 1.3 pad_maximum_fusion
  12.3 1.3 fusion.2.refs_0_
  13.6 161.5 %shard_map.220 = (bf16[8,256,2048]{2,1,0:T(8,128)(2,1)}, bf16[4,128,768]{2,1,0:T(8,128)(2,1)}, bf16[4,128,768]{2,1,0:T(8,128)(2,1)}, bf16[4,4,128,768]{3,2,1,0:T...) custom-call(bf16[256,2048]{1,0:T(8,128)(2,1)} %fusion.2.refs_0_, ...), custom_call_target="tpu_custom_call" | custom-call | bytes 390000000 | tf_op jit(solution)/shard_map/pallas_call | solution.py:827
  175.1 174.9 %shard_map.221 = (bf16[8,256,2048]{2,1,0:T(8,128)(2,1)}, bf16[8,256,384]{2,1,0:T(8,128)(2,1)}, bf16[8,256,768]{2,1,0:T(8,128)(2,1)}, bf16[512,768]{1,0:T(8,128)(...) custom-call(bf16[256,2048]{1,0:T(8,128)(2,1)} %get-tuple-element.53.rows_ref, ...), custom_call_target="tpu_custom_call" | custom-call | bytes 450000000 | tf_op jit(solution)/shard_map/pallas_call | solution.py:1307
  350.0 73.6 %shard_map.222 = (bf16[256,2048]{1,0:T(8,128)(2,1)}, f32[256,2048]{1,0:T(8,128)}, bf16[256,2048]{1,0:T(8,128)(2,1)}, f32[1,2048]{1,0:T(1,128)}, bf16[2,96,2048]{2,1,0:T(8,128)(2,1)}, /*index=5*/bf16[2048,768]{1,0:T(8,128)(2,1)}) custom-call(bf16[8,256,2048]{2,1,0:T(8,128)(2,1)} %get-tuple-element.59.rows_all, ...), custom_call_target="tpu_custom_call" | custom-call | bytes 195000000 | tf_op jit(solution)/shard_map/pallas_call | solution.py:1466
  423.6 70.5 %shard_map.223 = (f32[1,256]{1,0:T(1,128)}, bf16[2048,512]{1,0:T(8,128)(2,1)}, bf16[256,2048]{1,0:T(8,128)(2,1)}, bf16[4,256,2048]{2,1,0:T(8,128)(2,1)}, bf16[51...) custom-call(bf16[256,2048]{1,0:T(8,128)(2,1)} %get-tuple-element.67.branch_ref, bf16[1024,2048]{1,0:T(8,128)(2,1)} %bitcast.72, ...), custom_call_target="tpu_custom_call" | custom-call | bytes 270000000 | tf_op jit(solution)/shard_map/pallas_call | solution.py:1893
  494.1 1.3 pad_maximum_fusion.3.gains_ref
  495.4 68.0 %shard_map.224 = (f32[256,2048]{1,0:T(8,128)}, bf16[4,128,512]{2,1,0:T(8,128)(2,1)}, bf16[64,2048]{1,0:T(8,128)(2,1)}, bf16[4,128,768]{2,1,0:T(8,128)(2,1)}, f32[1,4352]{1,0:T(1,128)}) custom-call(bf16[4,256,2048]{2,1,0:T(8,128)(2,1)} %get-tuple-element.80.parts_ref, bf16[4,512,512]{2,1,0:T(8,128)(2,1)} %bitcast.80, bf16[4,64,2048]{2,1,0:T(8,128)(2,1)} %bitcast.91, ...), custom_call_target="tpu_custom_call" | custom-call | bytes 180000000 | tf_op jit(solution)/shard_map/pallas_call | solution.py:1604
  563.5 1.3 slice.55
  564.7 1.3 fusion.5
  566.0 1.8 convert_element_type.8
  567.8 1.0 convert_bitcast_fusion.2
  569.0 1.0 copy.58
  573.4 1.6 copy.61
  575.2 1.6 copy.62
  576.9 1.4 bitcast_convert_fusion
  578.2 1.0 copy.65
  579.2 1.3 copy.66
  (63 shorter events, 7.4 us)
Async XLA Ops:
  0.6 6.7 %copy-start.9 = (bf16[128,1024]{1,0:T(8,128)(2,1)S(1)}, bf16[128,1024]{1,0:T(8,128)(2,1)}, u32[]{:S(2)}) copy-start(bf16[128,1024]{1,0:T(8,128)(2,1)} %param.16) | copy-start | bytes 786436
  1.3 7.3 %copy-start.3 = (bf16[128,3072]{1,0:T(8,128)(2,1)S(1)}, bf16[128,3072]{1,0:T(8,128)(2,1)}, u32[]{:S(2)}) copy-start(bf16[128,3072]{1,0:T(8,128)(2,1)} %param.21) | copy-start | bytes 2359300
  2.9 6.0 %copy-start.11 = (s32[512]{0:T(512)}, s32[512]{0:T(512)S(1)}, u32[]{:S(2)}) copy-start(s32[512]{0:T(512)S(1)} %pad_add_fusion) | copy-start | bytes 6148
  8.9 1.1 copy-start.4
  10.8 1.5 copy-start
  10.8 1.5 copy-start.10
  423.6 70.5 %copy-start.12 = (f32[1,2048]{1,0:T(1,128)S(1)}, f32[1,2048]{1,0:T(1,128)}, u32[]{:S(2)}) copy-start(f32[1,2048]{1,0:T(1,128)} %get-tuple-element.85) | copy-start | bytes 24580
  563.4 6.6 %copy-start.8 = (bf16[4,128,512]{2,1,0:T(8,128)(2,1)S(1)}, bf16[4,128,512]{2,1,0:T(8,128)(2,1)}, u32[]{:S(2)}) copy-start(bf16[4,128,512]{2,1,0:T(8,128)(2,1)} %get-tuple-element.89) | copy-start | bytes 1572868
  569.0 3.0 copy-start.6
  571.0 1.5 copy-start.5
  575.2 1.6 copy-start.7
  575.2 3.0 copy-start.2
  576.9 2.4 copy-start.1

commit v6 on v5

--- a/solution.py
+++ b/solution.py
@@ -383,6 +383,29 @@
         self.to_pair[2].start()
         self.to_pair[1].start()
 
+    def start_near(self, near, marks):
+        self.copy.start()
+        self.to_pair[0].start()
+        copies = [
+            pltpu.make_async_copy(near.at[index], self.whole.at[1 + index], marks.take())
+            for index in range(2)
+        ]
+        for copy in copies:
+            copy.start()
+        for copy in copies:
+            copy.wait()
+        self.pass_x.start()
+        self.pass_y.start()
+        self.to_pair[2].start()
+        self.to_pair[1].start()
+
+    def finish_near(self):
+        for step in range(4):
+            arrived(self.whole.at[4 + step], self.recv[4 + step], self.place.pair)
+        for copy in [self.pass_x, self.pass_y] + self.to_pair:
+            copy.wait_send()
+        self.copy.wait()
+
     def last(self):
         arrived(self.far[0], self.recv[2], self.place.x)
         arrived(self.far[1], self.recv[3], self.place.y)
@@ -545,7 +568,6 @@
     qkv_ref,
     out_ref,
     gate_ref,
-    up_ref,
     down_ref,
     lengths_ref,
     id_col,
@@ -557,11 +579,10 @@
     upstream_ref,
     rows_all,
     gate_rows,
-    up_rows,
     gate_all,
     above_ref,
     below_ref,
-    upstream_all,
+    upstream_near,
     qkv_hbm,
     out_hbm,
     raw_hbm,
@@ -601,9 +622,12 @@
     gate_pieces = Exchange(
         place, lambda p, step: gate_ref.at[p], lambda p, step: gate_rows.at[p], marks
     )
-    up_pieces = Exchange(place, lambda p, step: up_ref.at[p], lambda p, step: up_rows.at[p], marks)
     tokens = TokensGather(place, rows_ref, rows_all, marks)
-    upstream = TokensGather(place, upstream_ref, upstream_all, marks)
+    upstream_recv = [marks.take(), marks.take()]
+    upstream = [
+        remote(upstream_ref, upstream_near.at[index], marks.take(), upstream_recv[index], to)
+        for index, to in enumerate((place.x, place.y))
+    ]
     qkv_line = LineGather(
         place, qkv_all.at[place.z], lambda z: qkv_all.at[z], marks.take(4), marks.take(4)
     )
@@ -740,10 +764,10 @@
     out_line.wait(3)
     out_planes[1].start()
     out_planes[3].start()
-    up_pieces.start()
     lax.fori_loop(1, 2, bucket, 0)
     out_planes[2].forward()
-    upstream.start()
+    for copy in upstream:
+        copy.start()
     lax.fori_loop(2, 3, bucket, 0)
     out_planes[1].forward()
     out_planes[3].forward()
@@ -759,7 +783,6 @@
         copy.wait()
     out_copy.start()
     heads_out.wait()
-    upstream.forward()
 
     def projected(core_step):
         block = jnp.concatenate([attended[p, core_step] for p in range(4)], axis=1)
@@ -779,13 +802,13 @@
     each_rows(rows, 16, norm_work)
     gate_line.wait(1)
     gate_line.wait(3)
-    upstream.last()
-    up_pieces.wait()
+    for index, to in enumerate((place.x, place.y)):
+        arrived(upstream_near.at[index], upstream_recv[index], to)
+        upstream[index].wait_send()
     gate_copy.wait()
     for copy in [qkv_copy, out_copy] + bucket_copies + table_copies:
         copy.wait()
-    upstream.finish()
-    parts = [lengths, qkv_pieces, gate_pieces, up_pieces, heads_out, qkv_line, gate_line, out_line]
+    parts = [lengths, qkv_pieces, gate_pieces, heads_out, qkv_line, gate_line, out_line]
     for part in parts + out_planes:
         part.finish()
 
@@ -805,7 +828,6 @@
     qkv_pieces,
     output_weight,
     gate_pieces,
-    up_pieces,
     down_weight,
     doc_lengths,
     row_ids,
@@ -829,11 +851,10 @@
         out_shape=(
             low_like(8, block_rows, width),
             low_like(*gate_pieces.shape),
-            low_like(*up_pieces.shape),
             low_like(4, *gate_pieces.shape),
             low_like(*down_weight.shape),
             low_like(*down_weight.shape),
-            low_like(8, block_rows, width),
+            low_like(2, block_rows, width),
             low_like(4, *qkv_pieces.shape),
             low_like(4, 4, *output_weight.shape),
             jax.ShapeDtypeStruct((2, 4, block_rows, head_part), jnp.float32),
@@ -846,8 +867,8 @@
             jax.ShapeDtypeStruct((block_rows, width), jnp.float32),
             low_like(block_rows, width),
         ),
-        in_specs=[ANYWHERE] * 6 + [WHOLE] * 7 + [ANYWHERE],
-        out_specs=(ANYWHERE,) * 13 + (WHOLE,) * 5,
+        in_specs=[ANYWHERE] * 5 + [WHOLE] * 7 + [ANYWHERE],
+        out_specs=(ANYWHERE,) * 12 + (WHOLE,) * 5,
         scratch_shapes=[
             pltpu.SemaphoreType.DMA((160,)),
             pltpu.VMEM((4,) + qkv_pieces.shape, LOW),
@@ -869,7 +890,6 @@
         qkv_pieces,
         output_weight,
         gate_pieces,
-        up_pieces,
         down_weight,
         lengths,
         row_ids[:, None],
@@ -1075,12 +1095,15 @@
 def units_kernel(
     rows_ref,
     upstream_ref,
-    line_ref,
+    near_ref,
+    pieces_ref,
     first_ref,
     down_ref,
     above_ref,
     below_ref,
     rows_all,
+    upstream_all,
+    line_ref,
     inner_out,
     second_grad,
     first_sum,
@@ -1104,8 +1127,13 @@
 ):
     place = Place()
     marks = Marks(marks_ref)
-    greet(place, [place.x, place.y, place.pair], True)
+    greet(place, [place.x, place.y, place.d, place.pair], True)
     tokens = TokensGather(place, rows_ref, rows_all, marks)
+    upstream_tokens = TokensGather(place, upstream_ref, upstream, marks)
+    pieces = Exchange(
+        place, lambda p, step: pieces_ref.at[p], lambda p, step: line_ref.at[p], marks
+    )
+    keep = pltpu.make_async_copy(upstream, upstream_all, marks.take())
     line = LineGather(place, line_ref, lambda z: second_mat.at[z], marks.take(4), marks.take(4))
     far_recv = marks.take(2)
     two = down_mat.at[:, place.at(2)]
@@ -1114,11 +1142,10 @@
     pass_down = remote(two, two, pass_mark, far_recv.at[1], place.down)
     pass_up = remote(two, two, pass_mark, far_recv.at[1], place.up)
     copies = [
-        pltpu.make_async_copy(line_ref, second_mat.at[place.z], marks.take()),
         pltpu.make_async_copy(first_ref, first_mat, marks.take()),
         pltpu.make_async_copy(down_ref, down_mat.at[:, place.z], marks.take()),
-        pltpu.make_async_copy(upstream_ref, upstream, marks.take()),
     ]
+    line_copy = pltpu.make_async_copy(line_ref, second_mat.at[place.z], marks.take())
     above = pltpu.make_async_copy(above_ref, down_mat.at[:, place.at(1)], marks.take())
     below = pltpu.make_async_copy(below_ref, down_mat.at[:, place.at(3)], marks.take())
     line_rows = first_sum.shape[0]
@@ -1139,19 +1166,25 @@
     all_rows = 8 * rows_ref.shape[0]
 
     to_two.start()
+    pieces.start()
     tokens.start()
     for copy in copies:
         copy.start()
     pl.when(place.z < 3)(above.start)
     pl.when(place.z > 0)(below.start)
     tokens.forward()
+    upstream_tokens.start_near(near_ref, marks)
+    pieces.wait()
+    line_copy.start()
     arrived(two, far_recv.at[0], place.two)
     pl.when(place.z == 1)(pass_down.start)
     pl.when(place.z == 2)(pass_up.start)
     line.start()
     tokens.last()
+    upstream_tokens.last()
     for copy in copies:
         copy.wait()
+    line_copy.wait()
     pl.when(place.z < 3)(above.wait)
     pl.when(place.z > 0)(below.wait)
 
@@ -1164,6 +1197,9 @@
         arrived(down_mat.at[:, 0], far_recv.at[1], place.two)
 
     tokens.finish()
+    upstream_tokens.finish_near()
+    keep.start()
+    pieces.finish()
 
     def first_work(block, values):
         grads = matmul_nt(upstream[block], down_mat[...].reshape(2 * half, width))
@@ -1219,6 +1255,7 @@
             ),
         )
 
+    keep.wait()
     store_marks = marks.take(4)
 
     def stores(slot, block):
@@ -1297,10 +1334,11 @@
     pl.when(place.z == 2)(pass_up.wait_send)
 
 
-def units_products(rows, upstream, second_rows, first_all, down_weight, above, below):
+def units_products(rows, upstream, near, second_pieces, first_all, down_weight, above, below):
     block_rows, width = rows.shape
     half = first_all.shape[1] // 2
     half_rows = down_weight.shape[1]
+    second_rows = jax.ShapeDtypeStruct((4 * second_pieces.shape[1], 2 * half), LOW)
     hidden = lambda count: jax.ShapeDtypeStruct((8, block_rows, count * half), LOW)
     sums = jax.ShapeDtypeStruct((4, block_rows, width), LOW)
     blocks = jax.ShapeDtypeStruct((8, block_rows, width), LOW)
@@ -1308,6 +1346,8 @@
         units_kernel,
         out_shape=(
             blocks,
+            blocks,
+            jax.ShapeDtypeStruct(second_pieces.shape, LOW),
             hidden(1),
             hidden(2),
             jax.ShapeDtypeStruct(second_rows.shape, LOW),
@@ -1315,12 +1355,12 @@
             sums,
             sums,
         ),
-        in_specs=[ANYWHERE] * 7,
-        out_specs=(ANYWHERE,) * 3 + (WHOLE,) * 4,
+        in_specs=[ANYWHERE] * 8,
+        out_specs=(ANYWHERE,) * 5 + (WHOLE,) * 4,
         scratch_shapes=[
-            pltpu.SemaphoreType.DMA((100,)),
+            pltpu.SemaphoreType.DMA((140,)),
             pltpu.VMEM(first_all.shape, LOW),
-            pltpu.VMEM((4,) + second_rows.shape, LOW),
+            pltpu.VMEM((4,) + second_pieces.shape, LOW),
             pltpu.VMEM((2, 4, half_rows, width), LOW),
             pltpu.VMEM((8, block_rows, width), LOW),
             pltpu.VMEM((2, block_rows, width), LOW),
@@ -1336,7 +1376,7 @@
         + FarScatter.scratch(block_rows, width) * 2,
         compiler_params=comm_params(1),
         cost_estimate=comm_cost(150),
-    )(rows, upstream, second_rows, first_all, down_weight, above, below)
+    )(rows, upstream, near, second_pieces, first_all, down_weight, above, below)
 
 
 def unit_grads_kernel(
@@ -1503,131 +1543,6 @@
     )
 
 
-def last_kernel(
-    parts_ref,
-    qkv_ref,
-    proj_ref,
-    second_ref,
-    input_ref,
-    hidden_ref,
-    norm_ref,
-    gains_ref,
-    grad_ref,
-    qkv_columns,
-    proj_out,
-    second_columns,
-    gains_out,
-    marks_ref,
-    qkv_sum,
-    row_sum,
-    gain_rows,
-    gain_mine,
-    gain_got,
-    *buffers,
-):
-    place = Place()
-    marks = Marks(marks_ref)
-    greet(place, [place.x, place.y, place.d, place.pair], True)
-    tokens = PlaneScatter(place, parts_ref, row_sum, buffers[:1], marks)
-    qkv_line = LineScatter(place, lambda z: qkv_ref.at[z], qkv_sum, buffers[1:2], marks)
-    proj_line = LineScatter(place, lambda z: proj_ref.at[z], proj_out, buffers[2:], marks)
-    rows = qkv_sum.shape[0] // 4
-    qkv_pieces = Exchange(
-        place,
-        lambda p, step: qkv_sum.at[pl.ds(pl.multiple_of(p * rows, rows), rows)],
-        lambda p, step: qkv_columns.at[p],
-        marks,
-    )
-    second_pieces = Exchange(
-        place, lambda p, step: second_ref.at[p], lambda p, step: second_columns.at[p], marks
-    )
-    near_z = {"f": place.z + 1 - 2 * (place.z % 2)}
-    rounds = [
-        remote(gain_mine.at[index], gain_got.at[index], marks.take(), marks.take(), to)
-        for index, to in enumerate((place.pair, place.x, place.y, near_z, place.two))
-    ]
-
-    tokens.start()
-    qkv_line.start()
-    qkv_line.middle()
-    tokens.middle()
-    second_pieces.start()
-    proj_line.start()
-    tokens.finish()
-    proj_line.middle()
-
-    qkv_line.finish()
-    qkv_pieces.start()
-    gain_rows[...] = jnp.zeros_like(gain_rows)
-    norm_row = norm_ref[...]
-
-    def work(rows):
-        values = f32(input_ref[rows])
-        scales = inv_rms(values)
-        upstream = row_sum[rows]
-        weighted = upstream * norm_row
-        inner_mean = jnp.mean(weighted * values, axis=-1, keepdims=True)
-        grad_ref[rows] = (
-            hidden_ref[rows]
-            + scales * weighted
-            - values * (scales * scales * scales) * inner_mean
-        )
-        parts = upstream * values * scales
-        gain_rows[...] += parts[:8] + parts[8:]
-
-    each_rows(row_sum.shape[0], 16, work)
-    width = norm_row.shape[1]
-    gain_mine[0, :, pl.ds(0, width)] = jnp.sum(gain_rows[...], axis=0, keepdims=True)
-    gain_mine[0, :, pl.ds(width, gains_ref.shape[1])] = gains_ref[...]
-    for index, copy in enumerate(rounds):
-        copy.start()
-        copy.wait()
-        summed = gain_mine[index] + gain_got[index]
-        if index < 4:
-            gain_mine[index + 1] = summed
-        else:
-            gains_out[...] = summed
-    proj_line.finish()
-    qkv_line.drain()
-    proj_line.drain()
-    tokens.drain()
-    qkv_pieces.wait()
-    qkv_pieces.finish()
-    second_pieces.wait()
-    second_pieces.finish()
-
-
-def last_sums(parts, qkv_parts, proj_parts, second_rows, layer_input, hidden_grad, norm, gains):
-    rows, width = parts.shape[1:]
-    qkv_rows, qkv_width = qkv_parts.shape[1:]
-    gain_width = width + gains.shape[1]
-    return pl.pallas_call(
-        last_kernel,
-        out_shape=(
-            jax.ShapeDtypeStruct((rows, width), jnp.float32),
-            jax.ShapeDtypeStruct((4, qkv_rows // 4, qkv_width), LOW),
-            jax.ShapeDtypeStruct(proj_parts.shape[1:], LOW),
-            jax.ShapeDtypeStruct(second_rows.shape, LOW),
-            jax.ShapeDtypeStruct((1, gain_width), jnp.float32),
-        ),
-        in_specs=[WHOLE] + [ANYWHERE] * 3 + [WHOLE] * 4,
-        out_specs=(WHOLE, ANYWHERE, WHOLE, ANYWHERE, WHOLE),
-        scratch_shapes=[
-            pltpu.SemaphoreType.DMA((100,)),
-            pltpu.VMEM((qkv_rows, qkv_width), LOW),
-            pltpu.VMEM((rows, width), jnp.float32),
-            pltpu.VMEM((8, width), jnp.float32),
-            pltpu.VMEM((5, 1, gain_width), jnp.float32),
-            pltpu.VMEM((5, 1, gain_width), jnp.float32),
-        ]
-        + PlaneScatter.scratch(rows, width)
-        + LineScatter.scratch(qkv_rows, qkv_width)
-        + LineScatter.scratch(*proj_parts.shape[1:]),
-        compiler_params=comm_params(5),
-        cost_estimate=comm_cost(60),
-    )(parts, qkv_parts, proj_parts, second_rows, layer_input, hidden_grad, norm, gains)
-
-
 def turn_pairs(values, cosine, sine):
     return values * cosine + pltpu.roll(values, HEAD_SIZE // 2, 1) * sine
 
@@ -1696,13 +1611,26 @@
     qkv_ref,
     second_part,
     first_rows,
-    head_gain,
+    input_ref,
+    hidden_ref,
+    norm_ref,
+    mlp_gain,
+    grad_ref,
+    qkv_columns,
+    proj_out,
+    first_columns,
+    second_columns,
+    gains_out,
+    marks_ref,
     qkv_part,
     proj_sum,
     grad_sums,
     line_sum,
-    first_columns,
-    marks_ref,
+    qkv_sum,
+    row_sum,
+    gain_rows,
+    gain_mine,
+    gain_got,
     out_mat,
     qkv_mat,
     attended,
@@ -1730,10 +1658,46 @@
         place,
         proj_part,
         proj_sum,
-        buffers[1:],
+        buffers[1:2],
         marks,
         (place.p, place.px, place.py, place.pd),
     )
+    tokens = PlaneScatter(place, grad_sums, row_sum, buffers[2:3], marks)
+    qkv_rows, proj_rows = qkv_sum.shape[0], proj_out.shape[0]
+    qkv_line = LineScatter(
+        place,
+        lambda z: qkv_part.at[pl.ds(pl.multiple_of(z * qkv_rows, 16), qkv_rows)],
+        qkv_sum,
+        buffers[3:4],
+        marks,
+        True,
+    )
+    proj_line = LineScatter(
+        place,
+        lambda z: proj_sum.at[pl.ds(pl.multiple_of(z * proj_rows, 16), proj_rows)],
+        proj_out,
+        buffers[4:],
+        marks,
+        True,
+    )
+    piece_rows, second_piece = qkv_rows // 4, line_sum.shape[0] // 4
+    qkv_pieces = Exchange(
+        place,
+        lambda p, step: qkv_sum.at[pl.ds(pl.multiple_of(p * piece_rows, 16), piece_rows)],
+        lambda p, step: qkv_columns.at[p],
+        marks,
+    )
+    second_pieces = Exchange(
+        place,
+        lambda p, step: line_sum.at[pl.ds(pl.multiple_of(p * second_piece, 16), second_piece)],
+        lambda p, step: second_columns.at[p],
+        marks,
+    )
+    near_z = {"f": place.z + 1 - 2 * (place.z % 2)}
+    rounds = [
+        remote(gain_mine.at[index], gain_got.at[index], marks.take(), marks.take(), to)
+        for index, to in enumerate((place.pair, place.x, place.y, near_z, place.two))
+    ]
     heads = Exchange(
         place, lambda p, step: own_grad.at[p], lambda p, step: heads_grad.at[step], marks
     )
@@ -1787,7 +1751,9 @@
     heads.wait()
     proj_plane.start()
     first_pieces.start()
-    head_gain[...] = jnp.zeros_like(head_gain)
+    head_width = 2 * HEAD_SIZE
+    head_gain = gain_mine.at[0, :, pl.ds(2 * width, head_width)]
+    head_gain[...] = jnp.zeros((1, head_width), jnp.float32)
 
     def sends(step):
         return remote(
@@ -1846,6 +1812,7 @@
         return carry
 
     lax.fori_loop(0, 4, own_work, 0)
+    tokens.start()
 
     def row_tile(index, carry):
         slab(index).wait()
@@ -1863,14 +1830,54 @@
 
     lax.fori_loop(0, tiles, row_tile, 0)
     second_line.finish()
+    qkv_line.start()
     proj_plane.finish()
+    tokens.middle()
+    second_pieces.start()
+    qkv_line.middle()
+    proj_line.start()
+    tokens.finish()
+    proj_line.middle()
+
+    gain_rows[...] = jnp.zeros_like(gain_rows)
+    norm_row = norm_ref[...]
+
+    def norm_work(part):
+        values = f32(input_ref[part])
+        scales = inv_rms(values)
+        upstream = row_sum[part]
+        weighted = upstream * norm_row
+        inner_mean = jnp.mean(weighted * values, axis=-1, keepdims=True)
+        grad_ref[part] = (
+            hidden_ref[part]
+            + scales * weighted
+            - values * (scales * scales * scales) * inner_mean
+        )
+        parts = upstream * values * scales
+        gain_rows[...] += parts[:8] + parts[8:]
+
+    each_rows(rows, 16, norm_work)
+    gain_mine[0, :, pl.ds(0, width)] = jnp.sum(gain_rows[...], axis=0, keepdims=True)
+    gain_mine[0, :, pl.ds(width, width)] = mlp_gain[...]
+    for index, copy in enumerate(rounds):
+        copy.start()
+        copy.wait()
+        summed = gain_mine[index] + gain_got[index]
+        if index < 4:
+            gain_mine[index + 1] = summed
+        else:
+            gains_out[...] = summed
+    qkv_line.finish()
+    qkv_pieces.start()
+    proj_line.finish()
     for step in range(4):
         sends(step).wait_send()
     heads.finish()
-    for part in (proj_plane, second_line):
+    for part in (proj_plane, second_line, qkv_line, proj_line, tokens):
         part.drain()
-    first_pieces.wait()
-    first_pieces.finish()
+    for part in (first_pieces, second_pieces, qkv_pieces):
+        part.wait()
+        part.finish()
 
 
 def heads_backward(
@@ -1884,26 +1891,46 @@
     qkv_all,
     second_part,
     first_rows,
+    layer_input,
+    hidden_grad,
+    norm,
+    mlp_gain,
 ):
     rows, width = branch.shape
     head_part = raw.shape[3]
     query_part = head_part - 2 * HEAD_SIZE
     line_rows, units = second_part.shape[1:]
+    qkv_rows = width // 4
     tile = 256
+    gain_width = 2 * width + 2 * HEAD_SIZE
+    pieces = jax.ShapeDtypeStruct((4, line_rows // 4, units), LOW)
     return pl.pallas_call(
         heads_back_kernel,
         out_shape=(
-            jax.ShapeDtypeStruct((1, 2 * HEAD_SIZE), jnp.float32),
-            jax.ShapeDtypeStruct((width, head_part), LOW),
-            jax.ShapeDtypeStruct((query_part, width), LOW),
-            jax.ShapeDtypeStruct((4, rows, width), LOW),
-            jax.ShapeDtypeStruct((line_rows, units), LOW),
-            jax.ShapeDtypeStruct((4, line_rows // 4, units), LOW),
+            jax.ShapeDtypeStruct((rows, width), jnp.float32),
+            jax.ShapeDtypeStruct((4, qkv_rows // 4, head_part), LOW),
+            jax.ShapeDtypeStruct((query_part // 4, width), LOW),
+            pieces,
+            pieces,
+            jax.ShapeDtypeStruct((1, gain_width), jnp.float32),
         ),
-        in_specs=[WHOLE] + [ANYWHERE] * 4 + [WHOLE] * len(tables) + [ANYWHERE] * 4,
-        out_specs=(WHOLE,) * 5 + (ANYWHERE,),
+        in_specs=[WHOLE]
+        + [ANYWHERE] * 4
+        + [WHOLE] * len(tables)
+        + [ANYWHERE] * 4
+        + [WHOLE] * 4,
+        out_specs=(WHOLE, ANYWHERE, WHOLE, ANYWHERE, ANYWHERE, WHOLE),
         scratch_shapes=[
-            pltpu.SemaphoreType.DMA((120,)),
+            pltpu.SemaphoreType.DMA((160,)),
+            pltpu.VMEM((width, head_part), LOW),
+            pltpu.VMEM((query_part, width), LOW),
+            pltpu.VMEM((4, rows, width), LOW),
+            pltpu.VMEM((line_rows, units), LOW),
+            pltpu.VMEM((qkv_rows, head_part), LOW),
+            pltpu.VMEM((rows, width), jnp.float32),
+            pltpu.VMEM((8, width), jnp.float32),
+            pltpu.VMEM((5, 1, gain_width), jnp.float32),
+            pltpu.VMEM((5, 1, gain_width), jnp.float32),
             pltpu.VMEM(out_all.shape, LOW),
             pltpu.VMEM(qkv_all.shape, LOW),
             pltpu.VMEM(attended.shape, LOW),
@@ -1917,9 +1944,12 @@
             pltpu.VMEM((4, query_part, width), LOW),
         ]
         + LineScatter.scratch(line_rows, units)
-        + PlaneScatter.scratch(query_part, width),
+        + PlaneScatter.scratch(query_part, width)
+        + PlaneScatter.scratch(rows, width)
+        + LineScatter.scratch(qkv_rows, head_part, True)
+        + LineScatter.scratch(query_part // 4, width, True),
         compiler_params=comm_params(3),
-        cost_estimate=comm_cost(90),
+        cost_estimate=comm_cost(120),
     )(
         branch,
         out_all,
@@ -1931,6 +1961,10 @@
         qkv_all,
         second_part,
         first_rows,
+        layer_input,
+        hidden_grad,
+        norm,
+        mlp_gain,
     )
 
 
@@ -2007,11 +2041,10 @@
     (
         normed_attn,
         _,
-        second_rows,
         first_all,
         above,
         below,
-        grad_all,
+        grad_near,
         qkv_all,
         out_all,
         qkv_raw,
@@ -2028,7 +2061,6 @@
         qkv_pieces,
         output_weight,
         half_pieces(0),
-        half_pieces(1),
         down_halves,
         doc_lengths,
         row_ids,
@@ -2046,11 +2078,22 @@
         row_ids[None, :],
         head_norms,
     )
-    rows_all, inner_low, second_grad, first_rows, grad_down_first, part_sums, grad_sums = (
+    (
+        rows_all,
+        grad_all,
+        _,
+        inner_low,
+        second_grad,
+        first_rows,
+        grad_down_first,
+        part_sums,
+        grad_sums,
+    ) = (
         units_products(
             normed_mlp,
-            grad_all,
-            second_rows.reshape(-1, 2 * half),
+            grad_out,
+            grad_near,
+            half_pieces(1),
             first_all.reshape(model_width, 2 * half),
             down_halves,
             above,
@@ -2077,34 +2120,23 @@
         grad_out,
         mlp_norm[None],
     )
-    (
-        head_gains,
-        grad_qkv_part,
-        grad_proj_part,
-        grad_sums,
-        second_rows,
-        first_columns,
-    ) = heads_backward(
-        branch_grad,
-        out_all.reshape(-1, model_width),
-        attended,
-        qkv_raw,
-        qkv_low,
-        tables,
-        normed_attn,
-        qkv_all.reshape(model_width, head_part),
-        grad_second.reshape(line_shape),
-        first_rows.reshape(4, weight_rows, 2 * half),
-    )
-    grad_input, grad_qkv_columns, grad_out_proj, second_columns, gains = last_sums(
-        grad_sums,
-        grad_qkv_part.reshape(4, 4 * weight_rows, head_part),
-        grad_proj_part.reshape((4,) + output_weight.shape),
-        second_rows.reshape(4, weight_rows, 2 * half),
-        layer_input,
-        hidden_grad,
-        attn_norm[None],
-        jnp.concatenate([mlp_gain_part, head_gains], axis=1),
+    grad_input, grad_qkv_columns, grad_out_proj, first_columns, second_columns, gains = (
+        heads_backward(
+            branch_grad,
+            out_all.reshape(-1, model_width),
+            attended,
+            qkv_raw,
+            qkv_low,
+            tables,
+            normed_attn,
+            qkv_all.reshape(model_width, head_part),
+            grad_second.reshape(line_shape),
+            first_rows.reshape(4, weight_rows, 2 * half),
+            layer_input,
+            hidden_grad,
+            attn_norm[None],
+            mlp_gain_part,
+        )
     )
     gains = gains.reshape(-1)
 

time: 587 us -> 567 us (0.966)
  Pallas kernels: 548 us -> 529 us
    pallas_call x3 -> x2, Pallas kernels: 313 us -> 303 us  [the longest x1 167 us: units_products(): pl.pallas_call(units_kernel, out_shape=(blocks, blocks, jax.ShapeDtypeStr...]
    pallas_call x1, Pallas kernels: 162 us -> 152 us  [first_part(): pl.pallas_call(lambda *refs: first_kernel(documents, *refs), out_shape=(l...]
where the time goes in v6:
time: 567 us; the launch traced here: 561 us
  Pallas kernels  529 us (93%)
  local copies, waits for them, and re-layouts  19.8 us (3%)
  other arithmetic  10.6 us (2%)
    pallas_call x1, Pallas kernels, units_products(): pl.pallas_call(units_kernel, out_shape=(blocks, blocks, jax.ShapeDtypeStr...  167 us
    pallas_call x1, Pallas kernels, first_part(): pl.pallas_call(lambda *refs: first_kernel(documents, *refs), out_shape=(l...  152 us
    pallas_call x1, Pallas kernels, heads_backward(): pl.pallas_call(heads_back_kernel, out_shape=(jax.ShapeDtypeStruct((rows,...  136 us
    pallas_call x1, Pallas kernels, unit_grads(): pl.pallas_call(unit_grads_kernel, out_shape=(jax.ShapeDtypeStruct((rows,...  73.6 us
    unnamed x36, local copies, waits for them, and re-layouts  11.7 us

profile of v6, /device:TPU:0, one launch (start us, length us, event | category | flops | bytes accessed | tf_op | source)
XLA Modules:
  0.0 560.5 jit_solution(1752820263226457219)
XLA Ops:
  1.3 1.6 fusion
  2.9 1.3 pad.4.refs_5_
  4.2 1.0 copy.33
  5.3 1.0 copy.35
  6.5 0.9 copy.43.refs_6_.id_col
  7.7 0.8 pad_maximum_fusion.2.refs_1_
  10.8 0.9 pad_maximum_fusion.1.pieces_ref
  12.0 0.9 pad_maximum_fusion.refs_3_
  12.9 1.3 fusion.2.refs_0_
  14.2 152.2 %shard_map.220 = (bf16[8,256,2048]{2,1,0:T(8,128)(2,1)}, bf16[4,128,768]{2,1,0:T(8,128)(2,1)}, bf16[4,4,128,768]{3,2,1,0:T(8,128)(2,1)}, bf16[2,96,2048]{2,1,0:T...) custom-call(bf16[256,2048]{1,0:T(8,128)(2,1)} %fusion.2.refs_0_, ...), custom_call_target="tpu_custom_call" | custom-call | bytes 390000000 | tf_op jit(solution)/shard_map/pallas_call | solution.py:849
  166.5 166.8 %shard_map.221 = (bf16[8,256,2048]{2,1,0:T(8,128)(2,1)}, bf16[8,256,2048]{2,1,0:T(8,128)(2,1)}, bf16[4,128,768]{2,1,0:T(8,128)(2,1)}, bf16[8,256,384]{2,1,0:T(8,...) custom-call(bf16[256,2048]{1,0:T(8,128)(2,1)} %get-tuple-element.48., ...), custom_call_target="tpu_custom_call" | custom-call | bytes 450000000 | tf_op jit(solution)/shard_map/pallas_call | solution.py:1345
  333.3 73.6 %shard_map.222 = (bf16[256,2048]{1,0:T(8,128)(2,1)}, f32[256,2048]{1,0:T(8,128)}, bf16[256,2048]{1,0:T(8,128)(2,1)}, f32[1,2048]{1,0:T(1,128)}, bf16[2,96,2048]{2,1,0:T(8,128)(2,1)}, /*index=5*/bf16[2048,768]{1,0:T(8,128)(2,1)}) custom-call(bf16[8,256,2048]{2,1,0:T(8,128)(2,1)} %get-tuple-element.53.rows_all, ...), custom_call_target="tpu_custom_call" | custom-call | bytes 195000000 | tf_op jit(solution)/shard_map/pallas_call | solution.py:1506
  406.9 136.2 %shard_map.223 = (f32[256,2048]{1,0:T(8,128)}, bf16[4,128,512]{2,1,0:T(8,128)(2,1)}, bf16[64,2048]{1,0:T(8,128)(2,1)}, bf16[4,128,768]{2,1,0:T(8,128)(2,1)}, bf1...) custom-call(bf16[256,2048]{1,0:T(8,128)(2,1)} %get-tuple-element.62.branch_ref, bf16[1024,2048]{1,0:T(8,128)(2,1)} %bitcast.68, ...), custom_call_target="tpu_custom_call" | custom-call | bytes 360000000 | tf_op jit(solution)/shard_map/pallas_call | solution.py:1907
  543.1 1.3 slice.55
  544.4 1.3 fusion.5
  545.7 1.8 convert_element_type.8
  547.5 1.0 convert_bitcast_fusion.2
  548.7 1.0 copy.58
  549.9 0.8 copy.60
  553.1 1.6 copy.61
  554.9 1.6 copy.62
  556.6 1.4 bitcast_convert_fusion
  557.9 1.0 copy.65
  558.9 1.3 copy.66
  (60 shorter events, 6.5 us)
Async XLA Ops:
  0.6 6.7 %copy-start.9 = (bf16[128,1024]{1,0:T(8,128)(2,1)S(1)}, bf16[128,1024]{1,0:T(8,128)(2,1)}, u32[]{:S(2)}) copy-start(bf16[128,1024]{1,0:T(8,128)(2,1)} %param.16) | copy-start | bytes 786436
  1.3 7.3 %copy-start.3 = (bf16[128,3072]{1,0:T(8,128)(2,1)S(1)}, bf16[128,3072]{1,0:T(8,128)(2,1)}, u32[]{:S(2)}) copy-start(bf16[128,3072]{1,0:T(8,128)(2,1)} %param.21) | copy-start | bytes 2359300
  2.9 6.0 %copy-start.11 = (s32[512]{0:T(512)}, s32[512]{0:T(512)S(1)}, u32[]{:S(2)}) copy-start(s32[512]{0:T(512)S(1)} %pad_add_fusion) | copy-start | bytes 6148
  8.9 1.1 copy-start.4
  10.8 2.2 copy-start
  10.8 2.2 copy-start.10
  543.1 6.6 %copy-start.8 = (bf16[4,128,512]{2,1,0:T(8,128)(2,1)S(1)}, bf16[4,128,512]{2,1,0:T(8,128)(2,1)}, u32[]{:S(2)}) copy-start(bf16[4,128,512]{2,1,0:T(8,128)(2,1)} %get-tuple-element.79) | copy-start | bytes 1572868
  548.7 3.0 copy-start.6
  550.7 1.5 copy-start.5
  554.9 1.6 copy-start.7
  554.9 3.0 copy-start.2
  556.6 2.4 copy-start.1

commit v7 on v6

--- a/solution.py
+++ b/solution.py
@@ -449,7 +449,7 @@
 class LineScatter:
     @staticmethod
     def scratch(rows, width, here=False):
-        return [pltpu.VMEM((4 if here else 6, rows, width), LOW)]
+        return [pltpu.VMEM((4 if here else 5, rows, width), LOW)]
 
     def __init__(self, place, part, out, buffers, marks, here=False):
         self.place, self.out, self.here = place, out, here
@@ -460,7 +460,7 @@
         if here:
             self.mid, self.own = part(place.at(2)), part(z)
         else:
-            self.mid, self.own = kept.at[4], kept.at[5]
+            self.mid, self.own = kept.at[4], self.passed
             self.load_mid = pltpu.make_async_copy(part(place.at(2)), self.mid, marks.take())
             self.load_own = pltpu.make_async_copy(part(z), self.own, marks.take())
         self.recv = [marks.take() for _ in range(4)]
@@ -480,8 +480,6 @@
             self.load_mid.start()
         pl.when((z == 1) | (z == 2))(self.to_down.start)
         pl.when((z == 1) | (z == 2))(self.to_up.start)
-        if not self.here:
-            self.load_own.start()
 
     def add(self, target, other):
         def work(rows):
@@ -504,6 +502,8 @@
         self.to_two.start()
         pl.when(z == 0)(self.to_up.start)
         pl.when(z == 3)(self.to_down.start)
+        if not self.here:
+            self.load_own.start()
 
     def finish(self):
         z = self.place.z
@@ -524,7 +524,7 @@
         out, own, two = self.out, self.own, self.two
 
         def work(rows):
-            out[rows] = low(f32(own[rows]) + f32(two[rows]))
+            out[rows] = (f32(own[rows]) + f32(two[rows])).astype(out.dtype)
 
         each_rows(self.rows, 16, work)
 
@@ -562,12 +562,51 @@
     return segment_col, segment_row, jnp.cos(angles), jnp.sin(angles)
 
 
+def units_split(half, half_rows, weights, out):
+    for p in range(4):
+        parts = []
+        for weight in weights:
+            for z in range(4):
+                start = ((z * 4 + p) * 2 + half) * half_rows
+                parts.append(f32(weight[:, start : start + half_rows]))
+        out[p] = low(jnp.concatenate(parts, axis=1))
+
+
+def units_joined(halves, outs, stage, marks):
+    width = stage.shape[2]
+    half_rows = width // 8
+    copies = []
+    for which, out in enumerate(outs):
+        for z in range(4):
+            slot = z % 2
+            if len(copies) > 1:
+                copies[-2].wait()
+            start = (4 * which + z) * half_rows
+            parts = [
+                f32(columns[p][:, start : start + half_rows])
+                for p in range(4)
+                for columns in halves
+            ]
+            stage[slot] = jnp.concatenate(parts, axis=1)
+            copies.append(
+                pltpu.make_async_copy(
+                    stage.at[slot], out.at[:, pl.ds(z * width, width)], marks.at[slot]
+                )
+            )
+            copies[-1].start()
+    for copy in copies[-2:]:
+        copy.wait()
+
+
 def first_kernel(
     documents,
-    rows_ref,
-    qkv_ref,
+    attn_norm,
+    query_ref,
+    key_ref,
+    value_ref,
+    gate_weight,
+    up_weight,
     out_ref,
-    gate_ref,
     down_ref,
     lengths_ref,
     id_col,
@@ -578,6 +617,7 @@
     norm_ref,
     upstream_ref,
     rows_all,
+    second_pieces,
     gate_rows,
     gate_all,
     above_ref,
@@ -595,6 +635,9 @@
     hidden,
     normed,
     marks_ref,
+    rows_ref,
+    qkv_ref,
+    halves,
     qkv_all,
     out_all,
     raw_out,
@@ -620,7 +663,7 @@
         place, lambda p, step: qkv_ref.at[p], lambda p, step: qkv_all.at[place.z, p], marks
     )
     gate_pieces = Exchange(
-        place, lambda p, step: gate_ref.at[p], lambda p, step: gate_rows.at[p], marks
+        place, lambda p, step: halves.at[0, p], lambda p, step: gate_rows.at[p], marks
     )
     tokens = TokensGather(place, rows_ref, rows_all, marks)
     upstream_recv = [marks.take(), marks.take()]
@@ -673,10 +716,27 @@
         pltpu.make_async_copy(sin_out, sin_hbm, marks.take()),
     ]
 
+    second_copy = pltpu.make_async_copy(halves.at[1], second_pieces, marks.take())
+    half_rows = down_ref.shape[1]
+
     lengths.start()
+    for p in range(4):
+        parts = []
+        for weight in (query_ref, key_ref, value_ref):
+            part = weight.shape[1] // 4
+            parts.append(weight[:, p * part : (p + 1) * part])
+        qkv_ref[p] = jnp.concatenate(parts, axis=1)
     qkv_pieces.start()
+    attn_row = attn_norm[...]
+
+    def rows_work(part):
+        values = f32(input_ref[part])
+        rows_ref[part] = low(values * inv_rms(values) * attn_row)
+
+    each_rows(rows, 16, rows_work)
+    tokens.start()
+    units_split(0, half_rows, (gate_weight, up_weight), halves.at[0])
     gate_pieces.start()
-    tokens.start()
     for copy in own_copies:
         copy.start()
     lengths.wait()
@@ -697,6 +757,8 @@
     lax.fori_loop(0, 2, table_work, 0)
     tokens.forward()
     out_planes[0].start()
+    units_split(1, half_rows, (gate_weight, up_weight), halves.at[1])
+    second_copy.start()
     lax.fori_loop(2, 4, table_work, 0)
     qkv_line.wait(2)
     out_line.start()
@@ -806,6 +868,7 @@
         arrived(upstream_near.at[index], upstream_recv[index], to)
         upstream[index].wait_send()
     gate_copy.wait()
+    second_copy.wait()
     for copy in [qkv_copy, out_copy] + bucket_copies + table_copies:
         copy.wait()
     parts = [lengths, qkv_pieces, gate_pieces, heads_out, qkv_line, gate_line, out_line]
@@ -824,10 +887,13 @@
 
 
 def first_part(
-    rows,
-    qkv_pieces,
+    attn_norm,
+    query_weight,
+    key_matrix,
+    value_matrix,
+    gate_weight,
+    up_weight,
     output_weight,
-    gate_pieces,
     down_weight,
     doc_lengths,
     row_ids,
@@ -836,9 +902,12 @@
     mlp_norm,
     grad_out,
 ):
-    block_rows, width = rows.shape
+    block_rows, width = layer_input.shape
     group_rows = 2 * block_rows
-    weight_rows, head_part = qkv_pieces.shape[1:]
+    weight_rows = query_weight.shape[0]
+    head_part = (query_weight.shape[1] + key_matrix.shape[1] + value_matrix.shape[1]) // 4
+    qkv_pieces = jax.ShapeDtypeStruct((4, weight_rows, head_part), LOW)
+    gate_pieces = jax.ShapeDtypeStruct((4, weight_rows, gate_weight.shape[1] // 4), LOW)
     query_part = head_part - 2 * HEAD_SIZE
     documents = doc_lengths.shape[1]
     lengths = jnp.pad(doc_lengths, ((0, 7), (0, HEAD_SIZE - documents)))
@@ -850,6 +919,7 @@
         lambda *refs: first_kernel(documents, *refs),
         out_shape=(
             low_like(8, block_rows, width),
+            low_like(*gate_pieces.shape),
             low_like(*gate_pieces.shape),
             low_like(4, *gate_pieces.shape),
             low_like(*down_weight.shape),
@@ -867,10 +937,13 @@
             jax.ShapeDtypeStruct((block_rows, width), jnp.float32),
             low_like(block_rows, width),
         ),
-        in_specs=[ANYWHERE] * 5 + [WHOLE] * 7 + [ANYWHERE],
-        out_specs=(ANYWHERE,) * 12 + (WHOLE,) * 5,
+        in_specs=[WHOLE] * 6 + [ANYWHERE] * 2 + [WHOLE] * 7 + [ANYWHERE],
+        out_specs=(ANYWHERE,) * 13 + (WHOLE,) * 5,
         scratch_shapes=[
             pltpu.SemaphoreType.DMA((160,)),
+            pltpu.VMEM((block_rows, width), LOW),
+            pltpu.VMEM(qkv_pieces.shape, LOW),
+            pltpu.VMEM((2,) + gate_pieces.shape, LOW),
             pltpu.VMEM((4,) + qkv_pieces.shape, LOW),
             pltpu.VMEM((4, 4) + output_weight.shape, LOW),
             pltpu.VMEM((2, 4, block_rows, head_part), jnp.float32),
@@ -886,10 +959,13 @@
         compiler_params=comm_params(0),
         cost_estimate=comm_cost(130),
     )(
-        rows,
-        qkv_pieces,
+        attn_norm[None],
+        query_weight,
+        key_matrix,
+        value_matrix,
+        gate_weight,
+        up_weight,
         output_weight,
-        gate_pieces,
         down_weight,
         lengths,
         row_ids[:, None],
@@ -1510,7 +1586,7 @@
             jax.ShapeDtypeStruct((rows, width), jnp.float32),
             jax.ShapeDtypeStruct((rows, width), LOW),
             jax.ShapeDtypeStruct((1, width), jnp.float32),
-            jax.ShapeDtypeStruct((2, half_rows, width), LOW),
+            jax.ShapeDtypeStruct((2, half_rows, width), jnp.float32),
             jax.ShapeDtypeStruct((width, 2 * half), LOW),
         ),
         in_specs=[ANYWHERE] * 7 + [WHOLE] * 3,
@@ -1616,18 +1692,25 @@
     norm_ref,
     mlp_gain,
     grad_ref,
+    query_out,
+    key_out,
+    value_out,
+    proj_out,
+    gate_out,
+    up_out,
+    attn_gain_out,
+    mlp_gain_out,
+    head_gain_out,
+    marks_ref,
     qkv_columns,
-    proj_out,
     first_columns,
     second_columns,
-    gains_out,
-    marks_ref,
+    joined_stage,
     qkv_part,
     proj_sum,
     grad_sums,
     line_sum,
     qkv_sum,
-    row_sum,
     gain_rows,
     gain_mine,
     gain_got,
@@ -1662,7 +1745,7 @@
         marks,
         (place.p, place.px, place.py, place.pd),
     )
-    tokens = PlaneScatter(place, grad_sums, row_sum, buffers[2:3], marks)
+    tokens = PlaneScatter(place, grad_sums, grad_ref, buffers[2:3], marks)
     qkv_rows, proj_rows = qkv_sum.shape[0], proj_out.shape[0]
     qkv_line = LineScatter(
         place,
@@ -1703,6 +1786,7 @@
     )
     to_pair = remote(branch_ref, branch.at[1], marks.take(), marks.take(), place.pair)
     loads = [
+        pltpu.make_async_copy(branch_ref, branch.at[0], marks.take()),
         pltpu.make_async_copy(out_ref, out_mat, marks.take()),
         pltpu.make_async_copy(attended_ref, attended, marks.take()),
         pltpu.make_async_copy(qkv_ref, qkv_mat, marks.take()),
@@ -1714,7 +1798,6 @@
     second_line.start()
     for copy in loads:
         copy.start()
-    branch[0] = branch_ref[...]
     for copy in loads:
         copy.wait()
 
@@ -1845,7 +1928,7 @@
     def norm_work(part):
         values = f32(input_ref[part])
         scales = inv_rms(values)
-        upstream = row_sum[part]
+        upstream = grad_ref[part]
         weighted = upstream * norm_row
         inner_mean = jnp.mean(weighted * values, axis=-1, keepdims=True)
         grad_ref[part] = (
@@ -1866,7 +1949,9 @@
         if index < 4:
             gain_mine[index + 1] = summed
         else:
-            gains_out[...] = summed
+            attn_gain_out[...] = summed[:, :width]
+            mlp_gain_out[...] = summed[:, width : 2 * width]
+            head_gain_out[...] = summed[:, 2 * width :]
     qkv_line.finish()
     qkv_pieces.start()
     proj_line.finish()
@@ -1875,9 +1960,20 @@
     heads.finish()
     for part in (proj_plane, second_line, qkv_line, proj_line, tokens):
         part.drain()
-    for part in (first_pieces, second_pieces, qkv_pieces):
+    for part in (first_pieces, second_pieces):
         part.wait()
         part.finish()
+    units_joined(
+        (first_columns, second_columns), (gate_out, up_out), joined_stage, marks.take(2)
+    )
+    qkv_pieces.wait()
+    qkv_pieces.finish()
+    for p in range(4):
+        start = 0
+        for out in (query_out, key_out, value_out):
+            part = out.shape[1] // 4
+            out[:, p * part : (p + 1) * part] = f32(qkv_columns[p][:, start : start + part])
+            start += part
 
 
 def heads_backward(
@@ -1903,31 +1999,39 @@
     qkv_rows = width // 4
     tile = 256
     gain_width = 2 * width + 2 * HEAD_SIZE
-    pieces = jax.ShapeDtypeStruct((4, line_rows // 4, units), LOW)
+    weight_rows = line_rows // 4
+    pieces = pltpu.VMEM((4, weight_rows, units), LOW)
+    wide = lambda *shape: jax.ShapeDtypeStruct(shape, jnp.float32)
     return pl.pallas_call(
         heads_back_kernel,
         out_shape=(
-            jax.ShapeDtypeStruct((rows, width), jnp.float32),
-            jax.ShapeDtypeStruct((4, qkv_rows // 4, head_part), LOW),
-            jax.ShapeDtypeStruct((query_part // 4, width), LOW),
-            pieces,
-            pieces,
-            jax.ShapeDtypeStruct((1, gain_width), jnp.float32),
+            wide(rows, width),
+            wide(weight_rows, 4 * query_part),
+            wide(weight_rows, 4 * HEAD_SIZE),
+            wide(weight_rows, 4 * HEAD_SIZE),
+            wide(query_part // 4, width),
+            wide(weight_rows, 4 * units),
+            wide(weight_rows, 4 * units),
+            wide(1, width),
+            wide(1, width),
+            wide(1, 2 * HEAD_SIZE),
         ),
-        in_specs=[WHOLE]
-        + [ANYWHERE] * 4
+        in_specs=[ANYWHERE] * 5
         + [WHOLE] * len(tables)
         + [ANYWHERE] * 4
         + [WHOLE] * 4,
-        out_specs=(WHOLE, ANYWHERE, WHOLE, ANYWHERE, ANYWHERE, WHOLE),
+        out_specs=(WHOLE,) * 5 + (ANYWHERE,) * 2 + (WHOLE,) * 3,
         scratch_shapes=[
             pltpu.SemaphoreType.DMA((160,)),
+            pltpu.VMEM((4, weight_rows, head_part), LOW),
+            pieces,
+            pieces,
+            pltpu.VMEM((2, weight_rows, units), jnp.float32),
             pltpu.VMEM((width, head_part), LOW),
             pltpu.VMEM((query_part, width), LOW),
             pltpu.VMEM((4, rows, width), LOW),
             pltpu.VMEM((line_rows, units), LOW),
             pltpu.VMEM((qkv_rows, head_part), LOW),
-            pltpu.VMEM((rows, width), jnp.float32),
             pltpu.VMEM((8, width), jnp.float32),
             pltpu.VMEM((5, 1, gain_width), jnp.float32),
             pltpu.VMEM((5, 1, gain_width), jnp.float32),
@@ -2018,28 +2122,12 @@
     down_rows = down_weight.shape[0]
     half_rows = down_rows // 2
     half = 4 * half_rows
-    qkv_pieces = jnp.concatenate(
-        [heads_of(query_weight), heads_of(key_matrix), heads_of(value_matrix)], axis=2
-    )
-    head_part = qkv_pieces.shape[2]
-    query_part = head_part - 2 * HEAD_SIZE
-    input_float = f32(layer_input)
-
-    def half_pieces(index):
-        return jnp.concatenate(
-            [
-                weight.reshape(weight_rows, 4, 4, 2, half_rows)[:, :, :, index]
-                .transpose(2, 0, 1, 3)
-                .reshape(4, weight_rows, half)
-                for weight in (gate_weight, up_weight)
-            ],
-            axis=2,
-        )
-
+    head_part = (query_weight.shape[1] + key_matrix.shape[1] + value_matrix.shape[1]) // 4
     down_halves = down_weight.reshape(2, half_rows, model_width)
     row_ids = row_ids_of(local_rows)
     (
         normed_attn,
+        second_pieces,
         _,
         first_all,
         above,
@@ -2057,10 +2145,13 @@
         hidden_state,
         normed_mlp,
     ) = first_part(
-        low(input_float * inv_rms(input_float) * attn_norm),
-        qkv_pieces,
+        attn_norm,
+        query_weight,
+        key_matrix,
+        value_matrix,
+        gate_weight,
+        up_weight,
         output_weight,
-        half_pieces(0),
         down_halves,
         doc_lengths,
         row_ids,
@@ -2093,7 +2184,7 @@
             normed_mlp,
             grad_out,
             grad_near,
-            half_pieces(1),
+            second_pieces,
             first_all.reshape(model_width, 2 * half),
             down_halves,
             above,
@@ -2120,7 +2211,18 @@
         grad_out,
         mlp_norm[None],
     )
-    grad_input, grad_qkv_columns, grad_out_proj, first_columns, second_columns, gains = (
+    (
+        grad_input,
+        grad_query,
+        grad_key,
+        grad_value,
+        grad_out_proj,
+        grad_gate,
+        grad_up,
+        attn_gain,
+        mlp_gain,
+        head_gains,
+    ) = (
         heads_backward(
             branch_grad,
             out_all.reshape(-1, model_width),
@@ -2138,29 +2240,19 @@
             mlp_gain_part,
         )
     )
-    gains = gains.reshape(-1)
-
-    def units_joined(offset):
-        halves = [
-            f32(columns[:, :, offset : offset + half]).reshape(4, weight_rows, 4, 1, half_rows)
-            for columns in (first_columns, second_columns)
-        ]
-        joined = jnp.concatenate(halves, axis=3)
-        return joined.transpose(1, 2, 0, 3, 4).reshape(weight_rows, -1)
-
     return (
         layer_out,
         grad_input,
-        gains[:model_width],
-        gains[2 * model_width :].reshape(2, HEAD_SIZE),
-        heads_back(grad_qkv_columns[:, :, :query_part]),
-        heads_back(grad_qkv_columns[:, :, query_part : query_part + HEAD_SIZE]),
-        heads_back(grad_qkv_columns[:, :, query_part + HEAD_SIZE :]),
-        f32(grad_out_proj),
-        gains[model_width : 2 * model_width],
-        units_joined(0),
-        units_joined(half),
-        f32(grad_down).reshape(down_weight.shape),
+        attn_gain.reshape(-1),
+        head_gains.reshape(2, HEAD_SIZE),
+        grad_query,
+        grad_key,
+        grad_value,
+        grad_out_proj,
+        mlp_gain.reshape(-1),
+        grad_gate,
+        grad_up,
+        grad_down.reshape(down_weight.shape),
     )
 
 

time: 567 us -> 550 us (0.970)
  other arithmetic: 10.6 us -> 0.61 us
    pallas_call x1, Pallas kernels: 152 us -> 146 us  [first_part(): pl.pallas_call(lambda *refs: first_kernel(documents, *refs), out_shape=(l...]
    unnamed x36 -> x38, local copies, waits for them, and re-layouts: 11.7 us -> 12.3 us
where the time goes in v7:
time: 550 us; the launch traced here: 545 us
  Pallas kernels  529 us (96%)
  local copies, waits for them, and re-layouts  14.4 us (3%)
    pallas_call x1, Pallas kernels, units_products(): pl.pallas_call(units_kernel, out_shape=(blocks, blocks, jax.ShapeDtypeStr...  169 us
    pallas_call x1, Pallas kernels, first_part(): pl.pallas_call(lambda *refs: first_kernel(documents, *refs), out_shape=(l...  146 us
    pallas_call x1, Pallas kernels, heads_backward(): pl.pallas_call(heads_back_kernel, out_shape=(wide(rows, width), wide(weig...  139 us
    pallas_call x1, Pallas kernels, unit_grads(): pl.pallas_call(unit_grads_kernel, out_shape=(jax.ShapeDtypeStruct((rows,...  75.5 us
    unnamed x38, local copies, waits for them, and re-layouts  12.3 us

profile of v7, /device:TPU:0, one launch (start us, length us, event | category | flops | bytes accessed | tf_op | source)
XLA Modules:
  0.0 545.0 jit_solution(3767510540011628105)
XLA Ops:
  0.7 0.6 maximum_bitcast_fusion.refs_11_
  1.3 0.0 copy-start.9
  1.3 1.3 pad.4.refs_8_
  2.5 0.9 copy.25.refs_9_.id_col
  3.4 0.0 copy-done.9
  3.4 145.8 %shard_map.220 = (bf16[8,256,2048]{2,1,0:T(8,128)(2,1)}, bf16[4,128,768]{2,1,0:T(8,128)(2,1)}, bf16[4,128,768]{2,1,0:T(8,128)(2,1)}, bf16[4,4,128,768]{3,2,1,0:T...) custom-call(f32[1,2048]{1,0:T(1,128)} %bitcast.28, ...), custom_call_target="tpu_custom_call" | custom-call | bytes 390000000 | tf_op jit(solution)/shard_map/pallas_call | solution.py:918
  149.2 168.6 %shard_map.221 = (bf16[8,256,2048]{2,1,0:T(8,128)(2,1)}, bf16[8,256,2048]{2,1,0:T(8,128)(2,1)}, bf16[4,128,768]{2,1,0:T(8,128)(2,1)}, bf16[8,256,384]{2,1,0:T(8,...) custom-call(bf16[256,2048]{1,0:T(8,128)(2,1)} %get-tuple-element.53., ...), custom_call_target="tpu_custom_call" | custom-call | bytes 450000000 | tf_op jit(solution)/shard_map/pallas_call | solution.py:1421
  317.8 75.5 %shard_map.222 = (bf16[256,2048]{1,0:T(8,128)(2,1)}, f32[256,2048]{1,0:T(8,128)}, bf16[256,2048]{1,0:T(8,128)(2,1)}, f32[1,2048]{1,0:T(1,128)}, f32[2,96,2048]{2,1,0:T(8,128)}, /*index=5*/bf16[2048,768]{1,0:T(8,128)(2,1)}) custom-call(bf16[8,256,2048]{2,1,0:T(8,128)(2,1)} %get-tuple-element.59.rows_all, ...), custom_call_target="tpu_custom_call" | custom-call | bytes 195000000 | tf_op jit(solution)/shard_map/pallas_call | solution.py:1582
  393.3 139.1 %shard_map.223 = (f32[256,2048]{1,0:T(8,128)}, f32[128,1024]{1,0:T(8,128)}, f32[128,512]{1,0:T(8,128)}, f32[128,512]{1,0:T(8,128)}, f32[64,2048]{1,0:T(8,128)}, ...) custom-call(bf16[256,2048]{1,0:T(8,128)(2,1)} %get-tuple-element.68., ...), custom_call_target="tpu_custom_call" | custom-call | bytes 360000000 | tf_op jit(solution)/shard_map/pallas_call | solution.py:2005
  532.4 1.0 copy.39
  533.4 1.0 copy-done
  534.4 0.0 copy-start.7
  534.4 1.3 copy.40
  535.7 0.6 copy.41
  536.3 0.6 copy.42
  536.9 0.8 copy.43
  537.7 0.7 copy.44
  538.4 0.7 copy.45
  539.1 0.8 copy.46
  539.9 0.6 copy.47
  540.5 1.1 copy.48
  541.6 1.1 copy.49
  542.8 0.8 copy-done.1
  543.6 1.1 copy.50
  (24 shorter events, 0.1 us)
Async XLA Ops:
  1.3 2.1 copy-start.9
  393.3 139.1 %copy-start.4 = (bf16[256,2048]{1,0:T(8,128)(2,1)S(1)}, bf16[256,2048]{1,0:T(8,128)(2,1)}, u32[]{:S(2)}) copy-start(bf16[256,2048]{1,0:T(8,128)(2,1)} %get-tuple-element.108) | copy-start | bytes 3145732
  532.4 2.0 copy-start
  534.4 1.3 copy-start.11
  534.4 2.0 copy-start.12
  534.4 2.5 copy-start.6
  534.4 3.3 copy-start.8
  534.4 4.0 copy-start.7
  535.7 3.4 copy-start.5
  535.7 4.2 copy-start.10
  535.7 4.8 copy-start.3
  539.1 2.5 copy-start.2
  541.6 2.0 copy-start.1

commit v8 on v7

--- a/solution.py
+++ b/solution.py
@@ -1303,9 +1303,9 @@
         )
     )
     blocks_of(slab, row_slab, slab_marks, 0, tiles, slab_work)
+    first_line.start()
     line.wait(1)
     line.wait(3)
-    first_line.start()
 
     def fetch(index):
         step, slot = 3 - index // 2, index % 2
@@ -1389,9 +1389,8 @@
     lax.fori_loop(0, 1, blocks, 0)
     grad_far.start()
     part_far.start()
-    lax.fori_loop(1, 2, blocks, 0)
     first_line.middle()
-    lax.fori_loop(2, 4, blocks, 0)
+    lax.fori_loop(1, 4, blocks, 0)
     for slot in range(2):
         for copy in stores(slot, 4 * (1 - slot)):
             copy.wait()
@@ -1527,11 +1526,10 @@
     down_part[...] = low(
         matmul_tn(inner[...].reshape(all_rows, half), upstream[...].reshape(all_rows, width))
     )
-    loads[2].wait()
-    blocks_of(slab, row_slab, slab_marks, 0, tiles // 2, slab_work)
     first_line.middle()
     second_line.start()
-    blocks_of(slab, row_slab, slab_marks, tiles // 2, tiles, slab_work)
+    loads[2].wait()
+    blocks_of(slab, row_slab, slab_marks, 0, tiles, slab_work)
     second_line.middle()
     part_near.start()
     gain_rows[...] = jnp.zeros_like(gain_rows)
@@ -1912,15 +1910,15 @@
         return carry
 
     lax.fori_loop(0, tiles, row_tile, 0)
+    qkv_line.start()
     second_line.finish()
-    qkv_line.start()
     proj_plane.finish()
+    proj_line.start()
     tokens.middle()
     second_pieces.start()
     qkv_line.middle()
-    proj_line.start()
+    proj_line.middle()
     tokens.finish()
-    proj_line.middle()
 
     gain_rows[...] = jnp.zeros_like(gain_rows)
     norm_row = norm_ref[...]

time: 550 us -> 532 us (0.967)
  Pallas kernels: 529 us -> 511 us
    pallas_call x1, Pallas kernels: 169 us -> 159 us  [units_products(): pl.pallas_call(units_kernel, out_shape=(blocks, blocks, jax.ShapeDtypeStr...]
    pallas_call x1, Pallas kernels: 75.5 us -> 70 us  [unit_grads(): pl.pallas_call(unit_grads_kernel, out_shape=(jax.ShapeDtypeStruct((rows,...]
where the time goes in v8:
time: 532 us; the launch traced here: 527 us
  Pallas kernels  511 us (96%)
  local copies, waits for them, and re-layouts  14.4 us (3%)
    pallas_call x1, Pallas kernels, units_products(): pl.pallas_call(units_kernel, out_shape=(blocks, blocks, jax.ShapeDtypeStr...  159 us
    pallas_call x1, Pallas kernels, first_part(): pl.pallas_call(lambda *refs: first_kernel(documents, *refs), out_shape=(l...  146 us
    pallas_call x1, Pallas kernels, heads_backward(): pl.pallas_call(heads_back_kernel, out_shape=(wide(rows, width), wide(weig...  135 us
    pallas_call x1, Pallas kernels, unit_grads(): pl.pallas_call(unit_grads_kernel, out_shape=(jax.ShapeDtypeStruct((rows,...  70 us
    unnamed x38, local copies, waits for them, and re-layouts  12.3 us

profile of v8, /device:TPU:0, one launch (start us, length us, event | category | flops | bytes accessed | tf_op | source)
XLA Modules:
  0.0 526.8 jit_solution(15185796505722265286)
XLA Ops:
  0.7 0.6 maximum_bitcast_fusion.refs_11_
  1.3 0.0 copy-start.9
  1.3 1.3 pad.4.refs_8_
  2.5 0.9 copy.25.refs_9_.id_col
  3.4 0.0 copy-done.9
  3.4 146.1 %shard_map.220 = (bf16[8,256,2048]{2,1,0:T(8,128)(2,1)}, bf16[4,128,768]{2,1,0:T(8,128)(2,1)}, bf16[4,128,768]{2,1,0:T(8,128)(2,1)}, bf16[4,4,128,768]{3,2,1,0:T...) custom-call(f32[1,2048]{1,0:T(1,128)} %bitcast.28, ...), custom_call_target="tpu_custom_call" | custom-call | bytes 390000000 | tf_op jit(solution)/shard_map/pallas_call | solution.py:918
  149.5 159.5 %shard_map.221 = (bf16[8,256,2048]{2,1,0:T(8,128)(2,1)}, bf16[8,256,2048]{2,1,0:T(8,128)(2,1)}, bf16[4,128,768]{2,1,0:T(8,128)(2,1)}, bf16[8,256,384]{2,1,0:T(8,...) custom-call(bf16[256,2048]{1,0:T(8,128)(2,1)} %get-tuple-element.53., ...), custom_call_target="tpu_custom_call" | custom-call | bytes 450000000 | tf_op jit(solution)/shard_map/pallas_call | solution.py:1420
  309.0 70.0 %shard_map.222 = (bf16[256,2048]{1,0:T(8,128)(2,1)}, f32[256,2048]{1,0:T(8,128)}, bf16[256,2048]{1,0:T(8,128)(2,1)}, f32[1,2048]{1,0:T(1,128)}, f32[2,96,2048]{2,1,0:T(8,128)}, /*index=5*/bf16[2048,768]{1,0:T(8,128)(2,1)}) custom-call(bf16[8,256,2048]{2,1,0:T(8,128)(2,1)} %get-tuple-element.59.rows_all, ...), custom_call_target="tpu_custom_call" | custom-call | bytes 195000000 | tf_op jit(solution)/shard_map/pallas_call | solution.py:1580
  379.0 135.2 %shard_map.223 = (f32[256,2048]{1,0:T(8,128)}, f32[128,1024]{1,0:T(8,128)}, f32[128,512]{1,0:T(8,128)}, f32[128,512]{1,0:T(8,128)}, f32[64,2048]{1,0:T(8,128)}, ...) custom-call(bf16[256,2048]{1,0:T(8,128)(2,1)} %get-tuple-element.68., ...), custom_call_target="tpu_custom_call" | custom-call | bytes 360000000 | tf_op jit(solution)/shard_map/pallas_call | solution.py:2003
  514.2 1.0 copy.39
  515.2 1.0 copy-done
  516.2 0.0 copy-start.7
  516.2 1.3 copy.40
  517.5 0.6 copy.41
  518.1 0.6 copy.42
  518.7 0.8 copy.43
  519.5 0.7 copy.44
  520.2 0.7 copy.45
  520.9 0.8 copy.46
  521.7 0.6 copy.47
  522.3 1.1 copy.48
  523.5 1.1 copy.49
  524.6 0.8 copy-done.1
  525.4 1.1 copy.50
  (24 shorter events, 0.1 us)
Async XLA Ops:
  1.3 2.1 copy-start.9
  379.0 135.3 %copy-start.4 = (bf16[256,2048]{1,0:T(8,128)(2,1)S(1)}, bf16[256,2048]{1,0:T(8,128)(2,1)}, u32[]{:S(2)}) copy-start(bf16[256,2048]{1,0:T(8,128)(2,1)} %get-tuple-element.108) | copy-start | bytes 3145732
  514.2 2.0 copy-start
  516.2 1.3 copy-start.11
  516.2 2.0 copy-start.12
  516.2 2.5 copy-start.6
  516.2 3.3 copy-start.8
  516.2 4.0 copy-start.7
  517.5 3.4 copy-start.5
  517.5 4.2 copy-start.10
  517.5 4.8 copy-start.3
  520.9 2.5 copy-start.2
  523.5 2.0 copy-start.1

commit v9 on v8

--- a/solution.py
+++ b/solution.py
@@ -769,8 +769,6 @@
     out_line.wait(2)
     out_planes[2].start()
     gate_pieces.wait()
-    gate_line.start()
-    gate_copy.start()
     for copy in table_copies:
         copy.start()
     qkv_copy.start()
@@ -821,9 +819,11 @@
         pl.when(step == 0)(heads_out.copy.start)
         return carry
 
-    lax.fori_loop(0, 1, bucket, 0)
     out_line.wait(1)
     out_line.wait(3)
+    gate_line.start()
+    gate_copy.start()
+    lax.fori_loop(0, 1, bucket, 0)
     out_planes[1].start()
     out_planes[3].start()
     lax.fori_loop(1, 2, bucket, 0)
@@ -1285,7 +1285,6 @@
         first_grad[block] = grad
 
     blocks_of(lambda block: rows_all.at[block], row_block, fetch_marks, 0, 8, first_work)
-    line.wait(2)
     tile = row_slab.shape[3]
     tiles = width // tile
 
@@ -1302,6 +1301,7 @@
             inner_first[...].reshape(all_rows, half), upstream[...].reshape(all_rows, width)
         )
     )
+    line.wait(2)
     blocks_of(slab, row_slab, slab_marks, 0, tiles, slab_work)
     first_line.start()
     line.wait(1)
@@ -1892,9 +1892,6 @@
         grad_sums[step] = low(grad + f32(grad_sums[step]))
         return carry
 
-    lax.fori_loop(0, 4, own_work, 0)
-    tokens.start()
-
     def row_tile(index, carry):
         slab(index).wait()
 
@@ -1911,6 +1908,8 @@
 
     lax.fori_loop(0, tiles, row_tile, 0)
     qkv_line.start()
+    lax.fori_loop(0, 4, own_work, 0)
+    tokens.start()
     second_line.finish()
     proj_plane.finish()
     proj_line.start()

time: 532 us -> 522 us (0.981)
  Pallas kernels: 511 us -> 501 us
where the time goes in v9:
time: 522 us; the launch traced here: 517 us
  Pallas kernels  501 us (96%)
  local copies, waits for them, and re-layouts  14.4 us (3%)
    pallas_call x1, Pallas kernels, units_products(): pl.pallas_call(units_kernel, out_shape=(blocks, blocks, jax.ShapeDtypeStr...  160 us
    pallas_call x1, Pallas kernels, first_part(): pl.pallas_call(lambda *refs: first_kernel(documents, *refs), out_shape=(l...  142 us
    pallas_call x1, Pallas kernels, heads_backward(): pl.pallas_call(heads_back_kernel, out_shape=(wide(rows, width), wide(weig...  133 us
    pallas_call x1, Pallas kernels, unit_grads(): pl.pallas_call(unit_grads_kernel, out_shape=(jax.ShapeDtypeStruct((rows,...  66.5 us
    unnamed x38, local copies, waits for them, and re-layouts  12.3 us

profile of v9, /device:TPU:0, one launch (start us, length us, event | category | flops | bytes accessed | tf_op | source)
XLA Modules:
  0.0 516.9 jit_solution(15429907857598433602)
XLA Ops:
  0.7 0.6 maximum_bitcast_fusion.refs_11_
  1.3 0.0 copy-start.9
  1.3 1.3 pad.4.refs_8_
  2.5 0.9 copy.25.refs_9_.id_col
  3.4 0.0 copy-done.9
  3.4 142.0 %shard_map.220 = (bf16[8,256,2048]{2,1,0:T(8,128)(2,1)}, bf16[4,128,768]{2,1,0:T(8,128)(2,1)}, bf16[4,128,768]{2,1,0:T(8,128)(2,1)}, bf16[4,4,128,768]{3,2,1,0:T...) custom-call(f32[1,2048]{1,0:T(1,128)} %bitcast.28, ...), custom_call_target="tpu_custom_call" | custom-call | bytes 390000000 | tf_op jit(solution)/shard_map/pallas_call | solution.py:918
  145.4 159.7 %shard_map.221 = (bf16[8,256,2048]{2,1,0:T(8,128)(2,1)}, bf16[8,256,2048]{2,1,0:T(8,128)(2,1)}, bf16[4,128,768]{2,1,0:T(8,128)(2,1)}, bf16[8,256,384]{2,1,0:T(8,...) custom-call(bf16[256,2048]{1,0:T(8,128)(2,1)} %get-tuple-element.53., ...), custom_call_target="tpu_custom_call" | custom-call | bytes 450000000 | tf_op jit(solution)/shard_map/pallas_call | solution.py:1420
  305.1 66.5 %shard_map.222 = (bf16[256,2048]{1,0:T(8,128)(2,1)}, f32[256,2048]{1,0:T(8,128)}, bf16[256,2048]{1,0:T(8,128)(2,1)}, f32[1,2048]{1,0:T(1,128)}, f32[2,96,2048]{2,1,0:T(8,128)}, /*index=5*/bf16[2048,768]{1,0:T(8,128)(2,1)}) custom-call(bf16[8,256,2048]{2,1,0:T(8,128)(2,1)} %get-tuple-element.59.rows_all, ...), custom_call_target="tpu_custom_call" | custom-call | bytes 195000000 | tf_op jit(solution)/shard_map/pallas_call | solution.py:1580
  371.6 132.8 %shard_map.223 = (f32[256,2048]{1,0:T(8,128)}, f32[128,1024]{1,0:T(8,128)}, f32[128,512]{1,0:T(8,128)}, f32[128,512]{1,0:T(8,128)}, f32[64,2048]{1,0:T(8,128)}, ...) custom-call(bf16[256,2048]{1,0:T(8,128)(2,1)} %get-tuple-element.68., ...), custom_call_target="tpu_custom_call" | custom-call | bytes 360000000 | tf_op jit(solution)/shard_map/pallas_call | solution.py:2002
  504.3 0.0 copy-start
  504.4 1.0 copy.39
  505.3 1.0 copy-done
  506.3 1.3 copy.40
  507.7 0.6 copy.41
  508.3 0.6 copy.42
  508.8 0.8 copy.43
  509.6 0.7 copy.44
  510.3 0.7 copy.45
  511.0 0.8 copy.46
  511.8 0.6 copy.47
  512.4 1.1 copy.48
  513.6 1.1 copy.49
  514.7 0.8 copy-done.1
  515.6 1.1 copy.50
  (24 shorter events, 0.1 us)
Async XLA Ops:
  1.3 2.1 copy-start.9
  371.5 132.8 %copy-start.4 = (bf16[256,2048]{1,0:T(8,128)(2,1)S(1)}, bf16[256,2048]{1,0:T(8,128)(2,1)}, u32[]{:S(2)}) copy-start(bf16[256,2048]{1,0:T(8,128)(2,1)} %get-tuple-element.108) | copy-start | bytes 3145732
  504.3 2.0 copy-start
  506.3 1.3 copy-start.11
  506.3 2.0 copy-start.12
  506.3 2.5 copy-start.6
  506.3 3.3 copy-start.8
  506.3 4.0 copy-start.7
  507.7 3.4 copy-start.5
  507.7 4.2 copy-start.10
  507.7 4.8 copy-start.3
  511.0 2.5 copy-start.2
  513.6 2.0 copy-start.1
